TPU v7x, 128 devices: a whole 4x4x4 slice. The times are simulated.
128 devices in a mesh: fsdp: 8 (over x_lo, z), ctx: 16 (over y, x_hi, core).
Axes of the slice: x: 4 (x_hi: 2, x_lo: 2; x = x_hi * 2 + x_lo), y: 4, z: 4, core: 2. Of those that a mesh axis runs over, the one named last changes fastest.
Arguments:
- query_in: bfloat16 [16384, 1024], P('ctx', 'fsdp'), may hold values from -6 to 6
- key_in: bfloat16 [16384, 1024], P('ctx', 'fsdp'), may hold values from -6 to 6
- value_in: bfloat16 [16384, 1024], P('ctx', 'fsdp'), may hold values from -6 to 6
- filt: bfloat16 [16384, 1024], P('ctx', 'fsdp'), may hold values from -1 to 1
- w_out: bfloat16 [1024, 8192], P(None, 'fsdp'), may hold values from -0.1875 to 0.1875
- d_out: bfloat16 [16384, 8192], P('ctx', 'fsdp'), may hold values from -6 to 6
Outputs:
- layer_out: bfloat16 [16384, 8192], P('ctx', 'fsdp')
- grad_query: bfloat16 [16384, 1024], P('ctx', 'fsdp')
- grad_key: bfloat16 [16384, 1024], P('ctx', 'fsdp')
- grad_value: bfloat16 [16384, 1024], P('ctx', 'fsdp')
- grad_weight: float32 [1024, 8192], P('ctx', 'fsdp')
All inputs are finite; a program needn't handle non-finite values.
Results may differ from a plain program's by a relative error of at most 0.025.
Values may be sent and summed in bfloat16 or wider, within the bound.
No kernel may reach another device: no remote copies, remote signals or barrier semaphores. Data moves between devices by JAX's collectives and lax.ppermute only.
A program may use at most 128 MiB of HBM per device.

v0:
```python
import math

import jax
import jax.numpy as jnp
from jax import lax
from jax.sharding import PartitionSpec as P

FAC = 1024


def angle_table(rows, cols, modulus):
    product = rows[:, None] * cols[None, :] % modulus
    return product.astype(jnp.float32) * (2.0 * math.pi / modulus)


def square_tables(order):
    index = jnp.arange(order, dtype=jnp.int32)
    angles = angle_table(index, index, order)
    return (jnp.cos(angles).astype(jnp.bfloat16), jnp.sin(angles).astype(jnp.bfloat16))


def first_table(length):
    angles = angle_table(
        jnp.arange(length, dtype=jnp.int32), jnp.arange(length // 2, dtype=jnp.int32), length
    )
    return jnp.concatenate([jnp.cos(angles), -jnp.sin(angles)], axis=0).astype(jnp.bfloat16)


def last_table(length):
    angles = angle_table(
        jnp.arange(length // 2, dtype=jnp.int32), jnp.arange(length, dtype=jnp.int32), length
    )
    return (jnp.concatenate([jnp.cos(angles), -jnp.sin(angles)], axis=1) / length).astype(
        jnp.bfloat16
    )


def apply_square(square, block):
    return jnp.einsum("kt,qtc->qkc", square, block, preferred_element_type=jnp.float32)


def spread_rows(values):
    return lax.all_to_all(values, "ctx", split_axis=2, concat_axis=1, tiled=True)


def spread_cols(values):
    return lax.all_to_all(values, "ctx", split_axis=1, concat_axis=2, tiled=True)


def to_spectrum(signal, tables):
    cosine, sine, first, last = tables
    seq_rows, width = signal.shape
    order = cosine.shape[0]
    ways = lax.axis_size("ctx")
    lanes = order // ways
    freq = first.shape[0] // 2
    local = signal.reshape(1, seq_rows // order, order, width)
    columns = spread_rows(local)[0]
    section = jnp.einsum("kt,tjc->kjc", first, columns, preferred_element_type=jnp.float32)
    real_part, imag_part = (section[:freq], section[freq:])
    offset = lax.axis_index("ctx") * lanes
    angles = angle_table(
        jnp.arange(freq, dtype=jnp.int32), offset + jnp.arange(lanes, dtype=jnp.int32), freq * order
    )
    tw_cos, tw_sin = (jnp.cos(angles)[:, :, None], jnp.sin(angles)[:, :, None])
    turned = jnp.stack(
        [real_part * tw_cos + imag_part * tw_sin, imag_part * tw_cos - real_part * tw_sin]
    ).astype(jnp.bfloat16)
    rows_now = spread_cols(turned)
    spec_re = apply_square(cosine, rows_now[0]) + apply_square(sine, rows_now[1])
    spec_im = apply_square(cosine, rows_now[1]) - apply_square(sine, rows_now[0])
    return (spec_re.astype(jnp.bfloat16), spec_im.astype(jnp.bfloat16))


def to_signal(spec_re, spec_im, tables):
    cosine, sine, first, last = tables
    lanes_freq, order, width = spec_re.shape
    ways = lax.axis_size("ctx")
    lanes = order // ways
    freq = last.shape[1] // 2
    back_re = (apply_square(cosine, spec_re) - apply_square(sine, spec_im)) / order
    back_im = (apply_square(cosine, spec_im) + apply_square(sine, spec_re)) / order
    offset = lax.axis_index("ctx") * lanes_freq
    angles = angle_table(
        offset + jnp.arange(lanes_freq, dtype=jnp.int32),
        jnp.arange(order, dtype=jnp.int32),
        freq * order,
    )
    tw_cos, tw_sin = (jnp.cos(angles)[:, :, None], jnp.sin(angles)[:, :, None])
    turned = jnp.stack(
        [back_re * tw_cos - back_im * tw_sin, back_im * tw_cos + back_re * tw_sin]
    ).astype(jnp.bfloat16)
    columns = spread_rows(turned).reshape(2 * freq, lanes, width)
    section = jnp.einsum("tk,kjc->tjc", last, columns, preferred_element_type=jnp.float32)
    returned = spread_cols(section.astype(jnp.bfloat16)[None])[0]
    return returned.reshape(-1, width)


def spectral_product(a_re, a_im, b_re, b_im):
    a_re, a_im = (a_re.astype(jnp.float32), a_im.astype(jnp.float32))
    b_re, b_im = (b_re.astype(jnp.float32), b_im.astype(jnp.float32))
    return (
        (a_re * b_re - a_im * b_im).astype(jnp.bfloat16),
        (a_re * b_im + a_im * b_re).astype(jnp.bfloat16),
    )


def on_device(query_in, key_in, value_in, filt, w_out, d_out):
    seq_rows, width = query_in.shape
    ways = lax.axis_size("ctx")
    order = FAC
    freq = 2 * seq_rows * ways // order
    cosine, sine = square_tables(order)
    tables = (cosine, sine, first_table(freq), last_table(freq))
    mixed = (key_in.astype(jnp.float32) * value_in.astype(jnp.float32)).astype(jnp.bfloat16)
    partial_y = lax.dot_general(
        d_out, w_out, (((1,), (1,)), ((), ())), preferred_element_type=jnp.float32
    )
    grad_y = lax.psum_scatter(
        partial_y.astype(jnp.bfloat16), "fsdp", scatter_dimension=1, tiled=True
    ).astype(jnp.float32)
    grad_z = (grad_y * query_in.astype(jnp.float32)).astype(jnp.bfloat16)
    mix_re, mix_im = to_spectrum(mixed, tables)
    fil_re, fil_im = to_spectrum(filt, tables)
    conv_re, conv_im = spectral_product(mix_re, mix_im, fil_re, fil_im)
    conv = to_signal(conv_re, conv_im, tables)
    grz_re, grz_im = to_spectrum(grad_z, tables)
    adj_re, adj_im = spectral_product(fil_re, -fil_im, grz_re, grz_im)
    grad_u = to_signal(adj_re, adj_im, tables)
    gated = (query_in.astype(jnp.float32) * conv.astype(jnp.float32)).astype(jnp.bfloat16)
    gated_all = lax.all_gather(gated, "fsdp", axis=1, tiled=True)
    layer_out = jnp.dot(gated_all, w_out, preferred_element_type=jnp.float32).astype(jnp.bfloat16)
    scale = 1.0 / math.sqrt(seq_rows * ways)
    grad_weight = lax.psum_scatter(
        (
            lax.dot_general(
                gated_all, d_out, (((0,), (0,)), ((), ())), preferred_element_type=jnp.float32
            )
            * scale
        ).astype(jnp.bfloat16),
        "ctx",
        scatter_dimension=0,
        tiled=True,
    ).astype(jnp.float32)
    grad_query = (grad_y * conv.astype(jnp.float32)).astype(jnp.bfloat16)
    grad_key = (grad_u.astype(jnp.float32) * value_in.astype(jnp.float32)).astype(jnp.bfloat16)
    grad_value = (grad_u.astype(jnp.float32) * key_in.astype(jnp.float32)).astype(jnp.bfloat16)
    return (layer_out, grad_query, grad_key, grad_value, grad_weight)


def solution(mesh):
    placed = (
        P("ctx", "fsdp"),
        P("ctx", "fsdp"),
        P("ctx", "fsdp"),
        P("ctx", "fsdp"),
        P(None, "fsdp"),
        P("ctx", "fsdp"),
    )
    return jax.shard_map(
        on_device,
        mesh=mesh,
        in_specs=placed,
        out_specs=(
            P("ctx", "fsdp"),
            P("ctx", "fsdp"),
            P("ctx", "fsdp"),
            P("ctx", "fsdp"),
            P("ctx", "fsdp"),
        ),
        check_vma=False,
    )
```

profile of v0, /device:TPU:0, one launch (start us, length us, event | category | flops | bytes accessed | tf_op | source)
XLA Modules:
  0.0 638.2 jit_solution(653153529161007435)
XLA Ops:
  7.2 1.5 copy-done
  8.8 5.3 convolution_convert_fusion
  14.0 3.9 copy.125
  20.0 2.2 reduce.2
  23.0 7.1 %all-to-all-start = ((bf16[16,2,4096]{2,1,0:T(2,128)(2,1)}), bf16[16,2,4096]{2,1,0:T(2,128)(2,1)S(1)}, u32[]{:S(2)}, u32[]{:S(2)}) async-start(bf16[16,2,4096]{2,1,0:T(2,128)(2,1)} %reshape.190), calls=%async_computation | async-start | bytes 524288 | tf_op jit(solution)/shard_map/all_to_all | solution.py:43
  30.6 2.2 reduce.1
  33.6 7.2 %all-to-all-done = bf16[16,2,4096]{2,1,0:T(2,128)(2,1)S(1)} async-done(((bf16[16,2,4096]{2,1,0:T(2,128)(2,1)}), bf16[16,2,4096]{2,1,0:T(2,128)(2,1)S(1)}, u32[]{:S(2)}, u32[]{:S(2)}) %all-to-all-start) | async-done | bytes 262176 | tf_op jit(solution)/shard_map/all_to_all | solution.py:43
  40.8 3.5 all-to-all-start.2
  44.9 12.0 %all-to-all-done.2 = bf16[16,2,4096]{2,1,0:T(2,128)(2,1)S(1)} async-done(((bf16[16,2,4096]{2,1,0:T(2,128)(2,1)}), bf16[16,2,4096]{2,1,0:T(2,128)(2,1)S(1)}, u32[]{:S(2)}, u32[]{:S(2)}) %all-to-all-start.2) | async-done | bytes 262176 | tf_op jit(solution)/shard_map/all_to_all | solution.py:43
  57.2 1.9 fusion.132
  59.1 7.1 %reduce-scatter.7.cloned.1.call-done = bf16[128,1024]{1,0:T(8,128)(2,1)} async-done(((bf16[1024,1024]{1,0:T(8,128)(2,1)}), bf16[128,1024]{1,0:T(8,128)(2,1)}) %reduce-scatter.7.cloned.1.call-update) | async-done | bytes 262160
  66.1 1.1 copy.126
  67.7 2.2 reduce
  70.7 6.2 all-to-all-start.6
  77.0 1.8 fusion.130
  78.8 7.7 %all-to-all-done.6 = bf16[16,2,4096]{2,1,0:T(2,128)(2,1)S(1)} async-done(((bf16[16,2,4096]{2,1,0:T(2,128)(2,1)}), bf16[16,2,4096]{2,1,0:T(2,128)(2,1)S(1)}, u32[]{:S(2)}, u32[]{:S(2)}) %all-to-all-start.6) | async-done | bytes 262176 | tf_op jit(solution)/shard_map/all_to_all | solution.py:43
  87.4 1.0 copy-done.1
  88.4 3.3 fusion.118
  91.7 1.4 copy.75
  93.1 3.7 all-to-all-start.1
  97.0 1.3 pad_maximum_fusion.1
  98.3 1.4 copy.83
  99.7 15.1 %all-to-all-done.1 = bf16[2,32,64,128]{3,2,0,1:T(8,128)(2,1)S(1)} async-done(((bf16[2,32,64,128]{3,2,0,1:T(8,128)(2,1)}), bf16[2,32,64,128]{3,2,0,1:T(8,128)(2,1)S(1)}, u32[]{:S(2)}, u32[]{:S(2)}) %all-to-all-start.1) | async-done | bytes 1048608 | tf_op jit(solution)/shard_map/all_to_all | solution.py:47
  114.8 4.3 all-to-all-start.3
  119.1 1.3 pad_maximum_fusion.3
  120.4 1.4 copy.100
  122.0 0.9 copy.79
  123.0 16.9 %fusion.22 = f32[2,128,1024]{2,1,0:T(8,128)} fusion(bf16[2,1024,128]{2,1,0:T(8,128)(2,1)S(1)} %bitcast.211), kind=kOutput, calls=%fused_computation.21 | convolution fusion | flops 552599552 | bytes 1572864 | tf_op jit(solution)/shard_map/kt,qtc->qkc/dot_general | solution.py:39
  139.9 7.3 %all-to-all-start.7 = ((bf16[2,32,64,128]{3,2,0,1:T(8,128)(2,1)}), bf16[2,32,64,128]{3,2,0,1:T(8,128)(2,1)S(1)}, u32[]{:S(2)}, u32[]{:S(2)}) async-start(bf16[2,32,64,128]{3,2,0,1:T(8,128)(2,1)} %copy.100), calls=%async_computation.7 | async-start | bytes 2097152 | tf_op jit(solution)/shard_map/all_to_all | solution.py:47
  147.3 1.3 copy.84
  148.7 16.2 %fusion.20 = f32[2,128,1024]{2,1,0:T(8,128)S(1)} fusion(bf16[2,1024,128]{2,1,0:T(8,128)(2,1)S(1)} %bitcast.215), kind=kOutput, calls=%fused_computation.20 | convolution fusion | flops 552599552 | bytes 1572864 | tf_op jit(solution)/shard_map/kt,qtc->qkc/dot_general | solution.py:39
  164.9 16.2 %fusion.24 = f32[2,128,1024]{2,1,0:T(8,128)S(1)} fusion(bf16[2,1024,128]{2,1,0:T(8,128)(2,1)S(1)} %bitcast.219), kind=kOutput, calls=%fused_computation.22 | convolution fusion | flops 552599552 | bytes 1572864 | tf_op jit(solution)/shard_map/kt,qtc->qkc/dot_general | solution.py:39
  181.1 18.0 %fusion.84 = bf16[2,128,1024]{2,1,0:T(8,128)(2,1)} fusion(f32[2,128,1024]{2,1,0:T(8,128)S(1)} %fusion.20, bf16[2,1024,128]{2,1,0:T(8,128)(2,1)S(1)} %bitcast.220), kind=kOutput, calls=%fused_computation.56 | convolution fusion | flops 553123840 | bytes 2097152 | tf_op jit(solution)/shard_map/kt,qtc->qkc/dot_general | solution.py:39
  199.2 18.4 %fusion.87 = bf16[2,128,1024]{2,1,0:T(8,128)(2,1)} fusion(f32[2,128,1024]{2,1,0:T(8,128)S(1)} %copy-done.14, bf16[2,1024,128]{2,1,0:T(8,128)(2,1)S(1)} %bitcast.213), kind=kOutput, calls=%fused_computation.57 | convolution fusion | flops 553123840 | bytes 2097152 | tf_op jit(solution)/shard_map/kt,qtc->qkc/dot_general | solution.py:39
  217.6 16.9 %fusion.26 = f32[2,128,1024]{2,1,0:T(8,128)} fusion(bf16[2,1024,128]{2,1,0:T(8,128)(2,1)S(1)} %bitcast.214), kind=kOutput, calls=%fused_computation.23 | convolution fusion | flops 552599552 | bytes 1572864 | tf_op jit(solution)/shard_map/kt,qtc->qkc/dot_general | solution.py:39
  234.5 17.7 %fusion.90 = bf16[2,128,1024]{2,1,0:T(8,128)(2,1)} fusion(f32[2,128,1024]{2,1,0:T(8,128)S(1)} %fusion.24, bf16[2,1024,128]{2,1,0:T(8,128)(2,1)S(1)} %bitcast.216), kind=kOutput, calls=%fused_computation.58 | convolution fusion | flops 553123840 | bytes 2097152 | tf_op jit(solution)/shard_map/kt,qtc->qkc/dot_general | solution.py:39
  252.4 16.3 %fusion.14 = f32[2,128,1024]{2,1,0:T(8,128)S(1)} fusion(bf16[2,1024,128]{2,1,0:T(8,128)(2,1)S(1)} %bitcast.217), kind=kOutput, calls=%fused_computation.17 | convolution fusion | flops 552599552 | bytes 1572864 | tf_op jit(solution)/shard_map/kt,qtc->qkc/dot_general | solution.py:39
  268.8 16.2 %fusion.12 = f32[2,128,1024]{2,1,0:T(8,128)S(1)} fusion(bf16[2,1024,128]{2,1,0:T(8,128)(2,1)S(1)} %bitcast.221), kind=kOutput, calls=%fused_computation.16 | convolution fusion | flops 552599552 | bytes 1572864 | tf_op jit(solution)/shard_map/kt,qtc->qkc/dot_general | solution.py:39
  285.0 16.6 %fusion.81 = bf16[2,128,1024]{2,1,0:T(8,128)(2,1)S(1)} fusion(f32[2,128,1024]{2,1,0:T(8,128)S(1)} %fusion.14, bf16[2,1024,128]{2,1,0:T(8,128)(2,1)S(1)} %bitcast.222), kind=kOutput, calls=%fused_computation.55 | convolution fusion | flops 553123840 | bytes 2097152 | tf_op jit(solution)/shard_map/kt,qtc->qkc/dot_general | solution.py:39
  301.6 16.4 %fusion.78 = bf16[2,128,1024]{2,1,0:T(8,128)(2,1)S(1)} fusion(f32[2,128,1024]{2,1,0:T(8,128)S(1)} %fusion.12, bf16[2,1024,128]{2,1,0:T(8,128)(2,1)S(1)} %bitcast.218), kind=kOutput, calls=%fused_computation.54 | convolution fusion | flops 553123840 | bytes 2097152 | tf_op jit(solution)/shard_map/kt,qtc->qkc/dot_general | solution.py:39
  318.0 16.9 %fusion.122 = (bf16[2,1024,128]{1,2,0:T(8,128)(2,1)S(1)}, bf16[2,1024,128]{1,2,0:T(8,128)(2,1)S(1)}, bf16[2,1024,128]{1,2,0:T(8,128)(2,1)S(1)}, bf16[2,1024,128]{1,2,0:T(8,128)(2,1)S(1)}) fusion(bf16[2,128,1024]{2,1,0:T(8,128)(2,1)S(1)} %fusion.78, bf16[2,128,1024]{2,1,0:T(8,128)(2,1)S(1)} %fusion.81, bf16[2,128,1024]{2,1,0:T(8,128)(2,1)S(1)} %copy-done.18, ...), kind=kOutput, calls=%fused_computation.109 | convolution fusion | flops 559415296 | bytes 6291456 | tf_op jit(solution)/shard_map/kt,qtc->qkc/dot_general | solution.py:39
  334.9 16.4 %fusion.16 = f32[2,128,1024]{2,1,0:T(8,128)S(1)} fusion(bf16[2,1024,128]{1,2,0:T(8,128)(2,1)S(1)} %get-tuple-element.20), kind=kOutput, calls=%fused_computation.18 | convolution fusion | flops 552599552 | bytes 1572864 | tf_op jit(solution)/shard_map/kt,qtc->qkc/dot_general | solution.py:39
  351.3 16.8 %fusion.18 = f32[2,128,1024]{2,1,0:T(8,128)S(1)} fusion(bf16[2,1024,128]{1,2,0:T(8,128)(2,1)S(1)} %get-tuple-element.19), kind=kOutput, calls=%fused_computation.19 | convolution fusion | flops 552599552 | bytes 1572864 | tf_op jit(solution)/shard_map/kt,qtc->qkc/dot_general | solution.py:39
  368.1 16.3 %fusion.63 = f32[2,128,1024]{2,1,0:T(8,128)S(1)} fusion(f32[2,128,1024]{2,1,0:T(8,128)S(1)} %fusion.16, bf16[2,1024,128]{1,2,0:T(8,128)(2,1)S(1)} %get-tuple-element.19), kind=kOutput, calls=%fused_computation.45 | convolution fusion | flops 552861696 | bytes 2621440 | tf_op jit(solution)/shard_map/kt,qtc->qkc/dot_general | solution.py:39
  384.4 16.5 %fusion.60 = f32[2,128,1024]{2,1,0:T(8,128)S(1)} fusion(f32[2,128,1024]{2,1,0:T(8,128)S(1)} %fusion.18, bf16[2,1024,128]{1,2,0:T(8,128)(2,1)S(1)} %get-tuple-element.20), kind=kOutput, calls=%fused_computation.44 | convolution fusion | flops 552861696 | bytes 2621440 | tf_op jit(solution)/shard_map/kt,qtc->qkc/dot_general | solution.py:39
  400.9 16.3 %fusion.10 = f32[2,128,1024]{2,1,0:T(8,128)S(1)} fusion(bf16[2,1024,128]{1,2,0:T(8,128)(2,1)S(1)} %get-tuple-element.16), kind=kOutput, calls=%fused_computation.15 | convolution fusion | flops 552599552 | bytes 1572864 | tf_op jit(solution)/shard_map/kt,qtc->qkc/dot_general | solution.py:39
  417.3 16.6 %fusion.8 = f32[2,128,1024]{2,1,0:T(8,128)S(1)} fusion(bf16[2,1024,128]{1,2,0:T(8,128)(2,1)S(1)} %get-tuple-element.15), kind=kOutput, calls=%fused_computation.14 | convolution fusion | flops 552599552 | bytes 1572864 | tf_op jit(solution)/shard_map/kt,qtc->qkc/dot_general | solution.py:39
  433.9 16.3 %fusion.72 = f32[2,128,1024]{2,1,0:T(8,128)S(1)} fusion(f32[2,128,1024]{2,1,0:T(8,128)S(1)} %fusion.10, bf16[2,1024,128]{1,2,0:T(8,128)(2,1)S(1)} %get-tuple-element.15), kind=kOutput, calls=%fused_computation.48 | convolution fusion | flops 552861696 | bytes 2621440 | tf_op jit(solution)/shard_map/kt,qtc->qkc/dot_general | solution.py:39
  450.2 18.0 %fusion.120 = (bf16[1,2,1024,128]{2,3,1,0:T(8,128)(2,1)}, bf16[1,2,1024,128]{2,3,1,0:T(8,128)(2,1)}, bf16[1,2,1024,128]{2,3,1,0:T(8,128)(2,1)S(1)}, bf16[1,2,1024,128]{2,3,1,0:T(8,128)(2,1)S(1)}) fusion(f32[2,128,1024]{2,1,0:T(8,128)S(1)} %fusion.72, f32[2,1024]{1,0:T(2,128)S(1)} %get-tuple-element.38, f32[2,1024]{1,0:T(2,128)S(1)} %get-tuple-element.37, ...), kind=kOutput, calls=%fused_computation.107 | convolution fusion | flops 557056000 | bytes 6832128 | tf_op jit(solution)/shard_map/kt,qtc->qkc/dot_general | solution.py:39
  468.3 2.0 copy.93
  470.3 7.3 %all-to-all-start.4 = ((bf16[2,2,1024,128]{3,1,0,2:T(2,128)(2,1)}), bf16[2,2,1024,128]{3,1,0,2:T(2,128)(2,1)S(1)}, u32[]{:S(2)}, u32[]{:S(2)}) async-start(bf16[2,2,1024,128]{3,1,0,2:T(2,128)(2,1)} %copy.93), calls=%async_computation.4 | async-start | bytes 2097152 | tf_op jit(solution)/shard_map/all_to_all | solution.py:43
  478.1 17.6 %all-to-all-done.4 = bf16[2,2,1024,128]{3,1,0,2:T(2,128)(2,1)S(1)} async-done(((bf16[2,2,1024,128]{3,1,0,2:T(2,128)(2,1)}), bf16[2,2,1024,128]{3,1,0,2:T(2,128)(2,1)S(1)}, u32[]{:S(2)}, u32[]{:S(2)}) %all-to-all-start.4) | async-done | bytes 1048608 | tf_op jit(solution)/shard_map/all_to_all | solution.py:43
  495.8 1.1 copy.95
  497.2 12.2 %all_to_all.120 = bf16[1,16,64,128]{3,2,0,1:T(8,128)(2,1)S(1)} all-to-all(bf16[1,16,64,128]{3,2,0,1:T(8,128)(2,1)S(1)} %copy.96), channel_id=1, replica_groups=mesh['fsdp'=8,'ctx'=16] {'ctx'}, dimensions={1} | all-to-all | bytes 524288 | tf_op jit(solution)/shard_map/all_to_all | solution.py:47
  510.4 40.0 %all-gather.2.cloned.1.call-done = bf16[1024,1024]{1,0:T(8,128)(2,1)} async-done(((bf16[1024,128]{1,0:T(8,128)(2,1)}), bf16[1024,1024]{1,0:T(8,128)(2,1)}) %all-gather.2.cloned.1.call-update) | async-done | bytes 2097168 | tf_op jit(solution)/shard_map/all_gather | solution.py:131
  550.4 5.3 multiply_convert_fusion
  555.7 1.3 pad_maximum_fusion.4
  557.1 2.0 copy.108
  559.1 24.5 %all_to_all.121 = bf16[2,2,1024,128]{3,1,0,2:T(2,128)(2,1)S(1)} all-to-all(bf16[2,2,1024,128]{3,1,0,2:T(2,128)(2,1)} %copy.108), channel_id=1, replica_groups=mesh['fsdp'=8,'ctx'=16] {'ctx'}, dimensions={2} | all-to-all | bytes 2097152 | tf_op jit(solution)/shard_map/all_to_all | solution.py:43
  583.8 1.1 copy.110
  585.2 15.0 %all_to_all.122 = bf16[1,16,64,128]{3,2,0,1:T(8,128)(2,1)S(1)} all-to-all(bf16[1,16,64,128]{3,2,0,1:T(8,128)(2,1)S(1)} %copy.111), channel_id=1, replica_groups=mesh['fsdp'=8,'ctx'=16] {'ctx'}, dimensions={1} | all-to-all | bytes 524288 | tf_op jit(solution)/shard_map/all_to_all | solution.py:47
  601.2 3.7 convolution_convert_fusion.1
  604.9 24.7 %reduce-scatter.5.cloned.1.call-done = bf16[64,1024]{1,0:T(8,128)(2,1)} async-done(((bf16[1024,1024]{1,0:T(8,128)(2,1)}), bf16[64,1024]{1,0:T(8,128)(2,1)}) %reduce-scatter.5.cloned.1.call-update) | async-done | bytes 131088 | tf_op jit(solution)/shard_map/reduce_scatter | solution.py:134
  629.6 1.6 convert_element_type.320
  (87 shorter events, 11.5 us)
Async XLA Ops:
  7.2 1.6 copy-start
  7.2 58.9 %reduce-scatter.7.cloned.1.call-start = ((), (), s32[]{:S(2)}) async-start(), calls=%async_computation.14 | async-start | bytes 2359296
  18.0 0.9 copy-start.4
  18.0 1.0 copy-start.6
  19.0 11.1 %copy-start.11 = (bf16[1024,128]{1,0:T(8,128)(2,1)S(1)}, bf16[1024,128]{1,0:T(8,128)(2,1)}, u32[]{:S(2)}) copy-start(bf16[1024,128]{1,0:T(8,128)(2,1)} %param.9) | copy-start | bytes 786436
  23.0 17.8 %all-to-all-start = ((bf16[16,2,4096]{2,1,0:T(2,128)(2,1)}), bf16[16,2,4096]{2,1,0:T(2,128)(2,1)S(1)}, u32[]{:S(2)}, u32[]{:S(2)}) async-start(bf16[16,2,4096]{2,1,0:T(2,128)(2,1)} %reshape.190), calls=%async_computation | async-start | bytes 524288 | tf_op jit(solution)/shard_map/all_to_all | solution.py:43
  40.8 16.1 %all-to-all-start.2 = ((bf16[16,2,4096]{2,1,0:T(2,128)(2,1)}), bf16[16,2,4096]{2,1,0:T(2,128)(2,1)S(1)}, u32[]{:S(2)}, u32[]{:S(2)}) async-start(bf16[16,2,4096]{2,1,0:T(2,128)(2,1)} %reshape.188), calls=%async_computation.2 | async-start | bytes 524288 | tf_op jit(solution)/shard_map/all_to_all | solution.py:43
  44.9 22.4 %copy-start.2 = (bf16[1024,128]{1,0:T(8,128)(2,1)S(1)}, bf16[1024,128]{1,0:T(8,128)(2,1)}, u32[]{:S(2)}) copy-start(bf16[1024,128]{1,0:T(8,128)(2,1)} %param.6) | copy-start | bytes 786436
  70.7 15.8 %all-to-all-start.6 = ((bf16[16,2,4096]{2,1,0:T(2,128)(2,1)}), bf16[16,2,4096]{2,1,0:T(2,128)(2,1)S(1)}, u32[]{:S(2)}, u32[]{:S(2)}) async-start(bf16[16,2,4096]{2,1,0:T(2,128)(2,1)} %reshape.192), calls=%async_computation.6 | async-start | bytes 524288 | tf_op jit(solution)/shard_map/all_to_all | solution.py:43
  86.8 1.6 copy-start.1
  93.1 21.6 %all-to-all-start.1 = ((bf16[2,32,64,128]{3,2,0,1:T(8,128)(2,1)}), bf16[2,32,64,128]{3,2,0,1:T(8,128)(2,1)S(1)}, u32[]{:S(2)}, u32[]{:S(2)}) async-start(bf16[2,32,64,128]{3,2,0,1:T(8,128)(2,1)} %copy.75), calls=%async_computation.1 | async-start | bytes 2097152 | tf_op jit(solution)/shard_map/all_to_all | solution.py:47
  114.8 25.2 %all-to-all-start.3 = ((bf16[2,32,64,128]{3,2,0,1:T(8,128)(2,1)}), bf16[2,32,64,128]{3,2,0,1:T(8,128)(2,1)}, u32[]{:S(2)}, u32[]{:S(2)}) async-start(bf16[2,32,64,128]{3,2,0,1:T(8,128)(2,1)} %copy.83), calls=%async_computation.3 | async-start | bytes 2097152 | tf_op jit(solution)/shard_map/all_to_all | solution.py:47
  122.0 1.0 copy-start.8
  139.9 112.2 %all-to-all-start.7 = ((bf16[2,32,64,128]{3,2,0,1:T(8,128)(2,1)}), bf16[2,32,64,128]{3,2,0,1:T(8,128)(2,1)S(1)}, u32[]{:S(2)}, u32[]{:S(2)}) async-start(bf16[2,32,64,128]{3,2,0,1:T(8,128)(2,1)} %copy.100), calls=%async_computation.7 | async-start | bytes 2097152 | tf_op jit(solution)/shard_map/all_to_all | solution.py:47
  181.1 18.1 %copy-start.10 = (bf16[1,2,16,64,128]{4,3,2,1,0:T(8,128)(2,1)S(1)}, bf16[1,2,16,64,128]{4,3,2,1,0:T(8,128)(2,1)}, u32[]{:S(2)}) copy-start(bf16[1,2,16,64,128]{4,3,2,1,0:T(8,128)(2,1)} %copy.79) | copy-start | bytes 1572868
  181.1 18.0 %copy-start.14 = (f32[2,128,1024]{2,1,0:T(8,128)S(1)}, f32[2,128,1024]{2,1,0:T(8,128)}, u32[]{:S(2)}) copy-start(f32[2,128,1024]{2,1,0:T(8,128)} %fusion.22) | copy-start | bytes 3145732
  301.5 16.4 %copy-start.9 = (bf16[1,2,16,64,128]{4,3,2,1,0:T(8,128)(2,1)S(1)}, bf16[1,2,16,64,128]{4,3,2,1,0:T(8,128)(2,1)}, u32[]{:S(2)}) copy-start(bf16[1,2,16,64,128]{4,3,2,1,0:T(8,128)(2,1)} %copy-done.8) | copy-start | bytes 1572868
  301.6 16.4 %copy-start.15 = (f32[2,128,1024]{2,1,0:T(8,128)S(1)}, f32[2,128,1024]{2,1,0:T(8,128)}, u32[]{:S(2)}) copy-start(f32[2,128,1024]{2,1,0:T(8,128)} %fusion.26) | copy-start | bytes 3145732
  301.6 16.4 %copy-start.16 = (bf16[2,128,1024]{2,1,0:T(8,128)(2,1)S(1)}, bf16[2,128,1024]{2,1,0:T(8,128)(2,1)}, u32[]{:S(2)}) copy-start(bf16[2,128,1024]{2,1,0:T(8,128)(2,1)} %fusion.84) | copy-start | bytes 1572868
  301.6 16.4 %copy-start.17 = (bf16[2,128,1024]{2,1,0:T(8,128)(2,1)S(1)}, bf16[2,128,1024]{2,1,0:T(8,128)(2,1)}, u32[]{:S(2)}) copy-start(bf16[2,128,1024]{2,1,0:T(8,128)(2,1)} %fusion.87) | copy-start | bytes 1572868
  301.6 16.4 %copy-start.18 = (bf16[2,128,1024]{2,1,0:T(8,128)(2,1)S(1)}, bf16[2,128,1024]{2,1,0:T(8,128)(2,1)}, u32[]{:S(2)}) copy-start(bf16[2,128,1024]{2,1,0:T(8,128)(2,1)} %fusion.90) | copy-start | bytes 1572868
  470.3 25.3 %all-to-all-start.4 = ((bf16[2,2,1024,128]{3,1,0,2:T(2,128)(2,1)}), bf16[2,2,1024,128]{3,1,0,2:T(2,128)(2,1)S(1)}, u32[]{:S(2)}, u32[]{:S(2)}) async-start(bf16[2,2,1024,128]{3,1,0,2:T(2,128)(2,1)} %copy.93), calls=%async_computation.4 | async-start | bytes 2097152 | tf_op jit(solution)/shard_map/all_to_all | solution.py:43
  477.6 72.8 %all-gather.2.cloned.1.call-start = ((), (), s32[]{:S(2)}) async-start(), calls=%async_computation.12 | async-start | bytes 2359296 | tf_op jit(solution)/shard_map/all_gather | solution.py:131
  495.8 13.6 %copy-start.3 = (bf16[1024,128]{1,0:T(8,128)(2,1)S(1)}, bf16[1024,128]{1,0:T(8,128)(2,1)}, u32[]{:S(2)}) copy-start(bf16[1024,128]{1,0:T(8,128)(2,1)} %param.6) | copy-start | bytes 786436
  510.3 119.2 %reduce-scatter.5.cloned.1.call-start = ((), (), s32[]{:S(2)}) async-start(), calls=%async_computation.13 | async-start | bytes 2228224 | tf_op jit(solution)/shard_map/reduce_scatter | solution.py:134
  583.8 16.5 %copy-start.5 = (bf16[1024,128]{1,0:T(8,128)(2,1)S(1)}, bf16[1024,128]{1,0:T(8,128)(2,1)}, u32[]{:S(2)}) copy-start(bf16[1024,128]{1,0:T(8,128)(2,1)} %param.8) | copy-start | bytes 786436
  583.8 16.5 %copy-start.7 = (bf16[1024,128]{1,0:T(8,128)(2,1)S(1)}, bf16[1024,128]{1,0:T(8,128)(2,1)}, u32[]{:S(2)}) copy-start(bf16[1024,128]{1,0:T(8,128)(2,1)} %param.7) | copy-start | bytes 786436
  583.8 17.4 %copy-start.13 = (bf16[1024,1024]{1,0:T(8,128)(2,1)S(1)}, bf16[1024,1024]{1,0:T(8,128)(2,1)}, u32[]{:S(2)}) copy-start(bf16[1024,1024]{1,0:T(8,128)(2,1)} %all-gather.2.cloned.1.call-done) | copy-start | bytes 6291460
  584.9 16.3 %copy-start.12 = (bf16[1024,1024]{1,0:T(8,128)(2,1)S(1)}, bf16[1024,1024]{1,0:T(8,128)(2,1)}, u32[]{:S(2)}) copy-start(bf16[1024,1024]{1,0:T(8,128)(2,1)} %param.10) | copy-start | bytes 6291460
Sparse Core Ops, SparseCore 0:
  18.1 47.9 reduce-scatter.6
  510.5 39.9 all-gather.1
  555.9 73.6 reduce-scatter.4
where the time goes:
time: 647 us; the launch traced here: 638 us
  matrix products  355 us (55%)
  waiting for transfers between devices  131 us (20%)
  blocking collectives  51.7 us (8%)
  starting transfers between devices  39.9 us (6%)
  local copies, waits for them, and re-layouts  27.3 us (4%)
  other arithmetic  18.2 us (3%)
  between operations  14.8 us (2%)
    dot_general x20, matrix products, apply_square(): jnp.einsum('kt,qtc->qkc', square, block, preferred_element_type=jnp.float32)  336 us
    all_to_all x4, waiting for transfers between devices, spread_rows(): lax.all_to_all(values, 'ctx', split_axis=2, concat_axis=1, tiled=True)  44.4 us
    all_gather x1, waiting for transfers between devices, on_device(): gated_all = lax.all_gather(gated, 'fsdp', axis=1, tiled=True)  40 us
    all_to_all x2, blocking collectives, spread_cols(): lax.all_to_all(values, 'ctx', split_axis=1, concat_axis=2, tiled=True)  27.2 us
    reduce_scatter x1, waiting for transfers between devices, on_device(): lax.psum_scatter((lax.dot_general(gated_all, d_out, (((0,), (0,)), ((), (...  24.7 us
    all_to_all x1, blocking collectives, spread_rows(): lax.all_to_all(values, 'ctx', split_axis=2, concat_axis=1, tiled=True)  24.5 us
    all_to_all x4, starting transfers between devices, spread_rows(): lax.all_to_all(values, 'ctx', split_axis=2, concat_axis=1, tiled=True)  24.2 us
    all_to_all x3, starting transfers between devices, spread_cols(): lax.all_to_all(values, 'ctx', split_axis=1, concat_axis=2, tiled=True)  15.3 us
  transfers between devices with their start and end apart: 10, of which 8 were waited for; matrix products, arithmetic and copies ran while one was open for 24% of the time, Pallas kernels for 0%

commit v1 on v0

v1 whole, which is shorter than its diff:
```python
import functools
import math

import jax
import jax.numpy as jnp
import numpy as np
from jax import lax
from jax.experimental import pallas as pl
from jax.experimental.pallas import tpu as pltpu
from jax.sharding import PartitionSpec as P

FAC = 1024
QF = 32
HALF = QF // 2 + 1
BF = jnp.bfloat16
F32 = jnp.float32
MIB = 1 << 20


def angles(rows, cols, modulus):
    product = (rows[:, None].astype(np.int64) * cols[None, :]) % modulus
    return (product.astype(np.float32) * np.float32(2.0 * math.pi / modulus)).astype(np.float64)


def host_tables(ways, group, sigs):
    k2, t2, t1 = np.arange(HALF), np.arange(ways), np.arange(FAC)
    eye = np.eye(group)
    a = angles(k2, t2, QF)
    steps = np.stack([np.cos(a), -np.sin(a)])
    first = np.einsum("rkt,sp,cd->srkctpd", steps, np.eye(sigs), eye)
    first = first.reshape(sigs * 2 * HALF * group, ways * sigs * group)
    weight = np.where((k2 == 0) | (k2 == QF // 2), 1.0, 2.0)
    b = angles(t2, k2, QF)
    back = np.stack([np.cos(b), -np.sin(b)], axis=1) * weight / (QF * FAC)
    last = np.einsum("trk,cd->tcrkd", back, eye).reshape(ways * group, 2 * HALF * group)
    s = angles(t1, t1, FAC)
    square = np.concatenate([np.cos(s), np.sin(s)])
    w = angles(k2, t1, QF * FAC)
    tc, ts = (np.repeat(f(w), group, axis=0).astype(np.float32) for f in (np.cos, np.sin))
    as_bf = lambda v: np.asarray(v, np.float32).astype(BF)
    return as_bf(first), as_bf(last), as_bf(square), tc, ts


def params(mib):
    return pltpu.CompilerParams(vmem_limit_bytes=mib * MIB)


VMEM = pl.BlockSpec(memory_space=pltpu.VMEM)
SMEM = pl.BlockSpec(memory_space=pltpu.SMEM)


def prep_kernel(k_ref, v_ref, f_ref, q_ref, send_ref, qt_ref):
    ways = send_ref.shape[0]
    mixed = k_ref[...].astype(F32) * v_ref[...].astype(F32)
    mixed_t = mixed.T.reshape(ways, 1, -1, FAC)
    filt_t = f_ref[...].astype(F32).T.reshape(ways, 1, -1, FAC)
    both = jnp.concatenate([mixed_t, filt_t], axis=1)
    send_ref[...] = both.reshape(send_ref.shape).astype(BF)
    qt_ref[...] = q_ref[...].astype(F32).T.astype(BF)


def turn(section, tc, ts):
    n = section.shape[0] // 2
    re, im = section[:n], section[n:]
    b_re, b_im = re * tc + im * ts, im * tc - re * ts
    return (
        jnp.concatenate([b_re, b_im], axis=0).astype(BF),
        jnp.concatenate([b_im, -b_re], axis=0).astype(BF),
    )


def cols_of(j, width):
    return pl.ds(pl.multiple_of(j * width, width), width)


def inverse(y_ref, square_ref, last_ref, tc_ref, ts_ref, out_ref, width):
    n = y_ref.shape[0] // 2

    def back(j, carry):
        cols = cols_of(j, width)
        c = jnp.dot(y_ref[...], square_ref[:, cols], preferred_element_type=F32)
        re, im = c[:n], c[n:]
        tc, ts = tc_ref[:, cols], ts_ref[:, cols]
        e = jnp.concatenate([re * tc - im * ts, im * tc + re * ts], axis=0).astype(BF)
        out_ref[:, cols] = jnp.dot(last_ref[...], e, preferred_element_type=F32).astype(BF)
        return carry

    lax.fori_loop(0, FAC // width, back, 0)


def put_spectrum(y_ref, cols, lower, re, im):
    y_ref[:, cols] = jnp.concatenate([re, im], axis=0).astype(BF)
    y_ref[:, lower] = jnp.concatenate([-im, re], axis=0).astype(BF)


def conv_kernel(width, r_ref, first_ref, last_ref, square_ref, tc_ref, ts_ref, z_ref, h_ref, x_ref, y_ref):
    n = tc_ref.shape[0]
    tc, ts = tc_ref[...], ts_ref[...]
    for s in range(2):
        rows = pl.ds(2 * n * s, 2 * n)
        section = jnp.dot(first_ref[rows, :], r_ref[...], preferred_element_type=F32)
        left, right = turn(section, tc, ts)
        x_ref[rows, pl.ds(0, FAC)] = left
        x_ref[rows, pl.ds(FAC, FAC)] = right

    def forth(j, carry):
        cols = cols_of(j, width)
        lower = pl.ds(pl.multiple_of(FAC + j * width, width), width)
        f = jnp.dot(x_ref[...], square_ref[:, cols], preferred_element_type=F32)
        u_re, u_im, h_re, h_im = f[:n], f[n : 2 * n], f[2 * n : 3 * n], f[3 * n :]
        h_ref[:, cols] = f[2 * n :].astype(BF)
        put_spectrum(y_ref, cols, lower, u_re * h_re - u_im * h_im, u_re * h_im + u_im * h_re)
        return carry

    lax.fori_loop(0, FAC // width, forth, 0)
    inverse(y_ref, square_ref, last_ref, tc_ref, ts_ref, z_ref, width)


def adjoint_kernel(width, r_ref, h_ref, first_ref, last_ref, square_ref, tc_ref, ts_ref, du_ref, x_ref, y_ref):
    n = tc_ref.shape[0]
    section = jnp.dot(first_ref[...], r_ref[...], preferred_element_type=F32)
    left, right = turn(section, tc_ref[...], ts_ref[...])
    x_ref[:, pl.ds(0, FAC)] = left
    x_ref[:, pl.ds(FAC, FAC)] = right

    def forth(j, carry):
        cols = cols_of(j, width)
        lower = pl.ds(pl.multiple_of(FAC + j * width, width), width)
        g = jnp.dot(x_ref[...], square_ref[:, cols], preferred_element_type=F32)
        g_re, g_im = g[:n], g[n:]
        h = h_ref[:, cols].astype(F32)
        h_re, h_im = h[:n], h[n:]
        put_spectrum(y_ref, cols, lower, h_re * g_re + h_im * g_im, h_re * g_im - h_im * g_re)
        return carry

    lax.fori_loop(0, FAC // width, forth, 0)
    inverse(y_ref, square_ref, last_ref, tc_ref, ts_ref, du_ref, width)


def weight_kernel(scale, at_ref, *refs):
    blocks, (d_ref, all_ref, away_ref, keep_ref, left_ref) = refs[:8], refs[8:]
    rows = blocks[0].shape[0]
    for i, block in enumerate(blocks):
        all_ref[pl.ds(pl.multiple_of(at_ref[i] * rows, rows), rows), :] = block[...]
    core = at_ref[8]
    half = rows // 2
    for out_ref, mine in ((away_ref, 1 - core), (keep_ref, core)):
        for g in range(8):
            start = pl.multiple_of(g * rows + mine * half, half)
            left_ref[pl.ds(g * half, half), :] = all_ref[pl.ds(start, half), :]

        def step(j, carry, out_ref=out_ref):
            cols = cols_of(j, 256)
            p = jnp.dot(left_ref[...], d_ref[:, cols], preferred_element_type=F32)
            out_ref[:, cols] = (p * scale).astype(BF)
            return carry

        lax.fori_loop(0, d_ref.shape[1] // 256, step, 0)


def finish_kernel(dy_ref, z_ref, du_ref, k_ref, v_ref, gq_ref, gk_ref, gv_ref):
    gq = dy_ref[...].astype(F32) * z_ref[...].astype(F32)
    gq_ref[...] = gq.T.astype(BF)
    du = du_ref[...].astype(F32).T
    gk_ref[...] = (du * v_ref[...].astype(F32)).astype(BF)
    gv_ref[...] = (du * k_ref[...].astype(F32)).astype(BF)


def call(kernel, outs, ins, scratch=(), mib=40, specs=None, flops=0):
    total = sum(math.prod(o.shape) * o.dtype.itemsize for o in (*outs, *ins))
    return pl.pallas_call(
        kernel,
        out_shape=outs,
        in_specs=specs or [VMEM] * len(ins),
        out_specs=[VMEM] * len(outs),
        scratch_shapes=scratch,
        compiler_params=params(mib),
        cost_estimate=pl.CostEstimate(flops=flops, bytes_accessed=total, transcendentals=0),
    )(*ins)


def shape(*dims, dtype=BF):
    return jax.ShapeDtypeStruct(dims, dtype)


def spread(values):
    return lax.all_to_all(values, "ctx", 0, 0, tiled=True)


def ring(gated):
    pair = [(i, i ^ 4) for i in range(8)]
    up = [(i, (i & 4) | ((i + 1) & 3)) for i in range(8)]
    down = [(i, (i & 4) | ((i - 1) & 3)) for i in range(8)]
    move = lambda v, p: lax.ppermute(v, "fsdp", p)
    other = move(gated, pair)
    own_up, own_down = move(gated, up), move(gated, down)
    other_up, other_down = move(other, up), move(other, down)
    own_far, other_far = move(own_up, up), move(other_down, down)
    me = lax.axis_index("fsdp")
    at = lambda flip, step: (me ^ 4 if flip else me) & 4 | ((me + step) & 3)
    blocks = (gated, other, own_up, own_down, other_up, other_down, own_far, other_far)
    places = (at(0, 0), at(1, 0), at(0, -1), at(0, 1), at(1, -1), at(1, 1), at(0, 2), at(1, 2))
    return blocks, places


def on_device(query_in, key_in, value_in, filt, w_out, d_out):
    seq_rows, width = query_in.shape
    ways = lax.axis_size("ctx")
    group = width // ways
    n = HALF * group
    first2, last, square, tc, ts = map(jnp.asarray, host_tables(ways, group, 2))
    first1 = jnp.asarray(host_tables(ways, group, 1)[0])

    send, query_t = call(
        prep_kernel,
        [shape(ways, 2 * group, seq_rows), shape(width, seq_rows)],
        [key_in, value_in, filt, query_in],
    )
    arrived = spread(send.reshape(ways * 2 * group, seq_rows))
    partial_y = lax.dot_general(w_out, d_out, (((1,), (1,)), ((), ())), preferred_element_type=F32)
    grad_y = lax.psum_scatter(partial_y.astype(BF), "fsdp", scatter_dimension=0, tiled=True)

    product = 2 * 2 * n * 2 * FAC * FAC
    conv, spectrum = call(
        functools.partial(conv_kernel, 256),
        [shape(ways * group, FAC), shape(2 * n, FAC)],
        [arrived, first2, last, square, tc, ts],
        [pltpu.VMEM((4 * n, 2 * FAC), BF), pltpu.VMEM((2 * n, 2 * FAC), BF)],
        flops=3 * product,
    )
    z = spread(conv)
    gated = (query_t.astype(F32) * z.astype(F32)).astype(BF)

    blocks, places = ring(gated)
    core = lax.axis_index("ctx") & 1
    at = jnp.stack([*places, core]).astype(jnp.int32)
    scale = 1.0 / math.sqrt(seq_rows * ways)
    channels, columns = w_out.shape
    gated_all, away, keep = call(
        functools.partial(weight_kernel, scale),
        [shape(channels, seq_rows), shape(channels // 2, columns), shape(channels // 2, columns)],
        [at, *blocks, d_out],
        [pltpu.VMEM((channels // 2, seq_rows), BF)],
        specs=[SMEM] + [VMEM] * 9,
        flops=2 * channels * seq_rows * columns,
    )
    swapped = lax.ppermute(away, "ctx", [(i, i ^ 1) for i in range(ways)])
    summed = (keep.astype(F32) + swapped.astype(F32)).astype(BF)
    groups = [list(range(c, ways, 2)) for c in range(2)]
    parts = lax.all_to_all(summed, "ctx", 0, 0, tiled=True, axis_index_groups=groups)
    grad_weight = jnp.sum(parts.reshape(ways // 2, channels // ways, columns).astype(F32), axis=0)
    layer_out = lax.dot_general(
        gated_all, w_out, (((0,), (0,)), ((), ())), preferred_element_type=F32
    ).astype(BF)

    grad_z = (grad_y.astype(F32) * query_t.astype(F32)).astype(BF)
    (adjoint,) = call(
        functools.partial(adjoint_kernel, 256),
        [shape(ways * group, FAC)],
        [spread(grad_z), spectrum, first1, last, square, tc, ts],
        [pltpu.VMEM((2 * n, 2 * FAC), BF), pltpu.VMEM((2 * n, 2 * FAC), BF)],
        flops=2 * product,
    )
    grad_u = spread(adjoint)
    like = shape(seq_rows, width)
    grad_query, grad_key, grad_value = call(
        finish_kernel, [like, like, like], [grad_y, z, grad_u, key_in, value_in]
    )
    return (layer_out, grad_query, grad_key, grad_value, grad_weight)


def solution(mesh):
    both = P("ctx", "fsdp")
    return jax.shard_map(
        on_device,
        mesh=mesh,
        in_specs=(both, both, both, both, P(None, "fsdp"), both),
        out_specs=(both, both, both, both, both),
        check_vma=False,
    )
```

time: 647 us -> 168 us (0.26); the launches traced: 638 us -> 167 us
  matrix products: 355 us -> 10.6 us
  waiting for transfers between devices: 131 us -> 29.7 us
  starting transfers between devices: 39.9 us -> 19.7 us
  Pallas kernels: 0 us -> 20.1 us
  local copies, waits for them, and re-layouts: 27.3 us -> 14.8 us
  other arithmetic: 18.2 us -> 6.54 us
    dot_general x28 -> x2, matrix products: 355 us -> 10.6 us  [the longest x1 5.3 us: on_device(): lax.dot_general(gated_all, w_out, (((0,), (0,)), ((), ())), preferred_ele...]
    all_to_all x7 -> x2, waiting for transfers between devices: 59.5 us -> 16.6 us  [the longest x1 9.67 us: on_device(): lax.all_to_all(summed, 'ctx', 0, 0, tiled=True, axis_index_groups=groups)]
    all_gather x1 -> x0, waiting for transfers between devices: 40 us -> none  [on_device(): gated_all = lax.all_gather(gated, 'fsdp', axis=1, tiled=True)]
    all_to_all x7 -> x2, starting transfers between devices: 39.5 us -> 8.61 us  [the longest x1 4.42 us: on_device(): lax.all_to_all(summed, 'ctx', 0, 0, tiled=True, axis_index_groups=groups)]
    reduce_scatter x1, waiting for transfers between devices: 24.7 us -> 0.01 us  [on_device(): lax.psum_scatter(partial_y.astype(BF), 'fsdp', scatter_dimension=0, tiled...]
    pallas_call x0 -> x5, Pallas kernels: none -> 20.1 us  [call(): pl.pallas_call(kernel, out_shape=outs, in_specs=specs or [VMEM] * len(ins...]
    ppermute x0 -> x8, waiting for transfers between devices: none -> 13.1 us  [the longest x7 13.1 us: ring(): move = lambda v, p: lax.ppermute(v, 'fsdp', p)]
    ppermute x0 -> x8, starting transfers between devices: none -> 11.1 us  [the longest x7 11.1 us: ring(): move = lambda v, p: lax.ppermute(v, 'fsdp', p)]
  transfers between devices with their start and end apart: 10 -> 11, of which waited for: 8 -> 7; matrix products, arithmetic and copies ran while one was open for 24% -> 5% of each run, Pallas kernels for 0% -> 9%
where the time goes in v1:
time: 168 us; the launch traced here: 167 us
  blocking collectives  51.1 us (30%)
  waiting for transfers between devices  29.7 us (18%)
  Pallas kernels  20.1 us (12%)
  starting transfers between devices  19.7 us (12%)
  local copies, waits for them, and re-layouts  14.8 us (9%)
  between operations  14.2 us (8%)
  matrix products  10.6 us (6%)
  other arithmetic  6.54 us (4%)
    all_to_all x3, blocking collectives, spread(): return lax.all_to_all(values, 'ctx', 0, 0, tiled=True)  51.1 us
    pallas_call x5, Pallas kernels, call(): pl.pallas_call(kernel, out_shape=outs, in_specs=specs or [VMEM] * len(ins...  20.1 us
    unnamed x62, local copies, waits for them, and re-layouts  14.7 us
    ppermute x7, waiting for transfers between devices, ring(): move = lambda v, p: lax.ppermute(v, 'fsdp', p)  13.1 us
    ppermute x7, starting transfers between devices, ring(): move = lambda v, p: lax.ppermute(v, 'fsdp', p)  11.1 us
    all_to_all x1, waiting for transfers between devices, on_device(): lax.all_to_all(summed, 'ctx', 0, 0, tiled=True, axis_index_groups=groups)  9.67 us
    all_to_all x1, waiting for transfers between devices, spread(): return lax.all_to_all(values, 'ctx', 0, 0, tiled=True)  6.94 us
    dot_general x1, matrix products, on_device(): lax.dot_general(gated_all, w_out, (((0,), (0,)), ((), ())), preferred_ele...  5.3 us
  transfers between devices with their start and end apart: 11, of which 7 were waited for; matrix products, arithmetic and copies ran while one was open for 5% of the time, Pallas kernels for 9%

profile of v1, /device:TPU:0, one launch (start us, length us, event | category | flops | bytes accessed | tf_op | source)
XLA Modules:
  0.0 166.8 jit_solution(4311009948591388493)
XLA Ops:
  7.2 0.0 copy-start
  7.2 0.0 reduce-scatter.2.cloned.1.call-start
  7.2 1.5 copy-done
  8.8 5.3 %convolution_convert_fusion = bf16[1024,1024]{1,0:T(8,128)(2,1)} fusion(bf16[1024,1024]{1,0:T(8,128)(2,1)S(1)} %copy-done, bf16[1024,1024]{1,0:T(8,128)(2,1)} %refs_8_.1), kind=kOutput, calls=%fused_computation.2 | convolution fusion | flops 2148532224 | bytes 6291456 | tf_op jit(solution)/shard_map/dot_general | solution.py:220
  14.1 0.0 copy-start.25
  14.1 0.0 reduce-scatter.2.cloned.1.call-update
  14.1 0.9 copy-done.2
  15.0 0.1 copy-done.4
  15.1 0.1 copy-done.9
  15.1 0.1 copy-done.10
  15.2 0.3 shard_map.155
  15.5 23.0 %all_to_all.50 = bf16[16,16,1024]{2,1,0:T(8,128)(2,1)S(1)} all-to-all(bf16[16,16,1024]{2,1,0:T(8,128)(2,1)S(1)} %get-tuple-element.16), channel_id=1, replica_groups=mesh['fsdp'=8,'ctx'=16] {'ctx'}, dimensions={0} | all-to-all | bytes 1048576 | tf_op jit(solution)/shard_map/all_to_all | solution.py:187
  38.5 0.0 copy-done.25
  38.5 0.0 copy-start.18
  38.5 2.2 %copy-done.18 = bf16[2048,1024]{1,0:T(8,128)(2,1)S(1)} copy-done((bf16[2048,1024]{1,0:T(8,128)(2,1)S(1)}, bf16[2048,1024]{1,0:T(8,128)(2,1)}, u32[]{:S(2)}) %copy-start.18) | copy-done | bytes 4194328
  40.8 6.7 %shard_map.156 = (bf16[128,1024]{1,0:T(8,128)(2,1)S(1)}, bf16[272,1024]{1,0:T(8,128)(2,1)S(1)}) custom-call(bf16[256,1024]{1,0:T(8,128)(2,1)S(1)} %bitcast.24, bf16[544,256]{1,0:T(8,128)(2,1)S(1)} %copy-done.24, bf16[128,272]{1,0:T(8,128)(2,1)S(1)} %copy-done.25, bf16[2048,1024]{1,0:T(8,128)(2,1)S(1)} %copy-done.18, f32[136,1024]{1,0:T(8,128)S(1)} %copy-done.22, ...), custom_call_target="tpu_custom_call" | custom-call | flops 3422552064 | bytes 7000064 | tf_op jit(solution)/shard_map/pallas_call | solution.py:171
  47.5 0.8 copy-done.27
  48.3 14.9 %all_to_all.51 = bf16[16,8,1024]{2,1,0:T(8,128)(2,1)S(1)} all-to-all(bf16[16,8,1024]{2,1,0:T(8,128)(2,1)S(1)} %bitcast.27), channel_id=1, replica_groups=mesh['fsdp'=8,'ctx'=16] {'ctx'}, dimensions={0} | all-to-all | bytes 524288 | tf_op jit(solution)/shard_map/all_to_all | solution.py:187
  63.2 1.8 %fusion.2 = (bf16[16,8,1024]{2,1,0:T(8,128)(2,1)}, bf16[128,1024]{1,0:T(8,128)(2,1)S(1)}) fusion(bf16[128,1024]{1,0:T(8,128)(2,1)S(1)} %get-tuple-element.15, bf16[128,1024]{1,0:T(8,128)(2,1)} %reduce-scatter.2.cloned.1.call-done.dy_ref, bf16[16,8,1024]{2,1,0:T(8,128)(2,1)S(1)} %all_to_all.51), kind=kLoop, calls=%fused_computation.8 | loop fusion | flops 917504 | bytes 1310720 | tf_op jit(solution)/shard_map/all_to_all | solution.py:187
  65.1 1.4 collective-permute-start
  66.4 0.0 collective-permute-start.1
  66.4 6.3 %collective-permute-done.refs_1_ = bf16[128,1024]{1,0:T(8,128)(2,1)S(1)} collective-permute-done((bf16[128,1024]{1,0:T(8,128)(2,1)S(1)}, bf16[128,1024]{1,0:T(8,128)(2,1)S(1)}, u32[]{:S(2)}, u32[]{:S(2)}) %collective-permute-start) | collective-permute-done | bytes 262176 | tf_op jit(solution)/shard_map/ppermute | solution.py:194
  72.7 4.0 %collective-permute-start.4 = (bf16[128,1024]{1,0:T(8,128)(2,1)S(1)}, bf16[128,1024]{1,0:T(8,128)(2,1)S(1)}, u32[]{:S(2)}, u32[]{:S(2)}) collective-permute-start(bf16[128,1024]{1,0:T(8,128)(2,1)S(1)} %collective-permute-done.refs_1_), channel_id=1, source_target_pairs={{0,48},{16,0},{32,16},{48,32},{64,112},{80,64},{96,80},{112,96},{1... | collective-permute-start | bytes 786440 | tf_op jit(solution)/shard_map/ppermute | solution.py:194
  76.7 0.0 collective-permute-start.2
  76.7 0.7 copy-done.6
  77.4 2.0 %collective-permute-start.3 = (bf16[128,1024]{1,0:T(8,128)(2,1)S(1)}, bf16[128,1024]{1,0:T(8,128)(2,1)}, u32[]{:S(2)}, u32[]{:S(2)}) collective-permute-start(bf16[128,1024]{1,0:T(8,128)(2,1)S(1)} %collective-permute-done.refs_1_), channel_id=1, source_target_pairs={{0,16},{16,32},{32,48},{48,0},{64,80},{80,96},{96,112},{112,64},{1... | collective-permute-start | bytes 786440 | tf_op jit(solution)/shard_map/ppermute | solution.py:194
  79.4 0.7 copy-done.12
  80.1 0.0 collective-permute-done.1.refs_2_
  80.1 0.0 collective-permute-start.5
  80.1 0.7 copy-done.14
  80.8 2.6 %collective-permute-done.4.refs_5_ = bf16[128,1024]{1,0:T(8,128)(2,1)S(1)} collective-permute-done((bf16[128,1024]{1,0:T(8,128)(2,1)S(1)}, bf16[128,1024]{1,0:T(8,128)(2,1)S(1)}, u32[]{:S(2)}, u32[]{:S(2)}) %collective-permute-start.4) | collective-permute-done | bytes 262176 | tf_op jit(solution)/shard_map/ppermute | solution.py:194
  83.4 3.7 %collective-permute-start.6 = (bf16[128,1024]{1,0:T(8,128)(2,1)S(1)}, bf16[128,1024]{1,0:T(8,128)(2,1)}, u32[]{:S(2)}, u32[]{:S(2)}) collective-permute-start(bf16[128,1024]{1,0:T(8,128)(2,1)S(1)} %collective-permute-done.4.refs_5_), channel_id=1, source_target_pairs={{0,48},{16,0},{32,16},{48,32},{64,112},{80,64},{96,80},{112,96},{1... | collective-permute-start | bytes 786440 | tf_op jit(solution)/shard_map/ppermute | solution.py:194
  87.1 0.7 copy-done.16
  87.8 0.1 stack.39.at_ref
  87.9 1.1 collective-permute-done.2.refs_3_
  89.0 1.7 %collective-permute-done.5.refs_6_ = bf16[128,1024]{1,0:T(8,128)(2,1)} collective-permute-done((bf16[128,1024]{1,0:T(8,128)(2,1)S(1)}, bf16[128,1024]{1,0:T(8,128)(2,1)}, u32[]{:S(2)}, u32[]{:S(2)}) %collective-permute-start.5) | collective-permute-done | bytes 262176 | tf_op jit(solution)/shard_map/ppermute | solution.py:194
  90.7 0.0 collective-permute-done.3.refs_4_
  90.7 1.4 collective-permute-done.6.refs_7_
  92.1 0.9 copy-done.7
  93.1 1.6 copy-done.11
  94.7 0.9 copy-done.13
  95.6 0.9 copy-done.15
  96.6 0.9 copy-done.17
  97.5 0.0 copy-start.26
  97.5 5.8 %shard_map.157 = (bf16[1024,1024]{1,0:T(8,128)(2,1)S(1)}, bf16[512,1024]{1,0:T(8,128)(2,1)}, bf16[512,1024]{1,0:T(8,128)(2,1)S(1)}) custom-call(s32[9]{0:T(128)S(1)} %stack.39.at_ref, bf16[128,1024]{1,0:T(8,128)(2,1)S(1)} %copy-done.7, bf16[128,1024]{1,0:T(8,128)(2,1)S(1)} %copy-done.13, bf16[128,1024]{1,0:T(8,128)(2,1)S(1)} %copy-done.15, ...), custom_call_target="tpu_custom_call" | custom-call | flops 2147483648 | bytes 8388644 | tf_op jit(solution)/shard_map/pallas_call | solution.py:171
  103.3 0.0 collective-permute-start.7
  103.3 0.0 copy-done.30
  103.3 13.2 %all_to_all.52 = bf16[16,8,1024]{2,1,0:T(8,128)(2,1)S(1)} all-to-all(bf16[16,8,1024]{2,1,0:T(8,128)(2,1)S(1)} %copy-done.30), channel_id=1, replica_groups=mesh['fsdp'=8,'ctx'=16] {'ctx'}, dimensions={0} | all-to-all | bytes 524288 | tf_op jit(solution)/shard_map/all_to_all | solution.py:187
  116.5 0.0 copy-done.26
  116.5 0.0 copy-done.28
  116.5 5.4 %shard_map.158 = bf16[128,1024]{1,0:T(8,128)(2,1)S(1)} custom-call(bf16[128,1024]{1,0:T(8,128)(2,1)S(1)} %bitcast.26, bf16[272,1024]{1,0:T(8,128)(2,1)S(1)} %copy-done.28, bf16[272,128]{1,0:T(8,128)(2,1)S(1)} %copy-done.26, bf16[128,272]{1,0:T(8,128)(2,1)S(1)} %copy-done.25, bf16[2048,1024]{1,0:T(8,128)(2,1)S(1)} %copy-done.19, f32[136,1024]{1,0:T(8,128)S(1)} %copy-done.23, ...), custom_call_target="tpu_custom_call" | custom-call | flops 2281701376 | bytes 6529024 | tf_op jit(solution)/shard_map/pallas_call | solution.py:171
  121.9 0.0 copy-done.29
  121.9 0.0 copy-start.8
  121.9 0.7 copy-done.8
  122.6 4.2 %all-to-all-start.3 = ((bf16[16,8,1024]{2,1,0:T(8,128)(2,1)}), bf16[16,8,1024]{2,1,0:T(8,128)(2,1)}, u32[]{:S(2)}, u32[]{:S(2)}) async-start(bf16[16,8,1024]{2,1,0:T(8,128)(2,1)} %bitcast.25), calls=%async_computation.4 | async-start | bytes 524288 | tf_op jit(solution)/shard_map/all_to_all | solution.py:187
  126.8 0.0 collective-permute-done.7
  126.8 2.6 %add_convert_fusion = bf16[512,1024]{1,0:T(8,128)(2,1)} fusion(bf16[512,1024]{1,0:T(8,128)(2,1)} %collective-permute-done.7, bf16[512,1024]{1,0:T(8,128)(2,1)S(1)} %get-tuple-element.23), kind=kLoop, calls=%fused_computation.1 | loop fusion | flops 2097152 | bytes 3145728 | tf_op jit(solution)/shard_map/convert_element_type | solution.py:248
  129.4 6.9 %all-to-all-done.3 = bf16[16,8,1024]{2,1,0:T(8,128)(2,1)} async-done(((bf16[16,8,1024]{2,1,0:T(8,128)(2,1)}), bf16[16,8,1024]{2,1,0:T(8,128)(2,1)}, u32[]{:S(2)}, u32[]{:S(2)}) %all-to-all-start.3) | async-done | bytes 262176 | tf_op jit(solution)/shard_map/all_to_all | solution.py:187
  136.4 4.4 %all-to-all-start.4 = ((bf16[8,64,1024]{2,1,0:T(8,128)(2,1)}), bf16[8,64,1024]{2,1,0:T(8,128)(2,1)}, u32[]{:S(2)}, u32[]{:S(2)}) async-start(bf16[8,64,1024]{2,1,0:T(8,128)(2,1)} %bitcast.28), calls=%async_computation.5 | async-start | bytes 2097152 | tf_op jit(solution)/shard_map/all_to_all | solution.py:250
  140.8 0.0 copy-done.1
  140.8 2.0 %shard_map.159 = (bf16[1024,128]{1,0:T(8,128)(2,1)}, bf16[1024,128]{1,0:T(8,128)(2,1)}, bf16[1024,128]{1,0:T(8,128)(2,1)}) custom-call(bf16[128,1024]{1,0:T(8,128)(2,1)S(1)} %copy-done.1, bf16[128,1024]{1,0:T(8,128)(2,1)S(1)} %bitcast.23, bf16[128,1024]{1,0:T(8,128)(2,1)} %bitcast.15.du_ref, bf16[1024,128]{1,0:T(8,128)(2,1)S(1)} %copy-done.3, ...), custom_call_target="tpu_custom_call" | custom-call | bytes 2097152 | tf_op jit(solution)/shard_map/pallas_call | solution.py:171
  142.8 5.3 %convolution_convert_fusion.1 = bf16[1024,1024]{1,0:T(8,128)(2,1)} fusion(bf16[1024,1024]{1,0:T(8,128)(2,1)} %copy-done.29, bf16[1024,1024]{1,0:T(8,128)(2,1)S(1)} %copy-done), kind=kOutput, calls=%fused_computation.3 | convolution fusion | flops 2148532224 | bytes 6291456 | tf_op jit(solution)/shard_map/dot_general | solution.py:252
  148.1 9.7 %all-to-all-done.4 = bf16[8,64,1024]{2,1,0:T(8,128)(2,1)} async-done(((bf16[8,64,1024]{2,1,0:T(8,128)(2,1)}), bf16[8,64,1024]{2,1,0:T(8,128)(2,1)}, u32[]{:S(2)}, u32[]{:S(2)}) %all-to-all-start.4) | async-done | bytes 1048608 | tf_op jit(solution)/shard_map/all_to_all | solution.py:250
  157.8 2.1 %convert_reduce_fusion = f32[64,1024]{1,0:T(8,128)} fusion(bf16[8,64,1024]{2,1,0:T(8,128)(2,1)} %all-to-all-done.4), kind=kLoop, calls=%fused_computation | loop fusion | flops 983040 | bytes 1310720 | tf_op jit(solution)/shard_map/reduce_sum | solution.py:251
  (35 shorter events, 0.1 us)
Async XLA Ops:
  7.2 1.6 copy-start
  7.2 56.1 %reduce-scatter.2.cloned.1.call-start = ((), (), s32[]{:S(2)}) async-start(), calls=%async_computation.6 | async-start | bytes 2359296 | tf_op jit(solution)/shard_map/reduce_scatter | solution.py:221
  14.0 0.9 copy-start.2
  14.0 1.0 copy-start.4
  14.0 1.1 copy-start.9
  14.0 1.2 copy-start.10
  14.1 24.4 %copy-start.25 = (bf16[128,272]{1,0:T(8,128)(2,1)S(1)}, bf16[128,272]{1,0:T(8,128)(2,1)}, u32[]{:S(2)}) copy-start(bf16[128,272]{1,0:T(8,128)(2,1)} %constant.34.clone.last_ref) | copy-start | bytes 208900
  15.2 23.3 %copy-start.20 = (f32[136,1024]{1,0:T(8,128)S(1)}, f32[136,1024]{1,0:T(8,128)}, u32[]{:S(2)}) copy-start(f32[136,1024]{1,0:T(8,128)} %constant.37.clone.ts_ref) | copy-start | bytes 1671172
  15.2 23.3 %copy-start.22 = (f32[136,1024]{1,0:T(8,128)S(1)}, f32[136,1024]{1,0:T(8,128)}, u32[]{:S(2)}) copy-start(f32[136,1024]{1,0:T(8,128)} %constant.36.clone.tc_ref) | copy-start | bytes 1671172
  15.2 23.3 %copy-start.24 = (bf16[544,256]{1,0:T(8,128)(2,1)S(1)}, bf16[544,256]{1,0:T(8,128)(2,1)}, u32[]{:S(2)}) copy-start(bf16[544,256]{1,0:T(8,128)(2,1)} %constant.33.clone.first_ref) | copy-start | bytes 835588
  38.5 2.2 %copy-start.18 = (bf16[2048,1024]{1,0:T(8,128)(2,1)S(1)}, bf16[2048,1024]{1,0:T(8,128)(2,1)}, u32[]{:S(2)}) copy-start(bf16[2048,1024]{1,0:T(8,128)(2,1)} %constant.35.clone.square_ref) | copy-start | bytes 12582916
  47.5 0.8 copy-start.27
  65.1 7.6 %collective-permute-start = (bf16[128,1024]{1,0:T(8,128)(2,1)S(1)}, bf16[128,1024]{1,0:T(8,128)(2,1)S(1)}, u32[]{:S(2)}, u32[]{:S(2)}) collective-permute-start(bf16[128,1024]{1,0:T(8,128)(2,1)S(1)} %get-tuple-element.26.refs_0_), channel_id=1, source_target_pairs={{0,64},{16,80},{32,96},{48,112},{64,0},{80,16},{96,32},{112,48},{1... | collective-permute-start | bytes 786440 | tf_op jit(solution)/shard_map/ppermute | solution.py:194
  66.4 13.7 %collective-permute-start.1 = (bf16[128,1024]{1,0:T(8,128)(2,1)S(1)}, bf16[128,1024]{1,0:T(8,128)(2,1)S(1)}, u32[]{:S(2)}, u32[]{:S(2)}) collective-permute-start(bf16[128,1024]{1,0:T(8,128)(2,1)S(1)} %get-tuple-element.26.refs_0_), channel_id=1, source_target_pairs={{0,16},{16,32},{32,48},{48,0},{64,80},{80,96},{96,112},{112,64},{1... | collective-permute-start | bytes 786440 | tf_op jit(solution)/shard_map/ppermute | solution.py:194
  72.7 10.7 %collective-permute-start.4 = (bf16[128,1024]{1,0:T(8,128)(2,1)S(1)}, bf16[128,1024]{1,0:T(8,128)(2,1)S(1)}, u32[]{:S(2)}, u32[]{:S(2)}) collective-permute-start(bf16[128,1024]{1,0:T(8,128)(2,1)S(1)} %collective-permute-done.refs_1_), channel_id=1, source_target_pairs={{0,48},{16,0},{32,16},{48,32},{64,112},{80,64},{96,80},{112,96},{1... | collective-permute-start | bytes 786440 | tf_op jit(solution)/shard_map/ppermute | solution.py:194
  76.7 12.4 %collective-permute-start.2 = (bf16[128,1024]{1,0:T(8,128)(2,1)S(1)}, bf16[128,1024]{1,0:T(8,128)(2,1)}, u32[]{:S(2)}, u32[]{:S(2)}) collective-permute-start(bf16[128,1024]{1,0:T(8,128)(2,1)S(1)} %get-tuple-element.26.refs_0_), channel_id=1, source_target_pairs={{0,48},{16,0},{32,16},{48,32},{64,112},{80,64},{96,80},{112,96},{1... | collective-permute-start | bytes 786440 | tf_op jit(solution)/shard_map/ppermute | solution.py:194
  76.7 0.7 copy-start.6
  77.4 13.4 %collective-permute-start.3 = (bf16[128,1024]{1,0:T(8,128)(2,1)S(1)}, bf16[128,1024]{1,0:T(8,128)(2,1)}, u32[]{:S(2)}, u32[]{:S(2)}) collective-permute-start(bf16[128,1024]{1,0:T(8,128)(2,1)S(1)} %collective-permute-done.refs_1_), channel_id=1, source_target_pairs={{0,16},{16,32},{32,48},{48,0},{64,80},{80,96},{96,112},{112,64},{1... | collective-permute-start | bytes 786440 | tf_op jit(solution)/shard_map/ppermute | solution.py:194
  79.4 0.7 copy-start.12
  80.1 10.7 %collective-permute-start.5 = (bf16[128,1024]{1,0:T(8,128)(2,1)S(1)}, bf16[128,1024]{1,0:T(8,128)(2,1)}, u32[]{:S(2)}, u32[]{:S(2)}) collective-permute-start(bf16[128,1024]{1,0:T(8,128)(2,1)S(1)} %collective-permute-done.1.refs_2_), channel_id=1, source_target_pairs={{0,16},{16,32},{32,48},{48,0},{64,80},{80,96},{96,112},{112,64},{1... | collective-permute-start | bytes 786440 | tf_op jit(solution)/shard_map/ppermute | solution.py:194
  80.1 0.7 copy-start.14
  83.4 8.7 %collective-permute-start.6 = (bf16[128,1024]{1,0:T(8,128)(2,1)S(1)}, bf16[128,1024]{1,0:T(8,128)(2,1)}, u32[]{:S(2)}, u32[]{:S(2)}) collective-permute-start(bf16[128,1024]{1,0:T(8,128)(2,1)S(1)} %collective-permute-done.4.refs_5_), channel_id=1, source_target_pairs={{0,48},{16,0},{32,16},{48,32},{64,112},{80,64},{96,80},{112,96},{1... | collective-permute-start | bytes 786440 | tf_op jit(solution)/shard_map/ppermute | solution.py:194
  87.1 0.7 copy-start.16
  92.1 0.9 copy-start.7
  93.1 1.6 copy-start.11
  94.6 0.9 copy-start.13
  95.6 0.9 copy-start.15
  96.6 0.9 copy-start.17
  97.5 5.8 %copy-start.30 = (bf16[16,8,1024]{2,1,0:T(8,128)(2,1)S(1)}, bf16[16,8,1024]{2,1,0:T(8,128)(2,1)}, u32[]{:S(2)}) copy-start(bf16[16,8,1024]{2,1,0:T(8,128)(2,1)} %get-tuple-element.25) | copy-start | bytes 786436
  97.5 19.0 %copy-start.19 = (bf16[2048,1024]{1,0:T(8,128)(2,1)S(1)}, bf16[2048,1024]{1,0:T(8,128)(2,1)}, u32[]{:S(2)}) copy-start(bf16[2048,1024]{1,0:T(8,128)(2,1)} %constant.35.clone.square_ref) | copy-start | bytes 12582916
  97.5 19.0 %copy-start.21 = (f32[136,1024]{1,0:T(8,128)S(1)}, f32[136,1024]{1,0:T(8,128)}, u32[]{:S(2)}) copy-start(f32[136,1024]{1,0:T(8,128)} %constant.37.clone.ts_ref) | copy-start | bytes 1671172
  97.5 19.0 %copy-start.23 = (f32[136,1024]{1,0:T(8,128)S(1)}, f32[136,1024]{1,0:T(8,128)}, u32[]{:S(2)}) copy-start(f32[136,1024]{1,0:T(8,128)} %constant.36.clone.tc_ref) | copy-start | bytes 1671172
  97.5 19.0 %copy-start.26 = (bf16[272,128]{1,0:T(8,128)(2,1)S(1)}, bf16[272,128]{1,0:T(8,128)(2,1)}, u32[]{:S(2)}) copy-start(bf16[272,128]{1,0:T(8,128)(2,1)} %constant.38.clone.first_ref) | copy-start | bytes 208900
  97.5 19.0 %copy-start.28 = (bf16[272,1024]{1,0:T(8,128)(2,1)S(1)}, bf16[272,1024]{1,0:T(8,128)(2,1)}, u32[]{:S(2)}) copy-start(bf16[272,1024]{1,0:T(8,128)(2,1)} %copy-done.27) | copy-start | bytes 1671172
  103.3 18.6 %copy-start.29 = (bf16[1024,1024]{1,0:T(8,128)(2,1)}, bf16[1024,1024]{1,0:T(8,128)(2,1)S(1)}, u32[]{:S(2)}) copy-start(bf16[1024,1024]{1,0:T(8,128)(2,1)S(1)} %get-tuple-element.18) | copy-start | bytes 6291460
  103.3 23.5 %collective-permute-start.7 = (bf16[512,1024]{1,0:T(8,128)(2,1)}, bf16[512,1024]{1,0:T(8,128)(2,1)}, u32[]{:S(2)}, u32[]{:S(2)}) collective-permute-start(bf16[512,1024]{1,0:T(8,128)(2,1)} %get-tuple-element.24), channel_id=1, source_target_pairs={{0,1},{1,0},{2,3},{3,2},{4,5},{5,4},{6,7},{7,6},{8,9},{9,8},{10,11... | collective-permute-start | bytes 3145736 | tf_op jit(solution)/shard_map/ppermute | solution.py:247
  121.9 0.7 copy-start.8
  122.6 13.8 %all-to-all-start.3 = ((bf16[16,8,1024]{2,1,0:T(8,128)(2,1)}), bf16[16,8,1024]{2,1,0:T(8,128)(2,1)}, u32[]{:S(2)}, u32[]{:S(2)}) async-start(bf16[16,8,1024]{2,1,0:T(8,128)(2,1)} %bitcast.25), calls=%async_computation.4 | async-start | bytes 524288 | tf_op jit(solution)/shard_map/all_to_all | solution.py:187
  129.4 11.4 %copy-start.1 = (bf16[128,1024]{1,0:T(8,128)(2,1)S(1)}, bf16[128,1024]{1,0:T(8,128)(2,1)}, u32[]{:S(2)}) copy-start(bf16[128,1024]{1,0:T(8,128)(2,1)} %reduce-scatter.2.cloned.1.call-done.dy_ref) | copy-start | bytes 786436
  129.4 11.4 %copy-start.3 = (bf16[1024,128]{1,0:T(8,128)(2,1)S(1)}, bf16[1024,128]{1,0:T(8,128)(2,1)}, u32[]{:S(2)}) copy-start(bf16[1024,128]{1,0:T(8,128)(2,1)} %k_ref.3) | copy-start | bytes 786436
  129.4 11.4 %copy-start.5 = (bf16[1024,128]{1,0:T(8,128)(2,1)S(1)}, bf16[1024,128]{1,0:T(8,128)(2,1)}, u32[]{:S(2)}) copy-start(bf16[1024,128]{1,0:T(8,128)(2,1)} %v_ref.3) | copy-start | bytes 786436
  136.4 21.4 %all-to-all-start.4 = ((bf16[8,64,1024]{2,1,0:T(8,128)(2,1)}), bf16[8,64,1024]{2,1,0:T(8,128)(2,1)}, u32[]{:S(2)}, u32[]{:S(2)}) async-start(bf16[8,64,1024]{2,1,0:T(8,128)(2,1)} %bitcast.28), calls=%async_computation.5 | async-start | bytes 2097152 | tf_op jit(solution)/shard_map/all_to_all | solution.py:250
Sparse Core Ops, SparseCore 0:
  14.2 48.5 reduce-scatter.1

commit v2 on v1

--- a/solution.py
+++ b/solution.py
@@ -20,6 +20,12 @@
 def angles(rows, cols, modulus):
     product = (rows[:, None].astype(np.int64) * cols[None, :]) % modulus
     return (product.astype(np.float32) * np.float32(2.0 * math.pi / modulus)).astype(np.float64)
+
+
+def channel_order(ways, group):
+    half = group // 2
+    ctx, h, r = np.meshgrid(np.arange(ways), np.arange(2), np.arange(half), indexing="ij")
+    return (h * ways * half + ctx * half + r).reshape(-1)
 
 
 def host_tables(ways, group, sigs):
@@ -49,14 +55,40 @@
 SMEM = pl.BlockSpec(memory_space=pltpu.SMEM)
 
 
-def prep_kernel(k_ref, v_ref, f_ref, q_ref, send_ref, qt_ref):
+def product_t(order, values):
+    return lax.dot_general(order, values, (((1,), (1,)), ((), ())), preferred_element_type=F32)
+
+
+def dy_kernel(w_ref, d_ref, out_ref):
+    out_ref[...] = product_t(w_ref[...], d_ref[...]).astype(BF)
+
+
+def prep_kernel(k_ref, v_ref, f_ref, order_ref, send_ref):
     ways = send_ref.shape[0]
-    mixed = k_ref[...].astype(F32) * v_ref[...].astype(F32)
-    mixed_t = mixed.T.reshape(ways, 1, -1, FAC)
-    filt_t = f_ref[...].astype(F32).T.reshape(ways, 1, -1, FAC)
-    both = jnp.concatenate([mixed_t, filt_t], axis=1)
-    send_ref[...] = both.reshape(send_ref.shape).astype(BF)
+    mixed = (k_ref[...].astype(F32) * v_ref[...].astype(F32)).astype(BF)
+    parts = [product_t(order_ref[...], x).reshape(ways, 1, -1, FAC) for x in (mixed, f_ref[...])]
+    send_ref[...] = jnp.concatenate(parts, axis=1).reshape(send_ref.shape).astype(BF)
+
+
+def turn_query_kernel(core_ref, q_ref, qt_ref, mine_ref, away_ref):
     qt_ref[...] = q_ref[...].astype(F32).T.astype(BF)
+    rows = mine_ref.shape[0]
+    for out_ref, half in ((mine_ref, core_ref[0]), (away_ref, 1 - core_ref[0])):
+        out_ref[...] = qt_ref[pl.ds(pl.multiple_of(half * rows, rows), rows), :]
+
+
+def gate_kernel(core_ref, z_ref, order_ref, q_mine_ref, q_theirs_ref, gated_ref, z_mine_ref, z_away_ref):
+    z = jnp.dot(order_ref[core_ref[0]], z_ref[...], preferred_element_type=F32)
+    n = z.shape[0] // 2
+    z_mine_ref[...] = z[:n].astype(BF)
+    z_away_ref[...] = z[n:].astype(BF)
+    gated_ref[pl.ds(0, n), :] = (z[:n] * q_mine_ref[...].astype(F32)).astype(BF)
+    gated_ref[pl.ds(n, n), :] = (z[n:] * q_theirs_ref[...].astype(F32)).astype(BF)
+
+
+def dz_kernel(dy_ref, qt_ref, order_ref, send_ref):
+    dz = (dy_ref[...].astype(F32) * qt_ref[...].astype(F32)).astype(BF)
+    send_ref[...] = jnp.dot(order_ref[...], dz, preferred_element_type=F32).astype(BF)
 
 
 def turn(section, tc, ts):
@@ -137,41 +169,41 @@
     inverse(y_ref, square_ref, last_ref, tc_ref, ts_ref, du_ref, width)
 
 
-def weight_kernel(scale, at_ref, *refs):
-    blocks, (d_ref, all_ref, away_ref, keep_ref, left_ref) = refs[:8], refs[8:]
-    rows = blocks[0].shape[0]
+def weight_kernel(scale, width, at_ref, *refs):
+    blocks, (d_ref, d_other_ref, part_ref, mine_ref, away_ref) = refs[:8], refs[8:]
+    n = blocks[0].shape[0] // 2
     for i, block in enumerate(blocks):
-        all_ref[pl.ds(pl.multiple_of(at_ref[i] * rows, rows), rows), :] = block[...]
-    core = at_ref[8]
-    half = rows // 2
-    for out_ref, mine in ((away_ref, 1 - core), (keep_ref, core)):
-        for g in range(8):
-            start = pl.multiple_of(g * rows + mine * half, half)
-            left_ref[pl.ds(g * half, half), :] = all_ref[pl.ds(start, half), :]
-
-        def step(j, carry, out_ref=out_ref):
-            cols = cols_of(j, 256)
-            p = jnp.dot(left_ref[...], d_ref[:, cols], preferred_element_type=F32)
-            out_ref[:, cols] = (p * scale).astype(BF)
-            return carry
-
-        lax.fori_loop(0, d_ref.shape[1] // 256, step, 0)
-
-
-def finish_kernel(dy_ref, z_ref, du_ref, k_ref, v_ref, gq_ref, gk_ref, gv_ref):
-    gq = dy_ref[...].astype(F32) * z_ref[...].astype(F32)
-    gq_ref[...] = gq.T.astype(BF)
-    du = du_ref[...].astype(F32).T
+        rows = pl.ds(pl.multiple_of(at_ref[i] * n, n), n)
+        mine_ref[rows, :] = block[pl.ds(0, n), :]
+        away_ref[rows, :] = block[pl.ds(n, n), :]
+
+    def step(j, carry):
+        cols = cols_of(j, width)
+        p = jnp.dot(mine_ref[...], d_ref[:, cols], preferred_element_type=F32)
+        p += jnp.dot(away_ref[...], d_other_ref[:, cols], preferred_element_type=F32)
+        part_ref[:, cols] = (p * scale).astype(BF)
+        return carry
+
+    lax.fori_loop(0, d_ref.shape[1] // width, step, 0)
+
+
+def finish_kernel(core_ref, dy_ref, z_mine_ref, z_theirs_ref, du_ref, order_ref, k_ref, v_ref, gq_ref, gk_ref, gv_ref, gq_t_ref):
+    n = z_mine_ref.shape[0]
+    for z_ref, half in ((z_mine_ref, core_ref[0]), (z_theirs_ref, 1 - core_ref[0])):
+        rows = pl.ds(pl.multiple_of(half * n, n), n)
+        gq_t_ref[rows, :] = dy_ref[rows, :].astype(F32) * z_ref[...].astype(F32)
+    gq_ref[...] = gq_t_ref[...].T.astype(BF)
+    du = jnp.dot(du_ref[...].astype(F32).T.astype(BF), order_ref[...], preferred_element_type=F32)
     gk_ref[...] = (du * v_ref[...].astype(F32)).astype(BF)
     gv_ref[...] = (du * k_ref[...].astype(F32)).astype(BF)
 
 
-def call(kernel, outs, ins, scratch=(), mib=40, specs=None, flops=0):
+def call(kernel, outs, ins, scratch=(), mib=16, flops=0, scalars=0):
     total = sum(math.prod(o.shape) * o.dtype.itemsize for o in (*outs, *ins))
     return pl.pallas_call(
         kernel,
         out_shape=outs,
-        in_specs=specs or [VMEM] * len(ins),
+        in_specs=[SMEM] * scalars + [VMEM] * (len(ins) - scalars),
         out_specs=[VMEM] * len(outs),
         scratch_shapes=scratch,
         compiler_params=params(mib),
@@ -203,68 +235,114 @@
     return blocks, places
 
 
+def dy_product(w_out, d_out, tile=256):
+    channels, depth = w_out.shape
+    rows = d_out.shape[0]
+    return pl.pallas_call(
+        dy_kernel,
+        out_shape=shape(channels, rows),
+        grid=(rows // tile,),
+        in_specs=[
+            pl.BlockSpec((channels, depth), lambda i: (0, 0)),
+            pl.BlockSpec((tile, depth), lambda i: (i, 0)),
+        ],
+        out_specs=pl.BlockSpec((channels, tile), lambda i: (0, i)),
+        compiler_params=params(20),
+        cost_estimate=pl.CostEstimate(
+            flops=2 * channels * depth * rows, bytes_accessed=6 * channels * rows, transcendentals=0
+        ),
+    )(w_out, d_out)
+
+
 def on_device(query_in, key_in, value_in, filt, w_out, d_out):
     seq_rows, width = query_in.shape
+    channels, columns = w_out.shape
     ways = lax.axis_size("ctx")
-    group = width // ways
+    group, half = width // ways, width // 2
     n = HALF * group
-    first2, last, square, tc, ts = map(jnp.asarray, host_tables(ways, group, 2))
-    first1 = jnp.asarray(host_tables(ways, group, 1)[0])
-
-    send, query_t = call(
-        prep_kernel,
-        [shape(ways, 2 * group, seq_rows), shape(width, seq_rows)],
-        [key_in, value_in, filt, query_in],
-    )
+    first2, last, square, tc, ts = host_tables(ways, group, 2)
+    first1 = host_tables(ways, group, 1)[0]
+    pick = np.arange(ways * group).reshape(ways // 2, 2, 2, group // 2).transpose(0, 2, 1, 3).reshape(-1)
+    last_z = last[pick]
+    order = channel_order(ways, group)
+    order_in = np.eye(width)[order].astype(BF)
+    slots = np.arange(width).reshape(ways, 2, group // 2).transpose(1, 0, 2)
+    order_z = np.stack([np.eye(width)[slots[list(s)].reshape(-1)] for s in ((0, 1), (1, 0))]).astype(BF)
+
+    ctx = lax.axis_index("ctx")
+    core = (ctx & 1).astype(jnp.int32)
+    core_at = core.reshape(1)
+    swap = lambda v: lax.ppermute(v, "ctx", [(i, i ^ 1) for i in range(ways)])
+
+    partial_y = dy_product(w_out, d_out)
+    grad_y = lax.psum_scatter(partial_y, "fsdp", scatter_dimension=0, tiled=True)
+    (send,) = call(prep_kernel, [shape(ways, 2 * group, seq_rows)], [key_in, value_in, filt, order_in])
     arrived = spread(send.reshape(ways * 2 * group, seq_rows))
-    partial_y = lax.dot_general(w_out, d_out, (((1,), (1,)), ((), ())), preferred_element_type=F32)
-    grad_y = lax.psum_scatter(partial_y.astype(BF), "fsdp", scatter_dimension=0, tiled=True)
+    d_other = swap(d_out)
+    query_t, q_mine, q_away = call(
+        turn_query_kernel,
+        [shape(width, seq_rows), shape(half, seq_rows), shape(half, seq_rows)],
+        [core_at, query_in],
+        scalars=1,
+    )
+    q_theirs = swap(q_away)
 
     product = 2 * 2 * n * 2 * FAC * FAC
     conv, spectrum = call(
         functools.partial(conv_kernel, 256),
         [shape(ways * group, FAC), shape(2 * n, FAC)],
-        [arrived, first2, last, square, tc, ts],
+        [arrived, first2, last_z, square, tc, ts],
         [pltpu.VMEM((4 * n, 2 * FAC), BF), pltpu.VMEM((2 * n, 2 * FAC), BF)],
+        mib=24,
         flops=3 * product,
     )
-    z = spread(conv)
-    gated = (query_t.astype(F32) * z.astype(F32)).astype(BF)
+    gated, z_mine, z_away = call(
+        gate_kernel,
+        [shape(width, seq_rows), shape(half, seq_rows), shape(half, seq_rows)],
+        [core_at, spread(conv), order_z, q_mine, q_theirs],
+        scalars=1,
+    )
+    z_theirs = swap(z_away)
 
     blocks, places = ring(gated)
-    core = lax.axis_index("ctx") & 1
-    at = jnp.stack([*places, core]).astype(jnp.int32)
+    at = jnp.stack(places).astype(jnp.int32)
     scale = 1.0 / math.sqrt(seq_rows * ways)
-    channels, columns = w_out.shape
-    gated_all, away, keep = call(
-        functools.partial(weight_kernel, scale),
-        [shape(channels, seq_rows), shape(channels // 2, columns), shape(channels // 2, columns)],
-        [at, *blocks, d_out],
-        [pltpu.VMEM((channels // 2, seq_rows), BF)],
-        specs=[SMEM] + [VMEM] * 9,
+    part, mine, away = call(
+        functools.partial(weight_kernel, scale, 256),
+        [shape(channels // 2, columns), shape(channels // 2, seq_rows), shape(channels // 2, seq_rows)],
+        [at, *blocks, d_out, d_other],
+        scalars=1,
+        mib=20,
         flops=2 * channels * seq_rows * columns,
     )
-    swapped = lax.ppermute(away, "ctx", [(i, i ^ 1) for i in range(ways)])
-    summed = (keep.astype(F32) + swapped.astype(F32)).astype(BF)
     groups = [list(range(c, ways, 2)) for c in range(2)]
-    parts = lax.all_to_all(summed, "ctx", 0, 0, tiled=True, axis_index_groups=groups)
+    parts = lax.all_to_all(part, "ctx", 0, 0, tiled=True, axis_index_groups=groups)
     grad_weight = jnp.sum(parts.reshape(ways // 2, channels // ways, columns).astype(F32), axis=0)
+
+    theirs = swap(away)
+    split = lambda v: v.reshape(-1, 1, half, seq_rows)
+    low, high = jnp.where(core == 0, mine, theirs), jnp.where(core == 0, theirs, mine)
+    gated_all = jnp.concatenate([split(low), split(high)], axis=1).reshape(channels, seq_rows)
     layer_out = lax.dot_general(
         gated_all, w_out, (((0,), (0,)), ((), ())), preferred_element_type=F32
     ).astype(BF)
 
-    grad_z = (grad_y.astype(F32) * query_t.astype(F32)).astype(BF)
+    (grad_z,) = call(dz_kernel, [shape(width, seq_rows)], [grad_y, query_t, order_in])
     (adjoint,) = call(
         functools.partial(adjoint_kernel, 256),
         [shape(ways * group, FAC)],
         [spread(grad_z), spectrum, first1, last, square, tc, ts],
         [pltpu.VMEM((2 * n, 2 * FAC), BF), pltpu.VMEM((2 * n, 2 * FAC), BF)],
+        mib=20,
         flops=2 * product,
     )
-    grad_u = spread(adjoint)
     like = shape(seq_rows, width)
     grad_query, grad_key, grad_value = call(
-        finish_kernel, [like, like, like], [grad_y, z, grad_u, key_in, value_in]
+        finish_kernel,
+        [like, like, like],
+        [core_at, grad_y, z_mine, z_theirs, spread(adjoint), order_in, key_in, value_in],
+        [pltpu.VMEM((width, seq_rows), F32)],
+        scalars=1,
     )
     return (layer_out, grad_query, grad_key, grad_value, grad_weight)
 

time: 168 us -> 177 us (1.054)
  blocking collectives: 51.1 us -> 22.8 us
  waiting for transfers between devices: 29.7 us -> 49.3 us
  local copies, waits for them, and re-layouts: 14.8 us -> 23.6 us
  Pallas kernels: 20.1 us -> 28.7 us
  starting transfers between devices: 19.7 us -> 26.4 us
  matrix products: 10.6 us -> 5.34 us
    all_to_all x3 -> x1, blocking collectives: 51.1 us -> 22.8 us  [spread(): return lax.all_to_all(values, 'ctx', 0, 0, tiled=True)]
    all_to_all x1 -> x3, waiting for transfers between devices: 6.94 us -> 20.3 us  [spread(): return lax.all_to_all(values, 'ctx', 0, 0, tiled=True)]
    unnamed x62 -> x72, local copies, waits for them, and re-layouts: 14.7 us -> 23.5 us
    pallas_call x5 -> x9, Pallas kernels: 20.1 us -> 28.7 us  [the longest x8 23.3 us: call(): pl.pallas_call(kernel, out_shape=outs, in_specs=[SMEM] * scalars + [VMEM]...]
    all_to_all x1 -> x3, starting transfers between devices: 4.19 us -> 10.8 us  [spread(): return lax.all_to_all(values, 'ctx', 0, 0, tiled=True)]
    all_to_all x1, waiting for transfers between devices: 9.67 us -> 15.1 us  [on_device(): lax.all_to_all(part, 'ctx', 0, 0, tiled=True, axis_index_groups=groups)]
    dot_general x1 -> x0, matrix products: 5.28 us -> none  [on_device(): lax.dot_general(w_out, d_out, (((1,), (1,)), ((), ())), preferred_element...]
    convert_element_type x1 -> x0, other arithmetic: 2.61 us -> none  [on_device(): summed = (keep.astype(F32) + swapped.astype(F32)).astype(BF)]
  transfers between devices with their start and end apart: 11 -> 16, of which waited for: 7 -> 10; matrix products, arithmetic and copies ran while one was open for 5% -> 6% of each run, Pallas kernels for 9% -> 13%
where the time goes in v2:
time: 177 us; the launch traced here: 175 us
  waiting for transfers between devices  49.3 us (28%)
  Pallas kernels  28.7 us (16%)
  starting transfers between devices  26.4 us (15%)
  local copies, waits for them, and re-layouts  23.6 us (13%)
  blocking collectives  22.8 us (13%)
  between operations  14.3 us (8%)
  matrix products  5.34 us (3%)
  other arithmetic  5.02 us (3%)
    unnamed x72, local copies, waits for them, and re-layouts  23.5 us
    pallas_call x8, Pallas kernels, call(): pl.pallas_call(kernel, out_shape=outs, in_specs=[SMEM] * scalars + [VMEM]...  23.3 us
    all_to_all x1, blocking collectives, spread(): return lax.all_to_all(values, 'ctx', 0, 0, tiled=True)  22.8 us
    all_to_all x3, waiting for transfers between devices, spread(): return lax.all_to_all(values, 'ctx', 0, 0, tiled=True)  20.3 us
    all_to_all x1, waiting for transfers between devices, on_device(): lax.all_to_all(part, 'ctx', 0, 0, tiled=True, axis_index_groups=groups)  15.1 us
    ppermute x7, waiting for transfers between devices, ring(): move = lambda v, p: lax.ppermute(v, 'fsdp', p)  12.9 us
    all_to_all x3, starting transfers between devices, spread(): return lax.all_to_all(values, 'ctx', 0, 0, tiled=True)  10.8 us
    ppermute x7, starting transfers between devices, ring(): move = lambda v, p: lax.ppermute(v, 'fsdp', p)  10.3 us
  transfers between devices with their start and end apart: 16, of which 10 were waited for; matrix products, arithmetic and copies ran while one was open for 6% of the time, Pallas kernels for 13%

profile of v2, /device:TPU:0, one launch (start us, length us, event | category | flops | bytes accessed | tf_op | source)
XLA Modules:
  0.0 175.4 jit_solution(5759635190771556573)
XLA Ops:
  7.2 0.0 reduce-scatter.2.cloned.1.call-start
  7.2 1.6 copy-done.8
  8.8 5.4 %shard_map.187 = bf16[1024,1024]{1,0:T(8,128)(2,1)} custom-call(bf16[1024,1024]{1,0:T(8,128)(2,1)S(1)} %copy-done.8, bf16[1024,1024]{1,0:T(8,128)(2,1)} %d_ref.1), custom_call_target="tpu_custom_call" | custom-call | flops 2147483648 | bytes 6291456 | tf_op jit(solution)/shard_map/pallas_call | solution.py:241
  14.3 0.1 collective-permute-start.8
  14.4 0.8 copy-done.2
  15.1 0.1 copy-done.3
  15.2 0.1 copy-done.6
  15.3 0.3 shard_map.182
  15.6 22.8 %all_to_all.50 = bf16[16,16,1024]{2,1,0:T(8,128)(2,1)S(1)} all-to-all(bf16[16,16,1024]{2,1,0:T(8,128)(2,1)S(1)} %shard_map.182), channel_id=1, replica_groups=mesh['fsdp'=8,'ctx'=16] {'ctx'}, dimensions={0} | all-to-all | bytes 1048576 | tf_op jit(solution)/shard_map/all_to_all | solution.py:219
  38.4 2.2 %copy-done.24 = bf16[2048,1024]{1,0:T(8,128)(2,1)S(1)} copy-done((bf16[2048,1024]{1,0:T(8,128)(2,1)S(1)}, bf16[2048,1024]{1,0:T(8,128)(2,1)}, u32[]{:S(2)}) %copy-start.24) | copy-done | bytes 4194328
  40.7 7.4 %shard_map.183 = (bf16[128,1024]{1,0:T(8,128)(2,1)}, bf16[272,1024]{1,0:T(8,128)(2,1)S(1)}) custom-call(bf16[256,1024]{1,0:T(8,128)(2,1)S(1)} %bitcast.28, bf16[544,256]{1,0:T(8,128)(2,1)S(1)} %copy-done.30, bf16[128,272]{1,0:T(8,128)(2,1)S(1)} %copy-done.32, bf16[2048,1024]{1,0:T(8,128)(2,1)S(1)} %copy-done.24, f32[136,1024]{1,0:T(8,128)S(1)} %copy-done.28, ...), custom_call_target="tpu_custom_call" | custom-call | flops 3422552064 | bytes 7000064 | tf_op jit(solution)/shard_map/pallas_call | solution.py:203
  48.1 0.8 copy-done.34
  48.9 3.5 %all-to-all-start.1 = ((bf16[16,8,1024]{2,1,0:T(8,128)(2,1)}), bf16[16,8,1024]{2,1,0:T(8,128)(2,1)S(1)}, u32[]{:S(2)}, u32[]{:S(2)}) async-start(bf16[16,8,1024]{2,1,0:T(8,128)(2,1)} %bitcast.10), calls=%async_computation.1 | async-start | bytes 524288 | tf_op jit(solution)/shard_map/all_to_all | solution.py:219
  52.5 0.2 shard_map.184
  52.6 0.4 collective-permute-start
  53.0 1.1 collective-permute-done.q_theirs_ref
  54.1 9.7 %all-to-all-done.1 = bf16[16,8,1024]{2,1,0:T(8,128)(2,1)S(1)} async-done(((bf16[16,8,1024]{2,1,0:T(8,128)(2,1)}), bf16[16,8,1024]{2,1,0:T(8,128)(2,1)S(1)}, u32[]{:S(2)}, u32[]{:S(2)}) %all-to-all-start.1) | async-done | bytes 262176 | tf_op jit(solution)/shard_map/all_to_all | solution.py:219
  63.8 0.9 shard_map.185
  64.7 0.4 collective-permute-start.1
  65.1 7.3 %collective-permute-done.1.refs_1_ = bf16[128,1024]{1,0:T(8,128)(2,1)S(1)} collective-permute-done((bf16[128,1024]{1,0:T(8,128)(2,1)S(1)}, bf16[128,1024]{1,0:T(8,128)(2,1)S(1)}, u32[]{:S(2)}, u32[]{:S(2)}) %collective-permute-start.1) | collective-permute-done | bytes 262176 | tf_op jit(solution)/shard_map/ppermute | solution.py:226
  72.4 4.2 %collective-permute-start.5 = (bf16[128,1024]{1,0:T(8,128)(2,1)S(1)}, bf16[128,1024]{1,0:T(8,128)(2,1)S(1)}, u32[]{:S(2)}, u32[]{:S(2)}) collective-permute-start(bf16[128,1024]{1,0:T(8,128)(2,1)S(1)} %collective-permute-done.1.refs_1_), channel_id=1, source_target_pairs={{0,48},{16,0},{32,16},{48,32},{64,112},{80,64},{96,80},{112,96},{1... | collective-permute-start | bytes 786440 | tf_op jit(solution)/shard_map/ppermute | solution.py:226
  76.6 0.0 collective-permute-start.3
  76.6 2.0 %collective-permute-start.4 = (bf16[128,1024]{1,0:T(8,128)(2,1)S(1)}, bf16[128,1024]{1,0:T(8,128)(2,1)S(1)}, u32[]{:S(2)}, u32[]{:S(2)}) collective-permute-start(bf16[128,1024]{1,0:T(8,128)(2,1)S(1)} %collective-permute-done.1.refs_1_), channel_id=1, source_target_pairs={{0,16},{16,32},{32,48},{48,0},{64,80},{80,96},{96,112},{112,64},{1... | collective-permute-start | bytes 786440 | tf_op jit(solution)/shard_map/ppermute | solution.py:226
  78.6 0.7 copy-done.10
  79.3 0.7 copy-done.12
  80.0 3.3 %collective-permute-done.5.refs_5_ = bf16[128,1024]{1,0:T(8,128)(2,1)S(1)} collective-permute-done((bf16[128,1024]{1,0:T(8,128)(2,1)S(1)}, bf16[128,1024]{1,0:T(8,128)(2,1)S(1)}, u32[]{:S(2)}, u32[]{:S(2)}) %collective-permute-start.5) | collective-permute-done | bytes 262176 | tf_op jit(solution)/shard_map/ppermute | solution.py:226
  83.3 3.7 %collective-permute-start.7 = (bf16[128,1024]{1,0:T(8,128)(2,1)S(1)}, bf16[128,1024]{1,0:T(8,128)(2,1)S(1)}, u32[]{:S(2)}, u32[]{:S(2)}) collective-permute-start(bf16[128,1024]{1,0:T(8,128)(2,1)S(1)} %collective-permute-done.5.refs_5_), channel_id=1, source_target_pairs={{0,48},{16,0},{32,16},{48,32},{64,112},{80,64},{96,80},{112,96},{1... | collective-permute-start | bytes 786440 | tf_op jit(solution)/shard_map/ppermute | solution.py:226
  87.0 0.7 copy-done.14
  87.7 0.1 stack.35.at_ref
  87.8 1.1 collective-permute-done.3.refs_3_
  89.0 0.7 copy-done.16
  89.7 0.3 collective-permute-done.6.refs_6_
  90.0 0.7 copy-done.20
  90.7 0.7 copy-done.18
  91.4 0.8 collective-permute-done.7.refs_7_
  92.1 0.7 copy-done.22
  92.8 0.9 copy-done.11
  93.8 0.9 copy-done.13
  94.7 0.9 copy-done.15
  95.7 0.9 copy-done.17
  96.6 0.9 copy-done.19
  97.6 0.9 copy-done.21
  98.5 0.9 copy-done.23
  99.5 6.3 %shard_map.186 = (bf16[512,1024]{1,0:T(8,128)(2,1)}, bf16[512,1024]{1,0:T(8,128)(2,1)S(1)}, bf16[512,1024]{1,0:T(8,128)(2,1)S(1)}) custom-call(s32[8]{0:T(128)S(1)} %stack.35.at_ref, bf16[128,1024]{1,0:T(8,128)(2,1)S(1)} %get-tuple-element.22.refs_0_, bf16[128,1024]{1,0:T(8,128)(2,1)S(1)} %copy-done.11, bf16[128,1024]{1,0:T(8,128)(2,1)S(1)} %copy-done.13, ...), custom_call_target="tpu_custom_call" | custom-call | flops 2147483648 | bytes 9437216 | tf_op jit(solution)/shard_map/pallas_call | solution.py:203
  105.8 4.3 %all-to-all-start.4 = ((bf16[8,64,1024]{2,1,0:T(8,128)(2,1)}), bf16[8,64,1024]{2,1,0:T(8,128)(2,1)}, u32[]{:S(2)}, u32[]{:S(2)}) async-start(bf16[8,64,1024]{2,1,0:T(8,128)(2,1)} %bitcast.21), calls=%async_computation.5 | async-start | bytes 2097152 | tf_op jit(solution)/shard_map/all_to_all | solution.py:319
  110.1 0.1 collective-permute-start.9
  110.2 0.5 collective-permute-start.10
  110.7 15.1 %all-to-all-done.4 = bf16[8,64,1024]{2,1,0:T(8,128)(2,1)} async-done(((bf16[8,64,1024]{2,1,0:T(8,128)(2,1)}), bf16[8,64,1024]{2,1,0:T(8,128)(2,1)}, u32[]{:S(2)}, u32[]{:S(2)}) %all-to-all-start.4) | async-done | bytes 1048608 | tf_op jit(solution)/shard_map/all_to_all | solution.py:319
  125.7 2.1 %convert_reduce_fusion = f32[64,1024]{1,0:T(8,128)} fusion(bf16[8,64,1024]{2,1,0:T(8,128)(2,1)} %all-to-all-done.4), kind=kLoop, calls=%fused_computation.1 | loop fusion | flops 983040 | bytes 1310720 | tf_op jit(solution)/shard_map/reduce_sum | solution.py:320
  127.9 0.9 copy-done
  128.8 0.9 shard_map.188
  129.8 3.5 %all-to-all-start.2 = ((bf16[16,8,1024]{2,1,0:T(8,128)(2,1)}), bf16[16,8,1024]{2,1,0:T(8,128)(2,1)S(1)}, u32[]{:S(2)}, u32[]{:S(2)}) async-start(bf16[16,8,1024]{2,1,0:T(8,128)(2,1)} %bitcast.17), calls=%async_computation.3 | async-start | bytes 524288 | tf_op jit(solution)/shard_map/all_to_all | solution.py:219
  133.3 1.4 broadcast_select_fusion.1
  134.7 1.5 pad_maximum_fusion
  136.2 6.6 %all-to-all-done.2 = bf16[16,8,1024]{2,1,0:T(8,128)(2,1)S(1)} async-done(((bf16[16,8,1024]{2,1,0:T(8,128)(2,1)}), bf16[16,8,1024]{2,1,0:T(8,128)(2,1)S(1)}, u32[]{:S(2)}, u32[]{:S(2)}) %all-to-all-start.2) | async-done | bytes 262176 | tf_op jit(solution)/shard_map/all_to_all | solution.py:219
  142.8 2.2 %copy-done.25 = bf16[2048,1024]{1,0:T(8,128)(2,1)S(1)} copy-done((bf16[2048,1024]{1,0:T(8,128)(2,1)S(1)}, bf16[2048,1024]{1,0:T(8,128)(2,1)}, u32[]{:S(2)}) %copy-start.25) | copy-done | bytes 4194328
  145.0 1.1 copy-done.27
  146.1 1.1 copy-done.29
  147.1 1.1 copy-done.35
  148.2 6.1 %shard_map.189 = bf16[128,1024]{1,0:T(8,128)(2,1)} custom-call(bf16[128,1024]{1,0:T(8,128)(2,1)S(1)} %bitcast.29, bf16[272,1024]{1,0:T(8,128)(2,1)S(1)} %copy-done.35, bf16[272,128]{1,0:T(8,128)(2,1)S(1)} %copy-done.33, bf16[128,272]{1,0:T(8,128)(2,1)S(1)} %copy-done.31, bf16[2048,1024]{1,0:T(8,128)(2,1)S(1)} %copy-done.25, f32[136,1024]{1,0:T(8,128)S(1)} %copy-done.29, ...), custom_call_target="tpu_custom_call" | custom-call | flops 2281701376 | bytes 6529024 | tf_op jit(solution)/shard_map/pallas_call | solution.py:203
  154.2 3.7 %all-to-all-start.3 = ((bf16[16,8,1024]{2,1,0:T(8,128)(2,1)}), bf16[16,8,1024]{2,1,0:T(8,128)(2,1)S(1)}, u32[]{:S(2)}, u32[]{:S(2)}) async-start(bf16[16,8,1024]{2,1,0:T(8,128)(2,1)} %bitcast.19), calls=%async_computation.4 | async-start | bytes 524288 | tf_op jit(solution)/shard_map/all_to_all | solution.py:219
  158.0 5.3 %convolution_convert_fusion = bf16[1024,1024]{1,0:T(8,128)(2,1)} fusion(bf16[1024,1024]{1,0:T(8,128)(2,1)} %bitcast.32, bf16[1024,1024]{1,0:T(8,128)(2,1)S(1)} %copy-done.9), kind=kOutput, calls=%fused_computation.2 | convolution fusion | flops 2148532224 | bytes 6291456 | tf_op jit(solution)/shard_map/dot_general | solution.py:326
  163.3 4.0 %all-to-all-done.3 = bf16[16,8,1024]{2,1,0:T(8,128)(2,1)S(1)} async-done(((bf16[16,8,1024]{2,1,0:T(8,128)(2,1)}), bf16[16,8,1024]{2,1,0:T(8,128)(2,1)S(1)}, u32[]{:S(2)}, u32[]{:S(2)}) %all-to-all-start.3) | async-done | bytes 262176 | tf_op jit(solution)/shard_map/all_to_all | solution.py:219
  167.3 1.2 shard_map.190
  (56 shorter events, 0.1 us)
Async XLA Ops:
  7.2 120.7 %reduce-scatter.2.cloned.1.call-start = ((), (), s32[]{:S(2)}) async-start(), calls=%async_computation.6 | async-start | bytes 2359296 | tf_op jit(solution)/shard_map/reduce_scatter | solution.py:278
  7.2 1.6 copy-start.8
  14.2 0.9 copy-start.2
  14.2 1.0 copy-start.3
  14.2 1.0 copy-start.4
  14.2 1.1 copy-start.6
  14.2 24.2 %copy-start.26 = (f32[136,1024]{1,0:T(8,128)S(1)}, f32[136,1024]{1,0:T(8,128)}, u32[]{:S(2)}) copy-start(f32[136,1024]{1,0:T(8,128)} %constant.46.clone.ts_ref) | copy-start | bytes 1671172
  14.2 24.2 %copy-start.28 = (f32[136,1024]{1,0:T(8,128)S(1)}, f32[136,1024]{1,0:T(8,128)}, u32[]{:S(2)}) copy-start(f32[136,1024]{1,0:T(8,128)} %constant.45.clone.tc_ref) | copy-start | bytes 1671172
  14.2 24.2 %copy-start.30 = (bf16[544,256]{1,0:T(8,128)(2,1)S(1)}, bf16[544,256]{1,0:T(8,128)(2,1)}, u32[]{:S(2)}) copy-start(bf16[544,256]{1,0:T(8,128)(2,1)} %constant.42.clone.first_ref) | copy-start | bytes 835588
  14.2 24.2 %copy-start.32 = (bf16[128,272]{1,0:T(8,128)(2,1)S(1)}, bf16[128,272]{1,0:T(8,128)(2,1)}, u32[]{:S(2)}) copy-start(bf16[128,272]{1,0:T(8,128)(2,1)} %constant.43.clone.last_ref) | copy-start | bytes 208900
  14.3 78.6 %collective-permute-start.8 = (bf16[1024,1024]{1,0:T(8,128)(2,1)}, bf16[1024,1024]{1,0:T(8,128)(2,1)}, u32[]{:S(2)}, u32[]{:S(2)}) collective-permute-start(bf16[1024,1024]{1,0:T(8,128)(2,1)} %d_ref.1), channel_id=1, source_target_pairs={{0,1},{1,0},{2,3},{3,2},{4,5},{5,4},{6,7},{7,6},{8,9},{9,8},{10,11... | collective-permute-start | bytes 6291464 | tf_op jit(solution)/shard_map/ppermute | solution.py:275
  38.4 2.2 %copy-start.24 = (bf16[2048,1024]{1,0:T(8,128)(2,1)S(1)}, bf16[2048,1024]{1,0:T(8,128)(2,1)}, u32[]{:S(2)}) copy-start(bf16[2048,1024]{1,0:T(8,128)(2,1)} %constant.44.clone.square_ref) | copy-start | bytes 12582916
  40.7 11.8 %copy-start.5 = (bf16[1024,128]{1,0:T(8,128)(2,1)S(1)}, bf16[1024,128]{1,0:T(8,128)(2,1)}, u32[]{:S(2)}) copy-start(bf16[1024,128]{1,0:T(8,128)(2,1)} %q_ref.1) | copy-start | bytes 786436
  40.7 23.1 %copy-start.7 = (bf16[2,128,128]{2,1,0:T(8,128)(2,1)S(1)}, bf16[2,128,128]{2,1,0:T(8,128)(2,1)}, u32[]{:S(2)}) copy-start(bf16[2,128,128]{2,1,0:T(8,128)(2,1)} %constant.47.clone.order_ref) | copy-start | bytes 196612
  48.1 0.8 copy-start.34
  48.9 14.9 %all-to-all-start.1 = ((bf16[16,8,1024]{2,1,0:T(8,128)(2,1)}), bf16[16,8,1024]{2,1,0:T(8,128)(2,1)S(1)}, u32[]{:S(2)}, u32[]{:S(2)}) async-start(bf16[16,8,1024]{2,1,0:T(8,128)(2,1)} %bitcast.10), calls=%async_computation.1 | async-start | bytes 524288 | tf_op jit(solution)/shard_map/all_to_all | solution.py:219
  52.6 1.4 collective-permute-start
  64.7 7.7 %collective-permute-start.1 = (bf16[128,1024]{1,0:T(8,128)(2,1)S(1)}, bf16[128,1024]{1,0:T(8,128)(2,1)S(1)}, u32[]{:S(2)}, u32[]{:S(2)}) collective-permute-start(bf16[128,1024]{1,0:T(8,128)(2,1)S(1)} %get-tuple-element.22.refs_0_), channel_id=1, source_target_pairs={{0,64},{16,80},{32,96},{48,112},{64,0},{80,16},{96,32},{112,48},{1... | collective-permute-start | bytes 786440 | tf_op jit(solution)/shard_map/ppermute | solution.py:226
  65.1 14.3 %collective-permute-start.2 = (bf16[128,1024]{1,0:T(8,128)(2,1)S(1)}, bf16[128,1024]{1,0:T(8,128)(2,1)S(1)}, u32[]{:S(2)}, u32[]{:S(2)}) collective-permute-start(bf16[128,1024]{1,0:T(8,128)(2,1)S(1)} %get-tuple-element.22.refs_0_), channel_id=1, source_target_pairs={{0,16},{16,32},{32,48},{48,0},{64,80},{80,96},{96,112},{112,64},{1... | collective-permute-start | bytes 786440 | tf_op jit(solution)/shard_map/ppermute | solution.py:226
  72.4 10.9 %collective-permute-start.5 = (bf16[128,1024]{1,0:T(8,128)(2,1)S(1)}, bf16[128,1024]{1,0:T(8,128)(2,1)S(1)}, u32[]{:S(2)}, u32[]{:S(2)}) collective-permute-start(bf16[128,1024]{1,0:T(8,128)(2,1)S(1)} %collective-permute-done.1.refs_1_), channel_id=1, source_target_pairs={{0,48},{16,0},{32,16},{48,32},{64,112},{80,64},{96,80},{112,96},{1... | collective-permute-start | bytes 786440 | tf_op jit(solution)/shard_map/ppermute | solution.py:226
  76.6 12.4 %collective-permute-start.3 = (bf16[128,1024]{1,0:T(8,128)(2,1)S(1)}, bf16[128,1024]{1,0:T(8,128)(2,1)S(1)}, u32[]{:S(2)}, u32[]{:S(2)}) collective-permute-start(bf16[128,1024]{1,0:T(8,128)(2,1)S(1)} %get-tuple-element.22.refs_0_), channel_id=1, source_target_pairs={{0,48},{16,0},{32,16},{48,32},{64,112},{80,64},{96,80},{112,96},{1... | collective-permute-start | bytes 786440 | tf_op jit(solution)/shard_map/ppermute | solution.py:226
  76.6 14.1 %collective-permute-start.4 = (bf16[128,1024]{1,0:T(8,128)(2,1)S(1)}, bf16[128,1024]{1,0:T(8,128)(2,1)S(1)}, u32[]{:S(2)}, u32[]{:S(2)}) collective-permute-start(bf16[128,1024]{1,0:T(8,128)(2,1)S(1)} %collective-permute-done.1.refs_1_), channel_id=1, source_target_pairs={{0,16},{16,32},{32,48},{48,0},{64,80},{80,96},{96,112},{112,64},{1... | collective-permute-start | bytes 786440 | tf_op jit(solution)/shard_map/ppermute | solution.py:226
  78.6 0.7 copy-start.10
  79.3 10.7 %collective-permute-start.6 = (bf16[128,1024]{1,0:T(8,128)(2,1)S(1)}, bf16[128,1024]{1,0:T(8,128)(2,1)S(1)}, u32[]{:S(2)}, u32[]{:S(2)}) collective-permute-start(bf16[128,1024]{1,0:T(8,128)(2,1)S(1)} %collective-permute-done.2.refs_2_), channel_id=1, source_target_pairs={{0,16},{16,32},{32,48},{48,0},{64,80},{80,96},{96,112},{112,64},{1... | collective-permute-start | bytes 786440 | tf_op jit(solution)/shard_map/ppermute | solution.py:226
  79.3 0.7 copy-start.12
  83.3 8.8 %collective-permute-start.7 = (bf16[128,1024]{1,0:T(8,128)(2,1)S(1)}, bf16[128,1024]{1,0:T(8,128)(2,1)S(1)}, u32[]{:S(2)}, u32[]{:S(2)}) collective-permute-start(bf16[128,1024]{1,0:T(8,128)(2,1)S(1)} %collective-permute-done.5.refs_5_), channel_id=1, source_target_pairs={{0,48},{16,0},{32,16},{48,32},{64,112},{80,64},{96,80},{112,96},{1... | collective-permute-start | bytes 786440 | tf_op jit(solution)/shard_map/ppermute | solution.py:226
  87.0 0.7 copy-start.14
  89.0 0.7 copy-start.16
  90.0 0.7 copy-start.20
  90.7 0.7 copy-start.18
  92.1 0.7 copy-start.22
  92.8 1.0 copy-start.11
  93.8 0.9 copy-start.13
  94.7 0.9 copy-start.15
  95.7 0.9 copy-start.17
  96.6 0.9 copy-start.19
  97.6 0.9 copy-start.21
  98.5 0.9 copy-start.23
  105.8 19.9 %all-to-all-start.4 = ((bf16[8,64,1024]{2,1,0:T(8,128)(2,1)}), bf16[8,64,1024]{2,1,0:T(8,128)(2,1)}, u32[]{:S(2)}, u32[]{:S(2)}) async-start(bf16[8,64,1024]{2,1,0:T(8,128)(2,1)} %bitcast.21), calls=%async_computation.5 | async-start | bytes 2097152 | tf_op jit(solution)/shard_map/all_to_all | solution.py:319
  110.1 23.2 %collective-permute-start.9 = (bf16[512,1024]{1,0:T(8,128)(2,1)S(1)}, bf16[512,1024]{1,0:T(8,128)(2,1)}, u32[]{:S(2)}, u32[]{:S(2)}) collective-permute-start(bf16[512,1024]{1,0:T(8,128)(2,1)S(1)} %get-tuple-element.24), channel_id=1, source_target_pairs={{0,1},{1,0},{2,3},{3,2},{4,5},{5,4},{6,7},{7,6},{8,9},{9,8},{10,11... | collective-permute-start | bytes 3145736 | tf_op jit(solution)/shard_map/ppermute | solution.py:275
  110.2 53.1 %collective-permute-start.10 = (bf16[64,1024]{1,0:T(8,128)(2,1)}, bf16[64,1024]{1,0:T(8,128)(2,1)S(1)}, u32[]{:S(2)}, u32[]{:S(2)}) collective-permute-start(bf16[64,1024]{1,0:T(8,128)(2,1)} %get-tuple-element.26), channel_id=1, source_target_pairs={{0,1},{1,0},{2,3},{3,2},{4,5},{5,4},{6,7},{7,6},{8,9},{9,8},{10,11... | collective-permute-start | bytes 393224 | tf_op jit(solution)/shard_map/ppermute | solution.py:275
  127.9 1.0 copy-start
  129.8 13.1 %all-to-all-start.2 = ((bf16[16,8,1024]{2,1,0:T(8,128)(2,1)}), bf16[16,8,1024]{2,1,0:T(8,128)(2,1)S(1)}, u32[]{:S(2)}, u32[]{:S(2)}) async-start(bf16[16,8,1024]{2,1,0:T(8,128)(2,1)} %bitcast.17), calls=%async_computation.3 | async-start | bytes 524288 | tf_op jit(solution)/shard_map/all_to_all | solution.py:219
  134.7 8.1 %copy-start.31 = (bf16[128,272]{1,0:T(8,128)(2,1)S(1)}, bf16[128,272]{1,0:T(8,128)(2,1)}, u32[]{:S(2)}) copy-start(bf16[128,272]{1,0:T(8,128)(2,1)} %constant.49.clone.last_ref) | copy-start | bytes 208900
  134.7 8.1 %copy-start.33 = (bf16[272,128]{1,0:T(8,128)(2,1)S(1)}, bf16[272,128]{1,0:T(8,128)(2,1)}, u32[]{:S(2)}) copy-start(bf16[272,128]{1,0:T(8,128)(2,1)} %constant.48.clone.first_ref) | copy-start | bytes 208900
  142.8 2.2 %copy-start.25 = (bf16[2048,1024]{1,0:T(8,128)(2,1)S(1)}, bf16[2048,1024]{1,0:T(8,128)(2,1)}, u32[]{:S(2)}) copy-start(bf16[2048,1024]{1,0:T(8,128)(2,1)} %constant.44.clone.square_ref) | copy-start | bytes 12582916
  145.0 1.1 copy-start.27
  146.1 1.1 copy-start.29
  147.1 1.1 copy-start.35
  148.2 9.8 %copy-start.9 = (bf16[1024,1024]{1,0:T(8,128)(2,1)S(1)}, bf16[1024,1024]{1,0:T(8,128)(2,1)}, u32[]{:S(2)}) copy-start(bf16[1024,1024]{1,0:T(8,128)(2,1)} %w_ref.1) | copy-start | bytes 6291460
  154.2 13.1 %all-to-all-start.3 = ((bf16[16,8,1024]{2,1,0:T(8,128)(2,1)}), bf16[16,8,1024]{2,1,0:T(8,128)(2,1)S(1)}, u32[]{:S(2)}, u32[]{:S(2)}) async-start(bf16[16,8,1024]{2,1,0:T(8,128)(2,1)} %bitcast.19), calls=%async_computation.4 | async-start | bytes 524288 | tf_op jit(solution)/shard_map/all_to_all | solution.py:219
  158.0 9.3 %copy-start.1 = (bf16[128,1024]{1,0:T(8,128)(2,1)S(1)}, bf16[128,1024]{1,0:T(8,128)(2,1)}, u32[]{:S(2)}) copy-start(bf16[128,1024]{1,0:T(8,128)(2,1)} %reduce-scatter.2.cloned.1.call-done.dy_ref) | copy-start | bytes 786436
Sparse Core Ops, SparseCore 0:
  14.4 48.6 reduce-scatter.1

commit v3 on v2

v3 whole, which is shorter than its diff:
```python
import functools
import math

import jax
import jax.numpy as jnp
import numpy as np
from jax import lax
from jax.experimental import pallas as pl
from jax.experimental.pallas import tpu as pltpu
from jax.sharding import PartitionSpec as P

ROW = 1024
FAC = 256
QF = 128
HALF = QF // 2 + 1
LANE_TILES = ROW // FAC
BF = jnp.bfloat16
F32 = jnp.float32
MIB = 1 << 20


def angles(rows, cols, modulus):
    product = (rows[:, None].astype(np.int64) * cols[None, :]) % modulus
    return (product.astype(np.float32) * np.float32(2.0 * math.pi / modulus)).astype(np.float64)


def channel_order(ways, group):
    half = group // 2
    ctx, h, r = np.meshgrid(np.arange(ways), np.arange(2), np.arange(half), indexing="ij")
    return (h * ways * half + ctx * half + r).reshape(-1)


def host_tables(ways, group):
    k2, t1 = np.arange(HALF), np.arange(FAC)
    t2 = (np.arange(LANE_TILES)[:, None] + LANE_TILES * np.arange(ways)[None, :]).reshape(-1)
    eye = np.eye(group)
    a = angles(k2, t2, QF)
    steps = np.stack([np.cos(a), -np.sin(a)])
    first = np.einsum("rkt,cd->rkctd", steps, eye).reshape(2 * HALF * group, t2.size * group)
    weight = np.where((k2 == 0) | (k2 == QF // 2), 1.0, 2.0) / (QF * FAC)
    b = angles(t2, k2, QF)
    back = np.concatenate([np.cos(b) * weight, (-np.sin(b) * weight)[:, 1:-1]], axis=1)
    last = np.einsum("tk,cd->tckd", back, eye).reshape(t2.size * group, -1)
    s = angles(t1, t1, FAC)
    square = np.concatenate([np.cos(s), np.sin(s)])
    w = angles(k2, t1, QF * FAC)
    tc, ts = (np.repeat(f(w), group, axis=0).astype(np.float32) for f in (np.cos, np.sin))
    as_bf = lambda v: np.asarray(v, np.float32).astype(BF)
    return as_bf(first), as_bf(last), as_bf(square), tc, ts


def params(mib):
    return pltpu.CompilerParams(vmem_limit_bytes=mib * MIB)


VMEM = pl.BlockSpec(memory_space=pltpu.VMEM)
ANY = pl.BlockSpec(memory_space=pl.ANY)
MOVES = ((0, 1), (0, -1), (1, 0), (0, 2), (1, 1), (1, -1), (1, 2))


def place(index, move):
    flip, step = move
    return ((index ^ 4) if flip else index) & 4 | ((index + step) & 3)


def dot(a, b):
    return jnp.dot(a, b, preferred_element_type=F32)


def my_core():
    return lax.axis_index("ctx") & 1


def rows_at(i, n):
    return pl.ds(pl.multiple_of(i * n, n), n)


def product_t(order, values):
    return lax.dot_general(order, values, (((1,), (1,)), ((), ())), preferred_element_type=F32)


def dy_kernel(step, w_hbm, d_hbm, *refs):
    outs, (w_ref, d_ref, w_sem, d_sem) = refs[:-4], refs[-4:]
    me = lax.axis_index("fsdp")
    n = outs[0].shape[0]
    copies = [
        pltpu.make_async_copy(w_hbm.at[rows_at(place(me, move), n), :], w_ref.at[pl.ds(i * n, n), :], w_sem.at[i])
        for i, move in enumerate(((0, 0), *MOVES))
    ]
    pieces = range(d_ref.shape[0] // step)
    parts = [
        pltpu.make_async_copy(d_hbm.at[pl.ds(i * step, step), :], d_ref.at[pl.ds(i * step, step), :], d_sem.at[i])
        for i in pieces
    ]
    for copy in (*copies, *parts):
        copy.start()
    for copy in copies:
        copy.wait()
    for i in pieces:
        parts[i].wait()
        rows = pl.ds(i * step, step)
        p = product_t(w_ref[...], d_ref[rows, :]).astype(BF)
        for j, out_ref in enumerate(outs):
            out_ref[:, rows] = p[j * n : (j + 1) * n]


def prep_kernel(k_ref, v_ref, f_ref, order_ref, send_ref):
    ways = send_ref.shape[0]
    mixed = (k_ref[...].astype(F32) * v_ref[...].astype(F32)).astype(BF)
    parts = [product_t(order_ref[...], x).reshape(ways, 1, -1, ROW) for x in (mixed, f_ref[...])]
    send_ref[...] = jnp.concatenate(parts, axis=1).reshape(send_ref.shape).astype(BF)


def turn_query_kernel(q_ref, qt_ref, mine_ref, away_ref):
    qt_ref[...] = q_ref[...].astype(F32).T.astype(BF)
    core, n = my_core(), mine_ref.shape[0]
    mine_ref[...] = qt_ref[rows_at(core, n), :]
    away_ref[...] = qt_ref[rows_at(1 - core, n), :]


def gate_kernel(z_ref, order_ref, q_mine_ref, q_theirs_ref, gated_ref, z_mine_ref, z_away_ref):
    z = dot(order_ref[my_core()], z_ref[...])
    n = z.shape[0] // 2
    z_mine_ref[...] = z[:n].astype(BF)
    z_away_ref[...] = z[n:].astype(BF)
    gated_ref[pl.ds(0, n), :] = (z[:n] * q_mine_ref[...].astype(F32)).astype(BF)
    gated_ref[pl.ds(n, n), :] = (z[n:] * q_theirs_ref[...].astype(F32)).astype(BF)


def dz_kernel(*refs):
    parts, (qt_ref, order_ref, send_ref, dy_ref) = refs[:8], refs[8:]
    dy = parts[0][...].astype(F32)
    for part in parts[1:]:
        dy += part[...].astype(F32)
    dy_ref[...] = dy
    dz = (dy * qt_ref[...].astype(F32)).astype(BF)
    send_ref[...] = dot(order_ref[...], dz).astype(BF)


def transform(x, first_ref, square_ref, tc_ref, ts_ref):
    x = jnp.concatenate([x[:, u * FAC : (u + 1) * FAC] for u in range(LANE_TILES)], axis=0)
    section = dot(first_ref[...], x)
    n = section.shape[0] // 2
    re, im, tc, ts = section[:n], section[n:], tc_ref[...], ts_ref[...]
    b_re, b_im = re * tc + im * ts, im * tc - re * ts
    left = jnp.concatenate([b_re, b_im], axis=0).astype(BF)
    right = jnp.concatenate([b_im, -b_re], axis=0).astype(BF)
    f = dot(left, square_ref[:FAC]) + dot(right, square_ref[FAC:])
    return f[:n], f[n:]


def put_signal(p_re, p_im, last_ref, square_ref, tc_ref, ts_ref, out_ref):
    n, group = p_re.shape[0], p_re.shape[0] // HALF
    left = jnp.concatenate([p_re, p_im], axis=0).astype(BF)
    right = jnp.concatenate([-p_im, p_re], axis=0).astype(BF)
    c = dot(left, square_ref[:FAC]) + dot(right, square_ref[FAC:])
    re, im, tc, ts = c[:n], c[n:], tc_ref[...], ts_ref[...]
    e_re, e_im = re * tc - im * ts, im * tc + re * ts
    e = jnp.concatenate([e_re, e_im[group : n - group]], axis=0).astype(BF)
    x = dot(last_ref[...], e).astype(BF)
    rows = out_ref.shape[0]
    for u in range(LANE_TILES):
        out_ref[:, pl.ds(u * FAC, FAC)] = x[u * rows : (u + 1) * rows]


def conv_kernel(r_ref, first_ref, last_ref, square_ref, tc_ref, ts_ref, z_ref, h_ref):
    rows = z_ref.shape[0]
    group = h_ref.shape[0] // (2 * HALF)
    r = r_ref[...].astype(F32).reshape(-1, 2, group, ROW)
    u, h = (
        transform(r[:, s].reshape(rows, ROW).astype(BF), first_ref, square_ref, tc_ref, ts_ref)
        for s in range(2)
    )
    h_ref[...] = jnp.concatenate(h, axis=0).astype(BF)
    p_re, p_im = u[0] * h[0] - u[1] * h[1], u[0] * h[1] + u[1] * h[0]
    put_signal(p_re, p_im, last_ref, square_ref, tc_ref, ts_ref, z_ref)


def adjoint_kernel(r_ref, h_ref, first_ref, last_ref, square_ref, tc_ref, ts_ref, du_ref):
    g_re, g_im = transform(r_ref[...], first_ref, square_ref, tc_ref, ts_ref)
    h = h_ref[...].astype(F32)
    n = h.shape[0] // 2
    h_re, h_im = h[:n], h[n:]
    q_re, q_im = h_re * g_re + h_im * g_im, h_re * g_im - h_im * g_re
    put_signal(q_re, q_im, last_ref, square_ref, tc_ref, ts_ref, du_ref)


def weight_kernel(scale, width, *refs):
    blocks, (d_ref, d_other_ref, part_ref, mine_ref, away_ref, sem) = refs[:8], refs[8:]
    me = lax.axis_index("fsdp")
    n = blocks[0].shape[0] // 2
    copies = []
    for i, (block, move) in enumerate(zip(blocks, RING_FROM)):
        rows = rows_at(place(me, move), n)
        for j, to_ref in enumerate((mine_ref, away_ref)):
            copies.append(pltpu.make_async_copy(block.at[pl.ds(j * n, n), :], to_ref.at[rows, :], sem.at[2 * i + j]))
    for copy in copies:
        copy.start()
    for copy in copies:
        copy.wait()

    for j in range(d_ref.shape[1] // width):
        cols = pl.ds(j * width, width)
        p = dot(mine_ref[...], d_ref[:, cols]) + dot(away_ref[...], d_other_ref[:, cols])
        part_ref[:, cols] = (p * scale).astype(BF)


def finish_kernel(dy_ref, z_mine_ref, z_theirs_ref, du_ref, order_ref, k_ref, v_ref, gq_ref, gk_ref, gv_ref, gq_t_ref):
    core, n = my_core(), z_mine_ref.shape[0]
    for z_ref, half in ((z_mine_ref, core), (z_theirs_ref, 1 - core)):
        rows = rows_at(half, n)
        gq_t_ref[rows, :] = dy_ref[rows, :] * z_ref[...].astype(F32)
    gq_ref[...] = gq_t_ref[...].T.astype(BF)
    du = dot(du_ref[...].astype(F32).T.astype(BF), order_ref[...])
    gk_ref[...] = (du * v_ref[...].astype(F32)).astype(BF)
    gv_ref[...] = (du * k_ref[...].astype(F32)).astype(BF)


def call(kernel, outs, ins, scratch=(), mib=16, flops=0, specs=None):
    total = sum(math.prod(o.shape) * o.dtype.itemsize for o in (*outs, *ins))
    return pl.pallas_call(
        kernel,
        out_shape=outs,
        in_specs=specs or [VMEM] * len(ins),
        out_specs=[VMEM] * len(outs),
        scratch_shapes=scratch,
        compiler_params=params(mib),
        cost_estimate=pl.CostEstimate(flops=flops, bytes_accessed=total, transcendentals=0),
    )(*ins)


def shape(*dims, dtype=BF):
    return jax.ShapeDtypeStruct(dims, dtype)


def spread(values):
    return lax.all_to_all(values, "ctx", 0, 0, tiled=True)


def move_over(values, move):
    return lax.ppermute(values, "fsdp", [(i, place(i, move)) for i in range(8)])


RING_FROM = ((0, 0), (1, 0), (0, -1), (0, 1), (1, -1), (1, 1), (0, 2), (1, 2))


def ring(gated):
    up, down = (0, 1), (0, -1)
    other = move_over(gated, (1, 0))
    own_up, own_down = move_over(gated, up), move_over(gated, down)
    other_up, other_down = move_over(other, up), move_over(other, down)
    own_far, other_far = move_over(own_up, up), move_over(other_down, down)
    return gated, other, own_up, own_down, other_up, other_down, own_far, other_far


def dy_product(w_out, d_out):
    channels, depth = w_out.shape
    rows = d_out.shape[0]
    n, step = channels // 8, 512
    return call(
        functools.partial(dy_kernel, step),
        [shape(n, rows)] * 8,
        [w_out, d_out],
        [
            pltpu.VMEM((channels, depth), BF),
            pltpu.VMEM((rows, depth), BF),
            pltpu.SemaphoreType.DMA((8,)),
            pltpu.SemaphoreType.DMA((rows // step,)),
        ],
        mib=20,
        flops=2 * channels * depth * rows,
        specs=[ANY, ANY],
    )


def on_device(query_in, key_in, value_in, filt, w_out, d_out):
    seq_rows, width = query_in.shape
    channels, columns = w_out.shape
    ways = lax.axis_size("ctx")
    group, half = width // ways, width // 2
    n = HALF * group
    first, last, square, tc, ts = host_tables(ways, group)
    pick = np.arange(ways * group).reshape(ways // 2, 2, 2, group // 2).transpose(0, 2, 1, 3).reshape(-1)
    last_z = last.reshape(LANE_TILES, ways * group, -1)[:, pick].reshape(last.shape)
    order = channel_order(ways, group)
    order_in = np.eye(width)[order].astype(BF)
    slots = np.arange(width).reshape(ways, 2, group // 2).transpose(1, 0, 2)
    order_z = np.stack([np.eye(width)[slots[list(s)].reshape(-1)] for s in ((0, 1), (1, 0))]).astype(BF)

    core = my_core()
    swap = lambda v: lax.ppermute(v, "ctx", [(i, i ^ 1) for i in range(ways)])
    rows_like, half_like = shape(width, seq_rows), shape(half, seq_rows)

    (send,) = call(prep_kernel, [shape(ways, 2 * group, seq_rows)], [key_in, value_in, filt, order_in])
    arrived = spread(send.reshape(ways * 2 * group, seq_rows))
    own_y, *sent_y = dy_product(w_out, d_out)
    parts_y = [own_y, *(move_over(v, move) for v, move in zip(sent_y, MOVES))]

    query_t, q_mine, q_away = call(turn_query_kernel, [rows_like, half_like, half_like], [query_in])
    q_theirs, d_other = swap(q_away), swap(d_out)

    forward = 2 * 2 * n * (first.shape[1] + 2 * FAC) * FAC
    tables = (square, tc, ts)
    conv, spectrum = call(
        conv_kernel,
        [rows_like, shape(2 * n, FAC)],
        [arrived, first, last_z, *tables],
        mib=32,
        flops=3 * forward,
    )
    gated, z_mine, z_away = call(
        gate_kernel, [rows_like, half_like, half_like], [spread(conv), order_z, q_mine, q_theirs]
    )
    z_theirs = swap(z_away)

    blocks = ring(gated)
    scale = 1.0 / math.sqrt(seq_rows * ways)
    part, mine, away = call(
        functools.partial(weight_kernel, scale, 512),
        [shape(channels // 2, columns), shape(channels // 2, seq_rows), shape(channels // 2, seq_rows)],
        [*blocks, d_out, d_other],
        [pltpu.SemaphoreType.DMA((16,))],
        mib=20,
        flops=2 * channels * seq_rows * columns,
        specs=[ANY] * 8 + [VMEM] * 2,
    )

    send_z, grad_y = call(
        dz_kernel, [rows_like, shape(width, seq_rows, dtype=F32)], [*parts_y, query_t, order_in]
    )
    (adjoint,) = call(
        adjoint_kernel,
        [rows_like],
        [spread(send_z), spectrum, first, last, *tables],
        mib=32,
        flops=2 * forward,
    )
    grad_u = spread(adjoint)

    part, grad_u = lax.optimization_barrier((part, grad_u))
    groups = [list(range(c, ways, 2)) for c in range(2)]
    parts = lax.all_to_all(part, "ctx", 0, 0, tiled=True, axis_index_groups=groups)
    grad_weight = jnp.sum(parts.reshape(ways // 2, channels // ways, columns).astype(F32), axis=0)

    theirs = swap(away)
    split = lambda v: v.reshape(-1, 1, half, seq_rows)
    low, high = jnp.where(core == 0, mine, theirs), jnp.where(core == 0, theirs, mine)
    gated_all = jnp.concatenate([split(low), split(high)], axis=1).reshape(channels, seq_rows)
    layer_out = lax.dot_general(
        gated_all, w_out, (((0,), (0,)), ((), ())), preferred_element_type=F32
    ).astype(BF)

    like = shape(seq_rows, width)
    grad_query, grad_key, grad_value = call(
        finish_kernel,
        [like, like, like],
        [grad_y, z_mine, z_theirs, grad_u, order_in, key_in, value_in],
        [pltpu.VMEM((width, seq_rows), F32)],
    )
    return (layer_out, grad_query, grad_key, grad_value, grad_weight)


def solution(mesh):
    both = P("ctx", "fsdp")
    return jax.shard_map(
        on_device,
        mesh=mesh,
        in_specs=(both, both, both, both, P(None, "fsdp"), both),
        out_specs=(both, both, both, both, both),
        check_vma=False,
    )
```

time: 177 us -> 155 us (0.88)
  starting transfers between devices: 26.4 us -> 50.8 us
  blocking collectives: 22.8 us -> 0 us
  between operations: 14.3 us -> 0.94 us
  Pallas kernels: 28.7 us -> 23.2 us
  waiting for transfers between devices: 49.3 us -> 44.9 us
  local copies, waits for them, and re-layouts: 23.6 us -> 26.9 us
    all_to_all x1 -> x0, blocking collectives: 22.8 us -> none  [spread(): return lax.all_to_all(values, 'ctx', 0, 0, tiled=True)]
    ppermute x7 -> x14, starting transfers between devices: 10.3 us -> 21.5 us  [move_over(): return lax.ppermute(values, 'fsdp', [(i, place(i, move)) for i in range(8)])]
    all_to_all x3 -> x4, starting transfers between devices: 10.8 us -> 21.3 us  [spread(): return lax.all_to_all(values, 'ctx', 0, 0, tiled=True)]
    all_to_all x3 -> x4, waiting for transfers between devices: 20.3 us -> 11.9 us  [spread(): return lax.all_to_all(values, 'ctx', 0, 0, tiled=True)]
    pallas_call x9, Pallas kernels: 28.7 us -> 23.2 us  [call(): pl.pallas_call(kernel, out_shape=outs, in_specs=specs or [VMEM] * len(ins...]
    ppermute x7 -> x14, waiting for transfers between devices: 12.9 us -> 17.2 us  [move_over(): return lax.ppermute(values, 'fsdp', [(i, place(i, move)) for i in range(8)])]
    unnamed x72 -> x84, local copies, waits for them, and re-layouts: 23.5 us -> 26.9 us
    all_to_all x1, starting transfers between devices: 4.25 us -> 6.98 us  [on_device(): lax.all_to_all(part, 'ctx', 0, 0, tiled=True, axis_index_groups=groups)]
  transfers between devices with their start and end apart: 16 -> 23, of which waited for: 10 -> 9; matrix products, arithmetic and copies ran while one was open for 6% -> 1% of each run, Pallas kernels for 13% -> 15%
where the time goes in v3:
time: 155 us; the launch traced here: 154 us
  starting transfers between devices  50.8 us (33%)
  waiting for transfers between devices  44.9 us (29%)
  local copies, waits for them, and re-layouts  26.9 us (17%)
  Pallas kernels  23.2 us (15%)
  matrix products  3.75 us (2%)
  other arithmetic  3.68 us (2%)
    unnamed x84, local copies, waits for them, and re-layouts  26.9 us
    pallas_call x9, Pallas kernels, call(): pl.pallas_call(kernel, out_shape=outs, in_specs=specs or [VMEM] * len(ins...  23.2 us
    ppermute x14, starting transfers between devices, move_over(): return lax.ppermute(values, 'fsdp', [(i, place(i, move)) for i in range(8)])  21.5 us
    all_to_all x4, starting transfers between devices, spread(): return lax.all_to_all(values, 'ctx', 0, 0, tiled=True)  21.3 us
    ppermute x14, waiting for transfers between devices, move_over(): return lax.ppermute(values, 'fsdp', [(i, place(i, move)) for i in range(8)])  17.2 us
    all_to_all x1, waiting for transfers between devices, on_device(): lax.all_to_all(part, 'ctx', 0, 0, tiled=True, axis_index_groups=groups)  13.8 us
    all_to_all x4, waiting for transfers between devices, spread(): return lax.all_to_all(values, 'ctx', 0, 0, tiled=True)  11.9 us
    all_to_all x1, starting transfers between devices, on_device(): lax.all_to_all(part, 'ctx', 0, 0, tiled=True, axis_index_groups=groups)  6.98 us
  transfers between devices with their start and end apart: 23, of which 9 were waited for; matrix products, arithmetic and copies ran while one was open for 1% of the time, Pallas kernels for 15%

profile of v3, /device:TPU:0, one launch (start us, length us, event | category | flops | bytes accessed | tf_op | source)
XLA Modules:
  0.0 154.2 jit_solution(12322407713028734346)
XLA Ops:
  0.7 0.9 copy-done.2
  1.7 0.9 copy-done.4
  2.6 0.8 copy-done.12
  3.4 0.9 copy-done.23
  4.3 1.1 shard_map.173
  5.4 7.2 %all-to-all-start = ((bf16[16,16,1024]{2,1,0:T(8,128)(2,1)}), bf16[16,16,1024]{2,1,0:T(8,128)(2,1)S(1)}, u32[]{:S(2)}, u32[]{:S(2)}) async-start(bf16[16,16,1024]{2,1,0:T(8,128)(2,1)} %shard_map.173), calls=%async_computation | async-start | bytes 1048576 | tf_op jit(solution)/shard_map/all_to_all | solution.py:237
  12.7 0.8 shard_map.175
  13.5 0.7 copy-done.16
  15.4 1.8 %copy-done.29 = bf16[1024,1024]{1,0:T(8,128)(2,1)S(1)} copy-done((bf16[1024,1024]{1,0:T(8,128)(2,1)S(1)}, bf16[1024,1024]{1,0:T(8,128)(2,1)}, u32[]{:S(2)}) %copy-start.29) | copy-done | bytes 2097176
  17.2 1.6 %copy-done.31 = bf16[1024,1024]{1,0:T(8,128)(2,1)S(1)} copy-done((bf16[1024,1024]{1,0:T(8,128)(2,1)S(1)}, bf16[1024,1024]{1,0:T(8,128)(2,1)}, u32[]{:S(2)}) %copy-start.31) | copy-done | bytes 2097176
  18.8 3.6 %shard_map.178 = (bf16[128,1024]{1,0:T(8,128)(2,1)S(1)}, bf16[128,1024]{1,0:T(8,128)(2,1)}, bf16[128,1024]{1,0:T(8,128)(2,1)}, bf16[128,1024]{1,0:T(8,128)(2,1)S...) custom-call(bf16[1024,1024]{1,0:T(8,128)(2,1)S(1)} %copy-done.31, ...), custom_call_target="tpu_custom_call" | custom-call | flops 2147483648 | bytes 6291456 | tf_op jit(solution)/shard_map/pallas_call | solution.py:221
  22.4 0.7 copy-done.18
  23.1 0.7 copy-done.34
  23.8 0.7 copy-done.35
  24.5 0.7 copy-done.36
  25.2 0.7 copy-done.37
  25.9 0.7 copy-done.38
  26.6 1.9 %collective-permute-start.10 = (bf16[128,1024]{1,0:T(8,128)(2,1)}, bf16[128,1024]{1,0:T(8,128)(2,1)}, u32[]{:S(2)}, u32[]{:S(2)}) collective-permute-start(bf16[128,1024]{1,0:T(8,128)(2,1)} %get-tuple-element.38), channel_id=1, source_target_pairs={{0,16},{16,32},{32,48},{48,0},{64,80},{80,96},{96,112},{112,64},{1... | collective-permute-start | bytes 786440 | tf_op jit(solution)/shard_map/ppermute | solution.py:241
  28.5 2.1 %collective-permute-start.11 = (bf16[128,1024]{1,0:T(8,128)(2,1)}, bf16[128,1024]{1,0:T(8,128)(2,1)}, u32[]{:S(2)}, u32[]{:S(2)}) collective-permute-start(bf16[128,1024]{1,0:T(8,128)(2,1)} %get-tuple-element.39), channel_id=1, source_target_pairs={{0,48},{16,0},{32,16},{48,32},{64,112},{80,64},{96,80},{112,96},{1... | collective-permute-start | bytes 786440 | tf_op jit(solution)/shard_map/ppermute | solution.py:241
  30.7 1.2 copy-done.41
  31.9 3.1 %shard_map.174 = (bf16[128,1024]{1,0:T(8,128)(2,1)S(1)}, bf16[1040,256]{1,0:T(8,128)(2,1)S(1)}) custom-call(bf16[256,1024]{1,0:T(8,128)(2,1)S(1)} %bitcast.20, bf16[1040,512]{1,0:T(8,128)(2,1)S(1)} %copy-done, bf16[512,1024]{1,0:T(8,128)(2,1)S(1)} %copy-done.41, bf16[512,256]{1,0:T(8,128)(2,1)S(1)} %copy-done.14, f32[520,256]{1,0:T(8,128)S(1)} %copy-done.7, ...), custom_call_target="tpu_custom_call" | custom-call | flops 1635778560 | bytes 4759552 | tf_op jit(solution)/shard_map/pallas_call | solution.py:221
  35.0 0.8 copy-done.8
  35.8 0.7 copy-done.22
  36.5 7.0 %all-to-all-start.1 = ((bf16[16,8,1024]{2,1,0:T(8,128)(2,1)}), bf16[16,8,1024]{2,1,0:T(8,128)(2,1)S(1)}, u32[]{:S(2)}, u32[]{:S(2)}) async-start(bf16[16,8,1024]{2,1,0:T(8,128)(2,1)} %bitcast.22), calls=%async_computation.1 | async-start | bytes 524288 | tf_op jit(solution)/shard_map/all_to_all | solution.py:237
  43.5 0.7 collective-permute-start.12
  44.2 1.9 %collective-permute-start.13 = (bf16[128,1024]{1,0:T(8,128)(2,1)}, bf16[128,1024]{1,0:T(8,128)(2,1)}, u32[]{:S(2)}, u32[]{:S(2)}) collective-permute-start(bf16[128,1024]{1,0:T(8,128)(2,1)} %copy-done.37), channel_id=1, source_target_pairs={{0,32},{16,48},{32,0},{48,16},{64,96},{80,112},{96,64},{112,80},{1... | collective-permute-start | bytes 786440 | tf_op jit(solution)/shard_map/ppermute | solution.py:241
  46.0 7.5 %all-to-all-done.1 = bf16[16,8,1024]{2,1,0:T(8,128)(2,1)S(1)} async-done(((bf16[16,8,1024]{2,1,0:T(8,128)(2,1)}), bf16[16,8,1024]{2,1,0:T(8,128)(2,1)S(1)}, u32[]{:S(2)}, u32[]{:S(2)}) %all-to-all-start.1) | async-done | bytes 262176 | tf_op jit(solution)/shard_map/all_to_all | solution.py:237
  53.5 0.9 copy-done.27
  54.4 1.8 %shard_map.176 = (bf16[128,1024]{1,0:T(8,128)(2,1)}, bf16[64,1024]{1,0:T(8,128)(2,1)S(1)}, bf16[64,1024]{1,0:T(8,128)(2,1)S(1)}) custom-call(bf16[128,1024]{1,0:T(8,128)(2,1)S(1)} %bitcast.19, bf16[2,128,128]{2,1,0:T(8,128)(2,1)S(1)} %copy-done.28, bf16[64,1024]{1,0:T(8,128)(2,1)S(1)} %copy-done.27, bf16[64,1024]{1,0:T(8,128)(2,1)} %collective-permute-done.q_theirs_ref), custom_call_target="tpu_custom_call" | custom-call | bytes 1114112 | tf_op jit(solution)/shard_map/pallas_call | solution.py:221
  56.9 0.7 copy-done.39
  57.6 1.4 collective-permute-start.1
  58.9 3.4 %collective-permute-start.15 = (bf16[128,1024]{1,0:T(8,128)(2,1)}, bf16[128,1024]{1,0:T(8,128)(2,1)S(1)}, u32[]{:S(2)}, u32[]{:S(2)}) collective-permute-start(bf16[128,1024]{1,0:T(8,128)(2,1)} %copy-done.35), channel_id=1, source_target_pairs={{0,112},{16,64},{32,80},{48,96},{64,48},{80,0},{96,16},{112,32},{1... | collective-permute-start | bytes 786440 | tf_op jit(solution)/shard_map/ppermute | solution.py:241
  62.3 1.5 collective-permute-start.16
  63.8 5.3 %collective-permute-done.14.refs_5_ = bf16[128,1024]{1,0:T(8,128)(2,1)S(1)} collective-permute-done((bf16[128,1024]{1,0:T(8,128)(2,1)}, bf16[128,1024]{1,0:T(8,128)(2,1)S(1)}, u32[]{:S(2)}, u32[]{:S(2)}) %collective-permute-start.14) | collective-permute-done | bytes 262176 | tf_op jit(solution)/shard_map/ppermute | solution.py:241
  69.1 3.0 %collective-permute-done.1.refs_1_ = bf16[128,1024]{1,0:T(8,128)(2,1)} collective-permute-done((bf16[128,1024]{1,0:T(8,128)(2,1)}, bf16[128,1024]{1,0:T(8,128)(2,1)}, u32[]{:S(2)}, u32[]{:S(2)}) %collective-permute-start.1) | collective-permute-done | bytes 262176 | tf_op jit(solution)/shard_map/ppermute | solution.py:241
  72.1 3.3 %collective-permute-start.5 = (bf16[128,1024]{1,0:T(8,128)(2,1)}, bf16[128,1024]{1,0:T(8,128)(2,1)}, u32[]{:S(2)}, u32[]{:S(2)}) collective-permute-start(bf16[128,1024]{1,0:T(8,128)(2,1)} %collective-permute-done.1.refs_1_), channel_id=1, source_target_pairs={{0,48},{16,0},{32,16},{48,32},{64,112},{80,64},{96,80},{112,96},{1... | collective-permute-start | bytes 786440 | tf_op jit(solution)/shard_map/ppermute | solution.py:241
  75.4 3.6 %collective-permute-done.15.refs_6_ = bf16[128,1024]{1,0:T(8,128)(2,1)S(1)} collective-permute-done((bf16[128,1024]{1,0:T(8,128)(2,1)}, bf16[128,1024]{1,0:T(8,128)(2,1)S(1)}, u32[]{:S(2)}, u32[]{:S(2)}) %collective-permute-start.15) | collective-permute-done | bytes 262176 | tf_op jit(solution)/shard_map/ppermute | solution.py:241
  79.1 5.2 %collective-permute-done.16.refs_7_ = bf16[128,1024]{1,0:T(8,128)(2,1)S(1)} collective-permute-done((bf16[128,1024]{1,0:T(8,128)(2,1)}, bf16[128,1024]{1,0:T(8,128)(2,1)S(1)}, u32[]{:S(2)}, u32[]{:S(2)}) %collective-permute-start.16) | collective-permute-done | bytes 262176 | tf_op jit(solution)/shard_map/ppermute | solution.py:241
  84.3 0.9 copy-done.17
  85.3 0.9 copy-done.19
  86.2 1.7 %shard_map.179 = (bf16[128,1024]{1,0:T(8,128)(2,1)S(1)}, f32[128,1024]{1,0:T(8,128)S(1)}) custom-call(bf16[128,1024]{1,0:T(8,128)(2,1)S(1)} %copy-done.19, bf16[128,1024]{1,0:T(8,128)(2,1)} %collective-permute-done.10.refs_1_, bf16[128,1024]{1,0:T(8,128)(2,1)} %collective-permute-done.11.refs_2_, bf16[128,1024]{1,0:T(8,128)(2,1)} %collective-permute-done.12.refs_3_, ...), custom_call_target="tpu_custom_call" | custom-call | bytes 3178496 | tf_op jit(solution)/shard_map/pallas_call | solution.py:221
  87.9 0.8 copy-done.10
  88.7 0.7 copy-done.21
  89.4 3.5 %all-to-all-start.2 = ((bf16[16,8,1024]{2,1,0:T(8,128)(2,1)}), bf16[16,8,1024]{2,1,0:T(8,128)(2,1)S(1)}, u32[]{:S(2)}, u32[]{:S(2)}) async-start(bf16[16,8,1024]{2,1,0:T(8,128)(2,1)} %bitcast.21), calls=%async_computation.2 | async-start | bytes 524288 | tf_op jit(solution)/shard_map/all_to_all | solution.py:237
  92.9 1.2 collective-permute-start.3
  94.1 0.9 collective-permute-start.4
  95.1 0.7 collective-permute-start.6
  95.8 2.5 %collective-permute-start.7 = (bf16[128,1024]{1,0:T(8,128)(2,1)}, bf16[128,1024]{1,0:T(8,128)(2,1)}, u32[]{:S(2)}, u32[]{:S(2)}) collective-permute-start(bf16[128,1024]{1,0:T(8,128)(2,1)} %collective-permute-done.5.refs_5_), channel_id=1, source_target_pairs={{0,48},{16,0},{32,16},{48,32},{64,112},{80,64},{96,80},{112,96},{1... | collective-permute-start | bytes 786440 | tf_op jit(solution)/shard_map/ppermute | solution.py:241
  98.3 4.1 %all-to-all-done.2 = bf16[16,8,1024]{2,1,0:T(8,128)(2,1)S(1)} async-done(((bf16[16,8,1024]{2,1,0:T(8,128)(2,1)}), bf16[16,8,1024]{2,1,0:T(8,128)(2,1)S(1)}, u32[]{:S(2)}, u32[]{:S(2)}) %all-to-all-start.2) | async-done | bytes 262176 | tf_op jit(solution)/shard_map/all_to_all | solution.py:237
  102.5 1.0 copy-done.9
  103.5 0.9 copy-done.15
  104.4 3.2 %shard_map.180 = bf16[128,1024]{1,0:T(8,128)(2,1)} custom-call(bf16[128,1024]{1,0:T(8,128)(2,1)S(1)} %bitcast.18, bf16[1040,256]{1,0:T(8,128)(2,1)S(1)} %copy-done.9, bf16[1040,512]{1,0:T(8,128)(2,1)S(1)} %copy-done, bf16[512,1024]{1,0:T(8,128)(2,1)S(1)} %copy-done.1, bf16[512,256]{1,0:T(8,128)(2,1)S(1)} %copy-done.15, f32[520,256]{1,0:T(8,128)S(1)} %copy-done.7, ...), custom_call_target="tpu_custom_call" | custom-call | flops 1090519040 | bytes 4497408 | tf_op jit(solution)/shard_map/pallas_call | solution.py:221
  107.7 3.5 %all-to-all-start.3 = ((bf16[16,8,1024]{2,1,0:T(8,128)(2,1)}), bf16[16,8,1024]{2,1,0:T(8,128)(2,1)S(1)}, u32[]{:S(2)}, u32[]{:S(2)}) async-start(bf16[16,8,1024]{2,1,0:T(8,128)(2,1)} %bitcast.10), calls=%async_computation.3 | async-start | bytes 524288 | tf_op jit(solution)/shard_map/all_to_all | solution.py:237
  111.3 1.6 %copy-done.30 = bf16[1024,1024]{1,0:T(8,128)(2,1)S(1)} copy-done((bf16[1024,1024]{1,0:T(8,128)(2,1)S(1)}, bf16[1024,1024]{1,0:T(8,128)(2,1)}, u32[]{:S(2)}) %copy-start.30) | copy-done | bytes 2097176
  112.9 6.6 %shard_map.177 = (bf16[512,1024]{1,0:T(8,128)(2,1)}, bf16[512,1024]{1,0:T(8,128)(2,1)S(1)}, bf16[512,1024]{1,0:T(8,128)(2,1)S(1)}) custom-call(bf16[128,1024]{1,0:T(8,128)(2,1)} %get-tuple-element.34.refs_0_, bf16[128,1024]{1,0:T(8,128)(2,1)} %collective-permute-done.1.refs_1_, bf16[128,1024]{1,0:T(8,128)(2,1)} %collective-permute-done.2.refs_2_, ...), custom_call_target="tpu_custom_call" | custom-call | flops 2147483648 | bytes 9437184 | tf_op jit(solution)/shard_map/pallas_call | solution.py:221
  119.5 1.0 copy-done.33
  120.7 7.0 %all-to-all-start.4 = ((bf16[8,64,1024]{2,1,0:T(8,128)(2,1)}), bf16[8,64,1024]{2,1,0:T(8,128)(2,1)}, u32[]{:S(2)}, u32[]{:S(2)}) async-start(bf16[8,64,1024]{2,1,0:T(8,128)(2,1)} %bitcast.12), calls=%async_computation.4 | async-start | bytes 2097152 | tf_op jit(solution)/shard_map/all_to_all | solution.py:342
  128.2 2.0 %collective-permute-done.17.z_theirs_ref = bf16[64,1024]{1,0:T(8,128)(2,1)S(1)} collective-permute-done((bf16[64,1024]{1,0:T(8,128)(2,1)S(1)}, bf16[64,1024]{1,0:T(8,128)(2,1)S(1)}, u32[]{:S(2)}, u32[]{:S(2)}) %collective-permute-start.17) | collective-permute-done | bytes 131104 | tf_op jit(solution)/shard_map/ppermute | solution.py:291
  130.3 1.3 shard_map.181
  131.6 13.8 %all-to-all-done.4 = bf16[8,64,1024]{2,1,0:T(8,128)(2,1)} async-done(((bf16[8,64,1024]{2,1,0:T(8,128)(2,1)}), bf16[8,64,1024]{2,1,0:T(8,128)(2,1)}, u32[]{:S(2)}, u32[]{:S(2)}) %all-to-all-start.4) | async-done | bytes 1048608 | tf_op jit(solution)/shard_map/all_to_all | solution.py:342
  145.4 2.1 %convert_reduce_fusion = f32[64,1024]{1,0:T(8,128)} fusion(bf16[8,64,1024]{2,1,0:T(8,128)(2,1)} %all-to-all-done.4), kind=kLoop, calls=%fused_computation.1 | loop fusion | flops 983040 | bytes 1310720 | tf_op jit(solution)/shard_map/reduce_sum | solution.py:343
  147.5 1.4 broadcast_select_fusion.1
  149.1 1.4 copy-done.32
  150.5 3.8 %convolution_convert_fusion = bf16[1024,1024]{1,0:T(8,128)(2,1)} fusion(bf16[1024,1024]{1,0:T(8,128)(2,1)S(1)} %bitcast.25, bf16[1024,1024]{1,0:T(8,128)(2,1)S(1)} %copy-done.32), kind=kOutput, calls=%fused_computation.2 | convolution fusion | flops 2148532224 | bytes 6291456 | tf_op jit(solution)/shard_map/dot_general | solution.py:349
  (79 shorter events, 2.9 us)
Async XLA Ops:
  0.6 110.6 %collective-permute-start.8 = (bf16[1024,1024]{1,0:T(8,128)(2,1)}, bf16[1024,1024]{1,0:T(8,128)(2,1)}, u32[]{:S(2)}, u32[]{:S(2)}) collective-permute-start(bf16[1024,1024]{1,0:T(8,128)(2,1)} %d_hbm.1), channel_id=1, source_target_pairs={{0,1},{1,0},{2,3},{3,2},{4,5},{5,4},{6,7},{7,6},{8,9},{9,8},{10,11... | collective-permute-start | bytes 6291464 | tf_op jit(solution)/shard_map/ppermute | solution.py:291
  0.7 1.0 copy-start.2
  1.7 0.9 copy-start.4
  2.6 0.8 copy-start.12
  3.4 0.9 copy-start.23
  4.3 8.3 %copy-start.20 = (bf16[1024,128]{1,0:T(8,128)(2,1)S(1)}, bf16[1024,128]{1,0:T(8,128)(2,1)}, u32[]{:S(2)}) copy-start(bf16[1024,128]{1,0:T(8,128)(2,1)} %q_ref.1) | copy-start | bytes 786436
  5.4 25.2 %all-to-all-start = ((bf16[16,16,1024]{2,1,0:T(8,128)(2,1)}), bf16[16,16,1024]{2,1,0:T(8,128)(2,1)S(1)}, u32[]{:S(2)}, u32[]{:S(2)}) async-start(bf16[16,16,1024]{2,1,0:T(8,128)(2,1)} %shard_map.173), calls=%async_computation | async-start | bytes 1048576 | tf_op jit(solution)/shard_map/all_to_all | solution.py:237
  13.5 0.7 copy-start.16
  14.2 0.7 copy-start.26
  14.9 15.8 %copy-start = (bf16[1040,512]{1,0:T(8,128)(2,1)S(1)}, bf16[1040,512]{1,0:T(8,128)(2,1)}, u32[]{:S(2)}) copy-start(bf16[1040,512]{1,0:T(8,128)(2,1)} %constant.27.clone.first_ref) | copy-start | bytes 3194884
  14.9 15.8 %copy-start.6 = (f32[520,256]{1,0:T(8,128)S(1)}, f32[520,256]{1,0:T(8,128)}, u32[]{:S(2)}) copy-start(f32[520,256]{1,0:T(8,128)} %constant.31.clone.ts_ref) | copy-start | bytes 1597444
  14.9 15.8 %copy-start.7 = (f32[520,256]{1,0:T(8,128)S(1)}, f32[520,256]{1,0:T(8,128)}, u32[]{:S(2)}) copy-start(f32[520,256]{1,0:T(8,128)} %constant.30.clone.tc_ref) | copy-start | bytes 1597444
  14.9 15.8 %copy-start.14 = (bf16[512,256]{1,0:T(8,128)(2,1)S(1)}, bf16[512,256]{1,0:T(8,128)(2,1)}, u32[]{:S(2)}) copy-start(bf16[512,256]{1,0:T(8,128)(2,1)} %constant.29.clone.square_ref) | copy-start | bytes 786436
  14.9 29.3 %collective-permute-start = (bf16[64,1024]{1,0:T(8,128)(2,1)}, bf16[64,1024]{1,0:T(8,128)(2,1)}, u32[]{:S(2)}, u32[]{:S(2)}) collective-permute-start(bf16[64,1024]{1,0:T(8,128)(2,1)} %get-tuple-element.33), channel_id=1, source_target_pairs={{0,1},{1,0},{2,3},{3,2},{4,5},{5,4},{6,7},{7,6},{8,9},{9,8},{10,11... | collective-permute-start | bytes 393224 | tf_op jit(solution)/shard_map/ppermute | solution.py:291
  15.4 1.8 %copy-start.29 = (bf16[1024,1024]{1,0:T(8,128)(2,1)S(1)}, bf16[1024,1024]{1,0:T(8,128)(2,1)}, u32[]{:S(2)}) copy-start(bf16[1024,1024]{1,0:T(8,128)(2,1)} %d_hbm.1) | copy-start | bytes 6291460
  17.2 1.6 %copy-start.31 = (bf16[1024,1024]{1,0:T(8,128)(2,1)S(1)}, bf16[1024,1024]{1,0:T(8,128)(2,1)}, u32[]{:S(2)}) copy-start(bf16[1024,1024]{1,0:T(8,128)(2,1)} %w_hbm.1) | copy-start | bytes 6291460
  22.4 0.7 copy-start.18
  23.1 0.7 copy-start.34
  23.8 0.7 copy-start.35
  24.5 0.7 copy-start.36
  25.2 0.7 copy-start.37
  25.9 0.7 copy-start.38
  26.6 31.0 %collective-permute-start.10 = (bf16[128,1024]{1,0:T(8,128)(2,1)}, bf16[128,1024]{1,0:T(8,128)(2,1)}, u32[]{:S(2)}, u32[]{:S(2)}) collective-permute-start(bf16[128,1024]{1,0:T(8,128)(2,1)} %get-tuple-element.38), channel_id=1, source_target_pairs={{0,16},{16,32},{32,48},{48,0},{64,80},{80,96},{96,112},{112,64},{1... | collective-permute-start | bytes 786440 | tf_op jit(solution)/shard_map/ppermute | solution.py:241
  28.5 29.1 %collective-permute-start.11 = (bf16[128,1024]{1,0:T(8,128)(2,1)}, bf16[128,1024]{1,0:T(8,128)(2,1)}, u32[]{:S(2)}, u32[]{:S(2)}) collective-permute-start(bf16[128,1024]{1,0:T(8,128)(2,1)} %get-tuple-element.39), channel_id=1, source_target_pairs={{0,48},{16,0},{32,16},{48,32},{64,112},{80,64},{96,80},{112,96},{1... | collective-permute-start | bytes 786440 | tf_op jit(solution)/shard_map/ppermute | solution.py:241
  30.7 1.2 copy-start.41
  31.9 21.6 %copy-start.28 = (bf16[2,128,128]{2,1,0:T(8,128)(2,1)S(1)}, bf16[2,128,128]{2,1,0:T(8,128)(2,1)}, u32[]{:S(2)}) copy-start(bf16[2,128,128]{2,1,0:T(8,128)(2,1)} %constant.32.clone.order_ref) | copy-start | bytes 196612
  31.9 52.4 %copy-start.13 = (bf16[128,128]{1,0:T(8,128)(2,1)S(1)}, bf16[128,128]{1,0:T(8,128)(2,1)}, u32[]{:S(2)}) copy-start(bf16[128,128]{1,0:T(8,128)(2,1)} %constant.26.clone.order_ref.refs_9_) | copy-start | bytes 98308
  35.0 0.8 copy-start.8
  35.8 0.7 copy-start.22
  36.5 65.9 %copy-start.1 = (bf16[512,1024]{1,0:T(8,128)(2,1)S(1)}, bf16[512,1024]{1,0:T(8,128)(2,1)}, u32[]{:S(2)}) copy-start(bf16[512,1024]{1,0:T(8,128)(2,1)} %constant.33.clone.last_ref) | copy-start | bytes 3145732
  36.5 17.0 %all-to-all-start.1 = ((bf16[16,8,1024]{2,1,0:T(8,128)(2,1)}), bf16[16,8,1024]{2,1,0:T(8,128)(2,1)S(1)}, u32[]{:S(2)}, u32[]{:S(2)}) async-start(bf16[16,8,1024]{2,1,0:T(8,128)(2,1)} %bitcast.22), calls=%async_computation.1 | async-start | bytes 524288 | tf_op jit(solution)/shard_map/all_to_all | solution.py:237
  43.5 15.4 %collective-permute-start.12 = (bf16[128,1024]{1,0:T(8,128)(2,1)}, bf16[128,1024]{1,0:T(8,128)(2,1)}, u32[]{:S(2)}, u32[]{:S(2)}) collective-permute-start(bf16[128,1024]{1,0:T(8,128)(2,1)} %copy-done.38), channel_id=1, source_target_pairs={{0,64},{16,80},{32,96},{48,112},{64,0},{80,16},{96,32},{112,48},{1... | collective-permute-start | bytes 786440 | tf_op jit(solution)/shard_map/ppermute | solution.py:241
  44.2 18.1 %collective-permute-start.13 = (bf16[128,1024]{1,0:T(8,128)(2,1)}, bf16[128,1024]{1,0:T(8,128)(2,1)}, u32[]{:S(2)}, u32[]{:S(2)}) collective-permute-start(bf16[128,1024]{1,0:T(8,128)(2,1)} %copy-done.37), channel_id=1, source_target_pairs={{0,32},{16,48},{32,0},{48,16},{64,96},{80,112},{96,64},{112,80},{1... | collective-permute-start | bytes 786440 | tf_op jit(solution)/shard_map/ppermute | solution.py:241
  53.5 0.9 copy-start.27
  56.9 0.7 copy-start.39
  57.6 11.6 %collective-permute-start.14 = (bf16[128,1024]{1,0:T(8,128)(2,1)}, bf16[128,1024]{1,0:T(8,128)(2,1)S(1)}, u32[]{:S(2)}, u32[]{:S(2)}) collective-permute-start(bf16[128,1024]{1,0:T(8,128)(2,1)} %copy-done.36), channel_id=1, source_target_pairs={{0,80},{16,96},{32,112},{48,64},{64,16},{80,32},{96,48},{112,0},{1... | collective-permute-start | bytes 786440 | tf_op jit(solution)/shard_map/ppermute | solution.py:241
  57.6 14.5 %collective-permute-start.1 = (bf16[128,1024]{1,0:T(8,128)(2,1)}, bf16[128,1024]{1,0:T(8,128)(2,1)}, u32[]{:S(2)}, u32[]{:S(2)}) collective-permute-start(bf16[128,1024]{1,0:T(8,128)(2,1)} %get-tuple-element.34.refs_0_), channel_id=1, source_target_pairs={{0,64},{16,80},{32,96},{48,112},{64,0},{80,16},{96,32},{112,48},{1... | collective-permute-start | bytes 786440 | tf_op jit(solution)/shard_map/ppermute | solution.py:241
  58.9 20.1 %collective-permute-start.15 = (bf16[128,1024]{1,0:T(8,128)(2,1)}, bf16[128,1024]{1,0:T(8,128)(2,1)S(1)}, u32[]{:S(2)}, u32[]{:S(2)}) collective-permute-start(bf16[128,1024]{1,0:T(8,128)(2,1)} %copy-done.35), channel_id=1, source_target_pairs={{0,112},{16,64},{32,80},{48,96},{64,48},{80,0},{96,16},{112,32},{1... | collective-permute-start | bytes 786440 | tf_op jit(solution)/shard_map/ppermute | solution.py:241
  62.3 22.0 %collective-permute-start.16 = (bf16[128,1024]{1,0:T(8,128)(2,1)}, bf16[128,1024]{1,0:T(8,128)(2,1)S(1)}, u32[]{:S(2)}, u32[]{:S(2)}) collective-permute-start(bf16[128,1024]{1,0:T(8,128)(2,1)} %copy-done.34), channel_id=1, source_target_pairs={{0,96},{16,112},{32,64},{48,80},{64,32},{80,48},{96,0},{112,16},{1... | collective-permute-start | bytes 786440 | tf_op jit(solution)/shard_map/ppermute | solution.py:241
  69.1 25.9 %collective-permute-start.2 = (bf16[128,1024]{1,0:T(8,128)(2,1)}, bf16[128,1024]{1,0:T(8,128)(2,1)}, u32[]{:S(2)}, u32[]{:S(2)}) collective-permute-start(bf16[128,1024]{1,0:T(8,128)(2,1)} %get-tuple-element.34.refs_0_), channel_id=1, source_target_pairs={{0,16},{16,32},{32,48},{48,0},{64,80},{80,96},{96,112},{112,64},{1... | collective-permute-start | bytes 786440 | tf_op jit(solution)/shard_map/ppermute | solution.py:241
  72.1 23.7 %collective-permute-start.5 = (bf16[128,1024]{1,0:T(8,128)(2,1)}, bf16[128,1024]{1,0:T(8,128)(2,1)}, u32[]{:S(2)}, u32[]{:S(2)}) collective-permute-start(bf16[128,1024]{1,0:T(8,128)(2,1)} %collective-permute-done.1.refs_1_), channel_id=1, source_target_pairs={{0,48},{16,0},{32,16},{48,32},{64,112},{80,64},{96,80},{112,96},{1... | collective-permute-start | bytes 786440 | tf_op jit(solution)/shard_map/ppermute | solution.py:241
  84.3 1.0 copy-start.17
  85.3 0.9 copy-start.19
  87.9 0.8 copy-start.10
  88.7 0.7 copy-start.21
  89.4 13.1 %all-to-all-start.2 = ((bf16[16,8,1024]{2,1,0:T(8,128)(2,1)}), bf16[16,8,1024]{2,1,0:T(8,128)(2,1)S(1)}, u32[]{:S(2)}, u32[]{:S(2)}) async-start(bf16[16,8,1024]{2,1,0:T(8,128)(2,1)} %bitcast.21), calls=%async_computation.2 | async-start | bytes 524288 | tf_op jit(solution)/shard_map/all_to_all | solution.py:237
  92.9 18.3 %collective-permute-start.3 = (bf16[128,1024]{1,0:T(8,128)(2,1)}, bf16[128,1024]{1,0:T(8,128)(2,1)}, u32[]{:S(2)}, u32[]{:S(2)}) collective-permute-start(bf16[128,1024]{1,0:T(8,128)(2,1)} %get-tuple-element.34.refs_0_), channel_id=1, source_target_pairs={{0,48},{16,0},{32,16},{48,32},{64,112},{80,64},{96,80},{112,96},{1... | collective-permute-start | bytes 786440 | tf_op jit(solution)/shard_map/ppermute | solution.py:241
  94.1 17.1 %collective-permute-start.4 = (bf16[128,1024]{1,0:T(8,128)(2,1)}, bf16[128,1024]{1,0:T(8,128)(2,1)}, u32[]{:S(2)}, u32[]{:S(2)}) collective-permute-start(bf16[128,1024]{1,0:T(8,128)(2,1)} %collective-permute-done.1.refs_1_), channel_id=1, source_target_pairs={{0,16},{16,32},{32,48},{48,0},{64,80},{80,96},{96,112},{112,64},{1... | collective-permute-start | bytes 786440 | tf_op jit(solution)/shard_map/ppermute | solution.py:241
  95.1 16.2 %collective-permute-start.6 = (bf16[128,1024]{1,0:T(8,128)(2,1)}, bf16[128,1024]{1,0:T(8,128)(2,1)}, u32[]{:S(2)}, u32[]{:S(2)}) collective-permute-start(bf16[128,1024]{1,0:T(8,128)(2,1)} %collective-permute-done.2.refs_2_), channel_id=1, source_target_pairs={{0,16},{16,32},{32,48},{48,0},{64,80},{80,96},{96,112},{112,64},{1... | collective-permute-start | bytes 786440 | tf_op jit(solution)/shard_map/ppermute | solution.py:241
  95.8 15.5 %collective-permute-start.7 = (bf16[128,1024]{1,0:T(8,128)(2,1)}, bf16[128,1024]{1,0:T(8,128)(2,1)}, u32[]{:S(2)}, u32[]{:S(2)}) collective-permute-start(bf16[128,1024]{1,0:T(8,128)(2,1)} %collective-permute-done.5.refs_5_), channel_id=1, source_target_pairs={{0,48},{16,0},{32,16},{48,32},{64,112},{80,64},{96,80},{112,96},{1... | collective-permute-start | bytes 786440 | tf_op jit(solution)/shard_map/ppermute | solution.py:241
  102.5 1.0 copy-start.9
  103.5 0.9 copy-start.15
  107.7 13.1 %all-to-all-start.3 = ((bf16[16,8,1024]{2,1,0:T(8,128)(2,1)}), bf16[16,8,1024]{2,1,0:T(8,128)(2,1)S(1)}, u32[]{:S(2)}, u32[]{:S(2)}) async-start(bf16[16,8,1024]{2,1,0:T(8,128)(2,1)} %bitcast.10), calls=%async_computation.3 | async-start | bytes 524288 | tf_op jit(solution)/shard_map/all_to_all | solution.py:237
  111.3 1.6 %copy-start.30 = (bf16[1024,1024]{1,0:T(8,128)(2,1)S(1)}, bf16[1024,1024]{1,0:T(8,128)(2,1)}, u32[]{:S(2)}) copy-start(bf16[1024,1024]{1,0:T(8,128)(2,1)} %d_hbm.1) | copy-start | bytes 6291460
  119.5 1.0 copy-start.33
  120.5 7.2 %copy-start.40 = (bf16[64,1024]{1,0:T(8,128)(2,1)S(1)}, bf16[64,1024]{1,0:T(8,128)(2,1)}, u32[]{:S(2)}) copy-start(bf16[64,1024]{1,0:T(8,128)(2,1)} %copy-done.39) | copy-start | bytes 393220
  120.5 9.8 %copy-start.3 = (bf16[1024,128]{1,0:T(8,128)(2,1)S(1)}, bf16[1024,128]{1,0:T(8,128)(2,1)}, u32[]{:S(2)}) copy-start(bf16[1024,128]{1,0:T(8,128)(2,1)} %k_ref.3) | copy-start | bytes 786436
  120.5 9.8 %copy-start.5 = (bf16[1024,128]{1,0:T(8,128)(2,1)S(1)}, bf16[1024,128]{1,0:T(8,128)(2,1)}, u32[]{:S(2)}) copy-start(bf16[1024,128]{1,0:T(8,128)(2,1)} %v_ref.3) | copy-start | bytes 786436
  120.5 9.8 %copy-start.11 = (f32[128,1024]{1,0:T(8,128)S(1)}, f32[128,1024]{1,0:T(8,128)}, u32[]{:S(2)}) copy-start(f32[128,1024]{1,0:T(8,128)} %copy-done.10) | copy-start | bytes 1572868
  120.5 9.8 %copy-start.25 = (bf16[64,1024]{1,0:T(8,128)(2,1)S(1)}, bf16[64,1024]{1,0:T(8,128)(2,1)}, u32[]{:S(2)}) copy-start(bf16[64,1024]{1,0:T(8,128)(2,1)} %copy-done.24) | copy-start | bytes 393220
  120.7 24.6 %all-to-all-start.4 = ((bf16[8,64,1024]{2,1,0:T(8,128)(2,1)}), bf16[8,64,1024]{2,1,0:T(8,128)(2,1)}, u32[]{:S(2)}, u32[]{:S(2)}) async-start(bf16[8,64,1024]{2,1,0:T(8,128)(2,1)} %bitcast.12), calls=%async_computation.4 | async-start | bytes 2097152 | tf_op jit(solution)/shard_map/all_to_all | solution.py:342
  127.7 19.8 %collective-permute-start.9 = (bf16[512,1024]{1,0:T(8,128)(2,1)}, bf16[512,1024]{1,0:T(8,128)(2,1)}, u32[]{:S(2)}, u32[]{:S(2)}) collective-permute-start(bf16[512,1024]{1,0:T(8,128)(2,1)} %copy-done.33), channel_id=1, source_target_pairs={{0,1},{1,0},{2,3},{3,2},{4,5},{5,4},{6,7},{7,6},{8,9},{9,8},{10,11... | collective-permute-start | bytes 3145736 | tf_op jit(solution)/shard_map/ppermute | solution.py:291
  127.8 2.5 %collective-permute-start.17 = (bf16[64,1024]{1,0:T(8,128)(2,1)S(1)}, bf16[64,1024]{1,0:T(8,128)(2,1)S(1)}, u32[]{:S(2)}, u32[]{:S(2)}) collective-permute-start(bf16[64,1024]{1,0:T(8,128)(2,1)S(1)} %copy-done.40), channel_id=1, source_target_pairs={{0,1},{1,0},{2,3},{3,2},{4,5},{5,4},{6,7},{7,6},{8,9},{9,8},{10,11... | collective-permute-start | bytes 393224 | tf_op jit(solution)/shard_map/ppermute | solution.py:291
  148.9 1.6 %copy-start.32 = (bf16[1024,1024]{1,0:T(8,128)(2,1)S(1)}, bf16[1024,1024]{1,0:T(8,128)(2,1)}, u32[]{:S(2)}) copy-start(bf16[1024,1024]{1,0:T(8,128)(2,1)} %w_hbm.1) | copy-start | bytes 6291460
  (1 other events, 0.6 us)

commit v4 on v3

v4 whole, which is shorter than its diff:
```python
import functools
import math

import jax
import jax.numpy as jnp
import numpy as np
from jax import lax
from jax.experimental import pallas as pl
from jax.experimental.pallas import tpu as pltpu
from jax.sharding import PartitionSpec as P

ROW = 1024
FAC = 256
QF = 128
HALF = QF // 2 + 1
LANE_TILES = ROW // FAC
BF = jnp.bfloat16
F32 = jnp.float32
MIB = 1 << 20


def angles(rows, cols, modulus):
    product = (rows[:, None].astype(np.int64) * cols[None, :]) % modulus
    return (product.astype(np.float32) * np.float32(2.0 * math.pi / modulus)).astype(np.float64)


def host_tables(ways, group):
    k2, t1 = np.arange(HALF), np.arange(FAC)
    t2 = (np.arange(LANE_TILES)[:, None] + LANE_TILES * np.arange(ways)[None, :]).reshape(-1)
    eye = np.eye(group)
    a = angles(k2, t2, QF)
    steps = np.stack([np.cos(a), -np.sin(a)])
    first = np.einsum("rkt,cd->rkctd", steps, eye).reshape(2 * HALF * group, t2.size * group)
    weight = np.where((k2 == 0) | (k2 == QF // 2), 1.0, 2.0) / (QF * FAC)
    b = angles(t2, k2, QF)
    back = np.concatenate([np.cos(b) * weight, (-np.sin(b) * weight)[:, 1:-1]], axis=1)
    last = np.einsum("tk,cd->tckd", back, eye).reshape(t2.size * group, -1)
    s = angles(t1, t1, FAC)
    square = np.concatenate([np.cos(s), np.sin(s)])
    w = angles(k2, t1, QF * FAC)
    tc, ts = (np.repeat(f(w), group, axis=0).astype(np.float32) for f in (np.cos, np.sin))
    as_bf = lambda v: np.asarray(v, np.float32).astype(BF)
    return as_bf(first), as_bf(last), as_bf(square), tc, ts


def params(mib):
    return pltpu.CompilerParams(vmem_limit_bytes=mib * MIB)


VMEM = pl.BlockSpec(memory_space=pltpu.VMEM)
ANY = pl.BlockSpec(memory_space=pl.ANY)
ALONG_Z = (0, 1, -1, 2)


def place(index, move):
    flip, step = move
    return ((index ^ 4) if flip else index) & 4 | ((index + step) & 3)


def dot(a, b):
    return jnp.dot(a, b, preferred_element_type=F32)


def my_core():
    return lax.axis_index("ctx") & 1


def rows_at(i, n):
    return pl.ds(pl.multiple_of(i * n, n), n)


def product_t(order, values):
    return lax.dot_general(order, values, (((1,), (1,)), ((), ())), preferred_element_type=F32)


def copy_all(copies):
    for copy in copies:
        copy.start()
    for copy in copies:
        copy.wait()


def iota(axis, n):
    return lax.broadcasted_iota(jnp.int32, (n, n), axis)


def order_in(ways, width):
    row, group = iota(0, width), width // ways
    r = group // 2
    channel = (row // r % 2) * (width // 2) + (row // group) * r + row % r
    return (channel == iota(1, width)).astype(F32).astype(BF)


def order_z(ways, width):
    row, r = iota(0, width), width // ways // 2
    core = (row // (width // 2)) ^ my_core()
    slot = (row % (width // 2) // r) * 2 * r + core * r + row % r
    return (slot == iota(1, width)).astype(F32).astype(BF)


def dy_kernel(step, w_hbm, d_hbm, *refs):
    outs, (w_ref, d_ref, p_ref, w_sem, d_sem, o_sem) = refs[:4], refs[4:]
    me = lax.axis_index("fsdp")
    n = outs[0].shape[0] // 2
    gather = [
        pltpu.make_async_copy(
            w_hbm.at[rows_at(place(me, (flip, z)), n), :],
            w_ref.at[pl.ds((2 * i + flip) * n, n), :],
            w_sem.at[2 * i + flip],
        )
        for i, z in enumerate(ALONG_Z)
        for flip in range(2)
    ]
    pieces = [pl.ds(i * step, step) for i in range(d_ref.shape[0] // step)]
    loads = [
        pltpu.make_async_copy(d_hbm.at[rows, :], d_ref.at[rows, :], d_sem.at[i]) for i, rows in enumerate(pieces)
    ]
    for copy in (*gather, *loads):
        copy.start()
    for copy in gather:
        copy.wait()
    stores = []
    for i, rows in enumerate(pieces):
        loads[i].wait()
        p_ref[:, rows] = product_t(w_ref[...], d_ref[rows, :]).astype(BF)
        for j, out in enumerate(outs):
            store = pltpu.make_async_copy(
                p_ref.at[pl.ds(2 * n * j, 2 * n), rows], out.at[:, rows], o_sem.at[i * len(outs) + j]
            )
            store.start()
            stores.append(store)
    for store in stores:
        store.wait()


def prep_kernel(k_ref, v_ref, f_ref, send_ref):
    width = k_ref.shape[1]
    ways = send_ref.shape[0] // (2 * 8)
    order = order_in(ways, width)
    mixed = (k_ref[...].astype(F32) * v_ref[...].astype(F32)).astype(BF)
    parts = [product_t(order, x).reshape(ways, 1, -1, ROW) for x in (mixed, f_ref[...])]
    send_ref[...] = jnp.concatenate(parts, axis=1).reshape(send_ref.shape).astype(BF)


def turn_query_kernel(q_ref, qt_ref, mine_ref, away_ref):
    qt_ref[...] = q_ref[...].astype(F32).T.astype(BF)
    core, n = my_core(), mine_ref.shape[0]
    mine_ref[...] = qt_ref[rows_at(core, n), :]
    away_ref[...] = qt_ref[rows_at(1 - core, n), :]


def gate_kernel(ways, z_ref, q_mine_ref, q_theirs_ref, gated_ref, z_mine_ref, z_away_ref):
    z = dot(order_z(ways, z_ref.shape[0]), z_ref[...])
    n = z.shape[0] // 2
    z_mine_ref[...] = z[:n].astype(BF)
    z_away_ref[...] = z[n:].astype(BF)
    gated_ref[pl.ds(0, n), :] = (z[:n] * q_mine_ref[...].astype(F32)).astype(BF)
    gated_ref[pl.ds(n, n), :] = (z[n:] * q_theirs_ref[...].astype(F32)).astype(BF)


def sum_kernel(a_ref, b_ref, c_ref, d_ref, keep_ref, send_ref):
    n = keep_ref.shape[0]
    for out_ref, rows in ((keep_ref, pl.ds(0, n)), (send_ref, pl.ds(n, n))):
        total = a_ref[rows, :].astype(F32) + b_ref[rows, :].astype(F32)
        total += c_ref[rows, :].astype(F32) + d_ref[rows, :].astype(F32)
        out_ref[...] = total.astype(out_ref.dtype)


def dz_kernel(ways, keep_ref, other_ref, qt_ref, send_ref, dy_ref):
    dy = keep_ref[...] + other_ref[...].astype(F32)
    dy_ref[...] = dy
    dz = (dy * qt_ref[...].astype(F32)).astype(BF)
    send_ref[...] = dot(order_in(ways, dz.shape[0]), dz).astype(BF)


def transform(x, first_ref, square_ref, tc_ref, ts_ref):
    x = jnp.concatenate([x[:, u * FAC : (u + 1) * FAC] for u in range(LANE_TILES)], axis=0)
    section = dot(first_ref[...], x)
    n = section.shape[0] // 2
    re, im, tc, ts = section[:n], section[n:], tc_ref[...], ts_ref[...]
    b_re, b_im = re * tc + im * ts, im * tc - re * ts
    left = jnp.concatenate([b_re, b_im], axis=0).astype(BF)
    right = jnp.concatenate([b_im, -b_re], axis=0).astype(BF)
    f = dot(left, square_ref[:FAC]) + dot(right, square_ref[FAC:])
    return f[:n], f[n:]


def signal(p_re, p_im, last_ref, square_ref, tc_ref, ts_ref):
    n, group = p_re.shape[0], p_re.shape[0] // HALF
    left = jnp.concatenate([p_re, p_im], axis=0).astype(BF)
    right = jnp.concatenate([-p_im, p_re], axis=0).astype(BF)
    c = dot(left, square_ref[:FAC]) + dot(right, square_ref[FAC:])
    re, im, tc, ts = c[:n], c[n:], tc_ref[...], ts_ref[...]
    e_re, e_im = re * tc - im * ts, im * tc + re * ts
    e = jnp.concatenate([e_re, e_im[group : n - group]], axis=0).astype(BF)
    x = dot(last_ref[...], e)
    rows = x.shape[0] // LANE_TILES
    return jnp.concatenate([x[u * rows : (u + 1) * rows] for u in range(LANE_TILES)], axis=1)


def conv_kernel(r_ref, first_ref, last_ref, square_ref, tc_ref, ts_ref, z_ref, h_ref):
    rows = z_ref.shape[0]
    group = h_ref.shape[0] // (2 * HALF)
    r = r_ref[...].astype(F32).reshape(-1, 2, group, ROW)
    u, h = (
        transform(r[:, s].reshape(rows, ROW).astype(BF), first_ref, square_ref, tc_ref, ts_ref)
        for s in range(2)
    )
    h_ref[...] = jnp.concatenate(h, axis=0).astype(BF)
    p_re, p_im = u[0] * h[0] - u[1] * h[1], u[0] * h[1] + u[1] * h[0]
    z_ref[...] = signal(p_re, p_im, last_ref, square_ref, tc_ref, ts_ref).astype(BF)


def adjoint_kernel(r_ref, h_ref, first_ref, last_ref, square_ref, tc_ref, ts_ref, keep_ref, away_ref):
    g_re, g_im = transform(r_ref[...], first_ref, square_ref, tc_ref, ts_ref)
    h = h_ref[...].astype(F32)
    n = h.shape[0] // 2
    h_re, h_im = h[:n], h[n:]
    q_re, q_im = h_re * g_re + h_im * g_im, h_re * g_im - h_im * g_re
    du = signal(q_re, q_im, last_ref, square_ref, tc_ref, ts_ref)
    half = du.shape[0] // 2
    low, high, first_core = du[:half], du[half:], my_core() == 0
    keep_ref[...] = jnp.where(first_core, low, high).astype(BF)
    away_ref[...] = jnp.where(first_core, high, low).astype(BF)


def weight_kernel(scale, width, *refs):
    blocks, (d_hbm, d_other_hbm, pack_hbm, mine_hbm, away_hbm) = refs[:8], refs[8:13]
    mine_ref, away_ref, d_ref, d_other_ref, part_ref, sem, d_sem, o_sem = refs[13:]
    me = lax.axis_index("fsdp")
    n = blocks[0].shape[0] // 2
    copies = []
    for i, (block, move) in enumerate(zip(blocks, RING_FROM)):
        rows = rows_at(place(me, move), n)
        for j, to_ref in enumerate((mine_ref, away_ref)):
            copies.append(pltpu.make_async_copy(block.at[pl.ds(j * n, n), :], to_ref.at[rows, :], sem.at[2 * i + j]))
    pieces = [pl.ds(j * width, width) for j in range(d_ref.shape[1] // width)]
    loads = [
        pltpu.make_async_copy(from_ref.at[:, cols], to_ref.at[:, cols], d_sem.at[2 * j + i])
        for j, cols in enumerate(pieces)
        for i, (from_ref, to_ref) in enumerate(((d_hbm, d_ref), (d_other_hbm, d_other_ref)))
    ]
    for copy in (*copies, *loads):
        copy.start()
    for copy in copies:
        copy.wait()
    stores = [
        pltpu.make_async_copy(mine_ref, mine_hbm, o_sem.at[0]),
        pltpu.make_async_copy(away_ref, away_hbm, o_sem.at[1]),
    ]
    for store in stores:
        store.start()
    for j, cols in enumerate(pieces):
        loads[2 * j].wait()
        loads[2 * j + 1].wait()
        p = dot(mine_ref[...], d_ref[:, cols]) + dot(away_ref[...], d_other_ref[:, cols])
        part_ref[:, cols] = (p * scale).astype(BF)
        for g in range(8):
            store = pltpu.make_async_copy(
                part_ref.at[pl.ds(g * n, n), cols], pack_hbm.at[g, pl.ds(0, n), cols], o_sem.at[2 + 8 * j + g]
            )
            store.start()
            stores.append(store)
    for store in stores:
        store.wait()


def pack_kernel(pack_in, keep_ref, got_ref, pack_hbm, both_ref, sem):
    del pack_in
    groups, rows, _ = both_ref.shape
    pieces = [ref[...].astype(F32).reshape(groups, rows // 2, ROW) for ref in (keep_ref, got_ref)]
    both_ref[...] = jnp.concatenate(pieces, axis=1).astype(BF)
    behind = pl.ds(pack_hbm.shape[1] - rows, rows)
    copy_all([pltpu.make_async_copy(both_ref, pack_hbm.at[:, behind, :], sem.at[0])])


def final_kernel(parts_ref, dy_ref, z_mine_ref, z_theirs_ref, k_ref, v_ref, gw_ref, gq_ref, gk_ref, gv_ref, gq_t_ref):
    core, n = my_core(), z_mine_ref.shape[0]
    groups, rows, _ = parts_ref.shape
    total = parts_ref[0, pl.ds(0, n), :].astype(F32)
    for g in range(1, groups):
        total += parts_ref[g, pl.ds(0, n), :].astype(F32)
    gw_ref[...] = total
    for z_ref, half in ((z_mine_ref, core), (z_theirs_ref, 1 - core)):
        own = rows_at(half, n)
        gq_t_ref[own, :] = dy_ref[own, :] * z_ref[...].astype(F32)
    gq_ref[...] = gq_t_ref[...].T.astype(BF)
    c = (rows - n) // 2
    du = parts_ref[:, pl.ds(n, 2 * c), :].astype(F32)
    keep, got = du[:, :c], du[:, c:]
    low, high = jnp.where(core == 0, keep, got), jnp.where(core == 0, got, keep)
    width = 2 * groups * c
    du = jnp.concatenate([low, high], axis=1).reshape(width, -1)
    du = dot(du.T.astype(BF), order_in(2 * groups, width))
    gk_ref[...] = (du * v_ref[...].astype(F32)).astype(BF)
    gv_ref[...] = (du * k_ref[...].astype(F32)).astype(BF)


def staged(kernel, n_in, n_out, n_after, staged_in, staged_out):
    def run(*refs):
        ins, refs = list(refs[:n_in]), refs[n_in + n_after :]
        outs, refs = list(refs[:n_out]), refs[n_out:]
        extra = len(staged_in) + len(staged_out) + 2
        own, extra = refs[: len(refs) - extra], refs[len(refs) - extra :]
        buffers, (in_sem, out_sem) = extra[:-2], extra[-2:]
        loads, stores = [], []
        for j, i in enumerate(staged_in):
            loads.append(pltpu.make_async_copy(ins[i], buffers[j], in_sem.at[j]))
            ins[i] = buffers[j]
        for j, i in enumerate(staged_out):
            buffer = buffers[len(staged_in) + j]
            stores.append(pltpu.make_async_copy(buffer, outs[i], out_sem.at[j]))
            outs[i] = buffer
        copy_all(loads)
        kernel(*ins, *outs, *own)
        copy_all(stores)

    return run


def call(kernel, outs, ins, scratch=(), mib=16, flops=0, specs=None, after=(), staged_in=(), staged_out=(), aliases=None):
    total = sum(math.prod(o.shape) * o.dtype.itemsize for o in (*outs, *ins))
    if after or staged_in or staged_out:
        kernel = staged(kernel, len(ins), len(outs), len(after), staged_in, staged_out)
        buffers = [pltpu.VMEM(ins[i].shape, ins[i].dtype) for i in staged_in]
        buffers += [pltpu.VMEM(outs[i].shape, outs[i].dtype) for i in staged_out]
        sems = [pltpu.SemaphoreType.DMA((max(len(x), 1),)) for x in (staged_in, staged_out)]
        scratch = [*scratch, *buffers, *sems]
    in_specs, out_specs = specs or ([VMEM] * len(ins), [VMEM] * len(outs))
    in_specs = [ANY if i in staged_in else s for i, s in enumerate(in_specs)]
    out_specs = [ANY if i in staged_out else s for i, s in enumerate(out_specs)]
    return pl.pallas_call(
        kernel,
        out_shape=outs,
        in_specs=[*in_specs, *([ANY] * len(after))],
        out_specs=out_specs,
        scratch_shapes=scratch,
        input_output_aliases=aliases or {},
        compiler_params=params(mib),
        cost_estimate=pl.CostEstimate(flops=flops, bytes_accessed=total, transcendentals=0),
    )(*ins, *after)


def shape(*dims, dtype=BF):
    return jax.ShapeDtypeStruct(dims, dtype)


def spread(values):
    return lax.all_to_all(values, "ctx", 0, 0, tiled=True)


def move_over(values, move):
    return lax.ppermute(values, "fsdp", [(i, place(i, move)) for i in range(8)])


RING_FROM = ((0, 0), (1, 0), (0, -1), (0, 1), (1, -1), (1, 1), (0, 2), (1, 2))


def ring(gated):
    up, down = (0, 1), (0, -1)
    other = move_over(gated, (1, 0))
    own_up, own_down = move_over(gated, up), move_over(gated, down)
    other_up, other_down = move_over(other, up), move_over(other, down)
    own_far, other_far = move_over(own_up, up), move_over(other_down, down)
    return gated, other, own_up, own_down, other_up, other_down, own_far, other_far


def dy_product(w_out, d_out, after):
    channels, depth = w_out.shape
    rows = d_out.shape[0]
    step = 512
    pieces = rows // step
    return call(
        functools.partial(dy_kernel, step),
        [shape(channels // 4, rows)] * 4,
        [w_out, d_out],
        [
            pltpu.VMEM((channels, depth), BF),
            pltpu.VMEM((rows, depth), BF),
            pltpu.VMEM((channels, rows), BF),
            pltpu.SemaphoreType.DMA((8,)),
            pltpu.SemaphoreType.DMA((pieces,)),
            pltpu.SemaphoreType.DMA((4 * pieces,)),
        ],
        mib=24,
        flops=2 * channels * depth * rows,
        specs=([ANY] * 2, [ANY] * 4),
        after=after,
    )


def weight_product(blocks, d_out, d_other, scale, pack_rows):
    rows, columns = d_out.shape
    half = blocks[0].shape[0] * 4
    width = 512
    pieces = columns // width
    return call(
        functools.partial(weight_kernel, scale, width),
        [shape(8, pack_rows, columns), shape(half, rows), shape(half, rows)],
        [*blocks, d_out, d_other],
        [
            pltpu.VMEM((half, rows), BF),
            pltpu.VMEM((half, rows), BF),
            pltpu.VMEM((rows, columns), BF),
            pltpu.VMEM((rows, columns), BF),
            pltpu.VMEM((half, columns), BF),
            pltpu.SemaphoreType.DMA((16,)),
            pltpu.SemaphoreType.DMA((2 * pieces,)),
            pltpu.SemaphoreType.DMA((2 + 8 * pieces,)),
        ],
        mib=24,
        flops=4 * half * rows * columns,
        specs=([ANY] * 10, [ANY] * 3),
    )


def on_device(query_in, key_in, value_in, filt, w_out, d_out):
    seq_rows, width = query_in.shape
    channels, columns = w_out.shape
    ways = lax.axis_size("ctx")
    group, half = width // ways, width // 2
    n = HALF * group
    first, last, square, tc, ts = host_tables(ways, group)
    slots = np.arange(ways * group).reshape(ways // 2, 2, 2, group // 2)
    pick = lambda rows: last.reshape(LANE_TILES, ways * group, -1)[:, rows.reshape(-1)].reshape(last.shape)
    last_z = pick(slots.transpose(0, 2, 1, 3))
    last_du = pick(slots.reshape(ways // 2, 2, group).transpose(1, 0, 2))

    swap = lambda v: lax.ppermute(v, "ctx", [(i, i ^ 1) for i in range(ways)])
    rows_like, half_like = shape(width, seq_rows), shape(half, seq_rows)

    (send,) = call(
        prep_kernel,
        [shape(ways * 2 * group, seq_rows)],
        [key_in, value_in, filt],
        staged_in=(0, 1, 2),
        staged_out=(0,),
    )
    arrived = spread(send)
    own_y, *sent_y = dy_product(w_out, d_out, [send])
    came_y = [move_over(v, (0, z)) for v, z in zip(sent_y, ALONG_Z[1:])]

    forward = 2 * 2 * n * (first.shape[1] + 2 * FAC) * FAC
    tables = (square, tc, ts)
    conv, spectrum = call(
        conv_kernel,
        [rows_like, shape(2 * n, FAC)],
        [arrived, first, last_z, *tables],
        mib=32,
        flops=3 * forward,
        staged_out=(0,),
    )
    query_t, q_mine, q_away = call(
        turn_query_kernel,
        [rows_like, half_like, half_like],
        [query_in],
        after=[conv],
        staged_in=(0,),
        staged_out=(0, 1, 2),
    )
    conv, d_late = lax.optimization_barrier((conv, d_out))
    q_theirs, d_other = swap(q_away), swap(d_late)
    gated, z_mine, z_away = call(
        functools.partial(gate_kernel, ways),
        [rows_like, half_like, half_like],
        [spread(conv), q_mine, q_theirs],
        after=[d_other],
        staged_in=(0, 1, 2),
        staged_out=(0, 1, 2),
    )
    z_theirs = swap(z_away)
    blocks = ring(gated)

    keep_y, away_y = call(
        sum_kernel,
        [shape(width, seq_rows, dtype=F32), rows_like],
        [own_y, *came_y],
        after=[gated],
        staged_in=(0, 1, 2, 3),
        staged_out=(0, 1),
    )
    send_z, grad_y = call(
        functools.partial(dz_kernel, ways),
        [rows_like, shape(width, seq_rows, dtype=F32)],
        [keep_y, move_over(away_y, (1, 0)), query_t],
        staged_in=(0, 1, 2),
        staged_out=(0, 1),
    )
    du_keep, du_away = call(
        adjoint_kernel,
        [half_like, half_like],
        [spread(send_z), spectrum, first, last_du, *tables],
        mib=32,
        flops=2 * forward,
        staged_out=(1,),
    )
    du_got = swap(du_away)

    scale = 1.0 / math.sqrt(seq_rows * ways)
    pack, mine, away = weight_product(blocks, d_out, d_other, scale, half + 2 * group)
    (pack,) = call(
        pack_kernel,
        [shape(*pack.shape)],
        [pack, du_keep, du_got],
        [pltpu.VMEM((ways // 2, 2 * group, columns), BF), pltpu.SemaphoreType.DMA((1,))],
        specs=([ANY, VMEM, VMEM], [ANY]),
        aliases={0: 0},
    )
    groups = [list(range(c, ways, 2)) for c in range(2)]
    parts = lax.all_to_all(pack, "ctx", 0, 0, tiled=True, axis_index_groups=groups)

    theirs = swap(away)
    core = my_core()
    split = lambda v: v.reshape(-1, 1, half, seq_rows)
    low, high = jnp.where(core == 0, mine, theirs), jnp.where(core == 0, theirs, mine)
    gated_all = jnp.concatenate([split(low), split(high)], axis=1).reshape(channels, seq_rows)
    layer_out = lax.dot_general(
        gated_all, w_out, (((0,), (0,)), ((), ())), preferred_element_type=F32
    ).astype(BF)

    like = shape(seq_rows, width)
    grad_weight, grad_query, grad_key, grad_value = call(
        final_kernel,
        [shape(channels // ways, columns, dtype=F32), like, like, like],
        [parts, grad_y, z_mine, z_theirs, key_in, value_in],
        [pltpu.VMEM((width, seq_rows), F32)],
        after=[layer_out],
    )
    return (layer_out, grad_query, grad_key, grad_value, grad_weight)


def solution(mesh):
    both = P("ctx", "fsdp")
    return jax.shard_map(
        on_device,
        mesh=mesh,
        in_specs=(both, both, both, both, P(None, "fsdp"), both),
        out_specs=(both, both, both, both, both),
        check_vma=False,
    )
```

time: 155 us -> 153 us (0.987)
  blocking collectives: 0 us -> 32.9 us
  starting transfers between devices: 50.8 us -> 24.5 us
  local copies, waits for them, and re-layouts: 26.9 us -> 14.2 us
  waiting for transfers between devices: 44.9 us -> 51 us
  other arithmetic: 3.68 us -> 1.56 us
    all_to_all x0 -> x2, blocking collectives: none -> 32.9 us  [spread(): return lax.all_to_all(values, 'ctx', 0, 0, tiled=True)]
    all_to_all x4 -> x1, starting transfers between devices: 21.3 us -> 3.53 us  [spread(): return lax.all_to_all(values, 'ctx', 0, 0, tiled=True)]
    unnamed x84 -> x54, local copies, waits for them, and re-layouts: 26.9 us -> 14.2 us
    ppermute x14 -> x11, waiting for transfers between devices: 17.2 us -> 27.6 us  [move_over(): return lax.ppermute(values, 'fsdp', [(i, place(i, move)) for i in range(8)])]
    ppermute x14 -> x11, starting transfers between devices: 21.5 us -> 16.4 us  [move_over(): return lax.ppermute(values, 'fsdp', [(i, place(i, move)) for i in range(8)])]
    all_to_all x4 -> x1, waiting for transfers between devices: 11.9 us -> 6.87 us  [spread(): return lax.all_to_all(values, 'ctx', 0, 0, tiled=True)]
    all_to_all x1, starting transfers between devices: 6.98 us -> 3.58 us  [on_device(): lax.all_to_all(pack, 'ctx', 0, 0, tiled=True, axis_index_groups=groups)]
    reduce_sum x1 -> x0, other arithmetic: 2.12 us -> none  [on_device(): jnp.sum(parts.reshape(ways // 2, channels // ways, columns).astype(F32),...]
  transfers between devices with their start and end apart: 23 -> 18, of which waited for: 9 -> 9; matrix products, arithmetic and copies ran while one was open for 1% -> 3% of each run, Pallas kernels for 15% -> 11%
where the time goes in v4:
time: 153 us; the launch traced here: 152 us
  waiting for transfers between devices  51 us (33%)
  blocking collectives  32.9 us (22%)
  starting transfers between devices  24.5 us (16%)
  Pallas kernels  24.1 us (16%)
  local copies, waits for them, and re-layouts  14.2 us (9%)
  matrix products  2.43 us (2%)
  other arithmetic  1.56 us (1%)
    all_to_all x2, blocking collectives, spread(): return lax.all_to_all(values, 'ctx', 0, 0, tiled=True)  32.9 us
    ppermute x11, waiting for transfers between devices, move_over(): return lax.ppermute(values, 'fsdp', [(i, place(i, move)) for i in range(8)])  27.6 us
    pallas_call x11, Pallas kernels, call(): pl.pallas_call(kernel, out_shape=outs, in_specs=[*in_specs, *[ANY] * len(...  24.1 us
    ppermute x11, starting transfers between devices, move_over(): return lax.ppermute(values, 'fsdp', [(i, place(i, move)) for i in range(8)])  16.4 us
    unnamed x54, local copies, waits for them, and re-layouts  14.2 us
    all_to_all x1, waiting for transfers between devices, on_device(): lax.all_to_all(pack, 'ctx', 0, 0, tiled=True, axis_index_groups=groups)  14.2 us
    all_to_all x1, waiting for transfers between devices, spread(): return lax.all_to_all(values, 'ctx', 0, 0, tiled=True)  6.87 us
    all_to_all x1, starting transfers between devices, on_device(): lax.all_to_all(pack, 'ctx', 0, 0, tiled=True, axis_index_groups=groups)  3.58 us
  transfers between devices with their start and end apart: 18, of which 9 were waited for; matrix products, arithmetic and copies ran while one was open for 3% of the time, Pallas kernels for 11%

profile of v4, /device:TPU:0, one launch (start us, length us, event | category | flops | bytes accessed | tf_op | source)
XLA Modules:
  0.0 151.8 jit_solution(18002692186667711673)
XLA Ops:
  0.6 0.0 copy-start.1
  0.7 1.0 copy-done.3
  1.7 0.9 copy-done.5
  2.6 0.9 copy-done.16
  3.6 0.5 shard_map.155.refs_2_
  4.1 19.3 %all_to_all.38 = bf16[16,16,1024]{2,1,0:T(8,128)(2,1)S(1)} all-to-all(bf16[16,16,1024]{2,1,0:T(8,128)(2,1)S(1)} %bitcast.15), channel_id=1, replica_groups=mesh['fsdp'=8,'ctx'=16] {'ctx'}, dimensions={0} | all-to-all | bytes 1048576 | tf_op jit(solution)/shard_map/all_to_all | solution.py:349
  23.3 0.0 copy-start.17
  23.4 0.9 copy-done.17
  24.3 1.2 copy-done.26
  25.5 3.8 %shard_map.156 = (bf16[128,1024]{1,0:T(8,128)(2,1)}, bf16[1040,256]{1,0:T(8,128)(2,1)S(1)}) custom-call(bf16[256,1024]{1,0:T(8,128)(2,1)S(1)} %bitcast.18, bf16[1040,512]{1,0:T(8,128)(2,1)S(1)} %copy-done.1, bf16[512,1024]{1,0:T(8,128)(2,1)S(1)} %copy-done.26, bf16[512,256]{1,0:T(8,128)(2,1)S(1)} %copy-done.17, f32[520,256]{1,0:T(8,128)S(1)} %copy-done.10, ...), custom_call_target="tpu_custom_call" | custom-call | flops 1635778560 | bytes 4759552 | tf_op jit(solution)/shard_map/pallas_call | solution.py:332
  29.4 0.8 copy-done.12
  30.1 3.5 %all-to-all-start.1 = ((bf16[16,8,1024]{2,1,0:T(8,128)(2,1)}), bf16[16,8,1024]{2,1,0:T(8,128)(2,1)S(1)}, u32[]{:S(2)}, u32[]{:S(2)}) async-start(bf16[16,8,1024]{2,1,0:T(8,128)(2,1)} %bitcast.2), calls=%async_computation.1 | async-start | bytes 524288 | tf_op jit(solution)/shard_map/all_to_all | solution.py:349
  33.7 0.6 shard_map.157
  34.3 0.6 copy-done.22
  34.9 0.4 collective-permute-start
  35.4 1.0 collective-permute-done.refs_2_
  36.3 6.9 %all-to-all-done.1 = bf16[16,8,1024]{2,1,0:T(8,128)(2,1)S(1)} async-done(((bf16[16,8,1024]{2,1,0:T(8,128)(2,1)}), bf16[16,8,1024]{2,1,0:T(8,128)(2,1)S(1)}, u32[]{:S(2)}, u32[]{:S(2)}) %all-to-all-start.1) | async-done | bytes 262176 | tf_op jit(solution)/shard_map/all_to_all | solution.py:349
  43.2 0.9 copy-done.23
  44.1 1.5 shard_map.158
  45.6 0.7 collective-permute-start.2
  46.3 1.9 %collective-permute-start.3 = (bf16[128,1024]{1,0:T(8,128)(2,1)S(1)}, bf16[128,1024]{1,0:T(8,128)(2,1)S(1)}, u32[]{:S(2)}, u32[]{:S(2)}) collective-permute-start(bf16[128,1024]{1,0:T(8,128)(2,1)S(1)} %get-tuple-element.37.refs_0_.refs_4_), channel_id=1, source_target_pairs={{0,16},{16,32},{32,48},{48,0},{64,80},{80,96},{96,112},{112,64},{1... | collective-permute-start | bytes 786440 | tf_op jit(solution)/shard_map/ppermute | solution.py:353
  48.2 5.2 %collective-permute-done.2.refs_1_ = bf16[128,1024]{1,0:T(8,128)(2,1)S(1)} collective-permute-done((bf16[128,1024]{1,0:T(8,128)(2,1)S(1)}, bf16[128,1024]{1,0:T(8,128)(2,1)S(1)}, u32[]{:S(2)}, u32[]{:S(2)}) %collective-permute-start.2) | collective-permute-done | bytes 262176 | tf_op jit(solution)/shard_map/ppermute | solution.py:353
  53.4 4.0 %collective-permute-start.6 = (bf16[128,1024]{1,0:T(8,128)(2,1)S(1)}, bf16[128,1024]{1,0:T(8,128)(2,1)S(1)}, u32[]{:S(2)}, u32[]{:S(2)}) collective-permute-start(bf16[128,1024]{1,0:T(8,128)(2,1)S(1)} %collective-permute-done.2.refs_1_), channel_id=1, source_target_pairs={{0,48},{16,0},{32,16},{48,32},{64,112},{80,64},{96,80},{112,96},{1... | collective-permute-start | bytes 786440 | tf_op jit(solution)/shard_map/ppermute | solution.py:353
  57.4 0.4 collective-permute-start.4
  57.8 1.6 %collective-permute-start.7 = (bf16[128,1024]{1,0:T(8,128)(2,1)S(1)}, bf16[128,1024]{1,0:T(8,128)(2,1)S(1)}, u32[]{:S(2)}, u32[]{:S(2)}) collective-permute-start(bf16[128,1024]{1,0:T(8,128)(2,1)S(1)} %collective-permute-done.3.refs_2_), channel_id=1, source_target_pairs={{0,16},{16,32},{32,48},{48,0},{64,80},{80,96},{96,112},{112,64},{1... | collective-permute-start | bytes 786440 | tf_op jit(solution)/shard_map/ppermute | solution.py:353
  59.4 0.0 collective-permute-start.5
  59.5 4.7 %collective-permute-done.6.refs_5_ = bf16[128,1024]{1,0:T(8,128)(2,1)S(1)} collective-permute-done((bf16[128,1024]{1,0:T(8,128)(2,1)S(1)}, bf16[128,1024]{1,0:T(8,128)(2,1)S(1)}, u32[]{:S(2)}, u32[]{:S(2)}) %collective-permute-start.6) | collective-permute-done | bytes 262176 | tf_op jit(solution)/shard_map/ppermute | solution.py:353
  64.2 3.7 %collective-permute-start.8 = (bf16[128,1024]{1,0:T(8,128)(2,1)S(1)}, bf16[128,1024]{1,0:T(8,128)(2,1)S(1)}, u32[]{:S(2)}, u32[]{:S(2)}) collective-permute-start(bf16[128,1024]{1,0:T(8,128)(2,1)S(1)} %collective-permute-done.6.refs_5_), channel_id=1, source_target_pairs={{0,48},{16,0},{32,16},{48,32},{64,112},{80,64},{96,80},{112,96},{1... | collective-permute-start | bytes 786440 | tf_op jit(solution)/shard_map/ppermute | solution.py:353
  67.9 4.3 %shard_map.160 = (bf16[256,1024]{1,0:T(8,128)(2,1)S(1)}, bf16[256,1024]{1,0:T(8,128)(2,1)S(1)}, bf16[256,1024]{1,0:T(8,128)(2,1)S(1)}, bf16[256,1024]{1,0:T(8,128)(2,1)S(1)}) custom-call(bf16[1024,1024]{1,0:T(8,128)(2,1)S(1)} %copy-done.24, bf16[1024,1024]{1,0:T(8,128)(2,1)} %refs_1_.4, bf16[256,1024]{1,0:T(8,128)(2,1)S(1)} %shard_map.155.refs_2_), custom_call_target="tpu_custom_call" | custom-call | flops 2147483648 | bytes 6291456 | tf_op jit(solution)/shard_map/pallas_call | solution.py:332
  72.2 0.1 collective-permute-start.10
  72.3 3.2 %collective-permute-start.11 = (bf16[256,1024]{1,0:T(8,128)(2,1)S(1)}, bf16[256,1024]{1,0:T(8,128)(2,1)S(1)}, u32[]{:S(2)}, u32[]{:S(2)}) collective-permute-start(bf16[256,1024]{1,0:T(8,128)(2,1)S(1)} %get-tuple-element.43), channel_id=1, source_target_pairs={{0,48},{16,0},{32,16},{48,32},{64,112},{80,64},{96,80},{112,96},{1... | collective-permute-start | bytes 1572872 | tf_op jit(solution)/shard_map/ppermute | solution.py:353
  75.5 0.0 copy-start.18
  75.5 7.7 %shard_map.159 = (bf16[8,80,1024]{2,1,0:T(8,128)(2,1)}, bf16[512,1024]{1,0:T(8,128)(2,1)S(1)}, bf16[512,1024]{1,0:T(8,128)(2,1)}) custom-call(bf16[128,1024]{1,0:T(8,128)(2,1)S(1)} %get-tuple-element.37.refs_0_.refs_4_, bf16[128,1024]{1,0:T(8,128)(2,1)S(1)} %collective-permute-done.2.refs_1_, bf16[128,1024]{1,0:T(8,128)(2,1)S(1)} %collective-permute-done.3.refs_2_, ...), custom_call_target="tpu_custom_call" | custom-call | flops 2147483648 | bytes 9699328 | tf_op jit(solution)/shard_map/pallas_call | solution.py:332
  83.2 0.0 copy-start.2
  83.2 0.0 copy-start.7
  83.2 0.0 copy-start.9
  83.2 0.0 copy-start.11
  83.3 0.3 collective-permute-start.9
  83.5 9.9 %collective-permute-done.10.refs_1_ = bf16[256,1024]{1,0:T(8,128)(2,1)S(1)} collective-permute-done((bf16[256,1024]{1,0:T(8,128)(2,1)S(1)}, bf16[256,1024]{1,0:T(8,128)(2,1)S(1)}, u32[]{:S(2)}, u32[]{:S(2)}) %collective-permute-start.10) | collective-permute-done | bytes 524320 | tf_op jit(solution)/shard_map/ppermute | solution.py:353
  93.5 2.0 %collective-permute-done.11.refs_2_ = bf16[256,1024]{1,0:T(8,128)(2,1)S(1)} collective-permute-done((bf16[256,1024]{1,0:T(8,128)(2,1)S(1)}, bf16[256,1024]{1,0:T(8,128)(2,1)S(1)}, u32[]{:S(2)}, u32[]{:S(2)}) %collective-permute-start.11) | collective-permute-done | bytes 524320 | tf_op jit(solution)/shard_map/ppermute | solution.py:353
  95.4 0.5 shard_map.161
  96.0 0.7 collective-permute-start.13
  96.6 5.8 %collective-permute-done.13.refs_1_ = bf16[128,1024]{1,0:T(8,128)(2,1)S(1)} collective-permute-done((bf16[128,1024]{1,0:T(8,128)(2,1)S(1)}, bf16[128,1024]{1,0:T(8,128)(2,1)S(1)}, u32[]{:S(2)}, u32[]{:S(2)}) %collective-permute-start.13) | collective-permute-done | bytes 262176 | tf_op jit(solution)/shard_map/ppermute | solution.py:353
  102.4 0.4 shard_map.162
  102.9 0.8 copy-done.14
  103.7 13.6 %all_to_all.39 = bf16[16,8,1024]{2,1,0:T(8,128)(2,1)S(1)} all-to-all(bf16[16,8,1024]{2,1,0:T(8,128)(2,1)S(1)} %bitcast.19), channel_id=1, replica_groups=mesh['fsdp'=8,'ctx'=16] {'ctx'}, dimensions={0} | all-to-all | bytes 524288 | tf_op jit(solution)/shard_map/all_to_all | solution.py:349
  117.3 2.7 %shard_map.163 = (bf16[64,1024]{1,0:T(8,128)(2,1)S(1)}, bf16[64,1024]{1,0:T(8,128)(2,1)S(1)}) custom-call(bf16[128,1024]{1,0:T(8,128)(2,1)S(1)} %bitcast.17, bf16[1040,256]{1,0:T(8,128)(2,1)S(1)} %copy-done.13, bf16[1040,512]{1,0:T(8,128)(2,1)S(1)} %copy-done.2, bf16[512,1024]{1,0:T(8,128)(2,1)S(1)} %copy-done.7, bf16[512,256]{1,0:T(8,128)(2,1)S(1)} %copy-done.18, ...), custom_call_target="tpu_custom_call" | custom-call | flops 1090519040 | bytes 4497408 | tf_op jit(solution)/shard_map/pallas_call | solution.py:332
  120.0 0.1 collective-permute-start.14
  120.1 1.3 collective-permute-done.14.got_ref
  121.5 0.8 shard_map.164
  122.2 3.6 %all-to-all-start.3 = ((bf16[8,80,1024]{2,1,0:T(8,128)(2,1)}), bf16[8,80,1024]{2,1,0:T(8,128)(2,1)S(1)}, u32[]{:S(2)}, u32[]{:S(2)}) async-start(bf16[8,80,1024]{2,1,0:T(8,128)(2,1)} %shard_map.164), calls=%async_computation.3 | async-start | bytes 2621440 | tf_op jit(solution)/shard_map/all_to_all | solution.py:510
  125.8 0.2 collective-permute-start.15
  126.1 1.4 broadcast_select_fusion.1
  127.4 0.2 pad_maximum_fusion
  127.6 1.4 copy-done.25
  129.0 2.4 %convolution_convert_fusion.refs_6_ = bf16[1024,1024]{1,0:T(8,128)(2,1)S(1)} fusion(bf16[1024,1024]{1,0:T(8,128)(2,1)S(1)} %bitcast.22, bf16[1024,1024]{1,0:T(8,128)(2,1)S(1)} %copy-done.25), kind=kOutput, calls=%fused_computation.1 | convolution fusion | flops 2148532224 | bytes 6291456 | tf_op jit(solution)/shard_map/dot_general | solution.py:517
  131.5 0.0 copy-start
  131.5 0.7 copy-done.20
  132.2 14.2 %all-to-all-done.3.refs_0_ = bf16[8,80,1024]{2,1,0:T(8,128)(2,1)S(1)} async-done(((bf16[8,80,1024]{2,1,0:T(8,128)(2,1)}), bf16[8,80,1024]{2,1,0:T(8,128)(2,1)S(1)}, u32[]{:S(2)}, u32[]{:S(2)}) %all-to-all-start.3) | async-done | bytes 1310752 | tf_op jit(solution)/shard_map/all_to_all | solution.py:510
  146.4 0.9 copy-done.4
  147.4 0.9 copy-done.6
  148.3 1.0 copy-done.15
  149.4 0.9 copy-done.21
  150.3 1.4 shard_map.165
  (42 shorter events, 0.1 us)
Async XLA Ops:
  0.6 22.7 %copy-start.1 = (bf16[1040,512]{1,0:T(8,128)(2,1)S(1)}, bf16[1040,512]{1,0:T(8,128)(2,1)}, u32[]{:S(2)}) copy-start(bf16[1040,512]{1,0:T(8,128)(2,1)} %constant.20.clone.refs_1_.refs_2_) | copy-start | bytes 3194884
  0.6 1.0 copy-start.3
  1.7 0.9 copy-start.5
  2.6 0.9 copy-start.16
  3.6 19.8 %copy-start.8 = (f32[520,256]{1,0:T(8,128)S(1)}, f32[520,256]{1,0:T(8,128)}, u32[]{:S(2)}) copy-start(f32[520,256]{1,0:T(8,128)} %constant.24.clone.refs_5_.refs_6_) | copy-start | bytes 1597444
  3.6 19.8 %copy-start.10 = (f32[520,256]{1,0:T(8,128)S(1)}, f32[520,256]{1,0:T(8,128)}, u32[]{:S(2)}) copy-start(f32[520,256]{1,0:T(8,128)} %constant.23.clone.refs_4_.refs_5_) | copy-start | bytes 1597444
  23.3 1.0 copy-start.17
  24.3 1.2 copy-start.26
  25.5 8.2 %copy-start.19 = (bf16[1024,128]{1,0:T(8,128)(2,1)S(1)}, bf16[1024,128]{1,0:T(8,128)(2,1)}, u32[]{:S(2)}) copy-start(bf16[1024,128]{1,0:T(8,128)(2,1)} %refs_0_.4) | copy-start | bytes 786436
  29.3 0.8 copy-start.12
  30.1 13.1 %collective-permute-start.1 = (bf16[1024,1024]{1,0:T(8,128)(2,1)}, bf16[1024,1024]{1,0:T(8,128)(2,1)S(1)}, u32[]{:S(2)}, u32[]{:S(2)}) collective-permute-start(bf16[1024,1024]{1,0:T(8,128)(2,1)} %refs_1_.4), channel_id=1, source_target_pairs={{0,1},{1,0},{2,3},{3,2},{4,5},{5,4},{6,7},{7,6},{8,9},{9,8},{10,11... | collective-permute-start | bytes 6291464 | tf_op jit(solution)/shard_map/ppermute | solution.py:429
  30.1 13.1 %all-to-all-start.1 = ((bf16[16,8,1024]{2,1,0:T(8,128)(2,1)}), bf16[16,8,1024]{2,1,0:T(8,128)(2,1)S(1)}, u32[]{:S(2)}, u32[]{:S(2)}) async-start(bf16[16,8,1024]{2,1,0:T(8,128)(2,1)} %bitcast.2), calls=%async_computation.1 | async-start | bytes 524288 | tf_op jit(solution)/shard_map/all_to_all | solution.py:349
  34.3 0.7 copy-start.22
  34.9 1.4 collective-permute-start
  43.2 0.9 copy-start.23
  44.1 23.8 %copy-start.24 = (bf16[1024,1024]{1,0:T(8,128)(2,1)S(1)}, bf16[1024,1024]{1,0:T(8,128)(2,1)}, u32[]{:S(2)}) copy-start(bf16[1024,1024]{1,0:T(8,128)(2,1)} %refs_0_.5) | copy-start | bytes 6291460
  45.6 7.8 %collective-permute-start.2 = (bf16[128,1024]{1,0:T(8,128)(2,1)S(1)}, bf16[128,1024]{1,0:T(8,128)(2,1)S(1)}, u32[]{:S(2)}, u32[]{:S(2)}) collective-permute-start(bf16[128,1024]{1,0:T(8,128)(2,1)S(1)} %get-tuple-element.37.refs_0_.refs_4_), channel_id=1, source_target_pairs={{0,64},{16,80},{32,96},{48,112},{64,0},{80,16},{96,32},{112,48},{1... | collective-permute-start | bytes 786440 | tf_op jit(solution)/shard_map/ppermute | solution.py:353
  46.3 11.6 %collective-permute-start.3 = (bf16[128,1024]{1,0:T(8,128)(2,1)S(1)}, bf16[128,1024]{1,0:T(8,128)(2,1)S(1)}, u32[]{:S(2)}, u32[]{:S(2)}) collective-permute-start(bf16[128,1024]{1,0:T(8,128)(2,1)S(1)} %get-tuple-element.37.refs_0_.refs_4_), channel_id=1, source_target_pairs={{0,16},{16,32},{32,48},{48,0},{64,80},{80,96},{96,112},{112,64},{1... | collective-permute-start | bytes 786440 | tf_op jit(solution)/shard_map/ppermute | solution.py:353
  53.4 10.8 %collective-permute-start.6 = (bf16[128,1024]{1,0:T(8,128)(2,1)S(1)}, bf16[128,1024]{1,0:T(8,128)(2,1)S(1)}, u32[]{:S(2)}, u32[]{:S(2)}) collective-permute-start(bf16[128,1024]{1,0:T(8,128)(2,1)S(1)} %collective-permute-done.2.refs_1_), channel_id=1, source_target_pairs={{0,48},{16,0},{32,16},{48,32},{64,112},{80,64},{96,80},{112,96},{1... | collective-permute-start | bytes 786440 | tf_op jit(solution)/shard_map/ppermute | solution.py:353
  57.4 14.8 %collective-permute-start.4 = (bf16[128,1024]{1,0:T(8,128)(2,1)S(1)}, bf16[128,1024]{1,0:T(8,128)(2,1)S(1)}, u32[]{:S(2)}, u32[]{:S(2)}) collective-permute-start(bf16[128,1024]{1,0:T(8,128)(2,1)S(1)} %get-tuple-element.37.refs_0_.refs_4_), channel_id=1, source_target_pairs={{0,48},{16,0},{32,16},{48,32},{64,112},{80,64},{96,80},{112,96},{1... | collective-permute-start | bytes 786440 | tf_op jit(solution)/shard_map/ppermute | solution.py:353
  57.8 17.6 %collective-permute-start.7 = (bf16[128,1024]{1,0:T(8,128)(2,1)S(1)}, bf16[128,1024]{1,0:T(8,128)(2,1)S(1)}, u32[]{:S(2)}, u32[]{:S(2)}) collective-permute-start(bf16[128,1024]{1,0:T(8,128)(2,1)S(1)} %collective-permute-done.3.refs_2_), channel_id=1, source_target_pairs={{0,16},{16,32},{32,48},{48,0},{64,80},{80,96},{96,112},{112,64},{1... | collective-permute-start | bytes 786440 | tf_op jit(solution)/shard_map/ppermute | solution.py:353
  59.4 16.0 %collective-permute-start.5 = (bf16[128,1024]{1,0:T(8,128)(2,1)S(1)}, bf16[128,1024]{1,0:T(8,128)(2,1)S(1)}, u32[]{:S(2)}, u32[]{:S(2)}) collective-permute-start(bf16[128,1024]{1,0:T(8,128)(2,1)S(1)} %collective-permute-done.2.refs_1_), channel_id=1, source_target_pairs={{0,16},{16,32},{32,48},{48,0},{64,80},{80,96},{96,112},{112,64},{1... | collective-permute-start | bytes 786440 | tf_op jit(solution)/shard_map/ppermute | solution.py:353
  64.2 11.3 %collective-permute-start.8 = (bf16[128,1024]{1,0:T(8,128)(2,1)S(1)}, bf16[128,1024]{1,0:T(8,128)(2,1)S(1)}, u32[]{:S(2)}, u32[]{:S(2)}) collective-permute-start(bf16[128,1024]{1,0:T(8,128)(2,1)S(1)} %collective-permute-done.6.refs_5_), channel_id=1, source_target_pairs={{0,48},{16,0},{32,16},{48,32},{64,112},{80,64},{96,80},{112,96},{1... | collective-permute-start | bytes 786440 | tf_op jit(solution)/shard_map/ppermute | solution.py:353
  72.2 21.3 %collective-permute-start.10 = (bf16[256,1024]{1,0:T(8,128)(2,1)S(1)}, bf16[256,1024]{1,0:T(8,128)(2,1)S(1)}, u32[]{:S(2)}, u32[]{:S(2)}) collective-permute-start(bf16[256,1024]{1,0:T(8,128)(2,1)S(1)} %get-tuple-element.42), channel_id=1, source_target_pairs={{0,16},{16,32},{32,48},{48,0},{64,80},{80,96},{96,112},{112,64},{1... | collective-permute-start | bytes 1572872 | tf_op jit(solution)/shard_map/ppermute | solution.py:353
  72.3 23.2 %collective-permute-start.11 = (bf16[256,1024]{1,0:T(8,128)(2,1)S(1)}, bf16[256,1024]{1,0:T(8,128)(2,1)S(1)}, u32[]{:S(2)}, u32[]{:S(2)}) collective-permute-start(bf16[256,1024]{1,0:T(8,128)(2,1)S(1)} %get-tuple-element.43), channel_id=1, source_target_pairs={{0,48},{16,0},{32,16},{48,32},{64,112},{80,64},{96,80},{112,96},{1... | collective-permute-start | bytes 1572872 | tf_op jit(solution)/shard_map/ppermute | solution.py:353
  75.5 20.0 %collective-permute-start.12 = (bf16[256,1024]{1,0:T(8,128)(2,1)S(1)}, bf16[256,1024]{1,0:T(8,128)(2,1)S(1)}, u32[]{:S(2)}, u32[]{:S(2)}) collective-permute-start(bf16[256,1024]{1,0:T(8,128)(2,1)S(1)} %get-tuple-element.44), channel_id=1, source_target_pairs={{0,32},{16,48},{32,0},{48,16},{64,96},{80,112},{96,64},{112,80},{1... | collective-permute-start | bytes 1572872 | tf_op jit(solution)/shard_map/ppermute | solution.py:353
  75.5 41.8 %copy-start.18 = (bf16[512,256]{1,0:T(8,128)(2,1)S(1)}, bf16[512,256]{1,0:T(8,128)(2,1)}, u32[]{:S(2)}) copy-start(bf16[512,256]{1,0:T(8,128)(2,1)} %constant.22.clone.refs_3_.refs_4_) | copy-start | bytes 786436
  83.2 34.1 %copy-start.2 = (bf16[1040,512]{1,0:T(8,128)(2,1)S(1)}, bf16[1040,512]{1,0:T(8,128)(2,1)}, u32[]{:S(2)}) copy-start(bf16[1040,512]{1,0:T(8,128)(2,1)} %constant.20.clone.refs_1_.refs_2_) | copy-start | bytes 3194884
  83.2 34.1 %copy-start.7 = (bf16[512,1024]{1,0:T(8,128)(2,1)S(1)}, bf16[512,1024]{1,0:T(8,128)(2,1)}, u32[]{:S(2)}) copy-start(bf16[512,1024]{1,0:T(8,128)(2,1)} %constant.25.clone.refs_3_) | copy-start | bytes 3145732
  83.2 34.0 %copy-start.9 = (f32[520,256]{1,0:T(8,128)S(1)}, f32[520,256]{1,0:T(8,128)}, u32[]{:S(2)}) copy-start(f32[520,256]{1,0:T(8,128)} %constant.24.clone.refs_5_.refs_6_) | copy-start | bytes 1597444
  83.2 34.0 %copy-start.11 = (f32[520,256]{1,0:T(8,128)S(1)}, f32[520,256]{1,0:T(8,128)}, u32[]{:S(2)}) copy-start(f32[520,256]{1,0:T(8,128)} %constant.23.clone.refs_4_.refs_5_) | copy-start | bytes 1597444
  83.3 34.0 %copy-start.13 = (bf16[1040,256]{1,0:T(8,128)(2,1)S(1)}, bf16[1040,256]{1,0:T(8,128)(2,1)}, u32[]{:S(2)}) copy-start(bf16[1040,256]{1,0:T(8,128)(2,1)} %copy-done.12) | copy-start | bytes 1597444
  83.3 42.8 %collective-permute-start.9 = (bf16[512,1024]{1,0:T(8,128)(2,1)}, bf16[512,1024]{1,0:T(8,128)(2,1)}, u32[]{:S(2)}, u32[]{:S(2)}) collective-permute-start(bf16[512,1024]{1,0:T(8,128)(2,1)} %get-tuple-element.39), channel_id=1, source_target_pairs={{0,1},{1,0},{2,3},{3,2},{4,5},{5,4},{6,7},{7,6},{8,9},{9,8},{10,11... | collective-permute-start | bytes 3145736 | tf_op jit(solution)/shard_map/ppermute | solution.py:429
  96.0 6.5 %collective-permute-start.13 = (bf16[128,1024]{1,0:T(8,128)(2,1)S(1)}, bf16[128,1024]{1,0:T(8,128)(2,1)S(1)}, u32[]{:S(2)}, u32[]{:S(2)}) collective-permute-start(bf16[128,1024]{1,0:T(8,128)(2,1)S(1)} %get-tuple-element.46), channel_id=1, source_target_pairs={{0,64},{16,80},{32,96},{48,112},{64,0},{80,16},{96,32},{112,48},{1... | collective-permute-start | bytes 786440 | tf_op jit(solution)/shard_map/ppermute | solution.py:353
  102.9 0.8 copy-start.14
  120.0 1.4 collective-permute-start.14
  122.2 24.2 %all-to-all-start.3 = ((bf16[8,80,1024]{2,1,0:T(8,128)(2,1)}), bf16[8,80,1024]{2,1,0:T(8,128)(2,1)S(1)}, u32[]{:S(2)}, u32[]{:S(2)}) async-start(bf16[8,80,1024]{2,1,0:T(8,128)(2,1)} %shard_map.164), calls=%async_computation.3 | async-start | bytes 2621440 | tf_op jit(solution)/shard_map/all_to_all | solution.py:510
  125.8 5.6 %collective-permute-start.15 = (bf16[64,1024]{1,0:T(8,128)(2,1)}, bf16[64,1024]{1,0:T(8,128)(2,1)S(1)}, u32[]{:S(2)}, u32[]{:S(2)}) collective-permute-start(bf16[64,1024]{1,0:T(8,128)(2,1)} %get-tuple-element.54), channel_id=1, source_target_pairs={{0,1},{1,0},{2,3},{3,2},{4,5},{5,4},{6,7},{7,6},{8,9},{9,8},{10,11... | collective-permute-start | bytes 393224 | tf_op jit(solution)/shard_map/ppermute | solution.py:429
  127.4 1.6 %copy-start.25 = (bf16[1024,1024]{1,0:T(8,128)(2,1)S(1)}, bf16[1024,1024]{1,0:T(8,128)(2,1)}, u32[]{:S(2)}) copy-start(bf16[1024,1024]{1,0:T(8,128)(2,1)} %refs_0_.5) | copy-start | bytes 6291460
  131.5 20.2 %copy-start = (bf16[1024,1024]{1,0:T(8,128)(2,1)}, bf16[1024,1024]{1,0:T(8,128)(2,1)S(1)}, u32[]{:S(2)}) copy-start(bf16[1024,1024]{1,0:T(8,128)(2,1)S(1)} %convolution_convert_fusion.refs_6_) | copy-start | bytes 6291460
  131.5 0.7 copy-start.20
  146.4 1.0 copy-start.4
  147.4 0.9 copy-start.6
  148.3 1.0 copy-start.15
  149.4 0.9 copy-start.21

commit v5 on v4

v5 whole, which is shorter than its diff:
```python
import functools
import math

import jax
import jax.numpy as jnp
import numpy as np
from jax import lax
from jax.experimental import pallas as pl
from jax.experimental.pallas import tpu as pltpu
from jax.sharding import PartitionSpec as P

ROW = 1024
FAC = 256
QF = 128
HALF = QF // 2 + 1
LANE_TILES = ROW // FAC
BF = jnp.bfloat16
F32 = jnp.float32
MIB = 1 << 20
MOST = 56


def angles(rows, cols, modulus):
    product = (rows[:, None].astype(np.int64) * cols[None, :]) % modulus
    return (product.astype(np.float32) * np.float32(2.0 * math.pi / modulus)).astype(np.float64)


def host_tables(ways, group):
    k2, t1 = np.arange(HALF), np.arange(FAC)
    t2 = (np.arange(LANE_TILES)[:, None] + LANE_TILES * np.arange(ways)[None, :]).reshape(-1)
    eye = np.eye(group)
    a = angles(k2, t2, QF)
    steps = np.stack([np.cos(a), -np.sin(a)])
    first = np.einsum("rkt,cd->rkctd", steps, eye).reshape(2 * HALF * group, t2.size * group)
    weight = np.where((k2 == 0) | (k2 == QF // 2), 1.0, 2.0) / (QF * FAC)
    b = angles(t2, k2, QF)
    back = np.concatenate([np.cos(b) * weight, (-np.sin(b) * weight)[:, 1:-1]], axis=1)
    last = np.einsum("tk,cd->tckd", back, eye).reshape(t2.size * group, -1)
    s = angles(t1, t1, FAC)
    square = np.concatenate([np.cos(s), np.sin(s)])
    w = angles(k2, t1, QF * FAC)
    twiddle = np.concatenate([np.repeat(f(w), group, axis=0) for f in (np.cos, np.sin)]).astype(np.float32)
    as_bf = lambda v: np.asarray(v, np.float32).astype(BF)
    return as_bf(first), as_bf(square), twiddle, as_bf(last)


def params(mib):
    return pltpu.CompilerParams(vmem_limit_bytes=mib * MIB)


VMEM = pl.BlockSpec(memory_space=pltpu.VMEM)
ANY = pl.BlockSpec(memory_space=pl.ANY)
DY_MOVES = ((0, 0), (0, 2), (1, 0), (1, 2), (0, 1), (1, 1), (0, -1), (1, -1))


def place(index, move):
    flip, step = move
    return ((index ^ 4) if flip else index) & 4 | ((index + step) & 3)


def dot(a, b):
    return jnp.dot(a, b, preferred_element_type=F32)


def my_core():
    return lax.axis_index("ctx") & 1


def rows_at(i, n):
    return pl.ds(pl.multiple_of(i * n, n), n)


def product_t(order, values):
    return lax.dot_general(order, values, (((1,), (1,)), ((), ())), preferred_element_type=F32)


def copy_all(copies):
    copies = list(copies)
    for copy in copies:
        copy.start()
    for copy in copies:
        copy.wait()


def iota(axis, n):
    return lax.broadcasted_iota(jnp.int32, (n, n), axis)


def order_in(ways, width):
    row, group = iota(0, width), width // ways
    r = group // 2
    channel = (row // r % 2) * (width // 2) + (row // group) * r + row % r
    return (channel == iota(1, width)).astype(F32).astype(BF)


def order_z(ways, width):
    row, r = iota(0, width), width // ways // 2
    core = (row // (width // 2)) ^ my_core()
    slot = (row % (width // 2) // r) * 2 * r + core * r + row % r
    return (slot == iota(1, width)).astype(F32).astype(BF)


def dy_kernel(step, w_hbm, d_hbm, *refs):
    outs, (w_ref, d_ref, p_ref, w_sem, d_sem, o_sem) = refs[:4], refs[4:]
    me = lax.axis_index("fsdp")
    n = outs[0].shape[0] // 2
    gather = [
        pltpu.make_async_copy(w_hbm.at[rows_at(place(me, move), n), :], w_ref.at[pl.ds(i * n, n), :], w_sem.at[i])
        for i, move in enumerate(DY_MOVES)
    ]
    pieces = [pl.ds(i * step, step) for i in range(d_ref.shape[0] // step)]
    loads = [
        pltpu.make_async_copy(d_hbm.at[rows, :], d_ref.at[rows, :], d_sem.at[i]) for i, rows in enumerate(pieces)
    ]
    for copy in (*gather, *loads):
        copy.start()
    for copy in gather:
        copy.wait()
    stores = []
    for i, rows in enumerate(pieces):
        loads[i].wait()
        p_ref[:, rows] = product_t(w_ref[...], d_ref[rows, :]).astype(BF)
        for j, out in enumerate(outs):
            store = pltpu.make_async_copy(
                p_ref.at[pl.ds(2 * n * j, 2 * n), rows], out.at[:, rows], o_sem.at[i * len(outs) + j]
            )
            store.start()
            stores.append(store)
    for store in stores:
        store.wait()


def prep_kernel(k_ref, v_ref, f_ref, send_ref):
    width = k_ref.shape[1]
    ways = send_ref.shape[0] // (2 * 8)
    order = order_in(ways, width)
    mixed = (k_ref[...].astype(F32) * v_ref[...].astype(F32)).astype(BF)
    parts = [product_t(order, x).reshape(ways, 1, -1, ROW) for x in (mixed, f_ref[...])]
    send_ref[...] = jnp.concatenate(parts, axis=1).reshape(send_ref.shape).astype(BF)


def turn_query_kernel(q_ref, qt_ref, mine_ref, away_ref):
    qt_ref[...] = q_ref[...].astype(F32).T.astype(BF)
    core, n = my_core(), mine_ref.shape[0]
    mine_ref[...] = qt_ref[rows_at(core, n), :]
    away_ref[...] = qt_ref[rows_at(1 - core, n), :]


def gate_kernel(ways, z_ref, q_mine_ref, q_theirs_ref, gated_ref, z_mine_ref, z_away_ref):
    z = dot(order_z(ways, z_ref.shape[0]), z_ref[...])
    n = z.shape[0] // 2
    z_mine_ref[...] = z[:n].astype(BF)
    z_away_ref[...] = z[n:].astype(BF)
    gated_ref[pl.ds(0, n), :] = (z[:n] * q_mine_ref[...].astype(F32)).astype(BF)
    gated_ref[pl.ds(n, n), :] = (z[n:] * q_theirs_ref[...].astype(F32)).astype(BF)


def sum_kernel(own_ref, x_ref, up_ref, down_ref, keep_ref, far_ref, side_ref):
    n = keep_ref.shape[0]
    near, second = pl.ds(0, n), pl.ds(n, n)
    own = own_ref[near, :].astype(F32) + x_ref[near, :].astype(F32)
    keep_ref[...] = own + (up_ref[near, :].astype(F32) + down_ref[near, :].astype(F32))
    far_ref[...] = (own_ref[second, :].astype(F32) + x_ref[second, :].astype(F32)).astype(BF)
    side_ref[...] = (up_ref[second, :].astype(F32) + down_ref[second, :].astype(F32)).astype(BF)


def dz_kernel(ways, keep_ref, far_ref, side_ref, qt_ref, send_ref):
    dy = keep_ref[...] + (far_ref[...].astype(F32) + side_ref[...].astype(F32))
    dz = (dy * qt_ref[...].astype(F32)).astype(BF)
    send_ref[...] = dot(order_in(ways, dz.shape[0]), dz).astype(BF)


def query_kernel(keep_ref, far_ref, side_ref, z_mine_ref, z_theirs_ref, gq_ref, gq_t_ref):
    gq_t_ref[...] = keep_ref[...] + (far_ref[...].astype(F32) + side_ref[...].astype(F32))
    core, n = my_core(), z_mine_ref.shape[0]
    for z_ref, half in ((z_mine_ref, core), (z_theirs_ref, 1 - core)):
        own = rows_at(half, n)
        gq_t_ref[own, :] *= z_ref[...].astype(F32)
    gq_ref[...] = gq_t_ref[...].T.astype(BF)


class Tables:
    def __init__(self, hbm, vmem, sem):
        self.refs = dict(zip(("first", "square", "twiddle", "last"), vmem))
        self.loads = {
            name: pltpu.make_async_copy(x, to, sem.at[i]) for i, (name, x, to) in enumerate(zip(self.refs, hbm, vmem))
        }

    def start(self):
        for load in self.loads.values():
            load.start()

    def __getitem__(self, name):
        if name in self.loads:
            self.loads.pop(name).wait()
        return self.refs[name]


def times_square(left, right, tables):
    square = tables["square"]
    return dot(left, square[:FAC]) + dot(right, square[FAC:])


def transform(x, tables):
    x = jnp.concatenate([x[:, u * FAC : (u + 1) * FAC] for u in range(LANE_TILES)], axis=0)
    section = dot(tables["first"][...], x)
    n = section.shape[0] // 2
    twiddle = tables["twiddle"]
    re, im, tc, ts = section[:n], section[n:], twiddle[:n], twiddle[n:]
    b_re, b_im = re * tc + im * ts, im * tc - re * ts
    left = jnp.concatenate([b_re, b_im], axis=0).astype(BF)
    right = jnp.concatenate([b_im, -b_re], axis=0).astype(BF)
    f = times_square(left, right, tables)
    return f[:n], f[n:]


def signal(p_re, p_im, tables):
    n, group = p_re.shape[0], p_re.shape[0] // HALF
    left = jnp.concatenate([p_re, p_im], axis=0).astype(BF)
    right = jnp.concatenate([-p_im, p_re], axis=0).astype(BF)
    c = times_square(left, right, tables)
    twiddle = tables["twiddle"]
    re, im, tc, ts = c[:n], c[n:], twiddle[:n], twiddle[n:]
    e_re, e_im = re * tc - im * ts, im * tc + re * ts
    e = jnp.concatenate([e_re, e_im[group : n - group]], axis=0).astype(BF)
    x = dot(tables["last"][...], e)
    rows = x.shape[0] // LANE_TILES
    return jnp.concatenate([x[u * rows : (u + 1) * rows] for u in range(LANE_TILES)], axis=1)


def conv_kernel(*refs):
    (r_hbm, *tables_hbm), (z_hbm, h_hbm) = refs[:5], refs[7:9]
    r_ref, z_ref, h_ref, *tables, table_sem, sem = refs[9:]
    tables = Tables(tables_hbm, tables, table_sem)
    load = pltpu.make_async_copy(r_hbm, r_ref, sem.at[0])
    load.start()
    tables.start()
    rows = z_ref.shape[0]
    group = h_ref.shape[0] // (2 * HALF)
    load.wait()
    r = r_ref[...].astype(F32).reshape(-1, 2, group, ROW)
    u, h = (transform(r[:, s].reshape(rows, ROW).astype(BF), tables) for s in range(2))
    h_ref[...] = jnp.concatenate(h, axis=0).astype(BF)
    h_store = pltpu.make_async_copy(h_ref, h_hbm, sem.at[1])
    h_store.start()
    p_re, p_im = u[0] * h[0] - u[1] * h[1], u[0] * h[1] + u[1] * h[0]
    z_ref[...] = signal(p_re, p_im, tables).astype(BF)
    z_store = pltpu.make_async_copy(z_ref, z_hbm, sem.at[2])
    z_store.start()
    h_store.wait()
    z_store.wait()


def adjoint_kernel(*refs):
    (r_hbm, h_hbm, *tables_hbm), outs = refs[:6], refs[7:9]
    r_ref, h_ref, keep_ref, away_ref, *tables, table_sem, sem = refs[9:]
    tables = Tables(tables_hbm, tables, table_sem)
    load = pltpu.make_async_copy(r_hbm, r_ref, sem.at[0])
    h_load = pltpu.make_async_copy(h_hbm, h_ref, sem.at[1])
    load.start()
    tables.start()
    h_load.start()
    load.wait()
    g_re, g_im = transform(r_ref[...], tables)
    h_load.wait()
    h = h_ref[...].astype(F32)
    n = h.shape[0] // 2
    h_re, h_im = h[:n], h[n:]
    q_re, q_im = h_re * g_re + h_im * g_im, h_re * g_im - h_im * g_re
    du = signal(q_re, q_im, tables)
    half = du.shape[0] // 2
    low, high, first_core = du[:half], du[half:], my_core() == 0
    keep_ref[...] = jnp.where(first_core, low, high).astype(BF)
    away_ref[...] = jnp.where(first_core, high, low).astype(BF)
    copy_all([pltpu.make_async_copy(x, to, sem.at[2 + i]) for i, (x, to) in enumerate(zip((away_ref, keep_ref), outs))])


def weight_kernel(scale, width, moves, *refs):
    count = len(moves)
    blocks, (d_ref, d_other_ref), refs = refs[:count], refs[count : count + 2], refs[-7:]
    pack_hbm, away_hbm, mine_ref, away_ref, part_ref, sem, o_sem = refs
    me = lax.axis_index("fsdp")
    n = blocks[0].shape[0] // 2
    places = [place(me, move) for move in moves]
    copy_all(
        pltpu.make_async_copy(block.at[pl.ds(j * n, n), :], to_ref.at[pl.ds(i * n, n), :], sem.at[2 * i + j])
        for i, block in enumerate(blocks)
        for j, to_ref in enumerate((mine_ref, away_ref))
    )
    stores = [pltpu.make_async_copy(away_ref, away_hbm, o_sem.at[0])]
    stores[0].start()
    for j in range(d_ref.shape[1] // width):
        cols = pl.ds(j * width, width)
        p = dot(mine_ref[...], d_ref[:, cols]) + dot(away_ref[...], d_other_ref[:, cols])
        part_ref[:, cols] = (p * scale).astype(BF)
        for i in range(count):
            store = pltpu.make_async_copy(
                part_ref.at[pl.ds(i * n, n), cols],
                pack_hbm.at[places[i], pl.ds(0, n), cols],
                o_sem.at[1 + j * count + i],
            )
            store.start()
            stores.append(store)
    for store in stores:
        store.wait()


def assemble_kernel(*refs):
    blocks, theirs, (all_hbm, sem) = refs[:8], refs[8:10], refs[10:]
    me, core = lax.axis_index("fsdp"), my_core()
    n = blocks[0].shape[0] // 2
    copies = []
    for i, (block, move) in enumerate(zip(blocks, RING_FROM)):
        start = 2 * place(me, move)
        other = theirs[i // 4].at[pl.ds(i % 4 * n, n), :]
        for j, (x, half) in enumerate(((block.at[pl.ds(0, n), :], core), (other, 1 - core))):
            copies.append(pltpu.make_async_copy(x, all_hbm.at[rows_at(start + half, n), :], sem.at[2 * i + j]))
    copy_all(copies)


def pack_kernel(pack_in, keep_ref, got_ref, pack_hbm, both_ref, sem):
    del pack_in
    groups, rows, _ = both_ref.shape
    pieces = [ref[...].astype(F32).reshape(groups, rows // 2, ROW) for ref in (keep_ref, got_ref)]
    both_ref[...] = jnp.concatenate(pieces, axis=1).astype(BF)
    behind = pl.ds(pack_hbm.shape[1] - rows, rows)
    copy_all([pltpu.make_async_copy(both_ref, pack_hbm.at[:, behind, :], sem.at[0])])


def final_kernel(parts_ref, k_ref, v_ref, gw_ref, gk_ref, gv_ref):
    n = gw_ref.shape[0]
    groups, rows, _ = parts_ref.shape
    total = parts_ref[0, pl.ds(0, n), :].astype(F32)
    for g in range(1, groups):
        total += parts_ref[g, pl.ds(0, n), :].astype(F32)
    gw_ref[...] = total
    c = (rows - n) // 2
    du = parts_ref[:, pl.ds(n, 2 * c), :].astype(F32)
    keep, got = du[:, :c], du[:, c:]
    first_core = my_core() == 0
    low, high = jnp.where(first_core, keep, got), jnp.where(first_core, got, keep)
    width = 2 * groups * c
    du = jnp.concatenate([low, high], axis=1).reshape(width, -1)
    du = dot(du.T.astype(BF), order_in(2 * groups, width))
    gk_ref[...] = (du * v_ref[...].astype(F32)).astype(BF)
    gv_ref[...] = (du * k_ref[...].astype(F32)).astype(BF)


def staged(kernel, n_in, n_out, n_after, staged_in, staged_out):
    def run(*refs):
        ins, refs = list(refs[:n_in]), refs[n_in + n_after :]
        outs, refs = list(refs[:n_out]), refs[n_out:]
        extra = len(staged_in) + len(staged_out) + 2
        own, extra = refs[: len(refs) - extra], refs[len(refs) - extra :]
        buffers, (in_sem, out_sem) = extra[:-2], extra[-2:]
        loads, stores = [], []
        for j, i in enumerate(staged_in):
            loads.append(pltpu.make_async_copy(ins[i], buffers[j], in_sem.at[j]))
            ins[i] = buffers[j]
        for j, i in enumerate(staged_out):
            buffer = buffers[len(staged_in) + j]
            stores.append(pltpu.make_async_copy(buffer, outs[i], out_sem.at[j]))
            outs[i] = buffer
        copy_all(loads)
        kernel(*ins, *outs, *own)
        copy_all(stores)

    return run


def call(kernel, outs, ins, scratch=(), mib=16, flops=0, specs=None, after=(), staged_in=(), staged_out=(), aliases=None):
    total = sum(math.prod(o.shape) * o.dtype.itemsize for o in (*outs, *ins))
    if after or staged_in or staged_out:
        kernel = staged(kernel, len(ins), len(outs), len(after), staged_in, staged_out)
        buffers = [pltpu.VMEM(ins[i].shape, ins[i].dtype) for i in staged_in]
        buffers += [pltpu.VMEM(outs[i].shape, outs[i].dtype) for i in staged_out]
        sems = [pltpu.SemaphoreType.DMA((max(len(x), 1),)) for x in (staged_in, staged_out)]
        scratch = [*scratch, *buffers, *sems]
    in_specs, out_specs = specs or ([VMEM] * len(ins), [VMEM] * len(outs))
    in_specs = [ANY if i in staged_in else s for i, s in enumerate(in_specs)]
    out_specs = [ANY if i in staged_out else s for i, s in enumerate(out_specs)]
    return pl.pallas_call(
        kernel,
        out_shape=outs,
        in_specs=[*in_specs, *([ANY] * len(after))],
        out_specs=out_specs,
        scratch_shapes=scratch,
        input_output_aliases=aliases or {},
        compiler_params=params(mib),
        cost_estimate=pl.CostEstimate(flops=0, bytes_accessed=0, transcendentals=0),
    )(*ins, *after)


def shape(*dims, dtype=BF):
    return jax.ShapeDtypeStruct(dims, dtype)


def spread(values):
    return lax.all_to_all(values, "ctx", 0, 0, tiled=True)


def move_over(values, move):
    return lax.ppermute(values, "fsdp", [(i, place(i, move)) for i in range(8)])


RING_FROM = ((0, 0), (1, 0), (0, -1), (0, 1), (1, -1), (1, 1), (0, 2), (1, 2))


def ring_near(gated):
    up, down = (0, 1), (0, -1)
    other = move_over(gated, (1, 0))
    own_up, own_down = move_over(gated, up), move_over(gated, down)
    return gated, other, own_up, own_down, move_over(other, up), move_over(other, down)


def ring_far(own_up, other_down):
    return move_over(own_up, (0, 1)), move_over(other_down, (0, -1))


def dy_product(w_out, d_out, after):
    channels, depth = w_out.shape
    rows = d_out.shape[0]
    step = 512
    pieces = rows // step
    return call(
        functools.partial(dy_kernel, step),
        [shape(channels // 4, rows)] * 4,
        [w_out, d_out],
        [
            pltpu.VMEM((channels, depth), BF),
            pltpu.VMEM((rows, depth), BF),
            pltpu.VMEM((channels, rows), BF),
            pltpu.SemaphoreType.DMA((8,)),
            pltpu.SemaphoreType.DMA((pieces,)),
            pltpu.SemaphoreType.DMA((4 * pieces,)),
        ],
        flops=2 * channels * depth * rows,
        mib=MOST,
        specs=([ANY] * 2, [ANY] * 4),
        after=after,
    )


def weight_product(blocks, moves, d_out, d_other, scale, pack_rows, so_far=(), after=()):
    rows, columns = d_out.shape
    n = blocks[0].shape[0] // 2
    count, width = len(moves), 512
    ins = [*blocks, d_out, d_other]
    return call(
        functools.partial(weight_kernel, scale, width, moves),
        [shape(8, pack_rows, columns), shape(count * n, rows)],
        [*ins, *so_far],
        [
            pltpu.VMEM((count * n, rows), BF),
            pltpu.VMEM((count * n, rows), BF),
            pltpu.VMEM((count * n, columns), BF),
            pltpu.SemaphoreType.DMA((2 * count,)),
            pltpu.SemaphoreType.DMA((1 + columns // width * count,)),
        ],
        flops=4 * count * n * rows * columns,
        specs=([ANY] * count + [VMEM] * 2 + [ANY] * len(so_far), [ANY] * 2),
        after=after,
        aliases={len(ins) + i: i for i in range(len(so_far))},
    )


def on_device(query_in, key_in, value_in, filt, w_out, d_out):
    seq_rows, width = query_in.shape
    channels, columns = w_out.shape
    ways = lax.axis_size("ctx")
    group, half = width // ways, width // 2
    n = HALF * group
    *tables, last = host_tables(ways, group)
    slots = np.arange(ways * group).reshape(ways // 2, 2, 2, group // 2)
    pick = lambda rows: last.reshape(LANE_TILES, ways * group, -1)[:, rows.reshape(-1)].reshape(last.shape)
    last_z = pick(slots.transpose(0, 2, 1, 3))
    last_du = pick(slots.reshape(ways // 2, 2, group).transpose(1, 0, 2))

    swap = lambda v: lax.ppermute(v, "ctx", [(i, i ^ 1) for i in range(ways)])
    rows_like, half_like = shape(width, seq_rows), shape(half, seq_rows)

    (send,) = call(
        prep_kernel,
        [shape(ways * 2 * group, seq_rows)],
        [key_in, value_in, filt],
        mib=MOST,
        staged_in=(0, 1, 2),
        staged_out=(0,),
    )
    arrived = spread(send)
    own_y, x_y, up_y, down_y = dy_product(w_out, d_out, [send])
    keep_y, far_y, side_y = call(
        sum_kernel,
        [shape(width, seq_rows, dtype=F32), rows_like, rows_like],
        [own_y, move_over(x_y, (1, 0)), move_over(up_y, (0, 1)), move_over(down_y, (0, -1))],
    )

    query_t, q_mine, q_away = call(
        turn_query_kernel, [rows_like, half_like, half_like], [query_in], after=[own_y], mib=MOST, staged_in=(0,), staged_out=(0, 1, 2)
    )
    q_theirs = swap(q_away)

    flops = 2 * 2 * n * (tables[0].shape[1] + 2 * FAC) * FAC
    table_buffers = [pltpu.VMEM(x.shape, x.dtype) for x in (*tables, last)] + [pltpu.SemaphoreType.DMA((4,))]
    spectrum_like = shape(2 * n, FAC)
    conv, spectrum = call(
        conv_kernel,
        [rows_like, spectrum_like],
        [arrived, *tables, last_z, q_theirs, far_y],
        [pltpu.VMEM(x.shape, x.dtype) for x in (arrived, rows_like, spectrum_like)]
        + [*table_buffers, pltpu.SemaphoreType.DMA((3,))],
        mib=MOST,
        flops=3 * flops,
        specs=([ANY] * 7, [ANY] * 2),
    )
    conv, d_late = lax.optimization_barrier((conv, d_out))
    d_other = swap(d_late)
    dy = (keep_y, move_over(far_y, (0, 2)), move_over(side_y, (1, 0)))
    (send_z,) = call(
        functools.partial(dz_kernel, ways), [rows_like], [*dy, query_t], staged_out=(0,)
    )
    gated, z_mine, z_away = call(
        functools.partial(gate_kernel, ways),
        [rows_like, half_like, half_like],
        [spread(conv), q_mine, q_theirs],
        after=[d_other, send_z],
    )
    z_theirs = swap(z_away)
    blocks = ring_near(gated)
    blocks = (*blocks, *ring_far(blocks[2], blocks[5]))
    like = shape(seq_rows, width)
    (grad_query,) = call(
        query_kernel, [like], [*dy, z_mine, z_theirs], [pltpu.VMEM((width, seq_rows), F32)], staged_out=(0,)
    )
    scale = 1.0 / math.sqrt(seq_rows * ways)
    weight = functools.partial(weight_product, d_out=d_out, d_other=d_other, scale=scale, pack_rows=half + 2 * group)
    pack, away = weight(blocks[:4], RING_FROM[:4])
    theirs_near = swap(away)
    du_away, du_keep = call(
        adjoint_kernel,
        [half_like, half_like],
        [spread(send_z), spectrum, *tables, last_du, theirs_near],
        [pltpu.VMEM(x.shape, x.dtype) for x in (rows_like, spectrum_like, half_like, half_like)]
        + [*table_buffers, pltpu.SemaphoreType.DMA((4,))],
        mib=MOST,
        flops=2 * flops,
        specs=([ANY] * 7, [ANY] * 2),
    )
    du_got = swap(du_away)
    pack, away = weight(blocks[4:], RING_FROM[4:], so_far=(pack,))
    (pack,) = call(
        pack_kernel,
        [shape(*pack.shape)],
        [pack, du_keep, du_got],
        [pltpu.VMEM((ways // 2, 2 * group, columns), BF), pltpu.SemaphoreType.DMA((1,))],
        specs=([ANY, VMEM, VMEM], [ANY]),
        aliases={0: 0},
    )
    groups = [list(range(c, ways, 2)) for c in range(2)]
    parts = lax.all_to_all(pack, "ctx", 0, 0, tiled=True, axis_index_groups=groups)

    (gated_all,) = call(
        assemble_kernel,
        [shape(channels, seq_rows)],
        [*blocks, theirs_near, swap(away)],
        [pltpu.SemaphoreType.DMA((16,))],
        specs=([ANY] * 10, [ANY]),
    )
    layer_out = lax.dot_general(
        gated_all, w_out, (((0,), (0,)), ((), ())), preferred_element_type=F32
    ).astype(BF)

    grad_weight, grad_key, grad_value = call(
        final_kernel,
        [shape(channels // ways, columns, dtype=F32), like, like],
        [parts, key_in, value_in],
        mib=MOST,
        after=[layer_out, grad_query],
        staged_in=(0, 1, 2),
        staged_out=(0, 1, 2),
    )
    return (layer_out, grad_query, grad_key, grad_value, grad_weight)


def solution(mesh):
    both = P("ctx", "fsdp")
    return jax.shard_map(
        on_device,
        mesh=mesh,
        in_specs=(both, both, both, both, P(None, "fsdp"), both),
        out_specs=(both, both, both, both, both),
        check_vma=False,
    )
```

time: 153 us -> 133 us (0.87)
  blocking collectives: 32.9 us -> 0 us
  starting transfers between devices: 24.5 us -> 41.9 us
  Pallas kernels: 24.1 us -> 41.3 us
  waiting for transfers between devices: 51 us -> 38.5 us
  local copies, waits for them, and re-layouts: 14.2 us -> 4.92 us
  other arithmetic: 1.56 us -> 0 us
    all_to_all x2 -> x0, blocking collectives: 32.9 us -> none  [spread(): return lax.all_to_all(values, 'ctx', 0, 0, tiled=True)]
    pallas_call x11 -> x14, Pallas kernels: 24.1 us -> 41.3 us  [call(): pl.pallas_call(kernel, out_shape=outs, in_specs=[*in_specs, *[ANY] * len(...]
    ppermute x11 -> x12, waiting for transfers between devices: 27.6 us -> 13.3 us  [move_over(): return lax.ppermute(values, 'fsdp', [(i, place(i, move)) for i in range(8)])]
    all_to_all x1 -> x3, starting transfers between devices: 3.53 us -> 14.5 us  [spread(): return lax.all_to_all(values, 'ctx', 0, 0, tiled=True)]
    unnamed x54 -> x48, local copies, waits for them, and re-layouts: 14.2 us -> 4.92 us
    all_to_all x1 -> x3, waiting for transfers between devices: 6.87 us -> 14.1 us  [spread(): return lax.all_to_all(values, 'ctx', 0, 0, tiled=True)]
    all_to_all x1, waiting for transfers between devices: 14.2 us -> 9.57 us  [on_device(): lax.all_to_all(pack, 'ctx', 0, 0, tiled=True, axis_index_groups=groups)]
    all_to_all x1, starting transfers between devices: 3.58 us -> 6.9 us  [on_device(): lax.all_to_all(pack, 'ctx', 0, 0, tiled=True, axis_index_groups=groups)]
  transfers between devices with their start and end apart: 18 -> 22, of which waited for: 9 -> 11; matrix products, arithmetic and copies ran while one was open for 3% -> 3% of each run, Pallas kernels for 11% -> 14%
where the time goes in v5:
time: 133 us; the launch traced here: 132 us
  starting transfers between devices  41.9 us (32%)
  Pallas kernels  41.3 us (31%)
  waiting for transfers between devices  38.5 us (29%)
  local copies, waits for them, and re-layouts  4.92 us (4%)
  matrix products  3.75 us (3%)
    pallas_call x14, Pallas kernels, call(): pl.pallas_call(kernel, out_shape=outs, in_specs=[*in_specs, *[ANY] * len(...  41.3 us
    ppermute x12, starting transfers between devices, move_over(): return lax.ppermute(values, 'fsdp', [(i, place(i, move)) for i in range(8)])  19.3 us
    all_to_all x3, starting transfers between devices, spread(): return lax.all_to_all(values, 'ctx', 0, 0, tiled=True)  14.5 us
    all_to_all x3, waiting for transfers between devices, spread(): return lax.all_to_all(values, 'ctx', 0, 0, tiled=True)  14.1 us
    ppermute x12, waiting for transfers between devices, move_over(): return lax.ppermute(values, 'fsdp', [(i, place(i, move)) for i in range(8)])  13.3 us
    all_to_all x1, waiting for transfers between devices, on_device(): lax.all_to_all(pack, 'ctx', 0, 0, tiled=True, axis_index_groups=groups)  9.57 us
    all_to_all x1, starting transfers between devices, on_device(): lax.all_to_all(pack, 'ctx', 0, 0, tiled=True, axis_index_groups=groups)  6.9 us
    unnamed x48, local copies, waits for them, and re-layouts  4.92 us
  transfers between devices with their start and end apart: 22, of which 11 were waited for; matrix products, arithmetic and copies ran while one was open for 3% of the time, Pallas kernels for 14%

profile of v5, /device:TPU:0, one launch (start us, length us, event | category | flops | bytes accessed | tf_op | source)
XLA Modules:
  0.0 131.6 jit_solution(2478491578019386910)
XLA Ops:
  0.6 2.3 %shard_map.146.refs_2_ = bf16[256,1024]{1,0:T(8,128)(2,1)} custom-call(bf16[1024,128]{1,0:T(8,128)(2,1)} %refs_1_.6, bf16[1024,128]{1,0:T(8,128)(2,1)} %refs_2_.5, bf16[1024,128]{1,0:T(8,128)(2,1)} %refs_2_.4), custom_call_target="tpu_custom_call" | custom-call | tf_op jit(solution)/shard_map/pallas_call | solution.py:382
  2.9 5.6 %shard_map.147 = (bf16[256,1024]{1,0:T(8,128)(2,1)}, bf16[256,1024]{1,0:T(8,128)(2,1)}, bf16[256,1024]{1,0:T(8,128)(2,1)}, bf16[256,1024]{1,0:T(8,128)(2,1)}) custom-call(bf16[1024,1024]{1,0:T(8,128)(2,1)} %refs_0_.4, bf16[1024,1024]{1,0:T(8,128)(2,1)} %refs_4_.5, bf16[256,1024]{1,0:T(8,128)(2,1)} %shard_map.146.refs_2_), custom_call_target="tpu_custom_call" | custom-call | tf_op jit(solution)/shard_map/pallas_call | solution.py:382
  8.6 1.7 %collective-permute-start.1 = (bf16[256,1024]{1,0:T(8,128)(2,1)}, bf16[256,1024]{1,0:T(8,128)(2,1)S(1)}, u32[]{:S(2)}, u32[]{:S(2)}) collective-permute-start(bf16[256,1024]{1,0:T(8,128)(2,1)} %get-tuple-element.33), channel_id=1, source_target_pairs={{0,64},{16,80},{32,96},{48,112},{64,0},{80,16},{96,32},{112,48},{1... | collective-permute-start | bytes 1572872 | tf_op jit(solution)/shard_map/ppermute | solution.py:403
  10.2 1.9 %collective-permute-start.2 = (bf16[256,1024]{1,0:T(8,128)(2,1)}, bf16[256,1024]{1,0:T(8,128)(2,1)S(1)}, u32[]{:S(2)}, u32[]{:S(2)}) collective-permute-start(bf16[256,1024]{1,0:T(8,128)(2,1)} %get-tuple-element.34), channel_id=1, source_target_pairs={{0,16},{16,32},{32,48},{48,0},{64,80},{80,96},{96,112},{112,64},{1... | collective-permute-start | bytes 1572872 | tf_op jit(solution)/shard_map/ppermute | solution.py:403
  12.1 2.1 %collective-permute-start.3 = (bf16[256,1024]{1,0:T(8,128)(2,1)}, bf16[256,1024]{1,0:T(8,128)(2,1)S(1)}, u32[]{:S(2)}, u32[]{:S(2)}) collective-permute-start(bf16[256,1024]{1,0:T(8,128)(2,1)} %get-tuple-element.35), channel_id=1, source_target_pairs={{0,48},{16,0},{32,16},{48,32},{64,112},{80,64},{96,80},{112,96},{1... | collective-permute-start | bytes 1572872 | tf_op jit(solution)/shard_map/ppermute | solution.py:403
  14.3 6.7 %all-to-all-start = ((bf16[16,16,1024]{2,1,0:T(8,128)(2,1)}), bf16[16,16,1024]{2,1,0:T(8,128)(2,1)S(1)}, u32[]{:S(2)}, u32[]{:S(2)}) async-start(bf16[16,16,1024]{2,1,0:T(8,128)(2,1)} %bitcast), calls=%async_computation | async-start | bytes 1048576 | tf_op jit(solution)/shard_map/all_to_all | solution.py:399
  21.0 1.9 %shard_map.148 = (bf16[128,1024]{1,0:T(8,128)(2,1)}, bf16[64,1024]{1,0:T(8,128)(2,1)}, bf16[64,1024]{1,0:T(8,128)(2,1)}) custom-call(bf16[1024,128]{1,0:T(8,128)(2,1)} %refs_0_.5, bf16[256,1024]{1,0:T(8,128)(2,1)} %get-tuple-element.31.refs_1_.own_ref), custom_call_target="tpu_custom_call" | custom-call | tf_op jit(solution)/shard_map/pallas_call | solution.py:382
  22.9 0.5 collective-permute-start
  23.4 0.0 collective-permute-done.1.x_ref
  23.4 2.7 %collective-permute-done.2.up_ref = bf16[256,1024]{1,0:T(8,128)(2,1)S(1)} collective-permute-done((bf16[256,1024]{1,0:T(8,128)(2,1)}, bf16[256,1024]{1,0:T(8,128)(2,1)S(1)}, u32[]{:S(2)}, u32[]{:S(2)}) %collective-permute-start.2) | collective-permute-done | bytes 524320 | tf_op jit(solution)/shard_map/ppermute | solution.py:403
  26.1 0.0 collective-permute-done.3.down_ref
  26.1 0.9 shard_map.149
  27.0 0.0 collective-permute-done.refs_5_.refs_2_
  27.0 6.4 %all-to-all-done = bf16[16,16,1024]{2,1,0:T(8,128)(2,1)S(1)} async-done(((bf16[16,16,1024]{2,1,0:T(8,128)(2,1)}), bf16[16,16,1024]{2,1,0:T(8,128)(2,1)S(1)}, u32[]{:S(2)}, u32[]{:S(2)}) %all-to-all-start) | async-done | bytes 524320 | tf_op jit(solution)/shard_map/all_to_all | solution.py:399
  33.4 0.8 copy-done.22
  34.2 6.3 %shard_map.150 = (bf16[128,1024]{1,0:T(8,128)(2,1)}, bf16[1040,256]{1,0:T(8,128)(2,1)}) custom-call(bf16[256,1024]{1,0:T(8,128)(2,1)} %bitcast.9, bf16[1040,512]{1,0:T(8,128)(2,1)} %constant.10.clone.refs_1_.refs_2_, bf16[512,256]{1,0:T(8,128)(2,1)} %constant.11.clone.refs_2_.refs_3_, f32[1040,256]{1,0:T(8,128)} %constant.12.clone.refs_3_.refs_4_, ...), custom_call_target="tpu_custom_call" | custom-call | tf_op jit(solution)/shard_map/pallas_call | solution.py:382
  40.5 0.1 collective-permute-start.4
  40.6 0.3 collective-permute-start.6
  40.9 3.4 %collective-permute-start.5 = (bf16[128,1024]{1,0:T(8,128)(2,1)}, bf16[128,1024]{1,0:T(8,128)(2,1)S(1)}, u32[]{:S(2)}, u32[]{:S(2)}) collective-permute-start(bf16[128,1024]{1,0:T(8,128)(2,1)} %copy-done.14), channel_id=1, source_target_pairs={{0,32},{16,48},{32,0},{48,16},{64,96},{80,112},{96,64},{112,80},{1... | collective-permute-start | bytes 786440 | tf_op jit(solution)/shard_map/ppermute | solution.py:403
  44.3 3.5 %all-to-all-start.1 = ((bf16[16,8,1024]{2,1,0:T(8,128)(2,1)}), bf16[16,8,1024]{2,1,0:T(8,128)(2,1)S(1)}, u32[]{:S(2)}, u32[]{:S(2)}) async-start(bf16[16,8,1024]{2,1,0:T(8,128)(2,1)} %bitcast.10), calls=%async_computation.1 | async-start | bytes 524288 | tf_op jit(solution)/shard_map/all_to_all | solution.py:399
  47.8 1.7 %collective-permute-done.6.refs_2_ = bf16[128,1024]{1,0:T(8,128)(2,1)S(1)} collective-permute-done((bf16[128,1024]{1,0:T(8,128)(2,1)}, bf16[128,1024]{1,0:T(8,128)(2,1)S(1)}, u32[]{:S(2)}, u32[]{:S(2)}) %collective-permute-start.6) | collective-permute-done | bytes 262176 | tf_op jit(solution)/shard_map/ppermute | solution.py:403
  49.5 1.6 %collective-permute-done.5.refs_1_ = bf16[128,1024]{1,0:T(8,128)(2,1)S(1)} collective-permute-done((bf16[128,1024]{1,0:T(8,128)(2,1)}, bf16[128,1024]{1,0:T(8,128)(2,1)S(1)}, u32[]{:S(2)}, u32[]{:S(2)}) %collective-permute-start.5) | collective-permute-done | bytes 262176 | tf_op jit(solution)/shard_map/ppermute | solution.py:403
  51.1 1.0 copy-done.15
  52.2 1.0 shard_map.151.refs_4_
  53.2 4.1 %all-to-all-done.1 = bf16[16,8,1024]{2,1,0:T(8,128)(2,1)S(1)} async-done(((bf16[16,8,1024]{2,1,0:T(8,128)(2,1)}), bf16[16,8,1024]{2,1,0:T(8,128)(2,1)S(1)}, u32[]{:S(2)}, u32[]{:S(2)}) %all-to-all-start.1) | async-done | bytes 262176 | tf_op jit(solution)/shard_map/all_to_all | solution.py:399
  57.3 0.0 collective-permute-done.4.refs_3_.refs_5_
  57.3 0.9 copy-done.18
  58.2 0.2 shard_map.152
  58.5 0.0 copy-start.16
  58.5 0.6 copy-done.16
  59.1 0.6 copy-done.20
  59.8 0.7 collective-permute-start.9
  60.5 1.3 %collective-permute-start.8 = (bf16[128,1024]{1,0:T(8,128)(2,1)S(1)}, bf16[128,1024]{1,0:T(8,128)(2,1)S(1)}, u32[]{:S(2)}, u32[]{:S(2)}) collective-permute-start(bf16[128,1024]{1,0:T(8,128)(2,1)S(1)} %get-tuple-element.44.refs_0_), channel_id=1, source_target_pairs={{0,16},{16,32},{32,48},{48,0},{64,80},{80,96},{96,112},{112,64},{1... | collective-permute-start | bytes 786440 | tf_op jit(solution)/shard_map/ppermute | solution.py:403
  61.8 1.8 %collective-permute-start.7 = (bf16[128,1024]{1,0:T(8,128)(2,1)S(1)}, bf16[128,1024]{1,0:T(8,128)(2,1)}, u32[]{:S(2)}, u32[]{:S(2)}) collective-permute-start(bf16[128,1024]{1,0:T(8,128)(2,1)S(1)} %get-tuple-element.44.refs_0_), channel_id=1, source_target_pairs={{0,64},{16,80},{32,96},{48,112},{64,0},{80,16},{96,32},{112,48},{1... | collective-permute-start | bytes 786440 | tf_op jit(solution)/shard_map/ppermute | solution.py:403
  63.6 3.9 %collective-permute-done.9.refs_3_ = bf16[128,1024]{1,0:T(8,128)(2,1)S(1)} collective-permute-done((bf16[128,1024]{1,0:T(8,128)(2,1)S(1)}, bf16[128,1024]{1,0:T(8,128)(2,1)S(1)}, u32[]{:S(2)}, u32[]{:S(2)}) %collective-permute-start.9) | collective-permute-done | bytes 262176 | tf_op jit(solution)/shard_map/ppermute | solution.py:403
  67.5 1.6 %collective-permute-done.8.refs_2_ = bf16[128,1024]{1,0:T(8,128)(2,1)S(1)} collective-permute-done((bf16[128,1024]{1,0:T(8,128)(2,1)S(1)}, bf16[128,1024]{1,0:T(8,128)(2,1)S(1)}, u32[]{:S(2)}, u32[]{:S(2)}) %collective-permute-start.8) | collective-permute-done | bytes 262176 | tf_op jit(solution)/shard_map/ppermute | solution.py:403
  69.1 0.0 collective-permute-done.7.refs_1_
  69.1 5.1 %shard_map.153 = (bf16[8,80,1024]{2,1,0:T(8,128)(2,1)}, bf16[256,1024]{1,0:T(8,128)(2,1)}) custom-call(bf16[128,1024]{1,0:T(8,128)(2,1)S(1)} %get-tuple-element.44.refs_0_, bf16[128,1024]{1,0:T(8,128)(2,1)} %collective-permute-done.7.refs_1_, bf16[128,1024]{1,0:T(8,128)(2,1)S(1)} %collective-permute-done.8.refs_2_, ...), custom_call_target="tpu_custom_call" | custom-call | tf_op jit(solution)/shard_map/pallas_call | solution.py:382
  74.3 0.1 collective-permute-start.14
  74.4 1.9 %collective-permute-start.11 = (bf16[128,1024]{1,0:T(8,128)(2,1)}, bf16[128,1024]{1,0:T(8,128)(2,1)}, u32[]{:S(2)}, u32[]{:S(2)}) collective-permute-start(bf16[128,1024]{1,0:T(8,128)(2,1)} %collective-permute-done.7.refs_1_), channel_id=1, source_target_pairs={{0,48},{16,0},{32,16},{48,32},{64,112},{80,64},{96,80},{112,96},{1... | collective-permute-start | bytes 786440 | tf_op jit(solution)/shard_map/ppermute | solution.py:403
  76.3 4.2 %all-to-all-start.2 = ((bf16[16,8,1024]{2,1,0:T(8,128)(2,1)}), bf16[16,8,1024]{2,1,0:T(8,128)(2,1)}, u32[]{:S(2)}, u32[]{:S(2)}) async-start(bf16[16,8,1024]{2,1,0:T(8,128)(2,1)} %bitcast.4), calls=%async_computation.2 | async-start | bytes 524288 | tf_op jit(solution)/shard_map/all_to_all | solution.py:399
  80.5 0.3 collective-permute-start.12
  80.8 0.9 collective-permute-start.10
  81.7 1.8 %collective-permute-done.11.refs_1_.refs_5_ = bf16[128,1024]{1,0:T(8,128)(2,1)} collective-permute-done((bf16[128,1024]{1,0:T(8,128)(2,1)}, bf16[128,1024]{1,0:T(8,128)(2,1)}, u32[]{:S(2)}, u32[]{:S(2)}) %collective-permute-start.11) | collective-permute-done | bytes 262176 | tf_op jit(solution)/shard_map/ppermute | solution.py:403
  83.4 3.0 %collective-permute-start.13 = (bf16[128,1024]{1,0:T(8,128)(2,1)}, bf16[128,1024]{1,0:T(8,128)(2,1)}, u32[]{:S(2)}, u32[]{:S(2)}) collective-permute-start(bf16[128,1024]{1,0:T(8,128)(2,1)} %collective-permute-done.11.refs_1_.refs_5_), channel_id=1, source_target_pairs={{0,48},{16,0},{32,16},{48,32},{64,112},{80,64},{96,80},{112,96},{1... | collective-permute-start | bytes 786440 | tf_op jit(solution)/shard_map/ppermute | solution.py:403
  86.5 3.6 %all-to-all-done.2 = bf16[16,8,1024]{2,1,0:T(8,128)(2,1)} async-done(((bf16[16,8,1024]{2,1,0:T(8,128)(2,1)}), bf16[16,8,1024]{2,1,0:T(8,128)(2,1)}, u32[]{:S(2)}, u32[]{:S(2)}) %all-to-all-start.2) | async-done | bytes 262176 | tf_op jit(solution)/shard_map/all_to_all | solution.py:399
  90.0 0.0 collective-permute-done.14.refs_8_.refs_6_
  90.0 0.8 copy-done.1
  90.9 5.2 %shard_map.157 = (bf16[64,1024]{1,0:T(8,128)(2,1)}, bf16[64,1024]{1,0:T(8,128)(2,1)}) custom-call(bf16[128,1024]{1,0:T(8,128)(2,1)} %bitcast.5.refs_0_, bf16[1040,256]{1,0:T(8,128)(2,1)} %get-tuple-element.51.refs_1_, bf16[1040,512]{1,0:T(8,128)(2,1)} %constant.10.clone.refs_1_.refs_2_, bf16[512,256]{1,0:T(8,128)(2,1)} %constant.11.clone.refs_2_.refs_3_, ...), custom_call_target="tpu_custom_call" | custom-call | tf_op jit(solution)/shard_map/pallas_call | solution.py:382
  96.1 0.1 collective-permute-start.17
  96.2 5.0 %shard_map.154 = (bf16[8,80,1024]{2,1,0:T(8,128)(2,1)}, bf16[256,1024]{1,0:T(8,128)(2,1)}) custom-call(bf16[128,1024]{1,0:T(8,128)(2,1)} %collective-permute-done.10.refs_0_.refs_4_, bf16[128,1024]{1,0:T(8,128)(2,1)} %collective-permute-done.11.refs_1_.refs_5_, ...), custom_call_target="tpu_custom_call", output_to_operand_aliasing={{0}: (6, {})} | custom-call | tf_op jit(solution)/shard_map/pallas_call | solution.py:382
  101.3 0.0 copy-start.17
  101.3 0.7 shard_map.158
  102.1 0.0 copy-start.5
  102.1 0.0 copy-start.7
  102.1 6.9 %all-to-all-start.3 = ((bf16[8,80,1024]{2,1,0:T(8,128)(2,1)}), bf16[8,80,1024]{2,1,0:T(8,128)(2,1)}, u32[]{:S(2)}, u32[]{:S(2)}) async-start(bf16[8,80,1024]{2,1,0:T(8,128)(2,1)} %shard_map.158), calls=%async_computation.3 | async-start | bytes 2621440 | tf_op jit(solution)/shard_map/all_to_all | solution.py:560
  109.0 0.5 collective-permute-start.16
  109.5 1.6 %collective-permute-done.16.refs_4_ = bf16[64,1024]{1,0:T(8,128)(2,1)S(1)} collective-permute-done((bf16[64,1024]{1,0:T(8,128)(2,1)S(1)}, bf16[64,1024]{1,0:T(8,128)(2,1)S(1)}, u32[]{:S(2)}, u32[]{:S(2)}) %collective-permute-start.16) | collective-permute-done | bytes 131104 | tf_op jit(solution)/shard_map/ppermute | solution.py:479
  111.1 1.1 shard_map.156.refs_4_
  112.2 0.0 copy-start.23
  112.3 3.0 %shard_map.155 = bf16[1024,1024]{1,0:T(8,128)(2,1)S(1)} custom-call(bf16[128,1024]{1,0:T(8,128)(2,1)S(1)} %get-tuple-element.44.refs_0_, bf16[128,1024]{1,0:T(8,128)(2,1)} %collective-permute-done.7.refs_1_, bf16[128,1024]{1,0:T(8,128)(2,1)S(1)} %copy-done.7, bf16[128,1024]{1,0:T(8,128)(2,1)S(1)} %copy-done.5, ...), custom_call_target="tpu_custom_call" | custom-call | tf_op jit(solution)/shard_map/pallas_call | solution.py:382
  115.3 3.8 %convolution_convert_fusion.refs_3_ = bf16[1024,1024]{1,0:T(8,128)(2,1)} fusion(bf16[1024,1024]{1,0:T(8,128)(2,1)S(1)} %shard_map.155, bf16[1024,1024]{1,0:T(8,128)(2,1)S(1)} %copy-done.23), kind=kOutput, calls=%fused_computation | convolution fusion | flops 2148532224 | bytes 6291456 | tf_op jit(solution)/shard_map/dot_general | solution.py:569
  119.0 9.6 %all-to-all-done.3.refs_0_ = bf16[8,80,1024]{2,1,0:T(8,128)(2,1)} async-done(((bf16[8,80,1024]{2,1,0:T(8,128)(2,1)}), bf16[8,80,1024]{2,1,0:T(8,128)(2,1)}, u32[]{:S(2)}, u32[]{:S(2)}) %all-to-all-start.3) | async-done | bytes 1310752 | tf_op jit(solution)/shard_map/all_to_all | solution.py:560
  128.6 2.8 %shard_map.159 = (f32[64,1024]{1,0:T(8,128)}, bf16[1024,128]{1,0:T(8,128)(2,1)}, bf16[1024,128]{1,0:T(8,128)(2,1)}) custom-call(bf16[8,80,1024]{2,1,0:T(8,128)(2,1)} %all-to-all-done.3.refs_0_, bf16[1024,128]{1,0:T(8,128)(2,1)} %refs_1_.6, bf16[1024,128]{1,0:T(8,128)(2,1)} %refs_2_.5, bf16[1024,1024]{1,0:T(8,128)(2,1)} %convolution_convert_fusion.refs_3_, ...), custom_call_target="tpu_custom_call" | custom-call | tf_op jit(solution)/shard_map/pallas_call | solution.py:382
  (43 shorter events, 0.1 us)
Async XLA Ops:
  8.6 17.6 %copy-start.3 = (bf16[256,1024]{1,0:T(8,128)(2,1)S(1)}, bf16[256,1024]{1,0:T(8,128)(2,1)}, u32[]{:S(2)}) copy-start(bf16[256,1024]{1,0:T(8,128)(2,1)} %get-tuple-element.31.refs_1_.own_ref) | copy-start | bytes 1572868
  8.6 14.9 %collective-permute-start.1 = (bf16[256,1024]{1,0:T(8,128)(2,1)}, bf16[256,1024]{1,0:T(8,128)(2,1)S(1)}, u32[]{:S(2)}, u32[]{:S(2)}) collective-permute-start(bf16[256,1024]{1,0:T(8,128)(2,1)} %get-tuple-element.33), channel_id=1, source_target_pairs={{0,64},{16,80},{32,96},{48,112},{64,0},{80,16},{96,32},{112,48},{1... | collective-permute-start | bytes 1572872 | tf_op jit(solution)/shard_map/ppermute | solution.py:403
  10.2 15.9 %collective-permute-start.2 = (bf16[256,1024]{1,0:T(8,128)(2,1)}, bf16[256,1024]{1,0:T(8,128)(2,1)S(1)}, u32[]{:S(2)}, u32[]{:S(2)}) collective-permute-start(bf16[256,1024]{1,0:T(8,128)(2,1)} %get-tuple-element.34), channel_id=1, source_target_pairs={{0,16},{16,32},{32,48},{48,0},{64,80},{80,96},{96,112},{112,64},{1... | collective-permute-start | bytes 1572872 | tf_op jit(solution)/shard_map/ppermute | solution.py:403
  12.1 14.0 %collective-permute-start.3 = (bf16[256,1024]{1,0:T(8,128)(2,1)}, bf16[256,1024]{1,0:T(8,128)(2,1)S(1)}, u32[]{:S(2)}, u32[]{:S(2)}) collective-permute-start(bf16[256,1024]{1,0:T(8,128)(2,1)} %get-tuple-element.35), channel_id=1, source_target_pairs={{0,48},{16,0},{32,16},{48,32},{64,112},{80,64},{96,80},{112,96},{1... | collective-permute-start | bytes 1572872 | tf_op jit(solution)/shard_map/ppermute | solution.py:403
  14.3 19.1 %all-to-all-start = ((bf16[16,16,1024]{2,1,0:T(8,128)(2,1)}), bf16[16,16,1024]{2,1,0:T(8,128)(2,1)S(1)}, u32[]{:S(2)}, u32[]{:S(2)}) async-start(bf16[16,16,1024]{2,1,0:T(8,128)(2,1)} %bitcast), calls=%async_computation | async-start | bytes 1048576 | tf_op jit(solution)/shard_map/all_to_all | solution.py:399
  22.9 4.0 %collective-permute-start = (bf16[64,1024]{1,0:T(8,128)(2,1)}, bf16[64,1024]{1,0:T(8,128)(2,1)S(1)}, u32[]{:S(2)}, u32[]{:S(2)}) collective-permute-start(bf16[64,1024]{1,0:T(8,128)(2,1)} %get-tuple-element.32), channel_id=1, source_target_pairs={{0,1},{1,0},{2,3},{3,2},{4,5},{5,4},{6,7},{7,6},{8,9},{9,8},{10,11... | collective-permute-start | bytes 393224 | tf_op jit(solution)/shard_map/ppermute | solution.py:479
  27.0 6.4 %copy-start.14 = (bf16[128,1024]{1,0:T(8,128)(2,1)}, bf16[128,1024]{1,0:T(8,128)(2,1)S(1)}, u32[]{:S(2)}) copy-start(bf16[128,1024]{1,0:T(8,128)(2,1)S(1)} %get-tuple-element.36.refs_6_) | copy-start | bytes 786436
  27.0 6.4 %copy-start.12 = (bf16[64,1024]{1,0:T(8,128)(2,1)}, bf16[64,1024]{1,0:T(8,128)(2,1)S(1)}, u32[]{:S(2)}) copy-start(bf16[64,1024]{1,0:T(8,128)(2,1)S(1)} %collective-permute-done.refs_5_.refs_2_) | copy-start | bytes 393220
  33.4 0.8 copy-start.22
  34.2 6.3 %copy-start = (bf16[1024,1024]{1,0:T(8,128)(2,1)S(1)}, bf16[1024,1024]{1,0:T(8,128)(2,1)}, u32[]{:S(2)}) copy-start(bf16[1024,1024]{1,0:T(8,128)(2,1)} %refs_4_.5) | copy-start | bytes 6291460
  40.5 16.9 %copy-start.13 = (bf16[64,1024]{1,0:T(8,128)(2,1)S(1)}, bf16[64,1024]{1,0:T(8,128)(2,1)}, u32[]{:S(2)}) copy-start(bf16[64,1024]{1,0:T(8,128)(2,1)} %copy-done.12) | copy-start | bytes 393220
  40.5 16.8 %collective-permute-start.4 = (bf16[1024,1024]{1,0:T(8,128)(2,1)S(1)}, bf16[1024,1024]{1,0:T(8,128)(2,1)}, u32[]{:S(2)}, u32[]{:S(2)}) collective-permute-start(bf16[1024,1024]{1,0:T(8,128)(2,1)S(1)} %copy-done), channel_id=1, source_target_pairs={{0,1},{1,0},{2,3},{3,2},{4,5},{5,4},{6,7},{7,6},{8,9},{9,8},{10,11... | collective-permute-start | bytes 6291464 | tf_op jit(solution)/shard_map/ppermute | solution.py:479
  40.6 8.9 %collective-permute-start.6 = (bf16[128,1024]{1,0:T(8,128)(2,1)}, bf16[128,1024]{1,0:T(8,128)(2,1)S(1)}, u32[]{:S(2)}, u32[]{:S(2)}) collective-permute-start(bf16[128,1024]{1,0:T(8,128)(2,1)} %get-tuple-element.42), channel_id=1, source_target_pairs={{0,64},{16,80},{32,96},{48,112},{64,0},{80,16},{96,32},{112,48},{1... | collective-permute-start | bytes 786440 | tf_op jit(solution)/shard_map/ppermute | solution.py:403
  40.9 10.2 %collective-permute-start.5 = (bf16[128,1024]{1,0:T(8,128)(2,1)}, bf16[128,1024]{1,0:T(8,128)(2,1)S(1)}, u32[]{:S(2)}, u32[]{:S(2)}) collective-permute-start(bf16[128,1024]{1,0:T(8,128)(2,1)} %copy-done.14), channel_id=1, source_target_pairs={{0,32},{16,48},{32,0},{48,16},{64,96},{80,112},{96,64},{112,80},{1... | collective-permute-start | bytes 786440 | tf_op jit(solution)/shard_map/ppermute | solution.py:403
  44.3 13.1 %all-to-all-start.1 = ((bf16[16,8,1024]{2,1,0:T(8,128)(2,1)}), bf16[16,8,1024]{2,1,0:T(8,128)(2,1)S(1)}, u32[]{:S(2)}, u32[]{:S(2)}) async-start(bf16[16,8,1024]{2,1,0:T(8,128)(2,1)} %bitcast.10), calls=%async_computation.1 | async-start | bytes 524288 | tf_op jit(solution)/shard_map/all_to_all | solution.py:399
  49.5 7.8 %copy-start.8 = (bf16[128,1024]{1,0:T(8,128)(2,1)}, bf16[128,1024]{1,0:T(8,128)(2,1)S(1)}, u32[]{:S(2)}) copy-start(bf16[128,1024]{1,0:T(8,128)(2,1)S(1)} %collective-permute-done.6.refs_2_) | copy-start | bytes 786436
  51.1 7.4 %copy-start.10 = (bf16[128,1024]{1,0:T(8,128)(2,1)}, bf16[128,1024]{1,0:T(8,128)(2,1)S(1)}, u32[]{:S(2)}) copy-start(bf16[128,1024]{1,0:T(8,128)(2,1)S(1)} %collective-permute-done.5.refs_1_) | copy-start | bytes 786436
  51.1 1.0 copy-start.15
  57.3 0.9 copy-start.18
  58.5 0.7 copy-start.16
  59.1 0.6 copy-start.20
  59.8 7.7 %collective-permute-start.9 = (bf16[128,1024]{1,0:T(8,128)(2,1)S(1)}, bf16[128,1024]{1,0:T(8,128)(2,1)S(1)}, u32[]{:S(2)}, u32[]{:S(2)}) collective-permute-start(bf16[128,1024]{1,0:T(8,128)(2,1)S(1)} %get-tuple-element.44.refs_0_), channel_id=1, source_target_pairs={{0,48},{16,0},{32,16},{48,32},{64,112},{80,64},{96,80},{112,96},{1... | collective-permute-start | bytes 786440 | tf_op jit(solution)/shard_map/ppermute | solution.py:403
  60.5 8.6 %collective-permute-start.8 = (bf16[128,1024]{1,0:T(8,128)(2,1)S(1)}, bf16[128,1024]{1,0:T(8,128)(2,1)S(1)}, u32[]{:S(2)}, u32[]{:S(2)}) collective-permute-start(bf16[128,1024]{1,0:T(8,128)(2,1)S(1)} %get-tuple-element.44.refs_0_), channel_id=1, source_target_pairs={{0,16},{16,32},{32,48},{48,0},{64,80},{80,96},{96,112},{112,64},{1... | collective-permute-start | bytes 786440 | tf_op jit(solution)/shard_map/ppermute | solution.py:403
  61.8 7.3 %collective-permute-start.7 = (bf16[128,1024]{1,0:T(8,128)(2,1)S(1)}, bf16[128,1024]{1,0:T(8,128)(2,1)}, u32[]{:S(2)}, u32[]{:S(2)}) collective-permute-start(bf16[128,1024]{1,0:T(8,128)(2,1)S(1)} %get-tuple-element.44.refs_0_), channel_id=1, source_target_pairs={{0,64},{16,80},{32,96},{48,112},{64,0},{80,16},{96,32},{112,48},{1... | collective-permute-start | bytes 786440 | tf_op jit(solution)/shard_map/ppermute | solution.py:403
  67.5 6.8 %copy-start.4 = (bf16[128,1024]{1,0:T(8,128)(2,1)}, bf16[128,1024]{1,0:T(8,128)(2,1)S(1)}, u32[]{:S(2)}) copy-start(bf16[128,1024]{1,0:T(8,128)(2,1)S(1)} %collective-permute-done.9.refs_3_) | copy-start | bytes 786436
  69.1 5.2 %copy-start.6 = (bf16[128,1024]{1,0:T(8,128)(2,1)}, bf16[128,1024]{1,0:T(8,128)(2,1)S(1)}, u32[]{:S(2)}) copy-start(bf16[128,1024]{1,0:T(8,128)(2,1)S(1)} %collective-permute-done.8.refs_2_) | copy-start | bytes 786436
  74.3 15.7 %collective-permute-start.14 = (bf16[256,1024]{1,0:T(8,128)(2,1)}, bf16[256,1024]{1,0:T(8,128)(2,1)S(1)}, u32[]{:S(2)}, u32[]{:S(2)}) collective-permute-start(bf16[256,1024]{1,0:T(8,128)(2,1)} %get-tuple-element.45), channel_id=1, source_target_pairs={{0,1},{1,0},{2,3},{3,2},{4,5},{5,4},{6,7},{7,6},{8,9},{9,8},{10,11... | collective-permute-start | bytes 1572872 | tf_op jit(solution)/shard_map/ppermute | solution.py:479
  74.4 9.0 %collective-permute-start.11 = (bf16[128,1024]{1,0:T(8,128)(2,1)}, bf16[128,1024]{1,0:T(8,128)(2,1)}, u32[]{:S(2)}, u32[]{:S(2)}) collective-permute-start(bf16[128,1024]{1,0:T(8,128)(2,1)} %collective-permute-done.7.refs_1_), channel_id=1, source_target_pairs={{0,48},{16,0},{32,16},{48,32},{64,112},{80,64},{96,80},{112,96},{1... | collective-permute-start | bytes 786440 | tf_op jit(solution)/shard_map/ppermute | solution.py:403
  76.3 13.8 %all-to-all-start.2 = ((bf16[16,8,1024]{2,1,0:T(8,128)(2,1)}), bf16[16,8,1024]{2,1,0:T(8,128)(2,1)}, u32[]{:S(2)}, u32[]{:S(2)}) async-start(bf16[16,8,1024]{2,1,0:T(8,128)(2,1)} %bitcast.4), calls=%async_computation.2 | async-start | bytes 524288 | tf_op jit(solution)/shard_map/all_to_all | solution.py:399
  80.5 15.7 %collective-permute-start.12 = (bf16[128,1024]{1,0:T(8,128)(2,1)}, bf16[128,1024]{1,0:T(8,128)(2,1)}, u32[]{:S(2)}, u32[]{:S(2)}) collective-permute-start(bf16[128,1024]{1,0:T(8,128)(2,1)} %copy-done.6), channel_id=1, source_target_pairs={{0,16},{16,32},{32,48},{48,0},{64,80},{80,96},{96,112},{112,64},{1... | collective-permute-start | bytes 786440 | tf_op jit(solution)/shard_map/ppermute | solution.py:403
  80.8 15.4 %collective-permute-start.10 = (bf16[128,1024]{1,0:T(8,128)(2,1)}, bf16[128,1024]{1,0:T(8,128)(2,1)}, u32[]{:S(2)}, u32[]{:S(2)}) collective-permute-start(bf16[128,1024]{1,0:T(8,128)(2,1)} %collective-permute-done.7.refs_1_), channel_id=1, source_target_pairs={{0,16},{16,32},{32,48},{48,0},{64,80},{80,96},{96,112},{112,64},{1... | collective-permute-start | bytes 786440 | tf_op jit(solution)/shard_map/ppermute | solution.py:403
  83.4 12.8 %collective-permute-start.13 = (bf16[128,1024]{1,0:T(8,128)(2,1)}, bf16[128,1024]{1,0:T(8,128)(2,1)}, u32[]{:S(2)}, u32[]{:S(2)}) collective-permute-start(bf16[128,1024]{1,0:T(8,128)(2,1)} %collective-permute-done.11.refs_1_.refs_5_), channel_id=1, source_target_pairs={{0,48},{16,0},{32,16},{48,32},{64,112},{80,64},{96,80},{112,96},{1... | collective-permute-start | bytes 786440 | tf_op jit(solution)/shard_map/ppermute | solution.py:403
  90.0 0.8 copy-start.1
  96.1 5.2 %collective-permute-start.17 = (bf16[64,1024]{1,0:T(8,128)(2,1)}, bf16[64,1024]{1,0:T(8,128)(2,1)S(1)}, u32[]{:S(2)}, u32[]{:S(2)}) collective-permute-start(bf16[64,1024]{1,0:T(8,128)(2,1)} %get-tuple-element.53), channel_id=1, source_target_pairs={{0,1},{1,0},{2,3},{3,2},{4,5},{5,4},{6,7},{7,6},{8,9},{9,8},{10,11... | collective-permute-start | bytes 393224 | tf_op jit(solution)/shard_map/ppermute | solution.py:479
  96.2 5.1 %copy-start.19 = (bf16[64,1024]{1,0:T(8,128)(2,1)S(1)}, bf16[64,1024]{1,0:T(8,128)(2,1)}, u32[]{:S(2)}) copy-start(bf16[64,1024]{1,0:T(8,128)(2,1)} %get-tuple-element.52.keep_ref) | copy-start | bytes 393220
  101.3 7.7 %copy-start.21 = (bf16[64,1024]{1,0:T(8,128)(2,1)S(1)}, bf16[64,1024]{1,0:T(8,128)(2,1)}, u32[]{:S(2)}) copy-start(bf16[64,1024]{1,0:T(8,128)(2,1)} %copy-done.20) | copy-start | bytes 393220
  101.3 9.8 %copy-start.9 = (bf16[128,1024]{1,0:T(8,128)(2,1)S(1)}, bf16[128,1024]{1,0:T(8,128)(2,1)}, u32[]{:S(2)}) copy-start(bf16[128,1024]{1,0:T(8,128)(2,1)} %copy-done.8) | copy-start | bytes 786436
  101.3 9.8 %copy-start.11 = (bf16[128,1024]{1,0:T(8,128)(2,1)S(1)}, bf16[128,1024]{1,0:T(8,128)(2,1)}, u32[]{:S(2)}) copy-start(bf16[128,1024]{1,0:T(8,128)(2,1)} %copy-done.10) | copy-start | bytes 786436
  101.3 9.8 %copy-start.17 = (bf16[64,1024]{1,0:T(8,128)(2,1)S(1)}, bf16[64,1024]{1,0:T(8,128)(2,1)}, u32[]{:S(2)}) copy-start(bf16[64,1024]{1,0:T(8,128)(2,1)} %copy-done.16) | copy-start | bytes 393220
  102.1 10.2 %copy-start.2 = (bf16[256,1024]{1,0:T(8,128)(2,1)S(1)}, bf16[256,1024]{1,0:T(8,128)(2,1)}, u32[]{:S(2)}) copy-start(bf16[256,1024]{1,0:T(8,128)(2,1)} %copy-done.1) | copy-start | bytes 1572868
  102.1 10.2 %copy-start.5 = (bf16[128,1024]{1,0:T(8,128)(2,1)S(1)}, bf16[128,1024]{1,0:T(8,128)(2,1)}, u32[]{:S(2)}) copy-start(bf16[128,1024]{1,0:T(8,128)(2,1)} %copy-done.4) | copy-start | bytes 786436
  102.1 10.2 %copy-start.7 = (bf16[128,1024]{1,0:T(8,128)(2,1)S(1)}, bf16[128,1024]{1,0:T(8,128)(2,1)}, u32[]{:S(2)}) copy-start(bf16[128,1024]{1,0:T(8,128)(2,1)} %copy-done.6) | copy-start | bytes 786436
  102.1 26.5 %all-to-all-start.3 = ((bf16[8,80,1024]{2,1,0:T(8,128)(2,1)}), bf16[8,80,1024]{2,1,0:T(8,128)(2,1)}, u32[]{:S(2)}, u32[]{:S(2)}) async-start(bf16[8,80,1024]{2,1,0:T(8,128)(2,1)} %shard_map.158), calls=%async_computation.3 | async-start | bytes 2621440 | tf_op jit(solution)/shard_map/all_to_all | solution.py:560
  109.0 3.2 %collective-permute-start.15 = (bf16[256,1024]{1,0:T(8,128)(2,1)}, bf16[256,1024]{1,0:T(8,128)(2,1)S(1)}, u32[]{:S(2)}, u32[]{:S(2)}) collective-permute-start(bf16[256,1024]{1,0:T(8,128)(2,1)} %get-tuple-element.47), channel_id=1, source_target_pairs={{0,1},{1,0},{2,3},{3,2},{4,5},{5,4},{6,7},{7,6},{8,9},{9,8},{10,11... | collective-permute-start | bytes 1572872 | tf_op jit(solution)/shard_map/ppermute | solution.py:479
  109.0 2.1 %collective-permute-start.16 = (bf16[64,1024]{1,0:T(8,128)(2,1)S(1)}, bf16[64,1024]{1,0:T(8,128)(2,1)S(1)}, u32[]{:S(2)}, u32[]{:S(2)}) collective-permute-start(bf16[64,1024]{1,0:T(8,128)(2,1)S(1)} %copy-done.21), channel_id=1, source_target_pairs={{0,1},{1,0},{2,3},{3,2},{4,5},{5,4},{6,7},{7,6},{8,9},{9,8},{10,11... | collective-permute-start | bytes 393224 | tf_op jit(solution)/shard_map/ppermute | solution.py:479
  112.2 3.1 %copy-start.23 = (bf16[1024,1024]{1,0:T(8,128)(2,1)S(1)}, bf16[1024,1024]{1,0:T(8,128)(2,1)}, u32[]{:S(2)}) copy-start(bf16[1024,1024]{1,0:T(8,128)(2,1)} %refs_0_.4) | copy-start | bytes 6291460

commit v6 on v5

v6 whole, which is shorter than its diff:
```python
import functools
import math
import typing

import jax
import jax.numpy as jnp
import numpy as np
from jax import lax
from jax.experimental import pallas as pl
from jax.experimental.pallas import tpu as pltpu
from jax.sharding import PartitionSpec as P

ROW = 1024
FAC = 256
QF = 128
HALF = QF // 2 + 1
LANE_TILES = ROW // FAC
BF = jnp.bfloat16
F32 = jnp.float32
MIB = 1 << 20
MOST = 56


def angles(rows, cols, modulus):
    product = (rows[:, None].astype(np.int64) * cols[None, :]) % modulus
    return (product.astype(np.float32) * np.float32(2.0 * math.pi / modulus)).astype(np.float64)


def host_tables(ways, group):
    k2, t1 = np.arange(HALF), np.arange(FAC)
    t2 = (np.arange(LANE_TILES)[:, None] + LANE_TILES * np.arange(ways)[None, :]).reshape(-1)
    eye = np.eye(group)
    a = angles(k2, t2, QF)
    steps = np.stack([np.cos(a), -np.sin(a)])
    first = np.einsum("rkt,cd->rkctd", steps, eye).reshape(2 * HALF * group, t2.size * group)
    weight = np.where((k2 == 0) | (k2 == QF // 2), 1.0, 2.0) / (QF * FAC)
    b = angles(t2, k2, QF)
    back = np.concatenate([np.cos(b) * weight, (-np.sin(b) * weight)[:, 1:-1]], axis=1)
    last = np.einsum("tk,cd->tckd", back, eye).reshape(t2.size * group, -1)
    s = angles(t1, t1, FAC)
    square = np.concatenate([np.cos(s), np.sin(s)])
    w = angles(k2, t1, QF * FAC)
    twiddle = np.concatenate([np.repeat(f(w), group, axis=0) for f in (np.cos, np.sin)]).astype(np.float32)
    as_bf = lambda v: np.asarray(v, np.float32).astype(BF)
    return as_bf(first), as_bf(square), twiddle, as_bf(last)


def params(mib):
    return pltpu.CompilerParams(vmem_limit_bytes=mib * MIB)


VMEM = pl.BlockSpec(memory_space=pltpu.VMEM)
ANY = pl.BlockSpec(memory_space=pl.ANY)
DY_MOVES = ((0, 0), (0, 2), (1, 0), (1, 2), (0, 1), (1, 1), (0, -1), (1, -1))
SLOT = {move: i for i, (flip, step) in enumerate(DY_MOVES) for move in ((flip, step % 4),)}


def place(index, move):
    flip, step = move
    return ((index ^ 4) if flip else index) & 4 | ((index + step) & 3)


def dot(a, b):
    return jnp.dot(a, b, preferred_element_type=F32)


def my_core():
    return lax.axis_index("ctx") & 1


def rows_at(i, n):
    return pl.ds(pl.multiple_of(i * n, n), n)


def product_t(order, values):
    return lax.dot_general(order, values, (((1,), (1,)), ((), ())), preferred_element_type=F32)


def copy_all(copies):
    copies = list(copies)
    for copy in copies:
        copy.start()
    for copy in copies:
        copy.wait()


def iota(axis, n):
    return lax.broadcasted_iota(jnp.int32, (n, n), axis)


def order_in(ways, width):
    row, group = iota(0, width), width // ways
    r = group // 2
    channel = (row // r % 2) * (width // 2) + (row // group) * r + row % r
    return (channel == iota(1, width)).astype(F32).astype(BF)


def order_z(ways, width):
    row = lax.broadcasted_iota(jnp.int32, (width, 2 * width), 0)
    column = lax.broadcasted_iota(jnp.int32, (width, 2 * width), 1)
    r = width // ways // 2
    core = (row // (width // 2)) ^ my_core()
    slot = (row % (width // 2) // r) * 4 * r + core * r + row % r
    return (slot == column).astype(F32).astype(BF)


def dy_kernel(step, moves, w_hbm, d_hbm, *refs):
    outs, (w_ref, d_ref, p_ref, w_sem, d_sem, o_sem) = refs[:-6], refs[-6:]
    me = lax.axis_index("fsdp")
    n = outs[0].shape[0] // 2
    gather = [
        pltpu.make_async_copy(w_hbm.at[rows_at(place(me, move), n), :], w_ref.at[pl.ds(i * n, n), :], w_sem.at[i])
        for i, move in enumerate(moves)
    ]
    pieces = [pl.ds(i * step, step) for i in range(d_ref.shape[0] // step)]
    loads = [
        pltpu.make_async_copy(d_hbm.at[rows, :], d_ref.at[rows, :], d_sem.at[i]) for i, rows in enumerate(pieces)
    ]
    for copy in (*gather, loads[0]):
        copy.start()
    for copy in gather:
        copy.wait()
    stores = []
    for i, rows in enumerate(pieces):
        loads[i].wait()
        if i + 1 < len(pieces):
            loads[i + 1].start()
        p_ref[:, rows] = product_t(w_ref[...], d_ref[rows, :]).astype(BF)
        for j, out in enumerate(outs):
            store = pltpu.make_async_copy(
                p_ref.at[pl.ds(2 * n * j, 2 * n), rows], out.at[:, rows], o_sem.at[i * len(outs) + j]
            )
            store.start()
            stores.append(store)
    for store in stores:
        store.wait()


def prep_kernel(k_ref, v_ref, f_ref, send_ref):
    width = k_ref.shape[1]
    ways = send_ref.shape[0] // (2 * 8)
    order = order_in(ways, width)
    mixed = (k_ref[...].astype(F32) * v_ref[...].astype(F32)).astype(BF)
    parts = [product_t(order, x).reshape(ways, 1, -1, ROW) for x in (mixed, f_ref[...])]
    send_ref[...] = jnp.concatenate(parts, axis=1).reshape(send_ref.shape).astype(BF)


def turn_query_kernel(q_ref, mine_ref, away_ref, qt_ref):
    qt_ref[...] = q_ref[...].astype(F32).T
    core, n = my_core(), mine_ref.shape[0]
    mine_ref[...] = qt_ref[rows_at(core, n), :].astype(BF)
    away_ref[...] = qt_ref[rows_at(1 - core, n), :].astype(BF)


def gate_kernel(ways, z_ref, q_mine_ref, q_theirs_ref, gated_ref, z_away_ref):
    z = dot(order_z(ways, gated_ref.shape[0]), z_ref[...])
    n = z.shape[0] // 2
    z_away_ref[...] = z[n:].astype(BF)
    gated_ref[pl.ds(0, n), :] = (z[:n] * q_mine_ref[...].astype(F32)).astype(BF)
    gated_ref[pl.ds(n, n), :] = (z[n:] * q_theirs_ref[...].astype(F32)).astype(BF)


def sum_kernel(own_ref, x_ref, up_ref, down_ref, keep_ref, far_ref, side_ref):
    n = keep_ref.shape[0]
    near, second = pl.ds(0, n), pl.ds(n, n)
    own = own_ref[near, :].astype(F32) + x_ref[near, :].astype(F32)
    keep_ref[...] = own + (up_ref[near, :].astype(F32) + down_ref[near, :].astype(F32))
    far_ref[...] = (own_ref[second, :].astype(F32) + x_ref[second, :].astype(F32)).astype(BF)
    side_ref[...] = (up_ref[second, :].astype(F32) + down_ref[second, :].astype(F32)).astype(BF)


def dz_kernel(ways, keep_ref, far_ref, side_ref, q_ref, z_ref, send_ref):
    dy = keep_ref[...] + (far_ref[...].astype(F32) + side_ref[...].astype(F32))
    dz = (dy * q_ref[...].astype(F32).T).astype(BF)
    pieces = (z_ref[...].astype(F32), dot(order_in(ways, dz.shape[0]), dz))
    both = jnp.concatenate([x.reshape(ways, 1, -1, ROW) for x in pieces], axis=1)
    send_ref[...] = both.reshape(send_ref.shape).astype(BF)


def query_kernel(ways, keep_ref, far_ref, side_ref, z_ref, z_theirs_ref, gq_ref, gq_t_ref):
    gq_t_ref[...] = keep_ref[...] + (far_ref[...].astype(F32) + side_ref[...].astype(F32))
    core, n = my_core(), z_theirs_ref.shape[0]
    z_mine = dot(order_z(ways, gq_t_ref.shape[0])[:n], z_ref[...]).astype(BF)
    for z, half in ((z_mine, core), (z_theirs_ref[...], 1 - core)):
        own = rows_at(half, n)
        gq_t_ref[own, :] *= z.astype(F32)
    gq_ref[...] = gq_t_ref[...].T.astype(BF)


class Tables(typing.NamedTuple):
    first: typing.Any
    square: typing.Any
    twiddle: typing.Any
    last: typing.Any


def times_square(left, right, tables):
    square = tables.square
    return dot(left, square[:FAC]) + dot(right, square[FAC:])


def transform(x, tables):
    x = jnp.concatenate([x[:, u * FAC : (u + 1) * FAC] for u in range(LANE_TILES)], axis=0)
    section = dot(tables.first[...], x)
    n = section.shape[0] // 2
    twiddle = tables.twiddle
    re, im, tc, ts = section[:n], section[n:], twiddle[:n], twiddle[n:]
    b_re, b_im = re * tc + im * ts, im * tc - re * ts
    left = jnp.concatenate([b_re, b_im], axis=0).astype(BF)
    right = jnp.concatenate([b_im, -b_re], axis=0).astype(BF)
    f = times_square(left, right, tables)
    return f[:n], f[n:]


def signal(p_re, p_im, tables):
    n, group = p_re.shape[0], p_re.shape[0] // HALF
    left = jnp.concatenate([p_re, p_im], axis=0).astype(BF)
    right = jnp.concatenate([-p_im, p_re], axis=0).astype(BF)
    c = times_square(left, right, tables)
    twiddle = tables.twiddle
    re, im, tc, ts = c[:n], c[n:], twiddle[:n], twiddle[n:]
    e_re, e_im = re * tc - im * ts, im * tc + re * ts
    e = jnp.concatenate([e_re, e_im[group : n - group]], axis=0).astype(BF)
    x = dot(tables.last[...], e)
    rows = x.shape[0] // LANE_TILES
    return jnp.concatenate([x[u * rows : (u + 1) * rows] for u in range(LANE_TILES)], axis=1)


def conv_kernel(r_ref, first_ref, square_ref, twiddle_ref, last_ref, z_ref, h_ref):
    tables = Tables(first_ref, square_ref, twiddle_ref, last_ref)
    rows = z_ref.shape[0]
    group = h_ref.shape[0] // (2 * HALF)
    r = r_ref[...].astype(F32).reshape(-1, 2, group, ROW)
    u, h = (transform(r[:, s].reshape(rows, ROW).astype(BF), tables) for s in range(2))
    h_ref[...] = jnp.concatenate(h, axis=0).astype(BF)
    p_re, p_im = u[0] * h[0] - u[1] * h[1], u[0] * h[1] + u[1] * h[0]
    z_ref[...] = signal(p_re, p_im, tables).astype(BF)


def adjoint_kernel(r_ref, h_ref, first_ref, square_ref, twiddle_ref, last_ref, du_ref):
    tables = Tables(first_ref, square_ref, twiddle_ref, last_ref)
    rows = du_ref.shape[0]
    group = h_ref.shape[0] // (2 * HALF)
    r = r_ref[...].astype(F32).reshape(-1, 2, group, ROW)[:, 1]
    g_re, g_im = transform(r.reshape(rows, ROW).astype(BF), tables)
    h = h_ref[...].astype(F32)
    n = h.shape[0] // 2
    h_re, h_im = h[:n], h[n:]
    q_re, q_im = h_re * g_re + h_im * g_im, h_re * g_im - h_im * g_re
    du_ref[...] = signal(q_re, q_im, tables).astype(BF)


def weight_rows(scale, moves, blocks, d_ref, d_other_ref, away_ref, part_ref, loaded=()):
    me, ctx = lax.axis_index("fsdp"), lax.axis_index("ctx")
    n = blocks[0].shape[0] // 2
    mine = jnp.concatenate([block[:n] for block in blocks], axis=0)
    away = jnp.concatenate([block[n:] for block in blocks], axis=0)
    away_ref[...] = away
    p = dot(mine, d_ref[...]) + dot(away, d_other_ref[...])
    p = (p * scale).astype(BF)
    for load in loaded:
        load.wait()
    for i, move in enumerate(moves):
        to = place(me, move)
        flip, step = (to ^ (ctx // 2)) & 1, (to // 2 - ctx // 4) & 3
        slot = jnp.int32(0)
        for (f, d), at in SLOT.items():
            slot = jnp.where((flip == f) & (step == d), at, slot)
        part_ref[rows_at(slot, n), :] = p[i * n : (i + 1) * n]


def near_kernel(scale, moves, *refs):
    count = len(moves)
    blocks, (d_ref, d_other_ref, part_ref, away_ref) = refs[:count], refs[count:]
    weight_rows(scale, moves, blocks, d_ref, d_other_ref, away_ref, part_ref)


def far_kernel(scale, moves, *refs):
    count = len(moves)
    blocks, (d_ref, d_other_ref, near_hbm), refs = refs[:count], refs[count : count + 3], refs[count + 3 :]
    outs, away_ref, (part_ref, sem) = refs[:4], refs[4], refs[5:]
    near = pltpu.make_async_copy(near_hbm, part_ref, sem.at[4])
    near.start()
    weight_rows(scale, moves, blocks, d_ref, d_other_ref, away_ref, part_ref, [near])
    n = outs[0].shape[0]
    copy_all(pltpu.make_async_copy(part_ref.at[pl.ds(i * n, n), :], out, sem.at[i]) for i, out in enumerate(outs))


def assemble_kernel(*refs):
    blocks, theirs, (all_hbm, sem) = refs[:8], refs[8:10], refs[10:]
    me, core = lax.axis_index("fsdp"), my_core()
    n = blocks[0].shape[0] // 2
    copies = []
    for i, (block, move) in enumerate(zip(blocks, RING_FROM)):
        start = 2 * place(me, move)
        other = theirs[i // 4].at[pl.ds(i % 4 * n, n), :]
        for j, (x, half) in enumerate(((block.at[pl.ds(0, n), :], core), (other, 1 - core))):
            copies.append(pltpu.make_async_copy(x, all_hbm.at[rows_at(start + half, n), :], sem.at[2 * i + j]))
    copy_all(copies)


def key_value_kernel(ways, du_ref, k_ref, v_ref, gk_ref, gv_ref):
    du = dot(du_ref[...].astype(F32).T.astype(BF), order_in(ways, du_ref.shape[0]))
    gk_ref[...] = (du * v_ref[...].astype(F32)).astype(BF)
    gv_ref[...] = (du * k_ref[...].astype(F32)).astype(BF)


def final_kernel(keep_ref, far_ref, side_ref, gw_ref):
    gw_ref[...] = keep_ref[...] + (far_ref[...].astype(F32) + side_ref[...].astype(F32))


def staged(kernel, n_in, n_out, n_after, staged_in, staged_out):
    def run(*refs):
        ins, refs = list(refs[:n_in]), refs[n_in + n_after :]
        outs, refs = list(refs[:n_out]), refs[n_out:]
        extra = len(staged_in) + len(staged_out) + 2
        own, extra = refs[: len(refs) - extra], refs[len(refs) - extra :]
        buffers, (in_sem, out_sem) = extra[:-2], extra[-2:]
        loads, stores = [], []
        for j, i in enumerate(staged_in):
            loads.append(pltpu.make_async_copy(ins[i], buffers[j], in_sem.at[j]))
            ins[i] = buffers[j]
        for j, i in enumerate(staged_out):
            buffer = buffers[len(staged_in) + j]
            stores.append(pltpu.make_async_copy(buffer, outs[i], out_sem.at[j]))
            outs[i] = buffer
        copy_all(loads)
        kernel(*ins, *outs, *own)
        copy_all(stores)

    return run


def call(kernel, outs, ins, scratch=(), mib=16, flops=0, specs=None, after=(), staged_in=(), staged_out=(), aliases=None):
    total = sum(math.prod(o.shape) * o.dtype.itemsize for o in (*outs, *ins))
    if after or staged_in or staged_out:
        kernel = staged(kernel, len(ins), len(outs), len(after), staged_in, staged_out)
        buffers = [pltpu.VMEM(ins[i].shape, ins[i].dtype) for i in staged_in]
        buffers += [pltpu.VMEM(outs[i].shape, outs[i].dtype) for i in staged_out]
        sems = [pltpu.SemaphoreType.DMA((max(len(x), 1),)) for x in (staged_in, staged_out)]
        scratch = [*scratch, *buffers, *sems]
    in_specs, out_specs = specs or ([VMEM] * len(ins), [VMEM] * len(outs))
    in_specs = [ANY if i in staged_in else s for i, s in enumerate(in_specs)]
    out_specs = [ANY if i in staged_out else s for i, s in enumerate(out_specs)]
    return pl.pallas_call(
        kernel,
        out_shape=outs,
        in_specs=[*in_specs, *([ANY] * len(after))],
        out_specs=out_specs,
        scratch_shapes=scratch,
        input_output_aliases=aliases or {},
        compiler_params=params(mib),
        cost_estimate=pl.CostEstimate(flops=0, bytes_accessed=0, transcendentals=0),
    )(*ins, *after)


def shape(*dims, dtype=BF):
    return jax.ShapeDtypeStruct(dims, dtype)


def spread(values):
    return lax.all_to_all(values, "ctx", 0, 0, tiled=True)


def move_over(values, move):
    return lax.ppermute(values, "fsdp", [(i, place(i, move)) for i in range(8)])


RING_FROM = ((0, 0), (1, 0), (0, -1), (0, 1), (1, -1), (1, 1), (0, 2), (1, 2))


def ring_first(gated):
    return move_over(gated, (1, 0)), move_over(gated, (0, 1)), move_over(gated, (0, -1))


def ring_rest(gated, other, own_up, own_down):
    other_up, other_down = move_over(other, (0, 1)), move_over(other, (0, -1))
    own_far, other_far = move_over(own_up, (0, 1)), move_over(other_down, (0, -1))
    return gated, other, own_up, own_down, other_up, other_down, own_far, other_far


def dy_product(w_out, d_out, moves, mib=MOST, after=()):
    channels, depth = w_out.shape
    rows = d_out.shape[0]
    step = 512
    pieces = rows // step
    count = len(moves)
    n = channels // 8
    return call(
        functools.partial(dy_kernel, step, moves),
        [shape(2 * n, rows)] * (count // 2),
        [w_out, d_out],
        [
            pltpu.VMEM((count * n, depth), BF),
            pltpu.VMEM((rows, depth), BF),
            pltpu.VMEM((count * n, rows), BF),
            pltpu.SemaphoreType.DMA((count,)),
            pltpu.SemaphoreType.DMA((pieces,)),
            pltpu.SemaphoreType.DMA((count // 2 * pieces,)),
        ],
        mib=mib,
        flops=2 * count * n * depth * rows,
        specs=([ANY] * 2, [ANY] * (count // 2)),
        after=after,
    )


def weight_product(blocks, moves, d_out, d_other, scale, after, near=()):
    rows, columns = d_out.shape
    n = blocks[0].shape[0] // 2
    count = len(moves)
    all_rows = 8 * n
    outs = [shape(all_rows // 4, columns)] * 4 if near else [shape(all_rows, columns)]
    ins = [*blocks, d_out, d_other]
    return call(
        functools.partial(far_kernel if near else near_kernel, scale, moves),
        [*outs, shape(count * n, rows)],
        [*ins, *near],
        [pltpu.VMEM((all_rows, columns), BF), pltpu.SemaphoreType.DMA((5,))] if near else [],
        flops=4 * count * n * rows * columns,
        specs=([VMEM] * len(ins) + [ANY] * len(near), [ANY if near else VMEM] * len(outs) + [VMEM]),
        after=after,
    )


def on_device(query_in, key_in, value_in, filt, w_out, d_out):
    seq_rows, width = query_in.shape
    channels, columns = w_out.shape
    ways = lax.axis_size("ctx")
    group, half = width // ways, width // 2
    n = HALF * group
    *tables, last = host_tables(ways, group)
    slots = np.arange(ways * group).reshape(ways // 2, 2, 2, group // 2)
    pick = lambda rows: last.reshape(LANE_TILES, ways * group, -1)[:, rows.reshape(-1)].reshape(last.shape)
    last_z = pick(slots.transpose(0, 2, 1, 3))

    swap = lambda v: lax.ppermute(v, "ctx", [(i, i ^ 1) for i in range(ways)])
    rows_like, half_like = shape(width, seq_rows), shape(half, seq_rows)

    x_y, up_y, down_y = dy_product(w_out, d_out, DY_MOVES[2:])
    (own_y,) = dy_product(w_out, d_out, DY_MOVES[:2], mib=16, after=[x_y])
    keep_y, far_y, side_y = call(
        sum_kernel,
        [shape(width, seq_rows, dtype=F32), rows_like, rows_like],
        [own_y, move_over(x_y, (1, 0)), move_over(up_y, (0, 1)), move_over(down_y, (0, -1))],
    )
    (send,) = call(
        prep_kernel,
        [shape(ways * 2 * group, seq_rows)],
        [key_in, value_in, filt],
        mib=MOST,
        after=[x_y],
        staged_in=(0, 1, 2),
        staged_out=(0,),
    )
    arrived = spread(send)

    flops = 2 * 2 * n * (tables[0].shape[1] + 2 * FAC) * FAC
    conv, spectrum = call(
        conv_kernel,
        [rows_like, shape(2 * n, FAC)],
        [arrived, *tables, last_z],
        mib=20,
        flops=3 * flops,
        after=[far_y],
        staged_out=(0,),
    )
    dy = (keep_y, move_over(far_y, (0, 2)), move_over(side_y, (1, 0)))
    (send,) = call(
        functools.partial(dz_kernel, ways), [shape(2 * width, seq_rows)], [*dy, query_in, conv], staged_out=(0,)
    )
    q_mine, q_away = call(
        turn_query_kernel,
        [half_like, half_like],
        [query_in],
        [pltpu.VMEM((width, seq_rows), F32)],
        after=[send],
    )
    q_theirs = swap(q_away)
    send, d_late = lax.optimization_barrier((send, d_out))
    d_other = swap(d_late)
    arrived = spread(send)
    gated, z_away = call(
        functools.partial(gate_kernel, ways),
        [rows_like, half_like],
        [arrived, q_mine, q_theirs],
        after=[d_other],
    )
    z_theirs = swap(z_away)
    other, own_up, own_down = ring_first(gated)
    like = shape(seq_rows, width)
    (grad_query,) = call(
        functools.partial(query_kernel, ways),
        [like],
        [*dy, arrived, z_theirs],
        [pltpu.VMEM((width, seq_rows), F32)],
        staged_out=(0,),
    )
    (adjoint,) = call(
        adjoint_kernel, [rows_like], [arrived, spectrum, *tables, last], mib=20, flops=2 * flops, staged_out=(0,)
    )
    other, adjoint = lax.optimization_barrier((other, adjoint))
    blocks = ring_rest(gated, other, own_up, own_down)
    grad_u = spread(adjoint)
    grad_key, grad_value = call(
        functools.partial(key_value_kernel, ways),
        [like, like],
        [grad_u, key_in, value_in],
        mib=MOST,
        staged_in=(0, 1, 2),
        staged_out=(0, 1),
    )

    weight = functools.partial(weight_product, d_out=d_out, d_other=d_other, scale=1.0 / math.sqrt(seq_rows * ways))
    near, away = weight(blocks[:4], RING_FROM[:4], after=[])
    theirs_near = swap(away)
    own_w, x_w, up_w, down_w, away = weight(blocks[4:], RING_FROM[4:], after=[grad_u], near=(near,))
    over_x = lambda v: lax.ppermute(v, "ctx", [(i, i ^ 2) for i in range(ways)])
    along_y = lambda v, step: lax.ppermute(v, "ctx", [(i, (i + 4 * step) % ways) for i in range(ways)])
    part_rows = shape(channels // ways, columns)
    keep_w, far_w, side_w = call(
        sum_kernel,
        [shape(channels // ways, columns, dtype=F32), part_rows, part_rows],
        [own_w, over_x(x_w), along_y(up_w, 1), along_y(down_w, -1)],
    )
    far_w, side_w = along_y(far_w, 2), over_x(side_w)

    (gated_all,) = call(
        assemble_kernel,
        [shape(channels, seq_rows)],
        [*blocks, theirs_near, swap(away)],
        [pltpu.SemaphoreType.DMA((16,))],
        specs=([ANY] * 10, [ANY]),
    )
    layer_out = lax.dot_general(
        gated_all, w_out, (((0,), (0,)), ((), ())), preferred_element_type=F32
    ).astype(BF)

    (grad_weight,) = call(
        final_kernel,
        [shape(channels // ways, columns, dtype=F32)],
        [keep_w, far_w, side_w],
        after=[layer_out, grad_query, grad_key],
    )
    return (layer_out, grad_query, grad_key, grad_value, grad_weight)


def solution(mesh):
    both = P("ctx", "fsdp")
    return jax.shard_map(
        on_device,
        mesh=mesh,
        in_specs=(both, both, both, both, P(None, "fsdp"), both),
        out_specs=(both, both, both, both, both),
        check_vma=False,
    )
```

time: 133 us -> 121 us (0.910)
  waiting for transfers between devices: 38.5 us -> 30.3 us
  Pallas kernels: 41.3 us -> 34.9 us
  local copies, waits for them, and re-layouts: 4.92 us -> 11.3 us
  starting transfers between devices: 41.9 us -> 39.1 us
  matrix products: 3.75 us -> 2.39 us
    all_to_all x1 -> x0, waiting for transfers between devices: 9.57 us -> none  [on_device(): lax.all_to_all(pack, 'ctx', 0, 0, tiled=True, axis_index_groups=groups)]
    ppermute x0 -> x5, starting transfers between devices: none -> 7.33 us  [the longest x3 3.81 us: on_device(): lax.ppermute(v, 'ctx', [(i, (i + 4 * step) % ways) for i in range(ways)])]
    all_to_all x1 -> x0, starting transfers between devices: 6.9 us -> none  [on_device(): lax.all_to_all(pack, 'ctx', 0, 0, tiled=True, axis_index_groups=groups)]
    unnamed x48 -> x56, local copies, waits for them, and re-layouts: 4.92 us -> 11.3 us
    pallas_call x14 -> x16, Pallas kernels: 41.3 us -> 34.9 us  [call(): pl.pallas_call(kernel, out_shape=outs, in_specs=[*in_specs, *[ANY] * len(...]
    ppermute x12, waiting for transfers between devices: 13.3 us -> 7.84 us  [move_over(): return lax.ppermute(values, 'fsdp', [(i, place(i, move)) for i in range(8)])]
    all_to_all x3, waiting for transfers between devices: 14.1 us -> 18.9 us  [spread(): return lax.all_to_all(values, 'ctx', 0, 0, tiled=True)]
    ppermute x12, starting transfers between devices: 19.3 us -> 16.3 us  [move_over(): return lax.ppermute(values, 'fsdp', [(i, place(i, move)) for i in range(8)])]
  transfers between devices with their start and end apart: 22 -> 25, of which waited for: 11 -> 12; matrix products, arithmetic and copies ran while one was open for 3% -> 2% of each run, Pallas kernels for 14% -> 22%
where the time goes in v6:
time: 121 us; the launch traced here: 119 us
  starting transfers between devices  39.1 us (32%)
  Pallas kernels  34.9 us (29%)
  waiting for transfers between devices  30.3 us (25%)
  local copies, waits for them, and re-layouts  11.3 us (9%)
  matrix products  2.39 us (2%)
    pallas_call x16, Pallas kernels, call(): pl.pallas_call(kernel, out_shape=outs, in_specs=[*in_specs, *[ANY] * len(...  34.9 us
    all_to_all x3, waiting for transfers between devices, spread(): return lax.all_to_all(values, 'ctx', 0, 0, tiled=True)  18.9 us
    ppermute x12, starting transfers between devices, move_over(): return lax.ppermute(values, 'fsdp', [(i, place(i, move)) for i in range(8)])  16.3 us
    all_to_all x3, starting transfers between devices, spread(): return lax.all_to_all(values, 'ctx', 0, 0, tiled=True)  14 us
    unnamed x56, local copies, waits for them, and re-layouts  11.3 us
    ppermute x12, waiting for transfers between devices, move_over(): return lax.ppermute(values, 'fsdp', [(i, place(i, move)) for i in range(8)])  7.84 us
    ppermute x3, starting transfers between devices, on_device(): lax.ppermute(v, 'ctx', [(i, (i + 4 * step) % ways) for i in range(ways)])  3.81 us
    ppermute x2, starting transfers between devices, on_device(): over_x = lambda v: lax.ppermute(v, 'ctx', [(i, i ^ 2) for i in range(ways)])  3.52 us
  transfers between devices with their start and end apart: 25, of which 12 were waited for; matrix products, arithmetic and copies ran while one was open for 2% of the time, Pallas kernels for 22%

profile of v6, /device:TPU:0, one launch (start us, length us, event | category | flops | bytes accessed | tf_op | source)
XLA Modules:
  0.0 119.2 jit_solution(309745360774263913)
XLA Ops:
  0.6 5.0 %shard_map.146 = (bf16[256,1024]{1,0:T(8,128)(2,1)}, bf16[256,1024]{1,0:T(8,128)(2,1)}, bf16[256,1024]{1,0:T(8,128)(2,1)}) custom-call(bf16[1024,1024]{1,0:T(8,128)(2,1)} %refs_0_.3, bf16[1024,1024]{1,0:T(8,128)(2,1)} %refs_4_.5), custom_call_target="tpu_custom_call" | custom-call | tf_op jit(solution)/shard_map/pallas_call | solution.py:345
  5.7 2.1 %collective-permute-start.1 = (bf16[256,1024]{1,0:T(8,128)(2,1)}, bf16[256,1024]{1,0:T(8,128)(2,1)}, u32[]{:S(2)}, u32[]{:S(2)}) collective-permute-start(bf16[256,1024]{1,0:T(8,128)(2,1)} %get-tuple-element.34), channel_id=1, source_target_pairs={{0,16},{16,32},{32,48},{48,0},{64,80},{80,96},{96,112},{112,64},{1... | collective-permute-start | bytes 1572872 | tf_op jit(solution)/shard_map/ppermute | solution.py:366
  7.7 2.2 %collective-permute-start.2 = (bf16[256,1024]{1,0:T(8,128)(2,1)}, bf16[256,1024]{1,0:T(8,128)(2,1)}, u32[]{:S(2)}, u32[]{:S(2)}) collective-permute-start(bf16[256,1024]{1,0:T(8,128)(2,1)} %get-tuple-element.35), channel_id=1, source_target_pairs={{0,48},{16,0},{32,16},{48,32},{64,112},{80,64},{96,80},{112,96},{1... | collective-permute-start | bytes 1572872 | tf_op jit(solution)/shard_map/ppermute | solution.py:366
  9.9 1.5 %collective-permute-start = (bf16[256,1024]{1,0:T(8,128)(2,1)}, bf16[256,1024]{1,0:T(8,128)(2,1)}, u32[]{:S(2)}, u32[]{:S(2)}) collective-permute-start(bf16[256,1024]{1,0:T(8,128)(2,1)} %get-tuple-element.33.refs_2_.refs_3_), channel_id=1, source_target_pairs={{0,64},{16,80},{32,96},{48,112},{64,0},{80,16},{96,32},{112,48},{1... | collective-permute-start | bytes 1572872 | tf_op jit(solution)/shard_map/ppermute | solution.py:366
  11.4 2.3 %shard_map.149 = bf16[256,1024]{1,0:T(8,128)(2,1)} custom-call(bf16[1024,128]{1,0:T(8,128)(2,1)} %refs_1_.6, bf16[1024,128]{1,0:T(8,128)(2,1)} %refs_2_.5, bf16[1024,128]{1,0:T(8,128)(2,1)} %refs_2_.4, bf16[256,1024]{1,0:T(8,128)(2,1)} %get-tuple-element.33.refs_2_.refs_3_), custom_call_target="tpu_custom_call" | custom-call | tf_op jit(solution)/shard_map/pallas_call | solution.py:345
  13.7 6.8 %all-to-all-start = ((bf16[16,16,1024]{2,1,0:T(8,128)(2,1)}), bf16[16,16,1024]{2,1,0:T(8,128)(2,1)}, u32[]{:S(2)}, u32[]{:S(2)}) async-start(bf16[16,16,1024]{2,1,0:T(8,128)(2,1)} %bitcast.14), calls=%async_computation | async-start | bytes 1048576 | tf_op jit(solution)/shard_map/all_to_all | solution.py:362
  20.6 1.6 %copy-done.1 = bf16[1024,1024]{1,0:T(8,128)(2,1)S(1)} copy-done((bf16[1024,1024]{1,0:T(8,128)(2,1)S(1)}, bf16[1024,1024]{1,0:T(8,128)(2,1)}, u32[]{:S(2)}) %copy-start.1) | copy-done | bytes 2097176
  22.1 1.2 %shard_map.147.own_ref = bf16[256,1024]{1,0:T(8,128)(2,1)S(1)} custom-call(bf16[1024,1024]{1,0:T(8,128)(2,1)S(1)} %copy-done.1, bf16[1024,1024]{1,0:T(8,128)(2,1)S(1)} %copy-done, bf16[256,1024]{1,0:T(8,128)(2,1)S(1)} %copy-done.8), custom_call_target="tpu_custom_call" | custom-call | tf_op jit(solution)/shard_map/pallas_call | solution.py:345
  23.4 1.5 %collective-permute-done.x_ref = bf16[256,1024]{1,0:T(8,128)(2,1)} collective-permute-done((bf16[256,1024]{1,0:T(8,128)(2,1)}, bf16[256,1024]{1,0:T(8,128)(2,1)}, u32[]{:S(2)}, u32[]{:S(2)}) %collective-permute-start) | collective-permute-done | bytes 524320 | tf_op jit(solution)/shard_map/ppermute | solution.py:366
  24.9 2.2 %shard_map.148 = (f32[128,1024]{1,0:T(8,128)S(1)}, bf16[128,1024]{1,0:T(8,128)(2,1)}, bf16[128,1024]{1,0:T(8,128)(2,1)}) custom-call(bf16[256,1024]{1,0:T(8,128)(2,1)S(1)} %shard_map.147.own_ref, bf16[256,1024]{1,0:T(8,128)(2,1)} %collective-permute-done.x_ref, bf16[256,1024]{1,0:T(8,128)(2,1)} %collective-permute-done.1.up_ref, ...), custom_call_target="tpu_custom_call" | custom-call | tf_op jit(solution)/shard_map/pallas_call | solution.py:345
  27.1 0.8 copy-done.10
  27.9 1.2 %collective-permute-start.4 = (bf16[128,1024]{1,0:T(8,128)(2,1)}, bf16[128,1024]{1,0:T(8,128)(2,1)}, u32[]{:S(2)}, u32[]{:S(2)}) collective-permute-start(bf16[128,1024]{1,0:T(8,128)(2,1)} %get-tuple-element.38), channel_id=1, source_target_pairs={{0,64},{16,80},{32,96},{48,112},{64,0},{80,16},{96,32},{112,48},{1... | collective-permute-start | bytes 786440 | tf_op jit(solution)/shard_map/ppermute | solution.py:366
  29.1 1.2 %collective-permute-start.3 = (bf16[128,1024]{1,0:T(8,128)(2,1)}, bf16[128,1024]{1,0:T(8,128)(2,1)}, u32[]{:S(2)}, u32[]{:S(2)}) collective-permute-start(bf16[128,1024]{1,0:T(8,128)(2,1)} %get-tuple-element.37.refs_5_), channel_id=1, source_target_pairs={{0,32},{16,48},{32,0},{48,16},{64,96},{80,112},{96,64},{112,80},{1... | collective-permute-start | bytes 786440 | tf_op jit(solution)/shard_map/ppermute | solution.py:366
  30.3 3.6 %all-to-all-done = bf16[16,16,1024]{2,1,0:T(8,128)(2,1)} async-done(((bf16[16,16,1024]{2,1,0:T(8,128)(2,1)}), bf16[16,16,1024]{2,1,0:T(8,128)(2,1)}, u32[]{:S(2)}, u32[]{:S(2)}) %all-to-all-start) | async-done | bytes 524320 | tf_op jit(solution)/shard_map/all_to_all | solution.py:362
  33.9 1.2 %copy-done.5 = bf16[1040,512]{1,0:T(8,128)(2,1)S(1)} copy-done((bf16[1040,512]{1,0:T(8,128)(2,1)S(1)}, bf16[1040,512]{1,0:T(8,128)(2,1)}, u32[]{:S(2)}) %copy-start.5) | copy-done | bytes 1064984
  35.1 1.2 %copy-done.19 = bf16[512,1024]{1,0:T(8,128)(2,1)S(1)} copy-done((bf16[512,1024]{1,0:T(8,128)(2,1)S(1)}, bf16[512,1024]{1,0:T(8,128)(2,1)}, u32[]{:S(2)}) %copy-start.19) | copy-done | bytes 1048600
  36.4 4.2 %shard_map.150 = (bf16[128,1024]{1,0:T(8,128)(2,1)S(1)}, bf16[1040,256]{1,0:T(8,128)(2,1)S(1)}) custom-call(bf16[256,1024]{1,0:T(8,128)(2,1)} %bitcast.1.refs_0_, bf16[1040,512]{1,0:T(8,128)(2,1)S(1)} %copy-done.5, bf16[512,256]{1,0:T(8,128)(2,1)S(1)} %copy-done.15, f32[1040,256]{1,0:T(8,128)S(1)} %copy-done.3, bf16[512,1024]{1,0:T(8,128)(2,1)S(1)} %copy-done.19, ...), custom_call_target="tpu_custom_call" | custom-call | tf_op jit(solution)/shard_map/pallas_call | solution.py:345
  40.6 2.4 %shard_map.151.refs_1_ = bf16[256,1024]{1,0:T(8,128)(2,1)} custom-call(f32[128,1024]{1,0:T(8,128)S(1)} %copy-done.11, bf16[128,1024]{1,0:T(8,128)(2,1)} %collective-permute-done.3.refs_1_, bf16[128,1024]{1,0:T(8,128)(2,1)} %collective-permute-done.4.refs_2_, bf16[1024,128]{1,0:T(8,128)(2,1)S(1)} %copy-done.20, bf16[128,1024]{1,0:T(8,128)(2,1)S(1)} %get-tuple-element.39.refs_4_), custom_call_target="tpu_custom_call" | custom-call | tf_op jit(solution)/shard_map/pallas_call | solution.py:345
  43.1 0.1 collective-permute-start.6
  43.2 3.7 %all-to-all-start.1 = ((bf16[16,16,1024]{2,1,0:T(8,128)(2,1)}), bf16[16,16,1024]{2,1,0:T(8,128)(2,1)S(1)}, u32[]{:S(2)}, u32[]{:S(2)}) async-start(bf16[16,16,1024]{2,1,0:T(8,128)(2,1)} %bitcast.2), calls=%async_computation.1 | async-start | bytes 1048576 | tf_op jit(solution)/shard_map/all_to_all | solution.py:362
  46.9 0.2 shard_map.152
  47.1 0.5 collective-permute-start.5
  47.6 1.0 collective-permute-done.5.refs_2_
  48.6 10.6 %all-to-all-done.1 = bf16[16,16,1024]{2,1,0:T(8,128)(2,1)S(1)} async-done(((bf16[16,16,1024]{2,1,0:T(8,128)(2,1)}), bf16[16,16,1024]{2,1,0:T(8,128)(2,1)S(1)}, u32[]{:S(2)}, u32[]{:S(2)}) %all-to-all-start.1) | async-done | bytes 524320 | tf_op jit(solution)/shard_map/all_to_all | solution.py:362
  59.2 0.3 shard_map.153
  59.5 0.6 copy-done.26
  60.2 0.6 collective-permute-start.7
  60.8 0.1 copy-done.6
  60.8 1.2 %copy-done.18 = bf16[512,1024]{1,0:T(8,128)(2,1)S(1)} copy-done((bf16[512,1024]{1,0:T(8,128)(2,1)S(1)}, bf16[512,1024]{1,0:T(8,128)(2,1)}, u32[]{:S(2)}) %copy-start.18) | copy-done | bytes 1048600
  62.1 1.0 copy-done.24
  63.1 2.5 %shard_map.154 = bf16[128,1024]{1,0:T(8,128)(2,1)S(1)} custom-call(bf16[256,1024]{1,0:T(8,128)(2,1)S(1)} %bitcast.9, bf16[1040,256]{1,0:T(8,128)(2,1)S(1)} %copy-done.24, bf16[1040,512]{1,0:T(8,128)(2,1)S(1)} %copy-done.6, bf16[512,256]{1,0:T(8,128)(2,1)S(1)} %copy-done.16, f32[1040,256]{1,0:T(8,128)S(1)} %copy-done.4, bf16[512,1024]{1,0:T(8,128)(2,1)S(1)} %copy-done.18), custom_call_target="tpu_custom_call" | custom-call | tf_op jit(solution)/shard_map/pallas_call | solution.py:345
  65.6 0.7 copy-done.17
  66.3 0.4 collective-permute-start.8
  66.8 0.9 collective-permute-done.7.refs_1_
  67.7 1.9 %collective-permute-start.11 = (bf16[128,1024]{1,0:T(8,128)(2,1)S(1)}, bf16[128,1024]{1,0:T(8,128)(2,1)}, u32[]{:S(2)}, u32[]{:S(2)}) collective-permute-start(bf16[128,1024]{1,0:T(8,128)(2,1)S(1)} %collective-permute-done.7.refs_1_), channel_id=1, source_target_pairs={{0,48},{16,0},{32,16},{48,32},{64,112},{80,64},{96,80},{112,96},{1... | collective-permute-start | bytes 786440 | tf_op jit(solution)/shard_map/ppermute | solution.py:366
  69.6 0.7 collective-permute-start.9
  70.3 1.4 %collective-permute-start.10 = (bf16[128,1024]{1,0:T(8,128)(2,1)S(1)}, bf16[128,1024]{1,0:T(8,128)(2,1)}, u32[]{:S(2)}, u32[]{:S(2)}) collective-permute-start(bf16[128,1024]{1,0:T(8,128)(2,1)S(1)} %collective-permute-done.7.refs_1_), channel_id=1, source_target_pairs={{0,16},{16,32},{32,48},{48,0},{64,80},{80,96},{96,112},{112,64},{1... | collective-permute-start | bytes 786440 | tf_op jit(solution)/shard_map/ppermute | solution.py:366
  71.7 5.2 %collective-permute-done.8.refs_2_ = bf16[128,1024]{1,0:T(8,128)(2,1)} collective-permute-done((bf16[128,1024]{1,0:T(8,128)(2,1)S(1)}, bf16[128,1024]{1,0:T(8,128)(2,1)}, u32[]{:S(2)}, u32[]{:S(2)}) %collective-permute-start.8) | collective-permute-done | bytes 262176 | tf_op jit(solution)/shard_map/ppermute | solution.py:366
  76.9 0.2 collective-permute-done.11.refs_1_.refs_5_
  77.1 3.2 %collective-permute-start.13 = (bf16[128,1024]{1,0:T(8,128)(2,1)}, bf16[128,1024]{1,0:T(8,128)(2,1)}, u32[]{:S(2)}, u32[]{:S(2)}) collective-permute-start(bf16[128,1024]{1,0:T(8,128)(2,1)} %collective-permute-done.11.refs_1_.refs_5_), channel_id=1, source_target_pairs={{0,48},{16,0},{32,16},{48,32},{64,112},{80,64},{96,80},{112,96},{1... | collective-permute-start | bytes 786440 | tf_op jit(solution)/shard_map/ppermute | solution.py:366
  80.2 3.5 %all-to-all-start.2 = ((bf16[16,8,1024]{2,1,0:T(8,128)(2,1)}), bf16[16,8,1024]{2,1,0:T(8,128)(2,1)S(1)}, u32[]{:S(2)}, u32[]{:S(2)}) async-start(bf16[16,8,1024]{2,1,0:T(8,128)(2,1)} %bitcast.13), calls=%async_computation.2 | async-start | bytes 524288 | tf_op jit(solution)/shard_map/all_to_all | solution.py:362
  83.8 3.6 %shard_map.155 = (bf16[512,1024]{1,0:T(8,128)(2,1)S(1)}, bf16[256,1024]{1,0:T(8,128)(2,1)}) custom-call(bf16[128,1024]{1,0:T(8,128)(2,1)S(1)} %get-tuple-element.44.refs_0_, bf16[128,1024]{1,0:T(8,128)(2,1)S(1)} %collective-permute-done.7.refs_1_, bf16[128,1024]{1,0:T(8,128)(2,1)} %collective-permute-done.8.refs_2_, ...), custom_call_target="tpu_custom_call" | custom-call | tf_op jit(solution)/shard_map/pallas_call | solution.py:345
  87.4 1.0 copy-done.13
  88.3 0.3 collective-permute-start.14
  88.6 4.7 %all-to-all-done.2 = bf16[16,8,1024]{2,1,0:T(8,128)(2,1)S(1)} async-done(((bf16[16,8,1024]{2,1,0:T(8,128)(2,1)}), bf16[16,8,1024]{2,1,0:T(8,128)(2,1)S(1)}, u32[]{:S(2)}, u32[]{:S(2)}) %all-to-all-start.2) | async-done | bytes 262176 | tf_op jit(solution)/shard_map/all_to_all | solution.py:362
  93.3 1.3 %copy-done.14 = bf16[512,1024]{1,0:T(8,128)(2,1)S(1)} copy-done((bf16[512,1024]{1,0:T(8,128)(2,1)S(1)}, bf16[512,1024]{1,0:T(8,128)(2,1)}, u32[]{:S(2)}) %copy-start.14) | copy-done | bytes 1048600
  94.6 3.5 %shard_map.156 = (bf16[128,1024]{1,0:T(8,128)(2,1)S(1)}, bf16[128,1024]{1,0:T(8,128)(2,1)S(1)}, bf16[128,1024]{1,0:T(8,128)(2,1)S(1)}, bf16[128,1024]{1,0:T(8,128)(2,1)S(1)}, bf16[256,1024]{1,0:T(8,128)(2,1)S(1)}) custom-call(bf16[128,1024]{1,0:T(8,128)(2,1)} %collective-permute-done.10.refs_0_.refs_4_, ...), custom_call_target="tpu_custom_call" | custom-call | tf_op jit(solution)/shard_map/pallas_call | solution.py:345
  98.2 0.1 collective-permute-start.15
  98.3 0.5 collective-permute-start.16
  98.8 0.6 collective-permute-start.17
  99.4 0.9 collective-permute-done.16.refs_4_
  100.3 2.3 %collective-permute-start.19 = (bf16[128,1024]{1,0:T(8,128)(2,1)S(1)}, bf16[128,1024]{1,0:T(8,128)(2,1)S(1)}, u32[]{:S(2)}, u32[]{:S(2)}) collective-permute-start(bf16[128,1024]{1,0:T(8,128)(2,1)S(1)} %get-tuple-element.57), channel_id=1, source_target_pairs={{0,12},{1,13},{2,14},{3,15},{4,0},{5,1},{6,2},{7,3},{8,4},{9,5},{1... | collective-permute-start | bytes 786440 | tf_op jit(solution)/shard_map/ppermute | solution.py:519
  102.6 2.1 %shard_map.158.refs_4_ = bf16[1024,128]{1,0:T(8,128)(2,1)} custom-call(f32[128,1024]{1,0:T(8,128)S(1)} %copy-done.12, bf16[128,1024]{1,0:T(8,128)(2,1)} %collective-permute-done.3.refs_1_, bf16[128,1024]{1,0:T(8,128)(2,1)} %collective-permute-done.4.refs_2_, bf16[256,1024]{1,0:T(8,128)(2,1)S(1)} %bitcast.10, bf16[64,1024]{1,0:T(8,128)(2,1)S(1)} %collective-permute-done.16.refs_4_), custom_call_target="tpu_custom_call" | custom-call | tf_op jit(solution)/shard_map/pallas_call | solution.py:345
  104.8 2.2 %shard_map.159 = (bf16[1024,128]{1,0:T(8,128)(2,1)}, bf16[1024,128]{1,0:T(8,128)(2,1)}) custom-call(bf16[128,1024]{1,0:T(8,128)(2,1)} %bitcast.12, bf16[1024,128]{1,0:T(8,128)(2,1)} %refs_1_.6, bf16[1024,128]{1,0:T(8,128)(2,1)} %refs_2_.5), custom_call_target="tpu_custom_call" | custom-call | tf_op jit(solution)/shard_map/pallas_call | solution.py:345
  107.0 1.6 %collective-permute-done.17.x_ref = bf16[128,1024]{1,0:T(8,128)(2,1)S(1)} collective-permute-done((bf16[128,1024]{1,0:T(8,128)(2,1)S(1)}, bf16[128,1024]{1,0:T(8,128)(2,1)S(1)}, u32[]{:S(2)}, u32[]{:S(2)}) %collective-permute-start.17) | collective-permute-done | bytes 262176 | tf_op jit(solution)/shard_map/ppermute | solution.py:518
  108.6 0.1 collective-permute-done.18.up_ref
  108.6 0.1 collective-permute-done.19.down_ref
  108.7 0.1 shard_map.160
  108.8 1.5 %collective-permute-start.20 = (bf16[64,1024]{1,0:T(8,128)(2,1)S(1)}, bf16[64,1024]{1,0:T(8,128)(2,1)S(1)}, u32[]{:S(2)}, u32[]{:S(2)}) collective-permute-start(bf16[64,1024]{1,0:T(8,128)(2,1)S(1)} %get-tuple-element.59), channel_id=1, source_target_pairs={{0,8},{1,9},{2,10},{3,11},{4,12},{5,13},{6,14},{7,15},{8,0},{9,1},... | collective-permute-start | bytes 393224 | tf_op jit(solution)/shard_map/ppermute | solution.py:519
  110.3 2.9 %collective-permute-start.21 = (bf16[64,1024]{1,0:T(8,128)(2,1)S(1)}, bf16[64,1024]{1,0:T(8,128)(2,1)S(1)}, u32[]{:S(2)}, u32[]{:S(2)}) collective-permute-start(bf16[64,1024]{1,0:T(8,128)(2,1)S(1)} %get-tuple-element.60), channel_id=1, source_target_pairs={{0,2},{1,3},{2,0},{3,1},{4,6},{5,7},{6,4},{7,5},{8,10},{9,11},{10,... | collective-permute-start | bytes 393224 | tf_op jit(solution)/shard_map/ppermute | solution.py:518
  113.2 2.1 %shard_map.157 = bf16[1024,1024]{1,0:T(8,128)(2,1)S(1)} custom-call(bf16[128,1024]{1,0:T(8,128)(2,1)S(1)} %get-tuple-element.44.refs_0_, bf16[128,1024]{1,0:T(8,128)(2,1)S(1)} %collective-permute-done.7.refs_1_, bf16[128,1024]{1,0:T(8,128)(2,1)} %collective-permute-done.8.refs_2_, bf16[128,1024]{1,0:T(8,128)(2,1)} %collective-permute-done.9.refs_3_, ...), custom_call_target="tpu_custom_call" | custom-call | tf_op jit(solution)/shard_map/pallas_call | solution.py:345
  115.4 2.4 %convolution_convert_fusion.refs_3_ = bf16[1024,1024]{1,0:T(8,128)(2,1)S(1)} fusion(bf16[1024,1024]{1,0:T(8,128)(2,1)S(1)} %shard_map.157, bf16[1024,1024]{1,0:T(8,128)(2,1)S(1)} %copy-done.2), kind=kOutput, calls=%fused_computation | convolution fusion | flops 2148532224 | bytes 6291456 | tf_op jit(solution)/shard_map/dot_general | solution.py:535
  117.8 0.9 shard_map.161
  118.7 0.5 copy-done.9
  (59 shorter events, 0.2 us)
Async XLA Ops:
  5.6 14.9 %copy-start = (bf16[1024,1024]{1,0:T(8,128)(2,1)S(1)}, bf16[1024,1024]{1,0:T(8,128)(2,1)}, u32[]{:S(2)}) copy-start(bf16[1024,1024]{1,0:T(8,128)(2,1)} %refs_4_.5) | copy-start | bytes 6291460
  5.6 14.9 %copy-start.8 = (bf16[256,1024]{1,0:T(8,128)(2,1)S(1)}, bf16[256,1024]{1,0:T(8,128)(2,1)}, u32[]{:S(2)}) copy-start(bf16[256,1024]{1,0:T(8,128)(2,1)} %get-tuple-element.33.refs_2_.refs_3_) | copy-start | bytes 1572868
  5.7 17.7 %collective-permute-start.1 = (bf16[256,1024]{1,0:T(8,128)(2,1)}, bf16[256,1024]{1,0:T(8,128)(2,1)}, u32[]{:S(2)}, u32[]{:S(2)}) collective-permute-start(bf16[256,1024]{1,0:T(8,128)(2,1)} %get-tuple-element.34), channel_id=1, source_target_pairs={{0,16},{16,32},{32,48},{48,0},{64,80},{80,96},{96,112},{112,64},{1... | collective-permute-start | bytes 1572872 | tf_op jit(solution)/shard_map/ppermute | solution.py:366
  7.7 15.7 %collective-permute-start.2 = (bf16[256,1024]{1,0:T(8,128)(2,1)}, bf16[256,1024]{1,0:T(8,128)(2,1)}, u32[]{:S(2)}, u32[]{:S(2)}) collective-permute-start(bf16[256,1024]{1,0:T(8,128)(2,1)} %get-tuple-element.35), channel_id=1, source_target_pairs={{0,48},{16,0},{32,16},{48,32},{64,112},{80,64},{96,80},{112,96},{1... | collective-permute-start | bytes 1572872 | tf_op jit(solution)/shard_map/ppermute | solution.py:366
  9.9 15.0 %collective-permute-start = (bf16[256,1024]{1,0:T(8,128)(2,1)}, bf16[256,1024]{1,0:T(8,128)(2,1)}, u32[]{:S(2)}, u32[]{:S(2)}) collective-permute-start(bf16[256,1024]{1,0:T(8,128)(2,1)} %get-tuple-element.33.refs_2_.refs_3_), channel_id=1, source_target_pairs={{0,64},{16,80},{32,96},{48,112},{64,0},{80,16},{96,32},{112,48},{1... | collective-permute-start | bytes 1572872 | tf_op jit(solution)/shard_map/ppermute | solution.py:366
  13.7 20.2 %all-to-all-start = ((bf16[16,16,1024]{2,1,0:T(8,128)(2,1)}), bf16[16,16,1024]{2,1,0:T(8,128)(2,1)}, u32[]{:S(2)}, u32[]{:S(2)}) async-start(bf16[16,16,1024]{2,1,0:T(8,128)(2,1)} %bitcast.14), calls=%async_computation | async-start | bytes 1048576 | tf_op jit(solution)/shard_map/all_to_all | solution.py:362
  20.5 1.6 %copy-start.1 = (bf16[1024,1024]{1,0:T(8,128)(2,1)S(1)}, bf16[1024,1024]{1,0:T(8,128)(2,1)}, u32[]{:S(2)}) copy-start(bf16[1024,1024]{1,0:T(8,128)(2,1)} %refs_0_.3) | copy-start | bytes 6291460
  23.4 10.5 %copy-start.3 = (f32[1040,256]{1,0:T(8,128)S(1)}, f32[1040,256]{1,0:T(8,128)}, u32[]{:S(2)}) copy-start(f32[1040,256]{1,0:T(8,128)} %constant.12.clone.refs_3_.refs_4_) | copy-start | bytes 3194884
  23.4 10.5 %copy-start.15 = (bf16[512,256]{1,0:T(8,128)(2,1)S(1)}, bf16[512,256]{1,0:T(8,128)(2,1)}, u32[]{:S(2)}) copy-start(bf16[512,256]{1,0:T(8,128)(2,1)} %constant.11.clone.refs_2_.refs_3_) | copy-start | bytes 786436
  27.1 0.8 copy-start.10
  27.9 12.7 %collective-permute-start.4 = (bf16[128,1024]{1,0:T(8,128)(2,1)}, bf16[128,1024]{1,0:T(8,128)(2,1)}, u32[]{:S(2)}, u32[]{:S(2)}) collective-permute-start(bf16[128,1024]{1,0:T(8,128)(2,1)} %get-tuple-element.38), channel_id=1, source_target_pairs={{0,64},{16,80},{32,96},{48,112},{64,0},{80,16},{96,32},{112,48},{1... | collective-permute-start | bytes 786440 | tf_op jit(solution)/shard_map/ppermute | solution.py:366
  29.1 11.5 %collective-permute-start.3 = (bf16[128,1024]{1,0:T(8,128)(2,1)}, bf16[128,1024]{1,0:T(8,128)(2,1)}, u32[]{:S(2)}, u32[]{:S(2)}) collective-permute-start(bf16[128,1024]{1,0:T(8,128)(2,1)} %get-tuple-element.37.refs_5_), channel_id=1, source_target_pairs={{0,32},{16,48},{32,0},{48,16},{64,96},{80,112},{96,64},{112,80},{1... | collective-permute-start | bytes 786440 | tf_op jit(solution)/shard_map/ppermute | solution.py:366
  33.9 1.2 %copy-start.5 = (bf16[1040,512]{1,0:T(8,128)(2,1)S(1)}, bf16[1040,512]{1,0:T(8,128)(2,1)}, u32[]{:S(2)}) copy-start(bf16[1040,512]{1,0:T(8,128)(2,1)} %constant.10.clone.refs_1_.refs_2_) | copy-start | bytes 3194884
  35.1 1.2 %copy-start.19 = (bf16[512,1024]{1,0:T(8,128)(2,1)S(1)}, bf16[512,1024]{1,0:T(8,128)(2,1)}, u32[]{:S(2)}) copy-start(bf16[512,1024]{1,0:T(8,128)(2,1)} %constant.13.clone.refs_4_) | copy-start | bytes 3145732
  36.4 4.3 %copy-start.11 = (f32[128,1024]{1,0:T(8,128)S(1)}, f32[128,1024]{1,0:T(8,128)}, u32[]{:S(2)}) copy-start(f32[128,1024]{1,0:T(8,128)} %copy-done.10) | copy-start | bytes 1572868
  36.4 4.3 %copy-start.20 = (bf16[1024,128]{1,0:T(8,128)(2,1)S(1)}, bf16[1024,128]{1,0:T(8,128)(2,1)}, u32[]{:S(2)}) copy-start(bf16[1024,128]{1,0:T(8,128)(2,1)} %refs_0_.5) | copy-start | bytes 786436
  40.6 2.5 %copy-start.23 = (bf16[1040,256]{1,0:T(8,128)(2,1)}, bf16[1040,256]{1,0:T(8,128)(2,1)S(1)}, u32[]{:S(2)}) copy-start(bf16[1040,256]{1,0:T(8,128)(2,1)S(1)} %get-tuple-element.45.refs_1_) | copy-start | bytes 1597444
  40.6 6.3 %copy-start.21 = (bf16[1024,128]{1,0:T(8,128)(2,1)S(1)}, bf16[1024,128]{1,0:T(8,128)(2,1)}, u32[]{:S(2)}) copy-start(bf16[1024,128]{1,0:T(8,128)(2,1)} %refs_0_.5) | copy-start | bytes 786436
  43.1 16.1 %collective-permute-start.6 = (bf16[1024,1024]{1,0:T(8,128)(2,1)S(1)}, bf16[1024,1024]{1,0:T(8,128)(2,1)}, u32[]{:S(2)}, u32[]{:S(2)}) collective-permute-start(bf16[1024,1024]{1,0:T(8,128)(2,1)S(1)} %copy-done), channel_id=1, source_target_pairs={{0,1},{1,0},{2,3},{3,2},{4,5},{5,4},{6,7},{7,6},{8,9},{9,8},{10,11... | collective-permute-start | bytes 6291464 | tf_op jit(solution)/shard_map/ppermute | solution.py:437
  43.2 16.0 %all-to-all-start.1 = ((bf16[16,16,1024]{2,1,0:T(8,128)(2,1)}), bf16[16,16,1024]{2,1,0:T(8,128)(2,1)S(1)}, u32[]{:S(2)}, u32[]{:S(2)}) async-start(bf16[16,16,1024]{2,1,0:T(8,128)(2,1)} %bitcast.2), calls=%async_computation.1 | async-start | bytes 1048576 | tf_op jit(solution)/shard_map/all_to_all | solution.py:362
  46.9 13.9 %copy-start.16 = (bf16[512,256]{1,0:T(8,128)(2,1)S(1)}, bf16[512,256]{1,0:T(8,128)(2,1)}, u32[]{:S(2)}) copy-start(bf16[512,256]{1,0:T(8,128)(2,1)} %constant.11.clone.refs_2_.refs_3_) | copy-start | bytes 786436
  47.1 1.5 %collective-permute-start.5 = (bf16[64,1024]{1,0:T(8,128)(2,1)S(1)}, bf16[64,1024]{1,0:T(8,128)(2,1)S(1)}, u32[]{:S(2)}, u32[]{:S(2)}) collective-permute-start(bf16[64,1024]{1,0:T(8,128)(2,1)S(1)} %get-tuple-element.42), channel_id=1, source_target_pairs={{0,1},{1,0},{2,3},{3,2},{4,5},{5,4},{6,7},{7,6},{8,9},{9,8},{10,11... | collective-permute-start | bytes 393224 | tf_op jit(solution)/shard_map/ppermute | solution.py:437
  59.2 1.5 %copy-start.4 = (f32[1040,256]{1,0:T(8,128)S(1)}, f32[1040,256]{1,0:T(8,128)}, u32[]{:S(2)}) copy-start(f32[1040,256]{1,0:T(8,128)} %constant.12.clone.refs_3_.refs_4_) | copy-start | bytes 3194884
  59.2 1.6 %copy-start.6 = (bf16[1040,512]{1,0:T(8,128)(2,1)S(1)}, bf16[1040,512]{1,0:T(8,128)(2,1)}, u32[]{:S(2)}) copy-start(bf16[1040,512]{1,0:T(8,128)(2,1)} %constant.10.clone.refs_1_.refs_2_) | copy-start | bytes 3194884
  59.5 0.7 copy-start.26
  60.2 7.6 %collective-permute-start.7 = (bf16[128,1024]{1,0:T(8,128)(2,1)S(1)}, bf16[128,1024]{1,0:T(8,128)(2,1)S(1)}, u32[]{:S(2)}, u32[]{:S(2)}) collective-permute-start(bf16[128,1024]{1,0:T(8,128)(2,1)S(1)} %get-tuple-element.44.refs_0_), channel_id=1, source_target_pairs={{0,64},{16,80},{32,96},{48,112},{64,0},{80,16},{96,32},{112,48},{1... | collective-permute-start | bytes 786440 | tf_op jit(solution)/shard_map/ppermute | solution.py:366
  60.8 1.2 %copy-start.18 = (bf16[512,1024]{1,0:T(8,128)(2,1)S(1)}, bf16[512,1024]{1,0:T(8,128)(2,1)}, u32[]{:S(2)}) copy-start(bf16[512,1024]{1,0:T(8,128)(2,1)} %constant.14.clone.refs_5_) | copy-start | bytes 3145732
  62.0 1.0 copy-start.24
  65.6 0.7 copy-start.17
  66.3 10.6 %collective-permute-start.8 = (bf16[128,1024]{1,0:T(8,128)(2,1)S(1)}, bf16[128,1024]{1,0:T(8,128)(2,1)}, u32[]{:S(2)}, u32[]{:S(2)}) collective-permute-start(bf16[128,1024]{1,0:T(8,128)(2,1)S(1)} %get-tuple-element.44.refs_0_), channel_id=1, source_target_pairs={{0,16},{16,32},{32,48},{48,0},{64,80},{80,96},{96,112},{112,64},{1... | collective-permute-start | bytes 786440 | tf_op jit(solution)/shard_map/ppermute | solution.py:366
  67.7 9.3 %collective-permute-start.11 = (bf16[128,1024]{1,0:T(8,128)(2,1)S(1)}, bf16[128,1024]{1,0:T(8,128)(2,1)}, u32[]{:S(2)}, u32[]{:S(2)}) collective-permute-start(bf16[128,1024]{1,0:T(8,128)(2,1)S(1)} %collective-permute-done.7.refs_1_), channel_id=1, source_target_pairs={{0,48},{16,0},{32,16},{48,32},{64,112},{80,64},{96,80},{112,96},{1... | collective-permute-start | bytes 786440 | tf_op jit(solution)/shard_map/ppermute | solution.py:366
  69.6 14.1 %collective-permute-start.9 = (bf16[128,1024]{1,0:T(8,128)(2,1)S(1)}, bf16[128,1024]{1,0:T(8,128)(2,1)}, u32[]{:S(2)}, u32[]{:S(2)}) collective-permute-start(bf16[128,1024]{1,0:T(8,128)(2,1)S(1)} %get-tuple-element.44.refs_0_), channel_id=1, source_target_pairs={{0,48},{16,0},{32,16},{48,32},{64,112},{80,64},{96,80},{112,96},{1... | collective-permute-start | bytes 786440 | tf_op jit(solution)/shard_map/ppermute | solution.py:366
  70.3 23.0 %collective-permute-start.10 = (bf16[128,1024]{1,0:T(8,128)(2,1)S(1)}, bf16[128,1024]{1,0:T(8,128)(2,1)}, u32[]{:S(2)}, u32[]{:S(2)}) collective-permute-start(bf16[128,1024]{1,0:T(8,128)(2,1)S(1)} %collective-permute-done.7.refs_1_), channel_id=1, source_target_pairs={{0,16},{16,32},{32,48},{48,0},{64,80},{80,96},{96,112},{112,64},{1... | collective-permute-start | bytes 786440 | tf_op jit(solution)/shard_map/ppermute | solution.py:366
  76.9 16.4 %collective-permute-start.12 = (bf16[128,1024]{1,0:T(8,128)(2,1)}, bf16[128,1024]{1,0:T(8,128)(2,1)}, u32[]{:S(2)}, u32[]{:S(2)}) collective-permute-start(bf16[128,1024]{1,0:T(8,128)(2,1)} %collective-permute-done.8.refs_2_), channel_id=1, source_target_pairs={{0,16},{16,32},{32,48},{48,0},{64,80},{80,96},{96,112},{112,64},{1... | collective-permute-start | bytes 786440 | tf_op jit(solution)/shard_map/ppermute | solution.py:366
  77.1 16.2 %collective-permute-start.13 = (bf16[128,1024]{1,0:T(8,128)(2,1)}, bf16[128,1024]{1,0:T(8,128)(2,1)}, u32[]{:S(2)}, u32[]{:S(2)}) collective-permute-start(bf16[128,1024]{1,0:T(8,128)(2,1)} %collective-permute-done.11.refs_1_.refs_5_), channel_id=1, source_target_pairs={{0,48},{16,0},{32,16},{48,32},{64,112},{80,64},{96,80},{112,96},{1... | collective-permute-start | bytes 786440 | tf_op jit(solution)/shard_map/ppermute | solution.py:366
  80.2 13.1 %all-to-all-start.2 = ((bf16[16,8,1024]{2,1,0:T(8,128)(2,1)}), bf16[16,8,1024]{2,1,0:T(8,128)(2,1)S(1)}, u32[]{:S(2)}, u32[]{:S(2)}) async-start(bf16[16,8,1024]{2,1,0:T(8,128)(2,1)} %bitcast.13), calls=%async_computation.2 | async-start | bytes 524288 | tf_op jit(solution)/shard_map/all_to_all | solution.py:362
  87.3 1.0 copy-start.13
  88.3 24.9 %collective-permute-start.14 = (bf16[256,1024]{1,0:T(8,128)(2,1)}, bf16[256,1024]{1,0:T(8,128)(2,1)}, u32[]{:S(2)}, u32[]{:S(2)}) collective-permute-start(bf16[256,1024]{1,0:T(8,128)(2,1)} %get-tuple-element.47), channel_id=1, source_target_pairs={{0,1},{1,0},{2,3},{3,2},{4,5},{5,4},{6,7},{7,6},{8,9},{9,8},{10,11... | collective-permute-start | bytes 1572872 | tf_op jit(solution)/shard_map/ppermute | solution.py:437
  93.3 4.9 %copy-start.7 = (bf16[16,8,1024]{2,1,0:T(8,128)(2,1)}, bf16[16,8,1024]{2,1,0:T(8,128)(2,1)S(1)}, u32[]{:S(2)}) copy-start(bf16[16,8,1024]{2,1,0:T(8,128)(2,1)S(1)} %all-to-all-done.2) | copy-start | bytes 786436
  93.3 1.3 %copy-start.14 = (bf16[512,1024]{1,0:T(8,128)(2,1)S(1)}, bf16[512,1024]{1,0:T(8,128)(2,1)}, u32[]{:S(2)}) copy-start(bf16[512,1024]{1,0:T(8,128)(2,1)} %copy-done.13) | copy-start | bytes 3145732
  94.6 3.6 %copy-start.27 = (bf16[64,1024]{1,0:T(8,128)(2,1)S(1)}, bf16[64,1024]{1,0:T(8,128)(2,1)}, u32[]{:S(2)}) copy-start(bf16[64,1024]{1,0:T(8,128)(2,1)} %copy-done.26) | copy-start | bytes 393220
  94.6 8.0 %copy-start.12 = (f32[128,1024]{1,0:T(8,128)S(1)}, f32[128,1024]{1,0:T(8,128)}, u32[]{:S(2)}) copy-start(f32[128,1024]{1,0:T(8,128)} %copy-done.10) | copy-start | bytes 1572868
  98.2 15.0 %collective-permute-start.15 = (bf16[256,1024]{1,0:T(8,128)(2,1)S(1)}, bf16[256,1024]{1,0:T(8,128)(2,1)S(1)}, u32[]{:S(2)}, u32[]{:S(2)}) collective-permute-start(bf16[256,1024]{1,0:T(8,128)(2,1)S(1)} %get-tuple-element.50), channel_id=1, source_target_pairs={{0,1},{1,0},{2,3},{3,2},{4,5},{5,4},{6,7},{7,6},{8,9},{9,8},{10,11... | collective-permute-start | bytes 1572872 | tf_op jit(solution)/shard_map/ppermute | solution.py:437
  98.3 2.1 %collective-permute-start.16 = (bf16[64,1024]{1,0:T(8,128)(2,1)S(1)}, bf16[64,1024]{1,0:T(8,128)(2,1)S(1)}, u32[]{:S(2)}, u32[]{:S(2)}) collective-permute-start(bf16[64,1024]{1,0:T(8,128)(2,1)S(1)} %copy-done.27), channel_id=1, source_target_pairs={{0,1},{1,0},{2,3},{3,2},{4,5},{5,4},{6,7},{7,6},{8,9},{9,8},{10,11... | collective-permute-start | bytes 393224 | tf_op jit(solution)/shard_map/ppermute | solution.py:437
  98.8 9.8 %collective-permute-start.17 = (bf16[128,1024]{1,0:T(8,128)(2,1)S(1)}, bf16[128,1024]{1,0:T(8,128)(2,1)S(1)}, u32[]{:S(2)}, u32[]{:S(2)}) collective-permute-start(bf16[128,1024]{1,0:T(8,128)(2,1)S(1)} %get-tuple-element.55), channel_id=1, source_target_pairs={{0,2},{1,3},{2,0},{3,1},{4,6},{5,7},{6,4},{7,5},{8,10},{9,11},{10,... | collective-permute-start | bytes 786440 | tf_op jit(solution)/shard_map/ppermute | solution.py:518
  99.4 9.2 %collective-permute-start.18 = (bf16[128,1024]{1,0:T(8,128)(2,1)S(1)}, bf16[128,1024]{1,0:T(8,128)(2,1)S(1)}, u32[]{:S(2)}, u32[]{:S(2)}) collective-permute-start(bf16[128,1024]{1,0:T(8,128)(2,1)S(1)} %get-tuple-element.56), channel_id=1, source_target_pairs={{0,4},{1,5},{2,6},{3,7},{4,8},{5,9},{6,10},{7,11},{8,12},{9,13},{1... | collective-permute-start | bytes 786440 | tf_op jit(solution)/shard_map/ppermute | solution.py:519
  100.3 8.3 %collective-permute-start.19 = (bf16[128,1024]{1,0:T(8,128)(2,1)S(1)}, bf16[128,1024]{1,0:T(8,128)(2,1)S(1)}, u32[]{:S(2)}, u32[]{:S(2)}) collective-permute-start(bf16[128,1024]{1,0:T(8,128)(2,1)S(1)} %get-tuple-element.57), channel_id=1, source_target_pairs={{0,12},{1,13},{2,14},{3,15},{4,0},{5,1},{6,2},{7,3},{8,4},{9,5},{1... | collective-permute-start | bytes 786440 | tf_op jit(solution)/shard_map/ppermute | solution.py:519
  108.8 9.0 %collective-permute-start.20 = (bf16[64,1024]{1,0:T(8,128)(2,1)S(1)}, bf16[64,1024]{1,0:T(8,128)(2,1)S(1)}, u32[]{:S(2)}, u32[]{:S(2)}) collective-permute-start(bf16[64,1024]{1,0:T(8,128)(2,1)S(1)} %get-tuple-element.59), channel_id=1, source_target_pairs={{0,8},{1,9},{2,10},{3,11},{4,12},{5,13},{6,14},{7,15},{8,0},{9,1},... | collective-permute-start | bytes 393224 | tf_op jit(solution)/shard_map/ppermute | solution.py:519
  110.3 5.0 %copy-start.2 = (bf16[1024,1024]{1,0:T(8,128)(2,1)S(1)}, bf16[1024,1024]{1,0:T(8,128)(2,1)}, u32[]{:S(2)}) copy-start(bf16[1024,1024]{1,0:T(8,128)(2,1)} %refs_0_.3) | copy-start | bytes 6291460
  110.3 7.5 %collective-permute-start.21 = (bf16[64,1024]{1,0:T(8,128)(2,1)S(1)}, bf16[64,1024]{1,0:T(8,128)(2,1)S(1)}, u32[]{:S(2)}, u32[]{:S(2)}) collective-permute-start(bf16[64,1024]{1,0:T(8,128)(2,1)S(1)} %get-tuple-element.60), channel_id=1, source_target_pairs={{0,2},{1,3},{2,0},{3,1},{4,6},{5,7},{6,4},{7,5},{8,10},{9,11},{10,... | collective-permute-start | bytes 393224 | tf_op jit(solution)/shard_map/ppermute | solution.py:518
  115.4 2.5 %copy-start.22 = (bf16[1024,128]{1,0:T(8,128)(2,1)S(1)}, bf16[1024,128]{1,0:T(8,128)(2,1)}, u32[]{:S(2)}) copy-start(bf16[1024,128]{1,0:T(8,128)(2,1)} %shard_map.158.refs_4_) | copy-start | bytes 786436
  115.4 2.5 %copy-start.25 = (bf16[1024,128]{1,0:T(8,128)(2,1)S(1)}, bf16[1024,128]{1,0:T(8,128)(2,1)}, u32[]{:S(2)}) copy-start(bf16[1024,128]{1,0:T(8,128)(2,1)} %get-tuple-element.30.refs_5_) | copy-start | bytes 786436
  117.8 1.4 %copy-start.9 = (bf16[1024,1024]{1,0:T(8,128)(2,1)}, bf16[1024,1024]{1,0:T(8,128)(2,1)S(1)}, u32[]{:S(2)}) copy-start(bf16[1024,1024]{1,0:T(8,128)(2,1)S(1)} %convolution_convert_fusion.refs_3_) | copy-start | bytes 6291460

commit v7 on v6

--- a/solution.py
+++ b/solution.py
@@ -52,6 +52,7 @@
 VMEM = pl.BlockSpec(memory_space=pltpu.VMEM)
 ANY = pl.BlockSpec(memory_space=pl.ANY)
 DY_MOVES = ((0, 0), (0, 2), (1, 0), (1, 2), (0, 1), (1, 1), (0, -1), (1, -1))
+DU_FROM = ((0, 0), (1, 0), (0, -1), (0, 1), (0, 2), (1, 2), (1, -1), (1, 1))
 SLOT = {move: i for i, (flip, step) in enumerate(DY_MOVES) for move in ((flip, step % 4),)}
 
 
@@ -237,9 +238,9 @@
     z_ref[...] = signal(p_re, p_im, tables).astype(BF)
 
 
-def adjoint_kernel(r_ref, h_ref, first_ref, square_ref, twiddle_ref, last_ref, du_ref):
+def adjoint_kernel(r_ref, h_ref, first_ref, square_ref, twiddle_ref, last_ref, away_ref, keep_ref):
     tables = Tables(first_ref, square_ref, twiddle_ref, last_ref)
-    rows = du_ref.shape[0]
+    rows = 2 * keep_ref.shape[0]
     group = h_ref.shape[0] // (2 * HALF)
     r = r_ref[...].astype(F32).reshape(-1, 2, group, ROW)[:, 1]
     g_re, g_im = transform(r.reshape(rows, ROW).astype(BF), tables)
@@ -247,12 +248,25 @@
     n = h.shape[0] // 2
     h_re, h_im = h[:n], h[n:]
     q_re, q_im = h_re * g_re + h_im * g_im, h_re * g_im - h_im * g_re
-    du_ref[...] = signal(q_re, q_im, tables).astype(BF)
+    du = signal(q_re, q_im, tables).reshape(-1, 2, group, ROW)
+    low, high, first_core = du[:, 0], du[:, 1], my_core() == 0
+    keep_ref[...] = jnp.where(first_core, low, high).reshape(keep_ref.shape).astype(BF)
+    away_ref[...] = jnp.where(first_core, high, low).reshape(keep_ref.shape).astype(BF)
+
+
+def slot_of(to):
+    ctx = lax.axis_index("ctx")
+    flip, step = (to ^ (ctx // 2)) & 1, (to // 2 - ctx // 4) & 3
+    slot = jnp.int32(0)
+    for (f, d), at in SLOT.items():
+        slot = jnp.where((flip == f) & (step == d), at, slot)
+    return slot
 
 
 def weight_rows(scale, moves, blocks, d_ref, d_other_ref, away_ref, part_ref, loaded=()):
-    me, ctx = lax.axis_index("fsdp"), lax.axis_index("ctx")
+    me = lax.axis_index("fsdp")
     n = blocks[0].shape[0] // 2
+    slot_rows = part_ref.shape[0] // 8
     mine = jnp.concatenate([block[:n] for block in blocks], axis=0)
     away = jnp.concatenate([block[n:] for block in blocks], axis=0)
     away_ref[...] = away
@@ -261,12 +275,8 @@
     for load in loaded:
         load.wait()
     for i, move in enumerate(moves):
-        to = place(me, move)
-        flip, step = (to ^ (ctx // 2)) & 1, (to // 2 - ctx // 4) & 3
-        slot = jnp.int32(0)
-        for (f, d), at in SLOT.items():
-            slot = jnp.where((flip == f) & (step == d), at, slot)
-        part_ref[rows_at(slot, n), :] = p[i * n : (i + 1) * n]
+        start = pl.multiple_of(slot_of(place(me, move)) * slot_rows, 16)
+        part_ref[pl.ds(start, n), :] = p[i * n : (i + 1) * n]
 
 
 def near_kernel(scale, moves, *refs):
@@ -277,13 +287,30 @@
 
 def far_kernel(scale, moves, *refs):
     count = len(moves)
-    blocks, (d_ref, d_other_ref, near_hbm), refs = refs[:count], refs[count : count + 3], refs[count + 3 :]
+    blocks, (d_ref, d_other_ref, keep_ref, got_ref, near_hbm), refs = refs[:count], refs[count : count + 5], refs[count + 5 :]
     outs, away_ref, (part_ref, sem) = refs[:4], refs[4], refs[5:]
     near = pltpu.make_async_copy(near_hbm, part_ref, sem.at[4])
     near.start()
     weight_rows(scale, moves, blocks, d_ref, d_other_ref, away_ref, part_ref, [near])
+    slot_rows = part_ref.shape[0] // 8
+    group = keep_ref.shape[0] // 8
+    keep, got = keep_ref[...].astype(F32), got_ref[...].astype(F32)
+    for j in range(8):
+        rows = slice(j * group, (j + 1) * group)
+        start = pl.multiple_of((slot_of(jnp.int32(j)) + 1) * slot_rows - 2 * group, 16)
+        part_ref[pl.ds(start, 2 * group), :] = jnp.concatenate([keep[rows], got[rows]], axis=0).astype(BF)
     n = outs[0].shape[0]
     copy_all(pltpu.make_async_copy(part_ref.at[pl.ds(i * n, n), :], out, sem.at[i]) for i, out in enumerate(outs))
+
+
+def part_sum_kernel(own_ref, x_ref, up_ref, down_ref, keep_ref, far_ref, side_ref, du_ref):
+    n = keep_ref.shape[0]
+    own, x, up, down = (ref[...].astype(F32) for ref in (own_ref, x_ref, up_ref, down_ref))
+    m = own.shape[0] // 2
+    keep_ref[...] = own[:n] + x[:n] + (up[:n] + down[:n])
+    for out_ref, a, b in ((far_ref, own, x), (side_ref, up, down)):
+        out_ref[...] = jnp.concatenate([a[m : m + n] + b[m : m + n], a[m + n :], b[m + n :]], axis=0).astype(BF)
+    du_ref[...] = jnp.concatenate([v[n:m] for v in (own, x, up, down)], axis=0).astype(BF)
 
 
 def assemble_kernel(*refs):
@@ -299,14 +326,22 @@
     copy_all(copies)
 
 
-def key_value_kernel(ways, du_ref, k_ref, v_ref, gk_ref, gv_ref):
-    du = dot(du_ref[...].astype(F32).T.astype(BF), order_in(ways, du_ref.shape[0]))
+def final_kernel(keep_ref, far_ref, side_ref, du_ref, k_ref, v_ref, gw_ref, gk_ref, gv_ref, du_t_ref):
+    n = gw_ref.shape[0]
+    far, side, du = far_ref[...].astype(F32), side_ref[...].astype(F32), du_ref[...].astype(F32)
+    gw_ref[...] = keep_ref[...] + (far[:n] + side[:n])
+    ctx, core = lax.axis_index("ctx"), my_core()
+    width = du_t_ref.shape[0]
+    group = width // 16
+    pieces = [du[i * 2 * group : (i + 1) * 2 * group] for i in range(4)]
+    pieces += [v[n + i * 2 * group : n + (i + 1) * 2 * group] for v in (far, side) for i in range(2)]
+    for piece, (flip, step) in zip(pieces, DU_FROM):
+        chip = ((ctx // 4 + step) & 3) * 2 + ((ctx // 2) & 1 ^ flip)
+        for rows, side_core in ((piece[:group], core), (piece[group:], 1 - core)):
+            du_t_ref[rows_at(2 * chip + side_core, group), :] = rows
+    du = dot(du_t_ref[...].T.astype(BF), order_in(16, width))
     gk_ref[...] = (du * v_ref[...].astype(F32)).astype(BF)
     gv_ref[...] = (du * k_ref[...].astype(F32)).astype(BF)
-
-
-def final_kernel(keep_ref, far_ref, side_ref, gw_ref):
-    gw_ref[...] = keep_ref[...] + (far_ref[...].astype(F32) + side_ref[...].astype(F32))
 
 
 def staged(kernel, n_in, n_out, n_after, staged_in, staged_out):
@@ -367,16 +402,6 @@
 
 
 RING_FROM = ((0, 0), (1, 0), (0, -1), (0, 1), (1, -1), (1, 1), (0, 2), (1, 2))
-
-
-def ring_first(gated):
-    return move_over(gated, (1, 0)), move_over(gated, (0, 1)), move_over(gated, (0, -1))
-
-
-def ring_rest(gated, other, own_up, own_down):
-    other_up, other_down = move_over(other, (0, 1)), move_over(other, (0, -1))
-    own_far, other_far = move_over(own_up, (0, 1)), move_over(other_down, (0, -1))
-    return gated, other, own_up, own_down, other_up, other_down, own_far, other_far
 
 
 def dy_product(w_out, d_out, moves, mib=MOST, after=()):
@@ -405,13 +430,13 @@
     )
 
 
-def weight_product(blocks, moves, d_out, d_other, scale, after, near=()):
+def weight_product(blocks, moves, d_out, d_other, scale, slot_rows, after=(), du=(), near=()):
     rows, columns = d_out.shape
     n = blocks[0].shape[0] // 2
     count = len(moves)
-    all_rows = 8 * n
+    all_rows = 8 * slot_rows
     outs = [shape(all_rows // 4, columns)] * 4 if near else [shape(all_rows, columns)]
-    ins = [*blocks, d_out, d_other]
+    ins = [*blocks, d_out, d_other, *du]
     return call(
         functools.partial(far_kernel if near else near_kernel, scale, moves),
         [*outs, shape(count * n, rows)],
@@ -487,7 +512,8 @@
         after=[d_other],
     )
     z_theirs = swap(z_away)
-    other, own_up, own_down = ring_first(gated)
+    own_far, other = move_over(gated, (0, 2)), move_over(gated, (1, 0))
+    own_up, own_down = move_over(gated, (0, 1)), move_over(gated, (0, -1))
     like = shape(seq_rows, width)
     (grad_query,) = call(
         functools.partial(query_kernel, ways),
@@ -496,31 +522,28 @@
         [pltpu.VMEM((width, seq_rows), F32)],
         staged_out=(0,),
     )
-    (adjoint,) = call(
-        adjoint_kernel, [rows_like], [arrived, spectrum, *tables, last], mib=20, flops=2 * flops, staged_out=(0,)
-    )
-    other, adjoint = lax.optimization_barrier((other, adjoint))
-    blocks = ring_rest(gated, other, own_up, own_down)
-    grad_u = spread(adjoint)
-    grad_key, grad_value = call(
-        functools.partial(key_value_kernel, ways),
-        [like, like],
-        [grad_u, key_in, value_in],
-        mib=MOST,
-        staged_in=(0, 1, 2),
-        staged_out=(0, 1),
-    )
-
-    weight = functools.partial(weight_product, d_out=d_out, d_other=d_other, scale=1.0 / math.sqrt(seq_rows * ways))
-    near, away = weight(blocks[:4], RING_FROM[:4], after=[])
+    du_away, du_keep = call(
+        adjoint_kernel, [half_like, half_like], [arrived, spectrum, *tables, last], mib=20, flops=2 * flops
+    )
+    other, own_up, own_down, du_away = lax.optimization_barrier((other, own_up, own_down, du_away))
+    du_got = swap(du_away)
+    other_up, other_down = move_over(other, (0, 1)), move_over(other, (0, -1))
+    other_far = move_over(own_far, (1, 0))
+    blocks = gated, other, own_up, own_down, other_up, other_down, own_far, other_far
+
+    slot_rows = half + 2 * group
+    scale = 1.0 / math.sqrt(seq_rows * ways)
+    weight = functools.partial(weight_product, d_out=d_out, d_other=d_other, scale=scale, slot_rows=slot_rows)
+    near, away = weight(blocks[:4], RING_FROM[:4])
     theirs_near = swap(away)
-    own_w, x_w, up_w, down_w, away = weight(blocks[4:], RING_FROM[4:], after=[grad_u], near=(near,))
+    own_w, x_w, up_w, down_w, away = weight(blocks[4:], RING_FROM[4:], du=(du_keep, du_got), near=(near,))
     over_x = lambda v: lax.ppermute(v, "ctx", [(i, i ^ 2) for i in range(ways)])
     along_y = lambda v, step: lax.ppermute(v, "ctx", [(i, (i + 4 * step) % ways) for i in range(ways)])
-    part_rows = shape(channels // ways, columns)
-    keep_w, far_w, side_w = call(
-        sum_kernel,
-        [shape(channels // ways, columns, dtype=F32), part_rows, part_rows],
+    part_like = shape(channels // ways, columns, dtype=F32)
+    onward = shape(half + 4 * group, columns)
+    keep_w, far_w, side_w, du_near = call(
+        part_sum_kernel,
+        [part_like, onward, onward, half_like],
         [own_w, over_x(x_w), along_y(up_w, 1), along_y(down_w, -1)],
     )
     far_w, side_w = along_y(far_w, 2), over_x(side_w)
@@ -536,11 +559,13 @@
         gated_all, w_out, (((0,), (0,)), ((), ())), preferred_element_type=F32
     ).astype(BF)
 
-    (grad_weight,) = call(
+    grad_weight, grad_key, grad_value = call(
         final_kernel,
-        [shape(channels // ways, columns, dtype=F32)],
-        [keep_w, far_w, side_w],
-        after=[layer_out, grad_query, grad_key],
+        [part_like, like, like],
+        [keep_w, far_w, side_w, du_near, key_in, value_in],
+        [pltpu.VMEM((width, columns), F32)],
+        after=[layer_out, grad_query],
+        staged_out=(0, 1, 2),
     )
     return (layer_out, grad_query, grad_key, grad_value, grad_weight)
 

time: 121 us -> 113 us (0.934)
  local copies, waits for them, and re-layouts: 11.3 us -> 6.15 us
  starting transfers between devices: 39.1 us -> 35.8 us
  waiting for transfers between devices: 30.3 us -> 32.6 us
  Pallas kernels: 34.9 us -> 33.5 us
    unnamed x56 -> x44, local copies, waits for them, and re-layouts: 11.3 us -> 6.15 us
    all_to_all x3 -> x2, waiting for transfers between devices: 18.9 us -> 14.2 us  [spread(): return lax.all_to_all(values, 'ctx', 0, 0, tiled=True)]
    ppermute x12, waiting for transfers between devices: 7.84 us -> 11.9 us  [move_over(): return lax.ppermute(values, 'fsdp', [(i, place(i, move)) for i in range(8)])]
    all_to_all x3 -> x2, starting transfers between devices: 14 us -> 10.5 us  [spread(): return lax.all_to_all(values, 'ctx', 0, 0, tiled=True)]
    ppermute x2, waiting for transfers between devices: 1.57 us -> 3.73 us  [on_device(): over_x = lambda v: lax.ppermute(v, 'ctx', [(i, i ^ 2) for i in range(ways)])]
    ppermute x3, waiting for transfers between devices: 0.12 us -> 1.76 us  [on_device(): lax.ppermute(v, 'ctx', [(i, (i + 4 * step) % ways) for i in range(ways)])]
    pallas_call x16 -> x15, Pallas kernels: 34.9 us -> 33.5 us  [call(): pl.pallas_call(kernel, out_shape=outs, in_specs=[*in_specs, *[ANY] * len(...]
where the time goes in v7:
time: 113 us; the launch traced here: 112 us
  starting transfers between devices  35.8 us (32%)
  Pallas kernels  33.5 us (30%)
  waiting for transfers between devices  32.6 us (29%)
  local copies, waits for them, and re-layouts  6.15 us (5%)
  matrix products  2.43 us (2%)
  between operations  1.16 us (1%)
    pallas_call x15, Pallas kernels, call(): pl.pallas_call(kernel, out_shape=outs, in_specs=[*in_specs, *[ANY] * len(...  33.5 us
    ppermute x12, starting transfers between devices, move_over(): return lax.ppermute(values, 'fsdp', [(i, place(i, move)) for i in range(8)])  15.3 us
    all_to_all x2, waiting for transfers between devices, spread(): return lax.all_to_all(values, 'ctx', 0, 0, tiled=True)  14.2 us
    ppermute x12, waiting for transfers between devices, move_over(): return lax.ppermute(values, 'fsdp', [(i, place(i, move)) for i in range(8)])  11.9 us
    all_to_all x2, starting transfers between devices, spread(): return lax.all_to_all(values, 'ctx', 0, 0, tiled=True)  10.5 us
    unnamed x44, local copies, waits for them, and re-layouts  6.15 us
    ppermute x3, starting transfers between devices, on_device(): lax.ppermute(v, 'ctx', [(i, (i + 4 * step) % ways) for i in range(ways)])  4.78 us
    ppermute x2, waiting for transfers between devices, on_device(): over_x = lambda v: lax.ppermute(v, 'ctx', [(i, i ^ 2) for i in range(ways)])  3.73 us
  transfers between devices with their start and end apart: 25, of which 12 were waited for; matrix products, arithmetic and copies ran while one was open for 2% of the time, Pallas kernels for 22%

profile of v7, /device:TPU:0, one launch (start us, length us, event | category | flops | bytes accessed | tf_op | source)
XLA Modules:
  0.0 111.7 jit_solution(8334684839174904774)
XLA Ops:
  0.6 5.0 %shard_map.146 = (bf16[256,1024]{1,0:T(8,128)(2,1)}, bf16[256,1024]{1,0:T(8,128)(2,1)}, bf16[256,1024]{1,0:T(8,128)(2,1)}) custom-call(bf16[1024,1024]{1,0:T(8,128)(2,1)} %refs_0_.3, bf16[1024,1024]{1,0:T(8,128)(2,1)} %refs_4_.5), custom_call_target="tpu_custom_call" | custom-call | tf_op jit(solution)/shard_map/pallas_call | solution.py:380
  5.6 0.0 copy-start.7
  5.6 2.1 %collective-permute-start.1 = (bf16[256,1024]{1,0:T(8,128)(2,1)}, bf16[256,1024]{1,0:T(8,128)(2,1)}, u32[]{:S(2)}, u32[]{:S(2)}) collective-permute-start(bf16[256,1024]{1,0:T(8,128)(2,1)} %get-tuple-element.40), channel_id=1, source_target_pairs={{0,16},{16,32},{32,48},{48,0},{64,80},{80,96},{96,112},{112,64},{1... | collective-permute-start | bytes 1572872 | tf_op jit(solution)/shard_map/ppermute | solution.py:401
  7.7 2.2 %collective-permute-start.2 = (bf16[256,1024]{1,0:T(8,128)(2,1)}, bf16[256,1024]{1,0:T(8,128)(2,1)}, u32[]{:S(2)}, u32[]{:S(2)}) collective-permute-start(bf16[256,1024]{1,0:T(8,128)(2,1)} %get-tuple-element.41), channel_id=1, source_target_pairs={{0,48},{16,0},{32,16},{48,32},{64,112},{80,64},{96,80},{112,96},{1... | collective-permute-start | bytes 1572872 | tf_op jit(solution)/shard_map/ppermute | solution.py:401
  9.9 1.5 %collective-permute-start = (bf16[256,1024]{1,0:T(8,128)(2,1)}, bf16[256,1024]{1,0:T(8,128)(2,1)}, u32[]{:S(2)}, u32[]{:S(2)}) collective-permute-start(bf16[256,1024]{1,0:T(8,128)(2,1)} %get-tuple-element.39.refs_2_.refs_3_), channel_id=1, source_target_pairs={{0,64},{16,80},{32,96},{48,112},{64,0},{80,16},{96,32},{112,48},{1... | collective-permute-start | bytes 1572872 | tf_op jit(solution)/shard_map/ppermute | solution.py:401
  11.4 2.3 %shard_map.149 = bf16[256,1024]{1,0:T(8,128)(2,1)} custom-call(bf16[1024,128]{1,0:T(8,128)(2,1)} %refs_4_.6, bf16[1024,128]{1,0:T(8,128)(2,1)} %refs_5_.1, bf16[1024,128]{1,0:T(8,128)(2,1)} %refs_2_.2, bf16[256,1024]{1,0:T(8,128)(2,1)} %get-tuple-element.39.refs_2_.refs_3_), custom_call_target="tpu_custom_call" | custom-call | tf_op jit(solution)/shard_map/pallas_call | solution.py:380
  13.7 6.8 %all-to-all-start = ((bf16[16,16,1024]{2,1,0:T(8,128)(2,1)}), bf16[16,16,1024]{2,1,0:T(8,128)(2,1)}, u32[]{:S(2)}, u32[]{:S(2)}) async-start(bf16[16,16,1024]{2,1,0:T(8,128)(2,1)} %bitcast.9), calls=%async_computation | async-start | bytes 1048576 | tf_op jit(solution)/shard_map/all_to_all | solution.py:397
  20.5 1.6 %copy-done.1 = bf16[1024,1024]{1,0:T(8,128)(2,1)S(1)} copy-done((bf16[1024,1024]{1,0:T(8,128)(2,1)S(1)}, bf16[1024,1024]{1,0:T(8,128)(2,1)}, u32[]{:S(2)}) %copy-start.1) | copy-done | bytes 2097176
  22.1 1.2 %shard_map.147.own_ref = bf16[256,1024]{1,0:T(8,128)(2,1)S(1)} custom-call(bf16[1024,1024]{1,0:T(8,128)(2,1)S(1)} %copy-done.1, bf16[1024,1024]{1,0:T(8,128)(2,1)S(1)} %copy-done, bf16[256,1024]{1,0:T(8,128)(2,1)S(1)} %copy-done.7), custom_call_target="tpu_custom_call" | custom-call | tf_op jit(solution)/shard_map/pallas_call | solution.py:380
  23.4 0.0 copy-start.3
  23.4 0.0 copy-start.16
  23.4 1.5 %collective-permute-done.x_ref = bf16[256,1024]{1,0:T(8,128)(2,1)} collective-permute-done((bf16[256,1024]{1,0:T(8,128)(2,1)}, bf16[256,1024]{1,0:T(8,128)(2,1)}, u32[]{:S(2)}, u32[]{:S(2)}) %collective-permute-start) | collective-permute-done | bytes 524320 | tf_op jit(solution)/shard_map/ppermute | solution.py:401
  24.9 2.2 %shard_map.148 = (f32[128,1024]{1,0:T(8,128)S(1)}, bf16[128,1024]{1,0:T(8,128)(2,1)}, bf16[128,1024]{1,0:T(8,128)(2,1)}) custom-call(bf16[256,1024]{1,0:T(8,128)(2,1)S(1)} %shard_map.147.own_ref, bf16[256,1024]{1,0:T(8,128)(2,1)} %collective-permute-done.x_ref, bf16[256,1024]{1,0:T(8,128)(2,1)} %collective-permute-done.1.up_ref, ...), custom_call_target="tpu_custom_call" | custom-call | tf_op jit(solution)/shard_map/pallas_call | solution.py:380
  27.1 0.8 copy-done.9
  27.9 1.2 %collective-permute-start.4 = (bf16[128,1024]{1,0:T(8,128)(2,1)}, bf16[128,1024]{1,0:T(8,128)(2,1)}, u32[]{:S(2)}, u32[]{:S(2)}) collective-permute-start(bf16[128,1024]{1,0:T(8,128)(2,1)} %get-tuple-element.44), channel_id=1, source_target_pairs={{0,64},{16,80},{32,96},{48,112},{64,0},{80,16},{96,32},{112,48},{1... | collective-permute-start | bytes 786440 | tf_op jit(solution)/shard_map/ppermute | solution.py:401
  29.1 1.2 %collective-permute-start.3 = (bf16[128,1024]{1,0:T(8,128)(2,1)}, bf16[128,1024]{1,0:T(8,128)(2,1)}, u32[]{:S(2)}, u32[]{:S(2)}) collective-permute-start(bf16[128,1024]{1,0:T(8,128)(2,1)} %get-tuple-element.43.refs_5_), channel_id=1, source_target_pairs={{0,32},{16,48},{32,0},{48,16},{64,96},{80,112},{96,64},{112,80},{1... | collective-permute-start | bytes 786440 | tf_op jit(solution)/shard_map/ppermute | solution.py:401
  30.3 3.6 %all-to-all-done = bf16[16,16,1024]{2,1,0:T(8,128)(2,1)} async-done(((bf16[16,16,1024]{2,1,0:T(8,128)(2,1)}), bf16[16,16,1024]{2,1,0:T(8,128)(2,1)}, u32[]{:S(2)}, u32[]{:S(2)}) %all-to-all-start) | async-done | bytes 524320 | tf_op jit(solution)/shard_map/all_to_all | solution.py:397
  33.9 1.2 %copy-done.5 = bf16[1040,512]{1,0:T(8,128)(2,1)S(1)} copy-done((bf16[1040,512]{1,0:T(8,128)(2,1)S(1)}, bf16[1040,512]{1,0:T(8,128)(2,1)}, u32[]{:S(2)}) %copy-start.5) | copy-done | bytes 1064984
  35.1 1.2 %copy-done.17 = bf16[512,1024]{1,0:T(8,128)(2,1)S(1)} copy-done((bf16[512,1024]{1,0:T(8,128)(2,1)S(1)}, bf16[512,1024]{1,0:T(8,128)(2,1)}, u32[]{:S(2)}) %copy-start.17) | copy-done | bytes 1048600
  36.3 4.2 %shard_map.150 = (bf16[128,1024]{1,0:T(8,128)(2,1)S(1)}, bf16[1040,256]{1,0:T(8,128)(2,1)S(1)}) custom-call(bf16[256,1024]{1,0:T(8,128)(2,1)} %bitcast.1.refs_0_, bf16[1040,512]{1,0:T(8,128)(2,1)S(1)} %copy-done.5, bf16[512,256]{1,0:T(8,128)(2,1)S(1)} %copy-done.16, f32[1040,256]{1,0:T(8,128)S(1)} %copy-done.3, bf16[512,1024]{1,0:T(8,128)(2,1)S(1)} %copy-done.17, ...), custom_call_target="tpu_custom_call" | custom-call | tf_op jit(solution)/shard_map/pallas_call | solution.py:380
  40.6 0.0 copy-start.19
  40.6 2.4 %shard_map.151.refs_1_ = bf16[256,1024]{1,0:T(8,128)(2,1)} custom-call(f32[128,1024]{1,0:T(8,128)S(1)} %copy-done.10, bf16[128,1024]{1,0:T(8,128)(2,1)} %collective-permute-done.3.refs_1_, bf16[128,1024]{1,0:T(8,128)(2,1)} %collective-permute-done.4.refs_2_, bf16[1024,128]{1,0:T(8,128)(2,1)S(1)} %copy-done.18, bf16[128,1024]{1,0:T(8,128)(2,1)S(1)} %get-tuple-element.45.refs_4_), custom_call_target="tpu_custom_call" | custom-call | tf_op jit(solution)/shard_map/pallas_call | solution.py:380
  43.0 0.1 collective-permute-start.6
  43.1 3.7 %all-to-all-start.1 = ((bf16[16,16,1024]{2,1,0:T(8,128)(2,1)}), bf16[16,16,1024]{2,1,0:T(8,128)(2,1)S(1)}, u32[]{:S(2)}, u32[]{:S(2)}) async-start(bf16[16,16,1024]{2,1,0:T(8,128)(2,1)} %bitcast.2), calls=%async_computation.1 | async-start | bytes 1048576 | tf_op jit(solution)/shard_map/all_to_all | solution.py:397
  46.8 0.2 shard_map.152
  47.1 0.5 collective-permute-start.5
  47.5 1.0 collective-permute-done.5.refs_2_
  48.5 10.7 %all-to-all-done.1 = bf16[16,16,1024]{2,1,0:T(8,128)(2,1)S(1)} async-done(((bf16[16,16,1024]{2,1,0:T(8,128)(2,1)}), bf16[16,16,1024]{2,1,0:T(8,128)(2,1)S(1)}, u32[]{:S(2)}, u32[]{:S(2)}) %all-to-all-start.1) | async-done | bytes 524320 | tf_op jit(solution)/shard_map/all_to_all | solution.py:397
  59.2 0.3 shard_map.153
  59.5 2.0 %collective-permute-start.9 = (bf16[128,1024]{1,0:T(8,128)(2,1)S(1)}, bf16[128,1024]{1,0:T(8,128)(2,1)S(1)}, u32[]{:S(2)}, u32[]{:S(2)}) collective-permute-start(bf16[128,1024]{1,0:T(8,128)(2,1)S(1)} %get-tuple-element.50.refs_0_), channel_id=1, source_target_pairs={{0,48},{16,0},{32,16},{48,32},{64,112},{80,64},{96,80},{112,96},{1... | collective-permute-start | bytes 786440 | tf_op jit(solution)/shard_map/ppermute | solution.py:401
  61.5 0.1 collective-permute-start.8
  61.6 0.6 collective-permute-start.7
  62.2 1.8 %collective-permute-start.12 = (bf16[128,1024]{1,0:T(8,128)(2,1)S(1)}, bf16[128,1024]{1,0:T(8,128)(2,1)S(1)}, u32[]{:S(2)}, u32[]{:S(2)}) collective-permute-start(bf16[128,1024]{1,0:T(8,128)(2,1)S(1)} %get-tuple-element.50.refs_0_), channel_id=1, source_target_pairs={{0,32},{16,48},{32,0},{48,16},{64,96},{80,112},{96,64},{112,80},{1... | collective-permute-start | bytes 786440 | tf_op jit(solution)/shard_map/ppermute | solution.py:401
  64.0 1.2 %copy-done.15 = bf16[512,1024]{1,0:T(8,128)(2,1)S(1)} copy-done((bf16[512,1024]{1,0:T(8,128)(2,1)S(1)}, bf16[512,1024]{1,0:T(8,128)(2,1)}, u32[]{:S(2)}) %copy-start.15) | copy-done | bytes 1048600
  65.2 2.5 %shard_map.154 = (bf16[64,1024]{1,0:T(8,128)(2,1)S(1)}, bf16[64,1024]{1,0:T(8,128)(2,1)S(1)}) custom-call(bf16[256,1024]{1,0:T(8,128)(2,1)S(1)} %bitcast.7, bf16[1040,256]{1,0:T(8,128)(2,1)S(1)} %copy-done.21, bf16[1040,512]{1,0:T(8,128)(2,1)S(1)} %copy-done.6, bf16[512,256]{1,0:T(8,128)(2,1)S(1)} %copy-done.16, f32[1040,256]{1,0:T(8,128)S(1)} %copy-done.4, ...), custom_call_target="tpu_custom_call" | custom-call | tf_op jit(solution)/shard_map/pallas_call | solution.py:380
  67.7 4.5 %collective-permute-done.9.refs_3_ = bf16[128,1024]{1,0:T(8,128)(2,1)S(1)} collective-permute-done((bf16[128,1024]{1,0:T(8,128)(2,1)S(1)}, bf16[128,1024]{1,0:T(8,128)(2,1)S(1)}, u32[]{:S(2)}, u32[]{:S(2)}) %collective-permute-start.9) | collective-permute-done | bytes 262176 | tf_op jit(solution)/shard_map/ppermute | solution.py:401
  72.2 3.4 %collective-permute-done.8.refs_2_ = bf16[128,1024]{1,0:T(8,128)(2,1)S(1)} collective-permute-done((bf16[128,1024]{1,0:T(8,128)(2,1)S(1)}, bf16[128,1024]{1,0:T(8,128)(2,1)S(1)}, u32[]{:S(2)}, u32[]{:S(2)}) %collective-permute-start.8) | collective-permute-done | bytes 262176 | tf_op jit(solution)/shard_map/ppermute | solution.py:401
  75.6 0.6 collective-permute-start.13
  76.2 0.4 collective-permute-start.11
  76.6 1.7 %collective-permute-start.10 = (bf16[128,1024]{1,0:T(8,128)(2,1)S(1)}, bf16[128,1024]{1,0:T(8,128)(2,1)S(1)}, u32[]{:S(2)}, u32[]{:S(2)}) collective-permute-start(bf16[128,1024]{1,0:T(8,128)(2,1)S(1)} %collective-permute-done.7.refs_1_), channel_id=1, source_target_pairs={{0,16},{16,32},{32,48},{48,0},{64,80},{80,96},{96,112},{112,64},{1... | collective-permute-start | bytes 786440 | tf_op jit(solution)/shard_map/ppermute | solution.py:401
  78.2 2.9 %shard_map.155 = (bf16[640,1024]{1,0:T(8,128)(2,1)S(1)}, bf16[256,1024]{1,0:T(8,128)(2,1)S(1)}) custom-call(bf16[128,1024]{1,0:T(8,128)(2,1)S(1)} %get-tuple-element.50.refs_0_, bf16[128,1024]{1,0:T(8,128)(2,1)S(1)} %collective-permute-done.7.refs_1_, bf16[128,1024]{1,0:T(8,128)(2,1)S(1)} %collective-permute-done.8.refs_2_, ...), custom_call_target="tpu_custom_call" | custom-call | tf_op jit(solution)/shard_map/pallas_call | solution.py:380
  81.1 0.6 collective-permute-start.14
  81.7 0.3 collective-permute-done.13.refs_3_.refs_7_
  82.0 0.6 collective-permute-done.11.refs_1_.refs_5_
  82.6 1.6 %collective-permute-done.10.refs_0_.refs_4_ = bf16[128,1024]{1,0:T(8,128)(2,1)S(1)} collective-permute-done((bf16[128,1024]{1,0:T(8,128)(2,1)S(1)}, bf16[128,1024]{1,0:T(8,128)(2,1)S(1)}, u32[]{:S(2)}, u32[]{:S(2)}) %collective-permute-start.10) | collective-permute-done | bytes 262176 | tf_op jit(solution)/shard_map/ppermute | solution.py:401
  84.2 3.6 %shard_map.156 = (bf16[160,1024]{1,0:T(8,128)(2,1)S(1)}, bf16[160,1024]{1,0:T(8,128)(2,1)S(1)}, bf16[160,1024]{1,0:T(8,128)(2,1)S(1)}, bf16[160,1024]{1,0:T(8,128)(2,1)S(1)}, bf16[256,1024]{1,0:T(8,128)(2,1)S(1)}) custom-call(bf16[128,1024]{1,0:T(8,128)(2,1)S(1)} %collective-permute-done.10.refs_0_.refs_4_, ...), custom_call_target="tpu_custom_call" | custom-call | tf_op jit(solution)/shard_map/pallas_call | solution.py:380
  87.8 0.1 collective-permute-start.16
  87.8 0.5 collective-permute-start.17
  88.3 2.3 %collective-permute-start.18 = (bf16[160,1024]{1,0:T(8,128)(2,1)S(1)}, bf16[160,1024]{1,0:T(8,128)(2,1)S(1)}, u32[]{:S(2)}, u32[]{:S(2)}) collective-permute-start(bf16[160,1024]{1,0:T(8,128)(2,1)S(1)} %get-tuple-element.63), channel_id=1, source_target_pairs={{0,2},{1,3},{2,0},{3,1},{4,6},{5,7},{6,4},{7,5},{8,10},{9,11},{10,... | collective-permute-start | bytes 983048 | tf_op jit(solution)/shard_map/ppermute | solution.py:540
  90.7 1.0 collective-permute-start.19
  91.6 2.3 %collective-permute-start.20 = (bf16[160,1024]{1,0:T(8,128)(2,1)S(1)}, bf16[160,1024]{1,0:T(8,128)(2,1)S(1)}, u32[]{:S(2)}, u32[]{:S(2)}) collective-permute-start(bf16[160,1024]{1,0:T(8,128)(2,1)S(1)} %get-tuple-element.65), channel_id=1, source_target_pairs={{0,12},{1,13},{2,14},{3,15},{4,0},{5,1},{6,2},{7,3},{8,4},{9,5},{1... | collective-permute-start | bytes 983048 | tf_op jit(solution)/shard_map/ppermute | solution.py:541
  93.9 2.1 %shard_map.158.refs_7_ = bf16[1024,128]{1,0:T(8,128)(2,1)} custom-call(f32[128,1024]{1,0:T(8,128)S(1)} %copy-done.11, bf16[128,1024]{1,0:T(8,128)(2,1)} %collective-permute-done.3.refs_1_, bf16[128,1024]{1,0:T(8,128)(2,1)} %collective-permute-done.4.refs_2_, bf16[256,1024]{1,0:T(8,128)(2,1)S(1)} %bitcast.8, bf16[64,1024]{1,0:T(8,128)(2,1)S(1)} %collective-permute-done.17.refs_4_), custom_call_target="tpu_custom_call" | custom-call | tf_op jit(solution)/shard_map/pallas_call | solution.py:380
  96.0 3.5 %collective-permute-done.18.x_ref = bf16[160,1024]{1,0:T(8,128)(2,1)S(1)} collective-permute-done((bf16[160,1024]{1,0:T(8,128)(2,1)S(1)}, bf16[160,1024]{1,0:T(8,128)(2,1)S(1)}, u32[]{:S(2)}, u32[]{:S(2)}) %collective-permute-start.18) | collective-permute-done | bytes 327712 | tf_op jit(solution)/shard_map/ppermute | solution.py:540
  99.6 1.8 %collective-permute-done.19.up_ref = bf16[160,1024]{1,0:T(8,128)(2,1)S(1)} collective-permute-done((bf16[160,1024]{1,0:T(8,128)(2,1)S(1)}, bf16[160,1024]{1,0:T(8,128)(2,1)S(1)}, u32[]{:S(2)}, u32[]{:S(2)}) %collective-permute-start.19) | collective-permute-done | bytes 327712 | tf_op jit(solution)/shard_map/ppermute | solution.py:541
  101.3 0.1 shard_map.159
  101.4 1.5 %collective-permute-start.21 = (bf16[96,1024]{1,0:T(8,128)(2,1)S(1)}, bf16[96,1024]{1,0:T(8,128)(2,1)S(1)}, u32[]{:S(2)}, u32[]{:S(2)}) collective-permute-start(bf16[96,1024]{1,0:T(8,128)(2,1)S(1)} %get-tuple-element.67), channel_id=1, source_target_pairs={{0,8},{1,9},{2,10},{3,11},{4,12},{5,13},{6,14},{7,15},{8,0},{9,1},... | collective-permute-start | bytes 589832 | tf_op jit(solution)/shard_map/ppermute | solution.py:541
  103.0 1.2 %collective-permute-start.22 = (bf16[96,1024]{1,0:T(8,128)(2,1)S(1)}, bf16[96,1024]{1,0:T(8,128)(2,1)S(1)}, u32[]{:S(2)}, u32[]{:S(2)}) collective-permute-start(bf16[96,1024]{1,0:T(8,128)(2,1)S(1)} %get-tuple-element.68), channel_id=1, source_target_pairs={{0,2},{1,3},{2,0},{3,1},{4,6},{5,7},{6,4},{7,5},{8,10},{9,11},{10,... | collective-permute-start | bytes 589832 | tf_op jit(solution)/shard_map/ppermute | solution.py:540
  104.2 3.2 %shard_map.157 = bf16[1024,1024]{1,0:T(8,128)(2,1)S(1)} custom-call(bf16[128,1024]{1,0:T(8,128)(2,1)S(1)} %get-tuple-element.50.refs_0_, bf16[128,1024]{1,0:T(8,128)(2,1)S(1)} %collective-permute-done.7.refs_1_, bf16[128,1024]{1,0:T(8,128)(2,1)S(1)} %collective-permute-done.8.refs_2_, bf16[128,1024]{1,0:T(8,128)(2,1)S(1)} %collective-permute-done.9.refs_3_, ...), custom_call_target="tpu_custom_call" | custom-call | tf_op jit(solution)/shard_map/pallas_call | solution.py:380
  107.4 0.0 copy-start.12
  107.5 0.0 copy-start.13
  107.5 0.0 copy-start.14
  107.5 2.4 %convolution_convert_fusion.refs_6_ = bf16[1024,1024]{1,0:T(8,128)(2,1)S(1)} fusion(bf16[1024,1024]{1,0:T(8,128)(2,1)S(1)} %shard_map.157, bf16[1024,1024]{1,0:T(8,128)(2,1)S(1)} %copy-done.2), kind=kOutput, calls=%fused_computation | convolution fusion | flops 2148532224 | bytes 6291456 | tf_op jit(solution)/shard_map/dot_general | solution.py:558
  109.9 0.2 collective-permute-done.22.refs_2_
  110.2 1.3 %shard_map.160 = (f32[64,1024]{1,0:T(8,128)}, bf16[1024,128]{1,0:T(8,128)(2,1)}, bf16[1024,128]{1,0:T(8,128)(2,1)}) custom-call(f32[64,1024]{1,0:T(8,128)S(1)} %get-tuple-element.66.refs_0_, bf16[96,1024]{1,0:T(8,128)(2,1)S(1)} %collective-permute-done.21.refs_1_, bf16[96,1024]{1,0:T(8,128)(2,1)S(1)} %collective-permute-done.22.refs_2_, ...), custom_call_target="tpu_custom_call" | custom-call | tf_op jit(solution)/shard_map/pallas_call | solution.py:380
  (46 shorter events, 0.1 us)
Async XLA Ops:
  5.6 14.9 %copy-start = (bf16[1024,1024]{1,0:T(8,128)(2,1)S(1)}, bf16[1024,1024]{1,0:T(8,128)(2,1)}, u32[]{:S(2)}) copy-start(bf16[1024,1024]{1,0:T(8,128)(2,1)} %refs_4_.5) | copy-start | bytes 6291460
  5.6 14.9 %copy-start.7 = (bf16[256,1024]{1,0:T(8,128)(2,1)S(1)}, bf16[256,1024]{1,0:T(8,128)(2,1)}, u32[]{:S(2)}) copy-start(bf16[256,1024]{1,0:T(8,128)(2,1)} %get-tuple-element.39.refs_2_.refs_3_) | copy-start | bytes 1572868
  5.6 17.8 %collective-permute-start.1 = (bf16[256,1024]{1,0:T(8,128)(2,1)}, bf16[256,1024]{1,0:T(8,128)(2,1)}, u32[]{:S(2)}, u32[]{:S(2)}) collective-permute-start(bf16[256,1024]{1,0:T(8,128)(2,1)} %get-tuple-element.40), channel_id=1, source_target_pairs={{0,16},{16,32},{32,48},{48,0},{64,80},{80,96},{96,112},{112,64},{1... | collective-permute-start | bytes 1572872 | tf_op jit(solution)/shard_map/ppermute | solution.py:401
  7.7 15.7 %collective-permute-start.2 = (bf16[256,1024]{1,0:T(8,128)(2,1)}, bf16[256,1024]{1,0:T(8,128)(2,1)}, u32[]{:S(2)}, u32[]{:S(2)}) collective-permute-start(bf16[256,1024]{1,0:T(8,128)(2,1)} %get-tuple-element.41), channel_id=1, source_target_pairs={{0,48},{16,0},{32,16},{48,32},{64,112},{80,64},{96,80},{112,96},{1... | collective-permute-start | bytes 1572872 | tf_op jit(solution)/shard_map/ppermute | solution.py:401
  9.9 15.0 %collective-permute-start = (bf16[256,1024]{1,0:T(8,128)(2,1)}, bf16[256,1024]{1,0:T(8,128)(2,1)}, u32[]{:S(2)}, u32[]{:S(2)}) collective-permute-start(bf16[256,1024]{1,0:T(8,128)(2,1)} %get-tuple-element.39.refs_2_.refs_3_), channel_id=1, source_target_pairs={{0,64},{16,80},{32,96},{48,112},{64,0},{80,16},{96,32},{112,48},{1... | collective-permute-start | bytes 1572872 | tf_op jit(solution)/shard_map/ppermute | solution.py:401
  13.7 20.2 %all-to-all-start = ((bf16[16,16,1024]{2,1,0:T(8,128)(2,1)}), bf16[16,16,1024]{2,1,0:T(8,128)(2,1)}, u32[]{:S(2)}, u32[]{:S(2)}) async-start(bf16[16,16,1024]{2,1,0:T(8,128)(2,1)} %bitcast.9), calls=%async_computation | async-start | bytes 1048576 | tf_op jit(solution)/shard_map/all_to_all | solution.py:397
  20.5 1.6 %copy-start.1 = (bf16[1024,1024]{1,0:T(8,128)(2,1)S(1)}, bf16[1024,1024]{1,0:T(8,128)(2,1)}, u32[]{:S(2)}) copy-start(bf16[1024,1024]{1,0:T(8,128)(2,1)} %refs_0_.3) | copy-start | bytes 6291460
  23.4 10.5 %copy-start.3 = (f32[1040,256]{1,0:T(8,128)S(1)}, f32[1040,256]{1,0:T(8,128)}, u32[]{:S(2)}) copy-start(f32[1040,256]{1,0:T(8,128)} %constant.12.clone.refs_3_.twiddle_ref) | copy-start | bytes 3194884
  23.4 10.5 %copy-start.16 = (bf16[512,256]{1,0:T(8,128)(2,1)S(1)}, bf16[512,256]{1,0:T(8,128)(2,1)}, u32[]{:S(2)}) copy-start(bf16[512,256]{1,0:T(8,128)(2,1)} %constant.11.clone.refs_2_.square_ref) | copy-start | bytes 786436
  27.1 0.8 copy-start.9
  27.9 12.7 %collective-permute-start.4 = (bf16[128,1024]{1,0:T(8,128)(2,1)}, bf16[128,1024]{1,0:T(8,128)(2,1)}, u32[]{:S(2)}, u32[]{:S(2)}) collective-permute-start(bf16[128,1024]{1,0:T(8,128)(2,1)} %get-tuple-element.44), channel_id=1, source_target_pairs={{0,64},{16,80},{32,96},{48,112},{64,0},{80,16},{96,32},{112,48},{1... | collective-permute-start | bytes 786440 | tf_op jit(solution)/shard_map/ppermute | solution.py:401
  29.1 11.5 %collective-permute-start.3 = (bf16[128,1024]{1,0:T(8,128)(2,1)}, bf16[128,1024]{1,0:T(8,128)(2,1)}, u32[]{:S(2)}, u32[]{:S(2)}) collective-permute-start(bf16[128,1024]{1,0:T(8,128)(2,1)} %get-tuple-element.43.refs_5_), channel_id=1, source_target_pairs={{0,32},{16,48},{32,0},{48,16},{64,96},{80,112},{96,64},{112,80},{1... | collective-permute-start | bytes 786440 | tf_op jit(solution)/shard_map/ppermute | solution.py:401
  33.9 1.2 %copy-start.5 = (bf16[1040,512]{1,0:T(8,128)(2,1)S(1)}, bf16[1040,512]{1,0:T(8,128)(2,1)}, u32[]{:S(2)}) copy-start(bf16[1040,512]{1,0:T(8,128)(2,1)} %constant.10.clone.refs_1_.first_ref) | copy-start | bytes 3194884
  35.1 1.2 %copy-start.17 = (bf16[512,1024]{1,0:T(8,128)(2,1)S(1)}, bf16[512,1024]{1,0:T(8,128)(2,1)}, u32[]{:S(2)}) copy-start(bf16[512,1024]{1,0:T(8,128)(2,1)} %constant.13.clone.refs_4_) | copy-start | bytes 3145732
  36.3 4.3 %copy-start.10 = (f32[128,1024]{1,0:T(8,128)S(1)}, f32[128,1024]{1,0:T(8,128)}, u32[]{:S(2)}) copy-start(f32[128,1024]{1,0:T(8,128)} %copy-done.9) | copy-start | bytes 1572868
  36.3 4.3 %copy-start.18 = (bf16[1024,128]{1,0:T(8,128)(2,1)S(1)}, bf16[1024,128]{1,0:T(8,128)(2,1)}, u32[]{:S(2)}) copy-start(bf16[1024,128]{1,0:T(8,128)(2,1)} %refs_0_.5) | copy-start | bytes 786436
  40.6 2.5 %copy-start.20 = (bf16[1040,256]{1,0:T(8,128)(2,1)}, bf16[1040,256]{1,0:T(8,128)(2,1)S(1)}, u32[]{:S(2)}) copy-start(bf16[1040,256]{1,0:T(8,128)(2,1)S(1)} %get-tuple-element.51.h_ref) | copy-start | bytes 1597444
  40.6 6.3 %copy-start.19 = (bf16[1024,128]{1,0:T(8,128)(2,1)S(1)}, bf16[1024,128]{1,0:T(8,128)(2,1)}, u32[]{:S(2)}) copy-start(bf16[1024,128]{1,0:T(8,128)(2,1)} %refs_0_.5) | copy-start | bytes 786436
  43.0 16.2 %collective-permute-start.6 = (bf16[1024,1024]{1,0:T(8,128)(2,1)S(1)}, bf16[1024,1024]{1,0:T(8,128)(2,1)}, u32[]{:S(2)}, u32[]{:S(2)}) collective-permute-start(bf16[1024,1024]{1,0:T(8,128)(2,1)S(1)} %copy-done), channel_id=1, source_target_pairs={{0,1},{1,0},{2,3},{3,2},{4,5},{5,4},{6,7},{7,6},{8,9},{9,8},{10,11... | collective-permute-start | bytes 6291464 | tf_op jit(solution)/shard_map/ppermute | solution.py:462
  43.1 16.1 %all-to-all-start.1 = ((bf16[16,16,1024]{2,1,0:T(8,128)(2,1)}), bf16[16,16,1024]{2,1,0:T(8,128)(2,1)S(1)}, u32[]{:S(2)}, u32[]{:S(2)}) async-start(bf16[16,16,1024]{2,1,0:T(8,128)(2,1)} %bitcast.2), calls=%async_computation.1 | async-start | bytes 1048576 | tf_op jit(solution)/shard_map/all_to_all | solution.py:397
  47.1 1.5 %collective-permute-start.5 = (bf16[64,1024]{1,0:T(8,128)(2,1)S(1)}, bf16[64,1024]{1,0:T(8,128)(2,1)S(1)}, u32[]{:S(2)}, u32[]{:S(2)}) collective-permute-start(bf16[64,1024]{1,0:T(8,128)(2,1)S(1)} %get-tuple-element.48), channel_id=1, source_target_pairs={{0,1},{1,0},{2,3},{3,2},{4,5},{5,4},{6,7},{7,6},{8,9},{9,8},{10,11... | collective-permute-start | bytes 393224 | tf_op jit(solution)/shard_map/ppermute | solution.py:462
  59.2 4.8 %copy-start.4 = (f32[1040,256]{1,0:T(8,128)S(1)}, f32[1040,256]{1,0:T(8,128)}, u32[]{:S(2)}) copy-start(f32[1040,256]{1,0:T(8,128)} %constant.12.clone.refs_3_.twiddle_ref) | copy-start | bytes 3194884
  59.2 4.8 %copy-start.6 = (bf16[1040,512]{1,0:T(8,128)(2,1)S(1)}, bf16[1040,512]{1,0:T(8,128)(2,1)}, u32[]{:S(2)}) copy-start(bf16[1040,512]{1,0:T(8,128)(2,1)} %constant.10.clone.refs_1_.first_ref) | copy-start | bytes 3194884
  59.2 4.8 %copy-start.21 = (bf16[1040,256]{1,0:T(8,128)(2,1)S(1)}, bf16[1040,256]{1,0:T(8,128)(2,1)}, u32[]{:S(2)}) copy-start(bf16[1040,256]{1,0:T(8,128)(2,1)} %copy-done.20) | copy-start | bytes 1597444
  59.5 12.7 %collective-permute-start.9 = (bf16[128,1024]{1,0:T(8,128)(2,1)S(1)}, bf16[128,1024]{1,0:T(8,128)(2,1)S(1)}, u32[]{:S(2)}, u32[]{:S(2)}) collective-permute-start(bf16[128,1024]{1,0:T(8,128)(2,1)S(1)} %get-tuple-element.50.refs_0_), channel_id=1, source_target_pairs={{0,48},{16,0},{32,16},{48,32},{64,112},{80,64},{96,80},{112,96},{1... | collective-permute-start | bytes 786440 | tf_op jit(solution)/shard_map/ppermute | solution.py:401
  61.5 14.1 %collective-permute-start.8 = (bf16[128,1024]{1,0:T(8,128)(2,1)S(1)}, bf16[128,1024]{1,0:T(8,128)(2,1)S(1)}, u32[]{:S(2)}, u32[]{:S(2)}) collective-permute-start(bf16[128,1024]{1,0:T(8,128)(2,1)S(1)} %get-tuple-element.50.refs_0_), channel_id=1, source_target_pairs={{0,16},{16,32},{32,48},{48,0},{64,80},{80,96},{96,112},{112,64},{1... | collective-permute-start | bytes 786440 | tf_op jit(solution)/shard_map/ppermute | solution.py:401
  61.6 14.0 %collective-permute-start.7 = (bf16[128,1024]{1,0:T(8,128)(2,1)S(1)}, bf16[128,1024]{1,0:T(8,128)(2,1)S(1)}, u32[]{:S(2)}, u32[]{:S(2)}) collective-permute-start(bf16[128,1024]{1,0:T(8,128)(2,1)S(1)} %get-tuple-element.50.refs_0_), channel_id=1, source_target_pairs={{0,64},{16,80},{32,96},{48,112},{64,0},{80,16},{96,32},{112,48},{1... | collective-permute-start | bytes 786440 | tf_op jit(solution)/shard_map/ppermute | solution.py:401
  62.2 13.4 %collective-permute-start.12 = (bf16[128,1024]{1,0:T(8,128)(2,1)S(1)}, bf16[128,1024]{1,0:T(8,128)(2,1)S(1)}, u32[]{:S(2)}, u32[]{:S(2)}) collective-permute-start(bf16[128,1024]{1,0:T(8,128)(2,1)S(1)} %get-tuple-element.50.refs_0_), channel_id=1, source_target_pairs={{0,32},{16,48},{32,0},{48,16},{64,96},{80,112},{96,64},{112,80},{1... | collective-permute-start | bytes 786440 | tf_op jit(solution)/shard_map/ppermute | solution.py:401
  64.0 1.2 %copy-start.15 = (bf16[512,1024]{1,0:T(8,128)(2,1)S(1)}, bf16[512,1024]{1,0:T(8,128)(2,1)}, u32[]{:S(2)}) copy-start(bf16[512,1024]{1,0:T(8,128)(2,1)} %constant.14.clone.last_ref) | copy-start | bytes 3145732
  75.6 6.4 %collective-permute-start.13 = (bf16[128,1024]{1,0:T(8,128)(2,1)S(1)}, bf16[128,1024]{1,0:T(8,128)(2,1)S(1)}, u32[]{:S(2)}, u32[]{:S(2)}) collective-permute-start(bf16[128,1024]{1,0:T(8,128)(2,1)S(1)} %collective-permute-done.12.refs_2_.refs_6_), channel_id=1, source_target_pairs={{0,64},{16,80},{32,96},{48,112},{64,0},{80,16},{96,32},{112,48},{1... | collective-permute-start | bytes 786440 | tf_op jit(solution)/shard_map/ppermute | solution.py:401
  76.2 6.4 %collective-permute-start.11 = (bf16[128,1024]{1,0:T(8,128)(2,1)S(1)}, bf16[128,1024]{1,0:T(8,128)(2,1)S(1)}, u32[]{:S(2)}, u32[]{:S(2)}) collective-permute-start(bf16[128,1024]{1,0:T(8,128)(2,1)S(1)} %collective-permute-done.7.refs_1_), channel_id=1, source_target_pairs={{0,48},{16,0},{32,16},{48,32},{64,112},{80,64},{96,80},{112,96},{1... | collective-permute-start | bytes 786440 | tf_op jit(solution)/shard_map/ppermute | solution.py:401
  76.6 7.6 %collective-permute-start.10 = (bf16[128,1024]{1,0:T(8,128)(2,1)S(1)}, bf16[128,1024]{1,0:T(8,128)(2,1)S(1)}, u32[]{:S(2)}, u32[]{:S(2)}) collective-permute-start(bf16[128,1024]{1,0:T(8,128)(2,1)S(1)} %collective-permute-done.7.refs_1_), channel_id=1, source_target_pairs={{0,16},{16,32},{32,48},{48,0},{64,80},{80,96},{96,112},{112,64},{1... | collective-permute-start | bytes 786440 | tf_op jit(solution)/shard_map/ppermute | solution.py:401
  78.2 3.5 %collective-permute-start.15 = (bf16[64,1024]{1,0:T(8,128)(2,1)S(1)}, bf16[64,1024]{1,0:T(8,128)(2,1)S(1)}, u32[]{:S(2)}, u32[]{:S(2)}) collective-permute-start(bf16[64,1024]{1,0:T(8,128)(2,1)S(1)} %get-tuple-element.58), channel_id=1, source_target_pairs={{0,1},{1,0},{2,3},{3,2},{4,5},{5,4},{6,7},{7,6},{8,9},{9,8},{10,11... | collective-permute-start | bytes 393224 | tf_op jit(solution)/shard_map/ppermute | solution.py:462
  81.1 23.1 %collective-permute-start.14 = (bf16[256,1024]{1,0:T(8,128)(2,1)S(1)}, bf16[256,1024]{1,0:T(8,128)(2,1)S(1)}, u32[]{:S(2)}, u32[]{:S(2)}) collective-permute-start(bf16[256,1024]{1,0:T(8,128)(2,1)S(1)} %get-tuple-element.56), channel_id=1, source_target_pairs={{0,1},{1,0},{2,3},{3,2},{4,5},{5,4},{6,7},{7,6},{8,9},{9,8},{10,11... | collective-permute-start | bytes 1572872 | tf_op jit(solution)/shard_map/ppermute | solution.py:462
  84.1 9.8 %copy-start.11 = (f32[128,1024]{1,0:T(8,128)S(1)}, f32[128,1024]{1,0:T(8,128)}, u32[]{:S(2)}) copy-start(f32[128,1024]{1,0:T(8,128)} %copy-done.9) | copy-start | bytes 1572868
  87.8 16.4 %collective-permute-start.16 = (bf16[256,1024]{1,0:T(8,128)(2,1)S(1)}, bf16[256,1024]{1,0:T(8,128)(2,1)S(1)}, u32[]{:S(2)}, u32[]{:S(2)}) collective-permute-start(bf16[256,1024]{1,0:T(8,128)(2,1)S(1)} %get-tuple-element.60), channel_id=1, source_target_pairs={{0,1},{1,0},{2,3},{3,2},{4,5},{5,4},{6,7},{7,6},{8,9},{9,8},{10,11... | collective-permute-start | bytes 1572872 | tf_op jit(solution)/shard_map/ppermute | solution.py:462
  87.8 3.8 %collective-permute-start.17 = (bf16[64,1024]{1,0:T(8,128)(2,1)S(1)}, bf16[64,1024]{1,0:T(8,128)(2,1)S(1)}, u32[]{:S(2)}, u32[]{:S(2)}) collective-permute-start(bf16[64,1024]{1,0:T(8,128)(2,1)S(1)} %get-tuple-element.61), channel_id=1, source_target_pairs={{0,1},{1,0},{2,3},{3,2},{4,5},{5,4},{6,7},{7,6},{8,9},{9,8},{10,11... | collective-permute-start | bytes 393224 | tf_op jit(solution)/shard_map/ppermute | solution.py:462
  88.3 11.2 %collective-permute-start.18 = (bf16[160,1024]{1,0:T(8,128)(2,1)S(1)}, bf16[160,1024]{1,0:T(8,128)(2,1)S(1)}, u32[]{:S(2)}, u32[]{:S(2)}) collective-permute-start(bf16[160,1024]{1,0:T(8,128)(2,1)S(1)} %get-tuple-element.63), channel_id=1, source_target_pairs={{0,2},{1,3},{2,0},{3,1},{4,6},{5,7},{6,4},{7,5},{8,10},{9,11},{10,... | collective-permute-start | bytes 983048 | tf_op jit(solution)/shard_map/ppermute | solution.py:540
  90.7 10.6 %collective-permute-start.19 = (bf16[160,1024]{1,0:T(8,128)(2,1)S(1)}, bf16[160,1024]{1,0:T(8,128)(2,1)S(1)}, u32[]{:S(2)}, u32[]{:S(2)}) collective-permute-start(bf16[160,1024]{1,0:T(8,128)(2,1)S(1)} %get-tuple-element.64), channel_id=1, source_target_pairs={{0,4},{1,5},{2,6},{3,7},{4,8},{5,9},{6,10},{7,11},{8,12},{9,13},{1... | collective-permute-start | bytes 983048 | tf_op jit(solution)/shard_map/ppermute | solution.py:541
  91.6 9.7 %collective-permute-start.20 = (bf16[160,1024]{1,0:T(8,128)(2,1)S(1)}, bf16[160,1024]{1,0:T(8,128)(2,1)S(1)}, u32[]{:S(2)}, u32[]{:S(2)}) collective-permute-start(bf16[160,1024]{1,0:T(8,128)(2,1)S(1)} %get-tuple-element.65), channel_id=1, source_target_pairs={{0,12},{1,13},{2,14},{3,15},{4,0},{5,1},{6,2},{7,3},{8,4},{9,5},{1... | collective-permute-start | bytes 983048 | tf_op jit(solution)/shard_map/ppermute | solution.py:541
  101.4 8.5 %collective-permute-start.21 = (bf16[96,1024]{1,0:T(8,128)(2,1)S(1)}, bf16[96,1024]{1,0:T(8,128)(2,1)S(1)}, u32[]{:S(2)}, u32[]{:S(2)}) collective-permute-start(bf16[96,1024]{1,0:T(8,128)(2,1)S(1)} %get-tuple-element.67), channel_id=1, source_target_pairs={{0,8},{1,9},{2,10},{3,11},{4,12},{5,13},{6,14},{7,15},{8,0},{9,1},... | collective-permute-start | bytes 589832 | tf_op jit(solution)/shard_map/ppermute | solution.py:541
  103.0 4.4 %copy-start.2 = (bf16[1024,1024]{1,0:T(8,128)(2,1)S(1)}, bf16[1024,1024]{1,0:T(8,128)(2,1)}, u32[]{:S(2)}) copy-start(bf16[1024,1024]{1,0:T(8,128)(2,1)} %refs_0_.3) | copy-start | bytes 6291460
  103.0 7.2 %collective-permute-start.22 = (bf16[96,1024]{1,0:T(8,128)(2,1)S(1)}, bf16[96,1024]{1,0:T(8,128)(2,1)S(1)}, u32[]{:S(2)}, u32[]{:S(2)}) collective-permute-start(bf16[96,1024]{1,0:T(8,128)(2,1)S(1)} %get-tuple-element.68), channel_id=1, source_target_pairs={{0,2},{1,3},{2,0},{3,1},{4,6},{5,7},{6,4},{7,5},{8,10},{9,11},{10,... | collective-permute-start | bytes 589832 | tf_op jit(solution)/shard_map/ppermute | solution.py:540
  107.4 2.7 %copy-start.12 = (bf16[1024,128]{1,0:T(8,128)(2,1)S(1)}, bf16[1024,128]{1,0:T(8,128)(2,1)}, u32[]{:S(2)}) copy-start(bf16[1024,128]{1,0:T(8,128)(2,1)} %refs_4_.6) | copy-start | bytes 786436
  107.5 2.7 %copy-start.13 = (bf16[1024,128]{1,0:T(8,128)(2,1)S(1)}, bf16[1024,128]{1,0:T(8,128)(2,1)}, u32[]{:S(2)}) copy-start(bf16[1024,128]{1,0:T(8,128)(2,1)} %refs_5_.1) | copy-start | bytes 786436
  107.5 2.7 %copy-start.14 = (bf16[1024,128]{1,0:T(8,128)(2,1)S(1)}, bf16[1024,128]{1,0:T(8,128)(2,1)}, u32[]{:S(2)}) copy-start(bf16[1024,128]{1,0:T(8,128)(2,1)} %shard_map.158.refs_7_) | copy-start | bytes 786436
  109.9 1.6 %copy-start.8 = (bf16[1024,1024]{1,0:T(8,128)(2,1)}, bf16[1024,1024]{1,0:T(8,128)(2,1)S(1)}, u32[]{:S(2)}) copy-start(bf16[1024,1024]{1,0:T(8,128)(2,1)S(1)} %convolution_convert_fusion.refs_6_) | copy-start | bytes 6291460

commit v8 on v7

--- a/solution.py
+++ b/solution.py
@@ -1,6 +1,5 @@
 import functools
 import math
-import typing
 
 import jax
 import jax.numpy as jnp
@@ -29,20 +28,15 @@
 def host_tables(ways, group):
     k2, t1 = np.arange(HALF), np.arange(FAC)
     t2 = (np.arange(LANE_TILES)[:, None] + LANE_TILES * np.arange(ways)[None, :]).reshape(-1)
-    eye = np.eye(group)
     a = angles(k2, t2, QF)
     steps = np.stack([np.cos(a), -np.sin(a)])
-    first = np.einsum("rkt,cd->rkctd", steps, eye).reshape(2 * HALF * group, t2.size * group)
-    weight = np.where((k2 == 0) | (k2 == QF // 2), 1.0, 2.0) / (QF * FAC)
-    b = angles(t2, k2, QF)
-    back = np.concatenate([np.cos(b) * weight, (-np.sin(b) * weight)[:, 1:-1]], axis=1)
-    last = np.einsum("tk,cd->tckd", back, eye).reshape(t2.size * group, -1)
+    first = np.einsum("rkt,cd->rkctd", steps, np.eye(group)).reshape(2 * HALF * group, t2.size * group)
     s = angles(t1, t1, FAC)
     square = np.concatenate([np.cos(s), np.sin(s)])
     w = angles(k2, t1, QF * FAC)
-    twiddle = np.concatenate([np.repeat(f(w), group, axis=0) for f in (np.cos, np.sin)]).astype(np.float32)
+    twiddle = np.concatenate([np.cos(w), np.sin(w)]).astype(np.float32)
     as_bf = lambda v: np.asarray(v, np.float32).astype(BF)
-    return as_bf(first), as_bf(square), twiddle, as_bf(last)
+    return as_bf(first), as_bf(square), twiddle
 
 
 def params(mib):
@@ -105,7 +99,7 @@
     return (slot == column).astype(F32).astype(BF)
 
 
-def dy_kernel(step, moves, w_hbm, d_hbm, *refs):
+def dy_kernel(step, moves, between, w_hbm, d_hbm, *refs):
     outs, (w_ref, d_ref, p_ref, w_sem, d_sem, o_sem) = refs[:-6], refs[-6:]
     me = lax.axis_index("fsdp")
     n = outs[0].shape[0] // 2
@@ -117,7 +111,8 @@
     loads = [
         pltpu.make_async_copy(d_hbm.at[rows, :], d_ref.at[rows, :], d_sem.at[i]) for i, rows in enumerate(pieces)
     ]
-    for copy in (*gather, loads[0]):
+    other_loads, other_work, other_stores = between or ((), None, ())
+    for copy in (*gather, loads[0], *other_loads):
         copy.start()
     for copy in gather:
         copy.wait()
@@ -133,17 +128,33 @@
             )
             store.start()
             stores.append(store)
+        if i == 0 and other_work:
+            for copy in other_loads:
+                copy.wait()
+            other_work()
+            for copy in other_stores:
+                copy.start()
+                stores.append(copy)
     for store in stores:
         store.wait()
 
 
-def prep_kernel(k_ref, v_ref, f_ref, send_ref):
-    width = k_ref.shape[1]
-    ways = send_ref.shape[0] // (2 * 8)
-    order = order_in(ways, width)
-    mixed = (k_ref[...].astype(F32) * v_ref[...].astype(F32)).astype(BF)
-    parts = [product_t(order, x).reshape(ways, 1, -1, ROW) for x in (mixed, f_ref[...])]
-    send_ref[...] = jnp.concatenate(parts, axis=1).reshape(send_ref.shape).astype(BF)
+def open_kernel(step, moves, w_hbm, d_hbm, k_hbm, v_hbm, f_hbm, *refs):
+    count = len(moves) // 2
+    outs, send_hbm, (k_ref, v_ref, f_ref, send_ref, sem), refs = refs[:count], refs[count], refs[-5:], refs[count + 1 : -5]
+    froms = zip((k_hbm, v_hbm, f_hbm), (k_ref, v_ref, f_ref))
+    loads = [pltpu.make_async_copy(x, to, sem.at[i]) for i, (x, to) in enumerate(froms)]
+
+    def mix():
+        width = k_ref.shape[1]
+        ways = send_ref.shape[0] // (2 * 8)
+        order = order_in(ways, width)
+        mixed = (k_ref[...].astype(F32) * v_ref[...].astype(F32)).astype(BF)
+        parts = [product_t(order, x).reshape(ways, 1, -1, ROW) for x in (mixed, f_ref[...])]
+        send_ref[...] = jnp.concatenate(parts, axis=1).reshape(send_ref.shape).astype(BF)
+
+    between = (loads, mix, [pltpu.make_async_copy(send_ref, send_hbm, sem.at[3])])
+    dy_kernel(step, moves, between, w_hbm, d_hbm, *outs, *refs)
 
 
 def turn_query_kernel(q_ref, mine_ref, away_ref, qt_ref):
@@ -188,11 +199,12 @@
     gq_ref[...] = gq_t_ref[...].T.astype(BF)
 
 
-class Tables(typing.NamedTuple):
-    first: typing.Any
-    square: typing.Any
-    twiddle: typing.Any
-    last: typing.Any
+class Tables:
+    def __init__(self, first, square, twiddle):
+        self.first, self.square = first, square
+        self.group = first.shape[0] // twiddle.shape[0]
+        rows = [jnp.broadcast_to(twiddle[i : i + 1, :], (self.group, FAC)) for i in range(twiddle.shape[0])]
+        self.twiddle = jnp.concatenate(rows, axis=0)
 
 
 def times_square(left, right, tables):
@@ -214,32 +226,35 @@
 
 
 def signal(p_re, p_im, tables):
-    n, group = p_re.shape[0], p_re.shape[0] // HALF
+    n, group = p_re.shape[0], tables.group
     left = jnp.concatenate([p_re, p_im], axis=0).astype(BF)
     right = jnp.concatenate([-p_im, p_re], axis=0).astype(BF)
     c = times_square(left, right, tables)
-    twiddle = tables.twiddle
-    re, im, tc, ts = c[:n], c[n:], twiddle[:n], twiddle[n:]
-    e_re, e_im = re * tc - im * ts, im * tc + re * ts
-    e = jnp.concatenate([e_re, e_im[group : n - group]], axis=0).astype(BF)
-    x = dot(tables.last[...], e)
+    re, im, tc, ts = c[:n], c[n:], tables.twiddle[:n], tables.twiddle[n:]
+    row = lax.broadcasted_iota(jnp.int32, re.shape, 0)
+    weight = jnp.where((row < group) | (row >= n - group), 1.0 / (QF * FAC), 2.0 / (QF * FAC))
+    e = jnp.concatenate([(re * tc - im * ts) * weight, (im * tc + re * ts) * weight], axis=0).astype(BF)
+    x = lax.dot_general(tables.first[...], e, (((0,), (0,)), ((), ())), preferred_element_type=F32)
     rows = x.shape[0] // LANE_TILES
     return jnp.concatenate([x[u * rows : (u + 1) * rows] for u in range(LANE_TILES)], axis=1)
 
 
-def conv_kernel(r_ref, first_ref, square_ref, twiddle_ref, last_ref, z_ref, h_ref):
-    tables = Tables(first_ref, square_ref, twiddle_ref, last_ref)
+def conv_kernel(r_ref, first_ref, square_ref, twiddle_ref, z_ref, h_ref):
+    tables = Tables(first_ref, square_ref, twiddle_ref)
     rows = z_ref.shape[0]
     group = h_ref.shape[0] // (2 * HALF)
     r = r_ref[...].astype(F32).reshape(-1, 2, group, ROW)
     u, h = (transform(r[:, s].reshape(rows, ROW).astype(BF), tables) for s in range(2))
     h_ref[...] = jnp.concatenate(h, axis=0).astype(BF)
     p_re, p_im = u[0] * h[0] - u[1] * h[1], u[0] * h[1] + u[1] * h[0]
-    z_ref[...] = signal(p_re, p_im, tables).astype(BF)
-
-
-def adjoint_kernel(r_ref, h_ref, first_ref, square_ref, twiddle_ref, last_ref, away_ref, keep_ref):
-    tables = Tables(first_ref, square_ref, twiddle_ref, last_ref)
+    z = signal(p_re, p_im, tables).astype(BF)
+    row, r = iota(0, rows), group // 2
+    source = row // (4 * r) * 4 * r + row // r % 2 * 2 * r + row // (2 * r) % 2 * r + row % r
+    z_ref[...] = dot((source == iota(1, rows)).astype(F32).astype(BF), z).astype(BF)
+
+
+def adjoint_kernel(r_ref, h_ref, first_ref, square_ref, twiddle_ref, away_ref, keep_ref):
+    tables = Tables(first_ref, square_ref, twiddle_ref)
     rows = 2 * keep_ref.shape[0]
     group = h_ref.shape[0] // (2 * HALF)
     r = r_ref[...].astype(F32).reshape(-1, 2, group, ROW)[:, 1]
@@ -404,28 +419,35 @@
 RING_FROM = ((0, 0), (1, 0), (0, -1), (0, 1), (1, -1), (1, 1), (0, 2), (1, 2))
 
 
-def dy_product(w_out, d_out, moves, mib=MOST, after=()):
+def dy_product(w_out, d_out, moves, signals=(), mib=MOST, after=()):
     channels, depth = w_out.shape
     rows = d_out.shape[0]
     step = 512
     pieces = rows // step
     count = len(moves)
     n = channels // 8
+    outs = [shape(2 * n, rows)] * (count // 2)
+    scratch = [
+        pltpu.VMEM((count * n, depth), BF),
+        pltpu.VMEM((rows, depth), BF),
+        pltpu.VMEM((count * n, rows), BF),
+        pltpu.SemaphoreType.DMA((count,)),
+        pltpu.SemaphoreType.DMA((pieces,)),
+        pltpu.SemaphoreType.DMA((count // 2 * pieces,)),
+    ]
+    kernel = functools.partial(dy_kernel, step, moves, None)
+    if signals:
+        kernel = functools.partial(open_kernel, step, moves)
+        outs.append(shape(2 * signals[0].shape[1], rows))
+        scratch += [pltpu.VMEM(x.shape, x.dtype) for x in (*signals, outs[-1])] + [pltpu.SemaphoreType.DMA((4,))]
     return call(
-        functools.partial(dy_kernel, step, moves),
-        [shape(2 * n, rows)] * (count // 2),
-        [w_out, d_out],
-        [
-            pltpu.VMEM((count * n, depth), BF),
-            pltpu.VMEM((rows, depth), BF),
-            pltpu.VMEM((count * n, rows), BF),
-            pltpu.SemaphoreType.DMA((count,)),
-            pltpu.SemaphoreType.DMA((pieces,)),
-            pltpu.SemaphoreType.DMA((count // 2 * pieces,)),
-        ],
+        kernel,
+        outs,
+        [w_out, d_out, *signals],
+        scratch,
         mib=mib,
         flops=2 * count * n * depth * rows,
-        specs=([ANY] * 2, [ANY] * (count // 2)),
+        specs=([ANY] * (2 + len(signals)), [ANY] * len(outs)),
         after=after,
     )
 
@@ -454,37 +476,25 @@
     ways = lax.axis_size("ctx")
     group, half = width // ways, width // 2
     n = HALF * group
-    *tables, last = host_tables(ways, group)
-    slots = np.arange(ways * group).reshape(ways // 2, 2, 2, group // 2)
-    pick = lambda rows: last.reshape(LANE_TILES, ways * group, -1)[:, rows.reshape(-1)].reshape(last.shape)
-    last_z = pick(slots.transpose(0, 2, 1, 3))
+    tables = host_tables(ways, group)
 
     swap = lambda v: lax.ppermute(v, "ctx", [(i, i ^ 1) for i in range(ways)])
     rows_like, half_like = shape(width, seq_rows), shape(half, seq_rows)
 
-    x_y, up_y, down_y = dy_product(w_out, d_out, DY_MOVES[2:])
+    x_y, up_y, down_y, send = dy_product(w_out, d_out, DY_MOVES[2:], (key_in, value_in, filt))
     (own_y,) = dy_product(w_out, d_out, DY_MOVES[:2], mib=16, after=[x_y])
     keep_y, far_y, side_y = call(
         sum_kernel,
         [shape(width, seq_rows, dtype=F32), rows_like, rows_like],
         [own_y, move_over(x_y, (1, 0)), move_over(up_y, (0, 1)), move_over(down_y, (0, -1))],
     )
-    (send,) = call(
-        prep_kernel,
-        [shape(ways * 2 * group, seq_rows)],
-        [key_in, value_in, filt],
-        mib=MOST,
-        after=[x_y],
-        staged_in=(0, 1, 2),
-        staged_out=(0,),
-    )
     arrived = spread(send)
 
-    flops = 2 * 2 * n * (tables[0].shape[1] + 2 * FAC) * FAC
+    flops = 2 * 2 * n * (4 * FAC) * FAC
     conv, spectrum = call(
         conv_kernel,
         [rows_like, shape(2 * n, FAC)],
-        [arrived, *tables, last_z],
+        [arrived, *tables],
         mib=20,
         flops=3 * flops,
         after=[far_y],
@@ -523,12 +533,12 @@
         staged_out=(0,),
     )
     du_away, du_keep = call(
-        adjoint_kernel, [half_like, half_like], [arrived, spectrum, *tables, last], mib=20, flops=2 * flops
-    )
-    other, own_up, own_down, du_away = lax.optimization_barrier((other, own_up, own_down, du_away))
+        adjoint_kernel, [half_like, half_like], [arrived, spectrum, *tables], mib=20, flops=2 * flops
+    )
+    other, own_far, du_away = lax.optimization_barrier((other, own_far, du_away))
     du_got = swap(du_away)
+    other_far = move_over(own_far, (1, 0))
     other_up, other_down = move_over(other, (0, 1)), move_over(other, (0, -1))
-    other_far = move_over(own_far, (1, 0))
     blocks = gated, other, own_up, own_down, other_up, other_down, own_far, other_far
 
     slot_rows = half + 2 * group

time: 113 us -> 110 us (0.973)
  local copies, waits for them, and re-layouts: 6.15 us -> 4.48 us
  waiting for transfers between devices: 32.6 us -> 31.2 us
    unnamed x44 -> x40, local copies, waits for them, and re-layouts: 6.15 us -> 4.48 us
    pallas_call x15 -> x14, Pallas kernels: 33.5 us -> 32.4 us  [call(): pl.pallas_call(kernel, out_shape=outs, in_specs=[*in_specs, *[ANY] * len(...]
  transfers between devices with their start and end apart: 25 -> 25, of which waited for: 12 -> 10; matrix products, arithmetic and copies ran while one was open for 2% -> 2% of each run, Pallas kernels for 22% -> 21%
where the time goes in v8:
time: 110 us; the launch traced here: 108 us
  starting transfers between devices  36.6 us (33%)
  Pallas kernels  32.4 us (29%)
  waiting for transfers between devices  31.2 us (28%)
  local copies, waits for them, and re-layouts  4.48 us (4%)
  matrix products  2.43 us (2%)
  between operations  1.2 us (1%)
    pallas_call x14, Pallas kernels, call(): pl.pallas_call(kernel, out_shape=outs, in_specs=[*in_specs, *[ANY] * len(...  32.4 us
    ppermute x12, starting transfers between devices, move_over(): return lax.ppermute(values, 'fsdp', [(i, place(i, move)) for i in range(8)])  16.2 us
    all_to_all x2, waiting for transfers between devices, spread(): return lax.all_to_all(values, 'ctx', 0, 0, tiled=True)  14.1 us
    ppermute x12, waiting for transfers between devices, move_over(): return lax.ppermute(values, 'fsdp', [(i, place(i, move)) for i in range(8)])  10.8 us
    all_to_all x2, starting transfers between devices, spread(): return lax.all_to_all(values, 'ctx', 0, 0, tiled=True)  10.8 us
    ppermute x3, starting transfers between devices, on_device(): lax.ppermute(v, 'ctx', [(i, (i + 4 * step) % ways) for i in range(ways)])  4.78 us
    unnamed x40, local copies, waits for them, and re-layouts  4.48 us
    ppermute x2, waiting for transfers between devices, on_device(): over_x = lambda v: lax.ppermute(v, 'ctx', [(i, i ^ 2) for i in range(ways)])  4.26 us
  transfers between devices with their start and end apart: 25, of which 10 were waited for; matrix products, arithmetic and copies ran while one was open for 2% of the time, Pallas kernels for 21%

profile of v8, /device:TPU:0, one launch (start us, length us, event | category | flops | bytes accessed | tf_op | source)
XLA Modules:
  0.0 108.3 jit_solution(12224444857478318727)
XLA Ops:
  0.6 5.4 %shard_map.128 = (bf16[256,1024]{1,0:T(8,128)(2,1)}, bf16[256,1024]{1,0:T(8,128)(2,1)}, bf16[256,1024]{1,0:T(8,128)(2,1)}, bf16[256,1024]{1,0:T(8,128)(2,1)}) custom-call(bf16[1024,1024]{1,0:T(8,128)(2,1)} %refs_0_.2, bf16[1024,1024]{1,0:T(8,128)(2,1)} %refs_4_.4, bf16[1024,128]{1,0:T(8,128)(2,1)} %refs_4_.5, bf16[1024,128]{1,0:T(8,128)(2,1)} %refs_5_.1, ...), custom_call_target="tpu_custom_call" | custom-call | tf_op jit(solution)/shard_map/pallas_call | solution.py:395
  6.1 2.1 %collective-permute-start.1 = (bf16[256,1024]{1,0:T(8,128)(2,1)}, bf16[256,1024]{1,0:T(8,128)(2,1)}, u32[]{:S(2)}, u32[]{:S(2)}) collective-permute-start(bf16[256,1024]{1,0:T(8,128)(2,1)} %get-tuple-element.40), channel_id=1, source_target_pairs={{0,16},{16,32},{32,48},{48,0},{64,80},{80,96},{96,112},{112,64},{1... | collective-permute-start | bytes 1572872 | tf_op jit(solution)/shard_map/ppermute | solution.py:416
  8.2 2.2 %collective-permute-start.2 = (bf16[256,1024]{1,0:T(8,128)(2,1)}, bf16[256,1024]{1,0:T(8,128)(2,1)}, u32[]{:S(2)}, u32[]{:S(2)}) collective-permute-start(bf16[256,1024]{1,0:T(8,128)(2,1)} %get-tuple-element.41), channel_id=1, source_target_pairs={{0,48},{16,0},{32,16},{48,32},{64,112},{80,64},{96,80},{112,96},{1... | collective-permute-start | bytes 1572872 | tf_op jit(solution)/shard_map/ppermute | solution.py:416
  10.4 1.5 %collective-permute-start = (bf16[256,1024]{1,0:T(8,128)(2,1)}, bf16[256,1024]{1,0:T(8,128)(2,1)}, u32[]{:S(2)}, u32[]{:S(2)}) collective-permute-start(bf16[256,1024]{1,0:T(8,128)(2,1)} %get-tuple-element.39.refs_2_), channel_id=1, source_target_pairs={{0,64},{16,80},{32,96},{48,112},{64,0},{80,16},{96,32},{112,48},{1... | collective-permute-start | bytes 1572872 | tf_op jit(solution)/shard_map/ppermute | solution.py:416
  11.8 6.8 %all-to-all-start = ((bf16[16,16,1024]{2,1,0:T(8,128)(2,1)}), bf16[16,16,1024]{2,1,0:T(8,128)(2,1)}, u32[]{:S(2)}, u32[]{:S(2)}) async-start(bf16[16,16,1024]{2,1,0:T(8,128)(2,1)} %bitcast.9), calls=%async_computation | async-start | bytes 1048576 | tf_op jit(solution)/shard_map/all_to_all | solution.py:412
  18.7 0.0 copy-start.1
  18.7 1.6 %copy-done.1 = bf16[1024,1024]{1,0:T(8,128)(2,1)S(1)} copy-done((bf16[1024,1024]{1,0:T(8,128)(2,1)S(1)}, bf16[1024,1024]{1,0:T(8,128)(2,1)}, u32[]{:S(2)}) %copy-start.1) | copy-done | bytes 2097176
  20.3 1.0 copy-done.19
  21.3 1.2 %shard_map.129.own_ref = bf16[256,1024]{1,0:T(8,128)(2,1)S(1)} custom-call(bf16[1024,1024]{1,0:T(8,128)(2,1)S(1)} %copy-done.1, bf16[1024,1024]{1,0:T(8,128)(2,1)S(1)} %copy-done, bf16[256,1024]{1,0:T(8,128)(2,1)S(1)} %copy-done.19), custom_call_target="tpu_custom_call" | custom-call | tf_op jit(solution)/shard_map/pallas_call | solution.py:395
  22.5 0.0 copy-start.3
  22.5 0.0 copy-start.12
  22.6 0.0 collective-permute-done.2.down_ref
  22.6 2.9 %collective-permute-done.x_ref = bf16[256,1024]{1,0:T(8,128)(2,1)} collective-permute-done((bf16[256,1024]{1,0:T(8,128)(2,1)}, bf16[256,1024]{1,0:T(8,128)(2,1)}, u32[]{:S(2)}, u32[]{:S(2)}) %collective-permute-start) | collective-permute-done | bytes 524320 | tf_op jit(solution)/shard_map/ppermute | solution.py:416
  25.5 2.2 %shard_map.130 = (f32[128,1024]{1,0:T(8,128)S(1)}, bf16[128,1024]{1,0:T(8,128)(2,1)}, bf16[128,1024]{1,0:T(8,128)(2,1)}) custom-call(bf16[256,1024]{1,0:T(8,128)(2,1)S(1)} %shard_map.129.own_ref, bf16[256,1024]{1,0:T(8,128)(2,1)} %collective-permute-done.x_ref, bf16[256,1024]{1,0:T(8,128)(2,1)} %collective-permute-done.1.up_ref, ...), custom_call_target="tpu_custom_call" | custom-call | tf_op jit(solution)/shard_map/pallas_call | solution.py:395
  27.7 0.8 copy-done.6
  28.5 1.5 %collective-permute-start.4 = (bf16[128,1024]{1,0:T(8,128)(2,1)}, bf16[128,1024]{1,0:T(8,128)(2,1)}, u32[]{:S(2)}, u32[]{:S(2)}) collective-permute-start(bf16[128,1024]{1,0:T(8,128)(2,1)} %get-tuple-element.44), channel_id=1, source_target_pairs={{0,64},{16,80},{32,96},{48,112},{64,0},{80,16},{96,32},{112,48},{1... | collective-permute-start | bytes 786440 | tf_op jit(solution)/shard_map/ppermute | solution.py:416
  30.0 1.8 %collective-permute-start.3 = (bf16[128,1024]{1,0:T(8,128)(2,1)}, bf16[128,1024]{1,0:T(8,128)(2,1)}, u32[]{:S(2)}, u32[]{:S(2)}) collective-permute-start(bf16[128,1024]{1,0:T(8,128)(2,1)} %get-tuple-element.43.refs_4_), channel_id=1, source_target_pairs={{0,32},{16,48},{32,0},{48,16},{64,96},{80,112},{96,64},{112,80},{1... | collective-permute-start | bytes 786440 | tf_op jit(solution)/shard_map/ppermute | solution.py:416
  31.8 3.5 %all-to-all-done = bf16[16,16,1024]{2,1,0:T(8,128)(2,1)} async-done(((bf16[16,16,1024]{2,1,0:T(8,128)(2,1)}), bf16[16,16,1024]{2,1,0:T(8,128)(2,1)}, u32[]{:S(2)}, u32[]{:S(2)}) %all-to-all-start) | async-done | bytes 524320 | tf_op jit(solution)/shard_map/all_to_all | solution.py:412
  35.3 0.0 copy-start.15
  35.3 1.0 copy-done.15
  36.3 4.5 %shard_map.131 = (bf16[128,1024]{1,0:T(8,128)(2,1)S(1)}, bf16[1040,256]{1,0:T(8,128)(2,1)S(1)}) custom-call(bf16[256,1024]{1,0:T(8,128)(2,1)} %bitcast.1.refs_0_, bf16[1040,512]{1,0:T(8,128)(2,1)S(1)} %copy-done.3, bf16[512,256]{1,0:T(8,128)(2,1)S(1)} %copy-done.12, f32[130,256]{1,0:T(8,128)S(1)} %copy-done.15, bf16[128,1024]{1,0:T(8,128)(2,1)} %get-tuple-element.43.refs_4_), custom_call_target="tpu_custom_call" | custom-call | tf_op jit(solution)/shard_map/pallas_call | solution.py:395
  40.8 0.0 copy-start.17
  40.8 0.0 copy-start.14
  40.8 0.0 collective-permute-done.3.refs_1_
  40.8 2.4 %shard_map.132.refs_1_ = bf16[256,1024]{1,0:T(8,128)(2,1)} custom-call(f32[128,1024]{1,0:T(8,128)S(1)} %copy-done.7, bf16[128,1024]{1,0:T(8,128)(2,1)} %collective-permute-done.3.refs_1_, bf16[128,1024]{1,0:T(8,128)(2,1)} %collective-permute-done.4.refs_2_, bf16[1024,128]{1,0:T(8,128)(2,1)S(1)} %copy-done.13, bf16[128,1024]{1,0:T(8,128)(2,1)S(1)} %get-tuple-element.46.refs_4_), custom_call_target="tpu_custom_call" | custom-call | tf_op jit(solution)/shard_map/pallas_call | solution.py:395
  43.2 0.1 collective-permute-start.6
  43.3 4.0 %all-to-all-start.1 = ((bf16[16,16,1024]{2,1,0:T(8,128)(2,1)}), bf16[16,16,1024]{2,1,0:T(8,128)(2,1)S(1)}, u32[]{:S(2)}, u32[]{:S(2)}) async-start(bf16[16,16,1024]{2,1,0:T(8,128)(2,1)} %bitcast.2), calls=%async_computation.1 | async-start | bytes 1048576 | tf_op jit(solution)/shard_map/all_to_all | solution.py:412
  47.4 0.0 copy-start.16
  47.4 0.2 shard_map.133
  47.6 0.5 collective-permute-start.5
  48.1 1.0 collective-permute-done.5.refs_2_
  49.1 10.6 %all-to-all-done.1 = bf16[16,16,1024]{2,1,0:T(8,128)(2,1)S(1)} async-done(((bf16[16,16,1024]{2,1,0:T(8,128)(2,1)}), bf16[16,16,1024]{2,1,0:T(8,128)(2,1)S(1)}, u32[]{:S(2)}, u32[]{:S(2)}) %all-to-all-start.1) | async-done | bytes 524320 | tf_op jit(solution)/shard_map/all_to_all | solution.py:412
  59.7 0.3 shard_map.134
  60.0 1.9 %collective-permute-start.8 = (bf16[128,1024]{1,0:T(8,128)(2,1)S(1)}, bf16[128,1024]{1,0:T(8,128)(2,1)S(1)}, u32[]{:S(2)}, u32[]{:S(2)}) collective-permute-start(bf16[128,1024]{1,0:T(8,128)(2,1)S(1)} %get-tuple-element.51.refs_0_), channel_id=1, source_target_pairs={{0,32},{16,48},{32,0},{48,16},{64,96},{80,112},{96,64},{112,80},{1... | collective-permute-start | bytes 786440 | tf_op jit(solution)/shard_map/ppermute | solution.py:416
  61.9 0.2 collective-permute-start.7
  62.1 1.3 %collective-permute-start.10 = (bf16[128,1024]{1,0:T(8,128)(2,1)S(1)}, bf16[128,1024]{1,0:T(8,128)(2,1)S(1)}, u32[]{:S(2)}, u32[]{:S(2)}) collective-permute-start(bf16[128,1024]{1,0:T(8,128)(2,1)S(1)} %get-tuple-element.51.refs_0_), channel_id=1, source_target_pairs={{0,48},{16,0},{32,16},{48,32},{64,112},{80,64},{96,80},{112,96},{1... | collective-permute-start | bytes 786440 | tf_op jit(solution)/shard_map/ppermute | solution.py:416
  63.4 2.7 %shard_map.135 = (bf16[64,1024]{1,0:T(8,128)(2,1)S(1)}, bf16[64,1024]{1,0:T(8,128)(2,1)S(1)}) custom-call(bf16[256,1024]{1,0:T(8,128)(2,1)S(1)} %bitcast.7, bf16[1040,256]{1,0:T(8,128)(2,1)S(1)} %copy-done.18, bf16[1040,512]{1,0:T(8,128)(2,1)S(1)} %copy-done.4, bf16[512,256]{1,0:T(8,128)(2,1)S(1)} %copy-done.12, f32[130,256]{1,0:T(8,128)S(1)} %copy-done.16), custom_call_target="tpu_custom_call" | custom-call | tf_op jit(solution)/shard_map/pallas_call | solution.py:395
  66.1 1.0 collective-permute-start.9
  67.1 3.2 %collective-permute-done.8.refs_2_.refs_6_ = bf16[128,1024]{1,0:T(8,128)(2,1)S(1)} collective-permute-done((bf16[128,1024]{1,0:T(8,128)(2,1)S(1)}, bf16[128,1024]{1,0:T(8,128)(2,1)S(1)}, u32[]{:S(2)}, u32[]{:S(2)}) %collective-permute-start.8) | collective-permute-done | bytes 262176 | tf_op jit(solution)/shard_map/ppermute | solution.py:416
  70.3 2.8 %collective-permute-start.12 = (bf16[128,1024]{1,0:T(8,128)(2,1)S(1)}, bf16[128,1024]{1,0:T(8,128)(2,1)S(1)}, u32[]{:S(2)}, u32[]{:S(2)}) collective-permute-start(bf16[128,1024]{1,0:T(8,128)(2,1)S(1)} %collective-permute-done.7.refs_1_), channel_id=1, source_target_pairs={{0,48},{16,0},{32,16},{48,32},{64,112},{80,64},{96,80},{112,96},{1... | collective-permute-start | bytes 786440 | tf_op jit(solution)/shard_map/ppermute | solution.py:416
  73.1 2.7 %collective-permute-done.10.refs_3_ = bf16[128,1024]{1,0:T(8,128)(2,1)S(1)} collective-permute-done((bf16[128,1024]{1,0:T(8,128)(2,1)S(1)}, bf16[128,1024]{1,0:T(8,128)(2,1)S(1)}, u32[]{:S(2)}, u32[]{:S(2)}) %collective-permute-start.10) | collective-permute-done | bytes 262176 | tf_op jit(solution)/shard_map/ppermute | solution.py:416
  75.8 1.0 collective-permute-done.9.refs_2_
  76.8 2.8 %shard_map.136 = (bf16[640,1024]{1,0:T(8,128)(2,1)S(1)}, bf16[256,1024]{1,0:T(8,128)(2,1)S(1)}) custom-call(bf16[128,1024]{1,0:T(8,128)(2,1)S(1)} %get-tuple-element.51.refs_0_, bf16[128,1024]{1,0:T(8,128)(2,1)S(1)} %collective-permute-done.7.refs_1_, bf16[128,1024]{1,0:T(8,128)(2,1)S(1)} %collective-permute-done.9.refs_2_, ...), custom_call_target="tpu_custom_call" | custom-call | tf_op jit(solution)/shard_map/pallas_call | solution.py:395
  79.7 0.1 collective-permute-start.14
  79.8 0.9 collective-permute-done.11.refs_0_.refs_4_
  80.7 3.6 %shard_map.137 = (bf16[160,1024]{1,0:T(8,128)(2,1)S(1)}, bf16[160,1024]{1,0:T(8,128)(2,1)S(1)}, bf16[160,1024]{1,0:T(8,128)(2,1)S(1)}, bf16[160,1024]{1,0:T(8,128)(2,1)S(1)}, bf16[256,1024]{1,0:T(8,128)(2,1)S(1)}) custom-call(bf16[128,1024]{1,0:T(8,128)(2,1)S(1)} %collective-permute-done.11.refs_0_.refs_4_, ...), custom_call_target="tpu_custom_call" | custom-call | tf_op jit(solution)/shard_map/pallas_call | solution.py:395
  84.3 0.1 collective-permute-start.16
  84.4 0.5 collective-permute-start.17
  84.9 1.6 %collective-permute-start.18 = (bf16[160,1024]{1,0:T(8,128)(2,1)S(1)}, bf16[160,1024]{1,0:T(8,128)(2,1)S(1)}, u32[]{:S(2)}, u32[]{:S(2)}) collective-permute-start(bf16[160,1024]{1,0:T(8,128)(2,1)S(1)} %get-tuple-element.63), channel_id=1, source_target_pairs={{0,2},{1,3},{2,0},{3,1},{4,6},{5,7},{6,4},{7,5},{8,10},{9,11},{10,... | collective-permute-start | bytes 983048 | tf_op jit(solution)/shard_map/ppermute | solution.py:550
  86.5 0.0 collective-permute-done.17.refs_4_
  86.5 3.2 %collective-permute-start.20 = (bf16[160,1024]{1,0:T(8,128)(2,1)S(1)}, bf16[160,1024]{1,0:T(8,128)(2,1)S(1)}, u32[]{:S(2)}, u32[]{:S(2)}) collective-permute-start(bf16[160,1024]{1,0:T(8,128)(2,1)S(1)} %get-tuple-element.65), channel_id=1, source_target_pairs={{0,12},{1,13},{2,14},{3,15},{4,0},{5,1},{6,2},{7,3},{8,4},{9,5},{1... | collective-permute-start | bytes 983048 | tf_op jit(solution)/shard_map/ppermute | solution.py:551
  89.7 2.1 %shard_map.139.refs_7_ = bf16[1024,128]{1,0:T(8,128)(2,1)} custom-call(f32[128,1024]{1,0:T(8,128)S(1)} %copy-done.8, bf16[128,1024]{1,0:T(8,128)(2,1)} %collective-permute-done.3.refs_1_, bf16[128,1024]{1,0:T(8,128)(2,1)} %collective-permute-done.4.refs_2_, bf16[256,1024]{1,0:T(8,128)(2,1)S(1)} %bitcast.8, bf16[64,1024]{1,0:T(8,128)(2,1)S(1)} %collective-permute-done.17.refs_4_), custom_call_target="tpu_custom_call" | custom-call | tf_op jit(solution)/shard_map/pallas_call | solution.py:395
  91.9 4.3 %collective-permute-done.18.x_ref = bf16[160,1024]{1,0:T(8,128)(2,1)S(1)} collective-permute-done((bf16[160,1024]{1,0:T(8,128)(2,1)S(1)}, bf16[160,1024]{1,0:T(8,128)(2,1)S(1)}, u32[]{:S(2)}, u32[]{:S(2)}) %collective-permute-start.18) | collective-permute-done | bytes 327712 | tf_op jit(solution)/shard_map/ppermute | solution.py:550
  96.1 1.0 collective-permute-done.19.up_ref
  97.1 0.1 shard_map.140
  97.3 1.5 %collective-permute-start.21 = (bf16[96,1024]{1,0:T(8,128)(2,1)S(1)}, bf16[96,1024]{1,0:T(8,128)(2,1)S(1)}, u32[]{:S(2)}, u32[]{:S(2)}) collective-permute-start(bf16[96,1024]{1,0:T(8,128)(2,1)S(1)} %get-tuple-element.67), channel_id=1, source_target_pairs={{0,8},{1,9},{2,10},{3,11},{4,12},{5,13},{6,14},{7,15},{8,0},{9,1},... | collective-permute-start | bytes 589832 | tf_op jit(solution)/shard_map/ppermute | solution.py:551
  98.8 2.0 %collective-permute-start.22 = (bf16[96,1024]{1,0:T(8,128)(2,1)S(1)}, bf16[96,1024]{1,0:T(8,128)(2,1)S(1)}, u32[]{:S(2)}, u32[]{:S(2)}) collective-permute-start(bf16[96,1024]{1,0:T(8,128)(2,1)S(1)} %get-tuple-element.68), channel_id=1, source_target_pairs={{0,2},{1,3},{2,0},{3,1},{4,6},{5,7},{6,4},{7,5},{8,10},{9,11},{10,... | collective-permute-start | bytes 589832 | tf_op jit(solution)/shard_map/ppermute | solution.py:550
  100.8 3.2 %shard_map.138 = bf16[1024,1024]{1,0:T(8,128)(2,1)S(1)} custom-call(bf16[128,1024]{1,0:T(8,128)(2,1)S(1)} %get-tuple-element.51.refs_0_, bf16[128,1024]{1,0:T(8,128)(2,1)S(1)} %collective-permute-done.7.refs_1_, bf16[128,1024]{1,0:T(8,128)(2,1)S(1)} %collective-permute-done.9.refs_2_, bf16[128,1024]{1,0:T(8,128)(2,1)S(1)} %collective-permute-done.10.refs_3_, ...), custom_call_target="tpu_custom_call" | custom-call | tf_op jit(solution)/shard_map/pallas_call | solution.py:395
  104.0 0.0 copy-start.9
  104.0 0.0 copy-start.10
  104.0 0.0 copy-start.11
  104.0 2.4 %convolution_convert_fusion.refs_6_ = bf16[1024,1024]{1,0:T(8,128)(2,1)S(1)} fusion(bf16[1024,1024]{1,0:T(8,128)(2,1)S(1)} %shard_map.138, bf16[1024,1024]{1,0:T(8,128)(2,1)S(1)} %copy-done.2), kind=kOutput, calls=%fused_computation | convolution fusion | flops 2148532224 | bytes 6291456 | tf_op jit(solution)/shard_map/dot_general | solution.py:568
  106.5 0.0 copy-start.5
  106.5 1.5 %shard_map.141 = (f32[64,1024]{1,0:T(8,128)}, bf16[1024,128]{1,0:T(8,128)(2,1)}, bf16[1024,128]{1,0:T(8,128)(2,1)}) custom-call(f32[64,1024]{1,0:T(8,128)S(1)} %get-tuple-element.66.refs_0_, bf16[96,1024]{1,0:T(8,128)(2,1)S(1)} %collective-permute-done.21.refs_1_, bf16[96,1024]{1,0:T(8,128)(2,1)S(1)} %collective-permute-done.22.refs_2_, ...), custom_call_target="tpu_custom_call" | custom-call | tf_op jit(solution)/shard_map/pallas_call | solution.py:395
  (41 shorter events, 0.1 us)
Async XLA Ops:
  0.6 18.0 %copy-start = (bf16[1024,1024]{1,0:T(8,128)(2,1)S(1)}, bf16[1024,1024]{1,0:T(8,128)(2,1)}, u32[]{:S(2)}) copy-start(bf16[1024,1024]{1,0:T(8,128)(2,1)} %refs_4_.4) | copy-start | bytes 6291460
  6.1 16.5 %collective-permute-start.1 = (bf16[256,1024]{1,0:T(8,128)(2,1)}, bf16[256,1024]{1,0:T(8,128)(2,1)}, u32[]{:S(2)}, u32[]{:S(2)}) collective-permute-start(bf16[256,1024]{1,0:T(8,128)(2,1)} %get-tuple-element.40), channel_id=1, source_target_pairs={{0,16},{16,32},{32,48},{48,0},{64,80},{80,96},{96,112},{112,64},{1... | collective-permute-start | bytes 1572872 | tf_op jit(solution)/shard_map/ppermute | solution.py:416
  8.2 14.4 %collective-permute-start.2 = (bf16[256,1024]{1,0:T(8,128)(2,1)}, bf16[256,1024]{1,0:T(8,128)(2,1)}, u32[]{:S(2)}, u32[]{:S(2)}) collective-permute-start(bf16[256,1024]{1,0:T(8,128)(2,1)} %get-tuple-element.41), channel_id=1, source_target_pairs={{0,48},{16,0},{32,16},{48,32},{64,112},{80,64},{96,80},{112,96},{1... | collective-permute-start | bytes 1572872 | tf_op jit(solution)/shard_map/ppermute | solution.py:416
  10.4 15.2 %collective-permute-start = (bf16[256,1024]{1,0:T(8,128)(2,1)}, bf16[256,1024]{1,0:T(8,128)(2,1)}, u32[]{:S(2)}, u32[]{:S(2)}) collective-permute-start(bf16[256,1024]{1,0:T(8,128)(2,1)} %get-tuple-element.39.refs_2_), channel_id=1, source_target_pairs={{0,64},{16,80},{32,96},{48,112},{64,0},{80,16},{96,32},{112,48},{1... | collective-permute-start | bytes 1572872 | tf_op jit(solution)/shard_map/ppermute | solution.py:416
  11.8 23.4 %all-to-all-start = ((bf16[16,16,1024]{2,1,0:T(8,128)(2,1)}), bf16[16,16,1024]{2,1,0:T(8,128)(2,1)}, u32[]{:S(2)}, u32[]{:S(2)}) async-start(bf16[16,16,1024]{2,1,0:T(8,128)(2,1)} %bitcast.9), calls=%async_computation | async-start | bytes 1048576 | tf_op jit(solution)/shard_map/all_to_all | solution.py:412
  18.7 1.6 %copy-start.1 = (bf16[1024,1024]{1,0:T(8,128)(2,1)S(1)}, bf16[1024,1024]{1,0:T(8,128)(2,1)}, u32[]{:S(2)}) copy-start(bf16[1024,1024]{1,0:T(8,128)(2,1)} %refs_0_.2) | copy-start | bytes 6291460
  20.3 1.0 copy-start.19
  22.5 12.7 %copy-start.3 = (bf16[1040,512]{1,0:T(8,128)(2,1)S(1)}, bf16[1040,512]{1,0:T(8,128)(2,1)}, u32[]{:S(2)}) copy-start(bf16[1040,512]{1,0:T(8,128)(2,1)} %constant.6.clone.refs_1_.first_ref) | copy-start | bytes 3194884
  22.5 12.7 %copy-start.12 = (bf16[512,256]{1,0:T(8,128)(2,1)S(1)}, bf16[512,256]{1,0:T(8,128)(2,1)}, u32[]{:S(2)}) copy-start(bf16[512,256]{1,0:T(8,128)(2,1)} %constant.7.clone.refs_2_.square_ref) | copy-start | bytes 786436
  27.7 0.8 copy-start.6
  28.5 12.2 %collective-permute-start.4 = (bf16[128,1024]{1,0:T(8,128)(2,1)}, bf16[128,1024]{1,0:T(8,128)(2,1)}, u32[]{:S(2)}, u32[]{:S(2)}) collective-permute-start(bf16[128,1024]{1,0:T(8,128)(2,1)} %get-tuple-element.44), channel_id=1, source_target_pairs={{0,64},{16,80},{32,96},{48,112},{64,0},{80,16},{96,32},{112,48},{1... | collective-permute-start | bytes 786440 | tf_op jit(solution)/shard_map/ppermute | solution.py:416
  30.0 10.8 %collective-permute-start.3 = (bf16[128,1024]{1,0:T(8,128)(2,1)}, bf16[128,1024]{1,0:T(8,128)(2,1)}, u32[]{:S(2)}, u32[]{:S(2)}) collective-permute-start(bf16[128,1024]{1,0:T(8,128)(2,1)} %get-tuple-element.43.refs_4_), channel_id=1, source_target_pairs={{0,32},{16,48},{32,0},{48,16},{64,96},{80,112},{96,64},{112,80},{1... | collective-permute-start | bytes 786440 | tf_op jit(solution)/shard_map/ppermute | solution.py:416
  35.3 5.5 %copy-start.7 = (f32[128,1024]{1,0:T(8,128)S(1)}, f32[128,1024]{1,0:T(8,128)}, u32[]{:S(2)}) copy-start(f32[128,1024]{1,0:T(8,128)} %copy-done.6) | copy-start | bytes 1572868
  35.3 5.5 %copy-start.13 = (bf16[1024,128]{1,0:T(8,128)(2,1)S(1)}, bf16[1024,128]{1,0:T(8,128)(2,1)}, u32[]{:S(2)}) copy-start(bf16[1024,128]{1,0:T(8,128)(2,1)} %refs_0_.3) | copy-start | bytes 786436
  35.3 1.0 copy-start.15
  40.8 2.5 %copy-start.17 = (bf16[1040,256]{1,0:T(8,128)(2,1)}, bf16[1040,256]{1,0:T(8,128)(2,1)S(1)}, u32[]{:S(2)}) copy-start(bf16[1040,256]{1,0:T(8,128)(2,1)S(1)} %get-tuple-element.52.h_ref) | copy-start | bytes 1597444
  40.8 6.6 %copy-start.14 = (bf16[1024,128]{1,0:T(8,128)(2,1)S(1)}, bf16[1024,128]{1,0:T(8,128)(2,1)}, u32[]{:S(2)}) copy-start(bf16[1024,128]{1,0:T(8,128)(2,1)} %refs_0_.3) | copy-start | bytes 786436
  43.2 16.5 %collective-permute-start.6 = (bf16[1024,1024]{1,0:T(8,128)(2,1)S(1)}, bf16[1024,1024]{1,0:T(8,128)(2,1)}, u32[]{:S(2)}, u32[]{:S(2)}) collective-permute-start(bf16[1024,1024]{1,0:T(8,128)(2,1)S(1)} %copy-done), channel_id=1, source_target_pairs={{0,1},{1,0},{2,3},{3,2},{4,5},{5,4},{6,7},{7,6},{8,9},{9,8},{10,11... | collective-permute-start | bytes 6291464 | tf_op jit(solution)/shard_map/ppermute | solution.py:481
  43.3 16.4 %all-to-all-start.1 = ((bf16[16,16,1024]{2,1,0:T(8,128)(2,1)}), bf16[16,16,1024]{2,1,0:T(8,128)(2,1)S(1)}, u32[]{:S(2)}, u32[]{:S(2)}) async-start(bf16[16,16,1024]{2,1,0:T(8,128)(2,1)} %bitcast.2), calls=%async_computation.1 | async-start | bytes 1048576 | tf_op jit(solution)/shard_map/all_to_all | solution.py:412
  47.4 16.0 %copy-start.16 = (f32[130,256]{1,0:T(8,128)S(1)}, f32[130,256]{1,0:T(8,128)}, u32[]{:S(2)}) copy-start(f32[130,256]{1,0:T(8,128)} %constant.8.clone.refs_3_.twiddle_ref) | copy-start | bytes 399364
  47.6 1.5 %collective-permute-start.5 = (bf16[64,1024]{1,0:T(8,128)(2,1)S(1)}, bf16[64,1024]{1,0:T(8,128)(2,1)S(1)}, u32[]{:S(2)}, u32[]{:S(2)}) collective-permute-start(bf16[64,1024]{1,0:T(8,128)(2,1)S(1)} %get-tuple-element.49), channel_id=1, source_target_pairs={{0,1},{1,0},{2,3},{3,2},{4,5},{5,4},{6,7},{7,6},{8,9},{9,8},{10,11... | collective-permute-start | bytes 393224 | tf_op jit(solution)/shard_map/ppermute | solution.py:481
  59.7 3.7 %copy-start.4 = (bf16[1040,512]{1,0:T(8,128)(2,1)S(1)}, bf16[1040,512]{1,0:T(8,128)(2,1)}, u32[]{:S(2)}) copy-start(bf16[1040,512]{1,0:T(8,128)(2,1)} %constant.6.clone.refs_1_.first_ref) | copy-start | bytes 3194884
  59.7 3.7 %copy-start.18 = (bf16[1040,256]{1,0:T(8,128)(2,1)S(1)}, bf16[1040,256]{1,0:T(8,128)(2,1)}, u32[]{:S(2)}) copy-start(bf16[1040,256]{1,0:T(8,128)(2,1)} %copy-done.17) | copy-start | bytes 1597444
  60.0 10.3 %collective-permute-start.8 = (bf16[128,1024]{1,0:T(8,128)(2,1)S(1)}, bf16[128,1024]{1,0:T(8,128)(2,1)S(1)}, u32[]{:S(2)}, u32[]{:S(2)}) collective-permute-start(bf16[128,1024]{1,0:T(8,128)(2,1)S(1)} %get-tuple-element.51.refs_0_), channel_id=1, source_target_pairs={{0,32},{16,48},{32,0},{48,16},{64,96},{80,112},{96,64},{112,80},{1... | collective-permute-start | bytes 786440 | tf_op jit(solution)/shard_map/ppermute | solution.py:416
  61.9 8.4 %collective-permute-start.7 = (bf16[128,1024]{1,0:T(8,128)(2,1)S(1)}, bf16[128,1024]{1,0:T(8,128)(2,1)S(1)}, u32[]{:S(2)}, u32[]{:S(2)}) collective-permute-start(bf16[128,1024]{1,0:T(8,128)(2,1)S(1)} %get-tuple-element.51.refs_0_), channel_id=1, source_target_pairs={{0,64},{16,80},{32,96},{48,112},{64,0},{80,16},{96,32},{112,48},{1... | collective-permute-start | bytes 786440 | tf_op jit(solution)/shard_map/ppermute | solution.py:416
  62.1 13.7 %collective-permute-start.10 = (bf16[128,1024]{1,0:T(8,128)(2,1)S(1)}, bf16[128,1024]{1,0:T(8,128)(2,1)S(1)}, u32[]{:S(2)}, u32[]{:S(2)}) collective-permute-start(bf16[128,1024]{1,0:T(8,128)(2,1)S(1)} %get-tuple-element.51.refs_0_), channel_id=1, source_target_pairs={{0,48},{16,0},{32,16},{48,32},{64,112},{80,64},{96,80},{112,96},{1... | collective-permute-start | bytes 786440 | tf_op jit(solution)/shard_map/ppermute | solution.py:416
  66.1 10.7 %collective-permute-start.9 = (bf16[128,1024]{1,0:T(8,128)(2,1)S(1)}, bf16[128,1024]{1,0:T(8,128)(2,1)S(1)}, u32[]{:S(2)}, u32[]{:S(2)}) collective-permute-start(bf16[128,1024]{1,0:T(8,128)(2,1)S(1)} %get-tuple-element.51.refs_0_), channel_id=1, source_target_pairs={{0,16},{16,32},{32,48},{48,0},{64,80},{80,96},{96,112},{112,64},{1... | collective-permute-start | bytes 786440 | tf_op jit(solution)/shard_map/ppermute | solution.py:416
  70.3 9.5 %collective-permute-start.13 = (bf16[128,1024]{1,0:T(8,128)(2,1)S(1)}, bf16[128,1024]{1,0:T(8,128)(2,1)S(1)}, u32[]{:S(2)}, u32[]{:S(2)}) collective-permute-start(bf16[128,1024]{1,0:T(8,128)(2,1)S(1)} %collective-permute-done.8.refs_2_.refs_6_), channel_id=1, source_target_pairs={{0,64},{16,80},{32,96},{48,112},{64,0},{80,16},{96,32},{112,48},{1... | collective-permute-start | bytes 786440 | tf_op jit(solution)/shard_map/ppermute | solution.py:416
  70.3 9.5 %collective-permute-start.12 = (bf16[128,1024]{1,0:T(8,128)(2,1)S(1)}, bf16[128,1024]{1,0:T(8,128)(2,1)S(1)}, u32[]{:S(2)}, u32[]{:S(2)}) collective-permute-start(bf16[128,1024]{1,0:T(8,128)(2,1)S(1)} %collective-permute-done.7.refs_1_), channel_id=1, source_target_pairs={{0,48},{16,0},{32,16},{48,32},{64,112},{80,64},{96,80},{112,96},{1... | collective-permute-start | bytes 786440 | tf_op jit(solution)/shard_map/ppermute | solution.py:416
  73.1 7.7 %collective-permute-start.11 = (bf16[128,1024]{1,0:T(8,128)(2,1)S(1)}, bf16[128,1024]{1,0:T(8,128)(2,1)S(1)}, u32[]{:S(2)}, u32[]{:S(2)}) collective-permute-start(bf16[128,1024]{1,0:T(8,128)(2,1)S(1)} %collective-permute-done.7.refs_1_), channel_id=1, source_target_pairs={{0,16},{16,32},{32,48},{48,0},{64,80},{80,96},{96,112},{112,64},{1... | collective-permute-start | bytes 786440 | tf_op jit(solution)/shard_map/ppermute | solution.py:416
  75.8 4.0 %collective-permute-start.15 = (bf16[64,1024]{1,0:T(8,128)(2,1)S(1)}, bf16[64,1024]{1,0:T(8,128)(2,1)S(1)}, u32[]{:S(2)}, u32[]{:S(2)}) collective-permute-start(bf16[64,1024]{1,0:T(8,128)(2,1)S(1)} %get-tuple-element.58), channel_id=1, source_target_pairs={{0,1},{1,0},{2,3},{3,2},{4,5},{5,4},{6,7},{7,6},{8,9},{9,8},{10,11... | collective-permute-start | bytes 393224 | tf_op jit(solution)/shard_map/ppermute | solution.py:481
  79.7 21.1 %collective-permute-start.14 = (bf16[256,1024]{1,0:T(8,128)(2,1)S(1)}, bf16[256,1024]{1,0:T(8,128)(2,1)S(1)}, u32[]{:S(2)}, u32[]{:S(2)}) collective-permute-start(bf16[256,1024]{1,0:T(8,128)(2,1)S(1)} %get-tuple-element.56), channel_id=1, source_target_pairs={{0,1},{1,0},{2,3},{3,2},{4,5},{5,4},{6,7},{7,6},{8,9},{9,8},{10,11... | collective-permute-start | bytes 1572872 | tf_op jit(solution)/shard_map/ppermute | solution.py:481
  80.7 9.0 %copy-start.8 = (f32[128,1024]{1,0:T(8,128)S(1)}, f32[128,1024]{1,0:T(8,128)}, u32[]{:S(2)}) copy-start(f32[128,1024]{1,0:T(8,128)} %copy-done.6) | copy-start | bytes 1572868
  84.3 16.4 %collective-permute-start.16 = (bf16[256,1024]{1,0:T(8,128)(2,1)S(1)}, bf16[256,1024]{1,0:T(8,128)(2,1)S(1)}, u32[]{:S(2)}, u32[]{:S(2)}) collective-permute-start(bf16[256,1024]{1,0:T(8,128)(2,1)S(1)} %get-tuple-element.60), channel_id=1, source_target_pairs={{0,1},{1,0},{2,3},{3,2},{4,5},{5,4},{6,7},{7,6},{8,9},{9,8},{10,11... | collective-permute-start | bytes 1572872 | tf_op jit(solution)/shard_map/ppermute | solution.py:481
  84.4 2.1 %collective-permute-start.17 = (bf16[64,1024]{1,0:T(8,128)(2,1)S(1)}, bf16[64,1024]{1,0:T(8,128)(2,1)S(1)}, u32[]{:S(2)}, u32[]{:S(2)}) collective-permute-start(bf16[64,1024]{1,0:T(8,128)(2,1)S(1)} %get-tuple-element.61), channel_id=1, source_target_pairs={{0,1},{1,0},{2,3},{3,2},{4,5},{5,4},{6,7},{7,6},{8,9},{9,8},{10,11... | collective-permute-start | bytes 393224 | tf_op jit(solution)/shard_map/ppermute | solution.py:481
  84.9 11.2 %collective-permute-start.18 = (bf16[160,1024]{1,0:T(8,128)(2,1)S(1)}, bf16[160,1024]{1,0:T(8,128)(2,1)S(1)}, u32[]{:S(2)}, u32[]{:S(2)}) collective-permute-start(bf16[160,1024]{1,0:T(8,128)(2,1)S(1)} %get-tuple-element.63), channel_id=1, source_target_pairs={{0,2},{1,3},{2,0},{3,1},{4,6},{5,7},{6,4},{7,5},{8,10},{9,11},{10,... | collective-permute-start | bytes 983048 | tf_op jit(solution)/shard_map/ppermute | solution.py:550
  86.5 10.6 %collective-permute-start.19 = (bf16[160,1024]{1,0:T(8,128)(2,1)S(1)}, bf16[160,1024]{1,0:T(8,128)(2,1)S(1)}, u32[]{:S(2)}, u32[]{:S(2)}) collective-permute-start(bf16[160,1024]{1,0:T(8,128)(2,1)S(1)} %get-tuple-element.64), channel_id=1, source_target_pairs={{0,4},{1,5},{2,6},{3,7},{4,8},{5,9},{6,10},{7,11},{8,12},{9,13},{1... | collective-permute-start | bytes 983048 | tf_op jit(solution)/shard_map/ppermute | solution.py:551
  86.5 10.6 %collective-permute-start.20 = (bf16[160,1024]{1,0:T(8,128)(2,1)S(1)}, bf16[160,1024]{1,0:T(8,128)(2,1)S(1)}, u32[]{:S(2)}, u32[]{:S(2)}) collective-permute-start(bf16[160,1024]{1,0:T(8,128)(2,1)S(1)} %get-tuple-element.65), channel_id=1, source_target_pairs={{0,12},{1,13},{2,14},{3,15},{4,0},{5,1},{6,2},{7,3},{8,4},{9,5},{1... | collective-permute-start | bytes 983048 | tf_op jit(solution)/shard_map/ppermute | solution.py:551
  97.3 9.2 %collective-permute-start.21 = (bf16[96,1024]{1,0:T(8,128)(2,1)S(1)}, bf16[96,1024]{1,0:T(8,128)(2,1)S(1)}, u32[]{:S(2)}, u32[]{:S(2)}) collective-permute-start(bf16[96,1024]{1,0:T(8,128)(2,1)S(1)} %get-tuple-element.67), channel_id=1, source_target_pairs={{0,8},{1,9},{2,10},{3,11},{4,12},{5,13},{6,14},{7,15},{8,0},{9,1},... | collective-permute-start | bytes 589832 | tf_op jit(solution)/shard_map/ppermute | solution.py:551
  98.8 5.2 %copy-start.2 = (bf16[1024,1024]{1,0:T(8,128)(2,1)S(1)}, bf16[1024,1024]{1,0:T(8,128)(2,1)}, u32[]{:S(2)}) copy-start(bf16[1024,1024]{1,0:T(8,128)(2,1)} %refs_0_.2) | copy-start | bytes 6291460
  98.8 7.7 %collective-permute-start.22 = (bf16[96,1024]{1,0:T(8,128)(2,1)S(1)}, bf16[96,1024]{1,0:T(8,128)(2,1)S(1)}, u32[]{:S(2)}, u32[]{:S(2)}) collective-permute-start(bf16[96,1024]{1,0:T(8,128)(2,1)S(1)} %get-tuple-element.68), channel_id=1, source_target_pairs={{0,2},{1,3},{2,0},{3,1},{4,6},{5,7},{6,4},{7,5},{8,10},{9,11},{10,... | collective-permute-start | bytes 589832 | tf_op jit(solution)/shard_map/ppermute | solution.py:550
  104.0 2.5 %copy-start.9 = (bf16[1024,128]{1,0:T(8,128)(2,1)S(1)}, bf16[1024,128]{1,0:T(8,128)(2,1)}, u32[]{:S(2)}) copy-start(bf16[1024,128]{1,0:T(8,128)(2,1)} %refs_4_.5) | copy-start | bytes 786436
  104.0 2.5 %copy-start.10 = (bf16[1024,128]{1,0:T(8,128)(2,1)S(1)}, bf16[1024,128]{1,0:T(8,128)(2,1)}, u32[]{:S(2)}) copy-start(bf16[1024,128]{1,0:T(8,128)(2,1)} %refs_5_.1) | copy-start | bytes 786436
  104.0 2.5 %copy-start.11 = (bf16[1024,128]{1,0:T(8,128)(2,1)S(1)}, bf16[1024,128]{1,0:T(8,128)(2,1)}, u32[]{:S(2)}) copy-start(bf16[1024,128]{1,0:T(8,128)(2,1)} %shard_map.139.refs_7_) | copy-start | bytes 786436
  106.5 1.6 %copy-start.5 = (bf16[1024,1024]{1,0:T(8,128)(2,1)}, bf16[1024,1024]{1,0:T(8,128)(2,1)S(1)}, u32[]{:S(2)}) copy-start(bf16[1024,1024]{1,0:T(8,128)(2,1)S(1)} %convolution_convert_fusion.refs_6_) | copy-start | bytes 6291460

commit v9 on v8

--- a/solution.py
+++ b/solution.py
@@ -172,7 +172,7 @@
     gated_ref[pl.ds(n, n), :] = (z[n:] * q_theirs_ref[...].astype(F32)).astype(BF)
 
 
-def sum_kernel(own_ref, x_ref, up_ref, down_ref, keep_ref, far_ref, side_ref):
+def sum_kernel(own_ref, up_ref, x_ref, down_ref, keep_ref, far_ref, side_ref):
     n = keep_ref.shape[0]
     near, second = pl.ds(0, n), pl.ds(n, n)
     own = own_ref[near, :].astype(F32) + x_ref[near, :].astype(F32)
@@ -486,7 +486,7 @@
     keep_y, far_y, side_y = call(
         sum_kernel,
         [shape(width, seq_rows, dtype=F32), rows_like, rows_like],
-        [own_y, move_over(x_y, (1, 0)), move_over(up_y, (0, 1)), move_over(down_y, (0, -1))],
+        [own_y, move_over(up_y, (0, 1)), move_over(x_y, (1, 0)), move_over(down_y, (0, -1))],
     )
     arrived = spread(send)
 
@@ -498,7 +498,6 @@
         mib=20,
         flops=3 * flops,
         after=[far_y],
-        staged_out=(0,),
     )
     dy = (keep_y, move_over(far_y, (0, 2)), move_over(side_y, (1, 0)))
     (send,) = call(
@@ -525,13 +524,6 @@
     own_far, other = move_over(gated, (0, 2)), move_over(gated, (1, 0))
     own_up, own_down = move_over(gated, (0, 1)), move_over(gated, (0, -1))
     like = shape(seq_rows, width)
-    (grad_query,) = call(
-        functools.partial(query_kernel, ways),
-        [like],
-        [*dy, arrived, z_theirs],
-        [pltpu.VMEM((width, seq_rows), F32)],
-        staged_out=(0,),
-    )
     du_away, du_keep = call(
         adjoint_kernel, [half_like, half_like], [arrived, spectrum, *tables], mib=20, flops=2 * flops
     )
@@ -544,9 +536,20 @@
     slot_rows = half + 2 * group
     scale = 1.0 / math.sqrt(seq_rows * ways)
     weight = functools.partial(weight_product, d_out=d_out, d_other=d_other, scale=scale, slot_rows=slot_rows)
-    near, away = weight(blocks[:4], RING_FROM[:4])
+    near, away = weight(blocks[:4], RING_FROM[:4], after=[z_theirs])
     theirs_near = swap(away)
     own_w, x_w, up_w, down_w, away = weight(blocks[4:], RING_FROM[4:], du=(du_keep, du_got), near=(near,))
+    (gated_all,) = call(
+        assemble_kernel,
+        [shape(channels, seq_rows)],
+        [*blocks, theirs_near, swap(away)],
+        [pltpu.SemaphoreType.DMA((16,))],
+        specs=([ANY] * 10, [ANY]),
+    )
+    layer_out = lax.dot_general(
+        gated_all, w_out, (((0,), (0,)), ((), ())), preferred_element_type=F32
+    ).astype(BF)
+
     over_x = lambda v: lax.ppermute(v, "ctx", [(i, i ^ 2) for i in range(ways)])
     along_y = lambda v, step: lax.ppermute(v, "ctx", [(i, (i + 4 * step) % ways) for i in range(ways)])
     part_like = shape(channels // ways, columns, dtype=F32)
@@ -555,26 +558,24 @@
         part_sum_kernel,
         [part_like, onward, onward, half_like],
         [own_w, over_x(x_w), along_y(up_w, 1), along_y(down_w, -1)],
-    )
+        after=[layer_out],
+    )
+    onward_w = far_w
     far_w, side_w = along_y(far_w, 2), over_x(side_w)
-
-    (gated_all,) = call(
-        assemble_kernel,
-        [shape(channels, seq_rows)],
-        [*blocks, theirs_near, swap(away)],
-        [pltpu.SemaphoreType.DMA((16,))],
-        specs=([ANY] * 10, [ANY]),
-    )
-    layer_out = lax.dot_general(
-        gated_all, w_out, (((0,), (0,)), ((), ())), preferred_element_type=F32
-    ).astype(BF)
+    (grad_query,) = call(
+        functools.partial(query_kernel, ways),
+        [like],
+        [*dy, arrived, z_theirs],
+        [pltpu.VMEM((width, seq_rows), F32)],
+        staged_out=(0,),
+        after=[onward_w],
+    )
 
     grad_weight, grad_key, grad_value = call(
         final_kernel,
         [part_like, like, like],
         [keep_w, far_w, side_w, du_near, key_in, value_in],
         [pltpu.VMEM((width, columns), F32)],
-        after=[layer_out, grad_query],
         staged_out=(0, 1, 2),
     )
     return (layer_out, grad_query, grad_key, grad_value, grad_weight)

time: 110 us -> 108 us (0.982)
  waiting for transfers between devices: 31.2 us -> 21.9 us
  starting transfers between devices: 36.6 us -> 43.8 us
    ppermute x12, waiting for transfers between devices: 10.8 us -> 4.11 us  [move_over(): return lax.ppermute(values, 'fsdp', [(i, place(i, move)) for i in range(8)])]
    ppermute x12, starting transfers between devices: 16.2 us -> 21.3 us  [move_over(): return lax.ppermute(values, 'fsdp', [(i, place(i, move)) for i in range(8)])]
    all_to_all x2, waiting for transfers between devices: 14.1 us -> 11.4 us  [spread(): return lax.all_to_all(values, 'ctx', 0, 0, tiled=True)]
    ppermute x3, waiting for transfers between devices: 1.01 us -> 3.36 us  [on_device(): lax.ppermute(v, 'ctx', [(i, (i + 4 * step) % ways) for i in range(ways)])]
    ppermute x2, waiting for transfers between devices: 4.26 us -> 2.06 us  [on_device(): over_x = lambda v: lax.ppermute(v, 'ctx', [(i, i ^ 2) for i in range(ways)])]
    all_to_all x2, starting transfers between devices: 10.8 us -> 12.9 us  [spread(): return lax.all_to_all(values, 'ctx', 0, 0, tiled=True)]
    unnamed x40 -> x38, local copies, waits for them, and re-layouts: 4.48 us -> 5.36 us
  transfers between devices with their start and end apart: 25 -> 25, of which waited for: 10 -> 11; matrix products, arithmetic and copies ran while one was open for 2% -> 2% of each run, Pallas kernels for 21% -> 21%
where the time goes in v9:
time: 108 us; the launch traced here: 107 us
  starting transfers between devices  43.8 us (41%)
  Pallas kernels  32.1 us (30%)
  waiting for transfers between devices  21.9 us (20%)
  local copies, waits for them, and re-layouts  5.36 us (5%)
  matrix products  2.43 us (2%)
  between operations  1.12 us (1%)
    pallas_call x14, Pallas kernels, call(): pl.pallas_call(kernel, out_shape=outs, in_specs=[*in_specs, *[ANY] * len(...  32.1 us
    ppermute x12, starting transfers between devices, move_over(): return lax.ppermute(values, 'fsdp', [(i, place(i, move)) for i in range(8)])  21.3 us
    all_to_all x2, starting transfers between devices, spread(): return lax.all_to_all(values, 'ctx', 0, 0, tiled=True)  12.9 us
    all_to_all x2, waiting for transfers between devices, spread(): return lax.all_to_all(values, 'ctx', 0, 0, tiled=True)  11.4 us
    unnamed x38, local copies, waits for them, and re-layouts  5.36 us
    ppermute x3, starting transfers between devices, on_device(): lax.ppermute(v, 'ctx', [(i, (i + 4 * step) % ways) for i in range(ways)])  4.78 us
    ppermute x12, waiting for transfers between devices, move_over(): return lax.ppermute(values, 'fsdp', [(i, place(i, move)) for i in range(8)])  4.11 us
    ppermute x2, starting transfers between devices, on_device(): over_x = lambda v: lax.ppermute(v, 'ctx', [(i, i ^ 2) for i in range(ways)])  3.61 us
  transfers between devices with their start and end apart: 25, of which 11 were waited for; matrix products, arithmetic and copies ran while one was open for 2% of the time, Pallas kernels for 21%

profile of v9, /device:TPU:0, one launch (start us, length us, event | category | flops | bytes accessed | tf_op | source)
XLA Modules:
  0.0 106.8 jit_solution(8260316149744843123)
XLA Ops:
  0.6 5.4 %shard_map.128 = (bf16[256,1024]{1,0:T(8,128)(2,1)}, bf16[256,1024]{1,0:T(8,128)(2,1)}, bf16[256,1024]{1,0:T(8,128)(2,1)}, bf16[256,1024]{1,0:T(8,128)(2,1)}) custom-call(bf16[1024,1024]{1,0:T(8,128)(2,1)} %refs_0_.2, bf16[1024,1024]{1,0:T(8,128)(2,1)} %refs_4_.4, bf16[1024,128]{1,0:T(8,128)(2,1)} %refs_4_.5, bf16[1024,128]{1,0:T(8,128)(2,1)} %refs_5_.1, ...), custom_call_target="tpu_custom_call" | custom-call | tf_op jit(solution)/shard_map/pallas_call | solution.py:395
  6.1 2.1 %collective-permute-start = (bf16[256,1024]{1,0:T(8,128)(2,1)}, bf16[256,1024]{1,0:T(8,128)(2,1)}, u32[]{:S(2)}, u32[]{:S(2)}) collective-permute-start(bf16[256,1024]{1,0:T(8,128)(2,1)} %get-tuple-element.40), channel_id=1, source_target_pairs={{0,16},{16,32},{32,48},{48,0},{64,80},{80,96},{96,112},{112,64},{1... | collective-permute-start | bytes 1572872 | tf_op jit(solution)/shard_map/ppermute | solution.py:416
  8.2 1.5 %collective-permute-start.1 = (bf16[256,1024]{1,0:T(8,128)(2,1)}, bf16[256,1024]{1,0:T(8,128)(2,1)}, u32[]{:S(2)}, u32[]{:S(2)}) collective-permute-start(bf16[256,1024]{1,0:T(8,128)(2,1)} %get-tuple-element.39.refs_2_), channel_id=1, source_target_pairs={{0,64},{16,80},{32,96},{48,112},{64,0},{80,16},{96,32},{112,48},{1... | collective-permute-start | bytes 1572872 | tf_op jit(solution)/shard_map/ppermute | solution.py:416
  9.6 2.2 %collective-permute-start.2 = (bf16[256,1024]{1,0:T(8,128)(2,1)}, bf16[256,1024]{1,0:T(8,128)(2,1)}, u32[]{:S(2)}, u32[]{:S(2)}) collective-permute-start(bf16[256,1024]{1,0:T(8,128)(2,1)} %get-tuple-element.41), channel_id=1, source_target_pairs={{0,48},{16,0},{32,16},{48,32},{64,112},{80,64},{96,80},{112,96},{1... | collective-permute-start | bytes 1572872 | tf_op jit(solution)/shard_map/ppermute | solution.py:416
  11.9 6.8 %all-to-all-start = ((bf16[16,16,1024]{2,1,0:T(8,128)(2,1)}), bf16[16,16,1024]{2,1,0:T(8,128)(2,1)}, u32[]{:S(2)}, u32[]{:S(2)}) async-start(bf16[16,16,1024]{2,1,0:T(8,128)(2,1)} %bitcast.9), calls=%async_computation | async-start | bytes 1048576 | tf_op jit(solution)/shard_map/all_to_all | solution.py:412
  18.7 0.0 copy-start.1
  18.7 1.6 %copy-done.1 = bf16[1024,1024]{1,0:T(8,128)(2,1)S(1)} copy-done((bf16[1024,1024]{1,0:T(8,128)(2,1)S(1)}, bf16[1024,1024]{1,0:T(8,128)(2,1)}, u32[]{:S(2)}) %copy-start.1) | copy-done | bytes 2097176
  20.3 1.0 copy-done.18
  21.3 1.2 %shard_map.129.own_ref = bf16[256,1024]{1,0:T(8,128)(2,1)S(1)} custom-call(bf16[1024,1024]{1,0:T(8,128)(2,1)S(1)} %copy-done.1, bf16[1024,1024]{1,0:T(8,128)(2,1)S(1)} %copy-done, bf16[256,1024]{1,0:T(8,128)(2,1)S(1)} %copy-done.18), custom_call_target="tpu_custom_call" | custom-call | tf_op jit(solution)/shard_map/pallas_call | solution.py:395
  22.5 0.0 copy-start.3
  22.6 0.0 copy-start.11
  22.6 0.0 collective-permute-done.up_ref
  22.6 0.6 collective-permute-done.1.x_ref
  23.2 0.0 collective-permute-done.2.down_ref
  23.2 2.2 %shard_map.130 = (f32[128,1024]{1,0:T(8,128)S(1)}, bf16[128,1024]{1,0:T(8,128)(2,1)}, bf16[128,1024]{1,0:T(8,128)(2,1)}) custom-call(bf16[256,1024]{1,0:T(8,128)(2,1)S(1)} %shard_map.129.own_ref, bf16[256,1024]{1,0:T(8,128)(2,1)} %collective-permute-done.up_ref, bf16[256,1024]{1,0:T(8,128)(2,1)} %collective-permute-done.1.x_ref, ...), custom_call_target="tpu_custom_call" | custom-call | tf_op jit(solution)/shard_map/pallas_call | solution.py:395
  25.4 0.8 copy-done.6
  26.2 3.7 %collective-permute-start.3 = (bf16[128,1024]{1,0:T(8,128)(2,1)}, bf16[128,1024]{1,0:T(8,128)(2,1)}, u32[]{:S(2)}, u32[]{:S(2)}) collective-permute-start(bf16[128,1024]{1,0:T(8,128)(2,1)} %get-tuple-element.43.refs_4_), channel_id=1, source_target_pairs={{0,32},{16,48},{32,0},{48,16},{64,96},{80,112},{96,64},{112,80},{1... | collective-permute-start | bytes 786440 | tf_op jit(solution)/shard_map/ppermute | solution.py:416
  29.9 1.5 %collective-permute-start.4 = (bf16[128,1024]{1,0:T(8,128)(2,1)}, bf16[128,1024]{1,0:T(8,128)(2,1)}, u32[]{:S(2)}, u32[]{:S(2)}) collective-permute-start(bf16[128,1024]{1,0:T(8,128)(2,1)} %get-tuple-element.44), channel_id=1, source_target_pairs={{0,64},{16,80},{32,96},{48,112},{64,0},{80,16},{96,32},{112,48},{1... | collective-permute-start | bytes 786440 | tf_op jit(solution)/shard_map/ppermute | solution.py:416
  31.4 0.7 all-to-all-done
  32.1 0.0 copy-start.14
  32.1 1.0 copy-done.14
  33.1 4.5 %shard_map.131 = (bf16[128,1024]{1,0:T(8,128)(2,1)S(1)}, bf16[1040,256]{1,0:T(8,128)(2,1)S(1)}) custom-call(bf16[256,1024]{1,0:T(8,128)(2,1)} %bitcast.1.refs_0_, bf16[1040,512]{1,0:T(8,128)(2,1)S(1)} %copy-done.3, bf16[512,256]{1,0:T(8,128)(2,1)S(1)} %copy-done.11, f32[130,256]{1,0:T(8,128)S(1)} %copy-done.14, bf16[128,1024]{1,0:T(8,128)(2,1)} %get-tuple-element.43.refs_4_), custom_call_target="tpu_custom_call" | custom-call | tf_op jit(solution)/shard_map/pallas_call | solution.py:395
  37.6 0.0 copy-start.16
  37.6 0.0 copy-start.13
  37.6 0.0 collective-permute-done.3.refs_1_
  37.6 2.4 %shard_map.132.refs_1_ = bf16[256,1024]{1,0:T(8,128)(2,1)} custom-call(f32[128,1024]{1,0:T(8,128)S(1)} %copy-done.7, bf16[128,1024]{1,0:T(8,128)(2,1)} %collective-permute-done.3.refs_1_, bf16[128,1024]{1,0:T(8,128)(2,1)} %collective-permute-done.4.refs_2_, bf16[1024,128]{1,0:T(8,128)(2,1)S(1)} %copy-done.12, bf16[128,1024]{1,0:T(8,128)(2,1)S(1)} %get-tuple-element.46.refs_4_), custom_call_target="tpu_custom_call" | custom-call | tf_op jit(solution)/shard_map/pallas_call | solution.py:395
  40.0 0.1 collective-permute-start.6
  40.1 6.1 %all-to-all-start.1 = ((bf16[16,16,1024]{2,1,0:T(8,128)(2,1)}), bf16[16,16,1024]{2,1,0:T(8,128)(2,1)S(1)}, u32[]{:S(2)}, u32[]{:S(2)}) async-start(bf16[16,16,1024]{2,1,0:T(8,128)(2,1)} %bitcast.2), calls=%async_computation.1 | async-start | bytes 1048576 | tf_op jit(solution)/shard_map/all_to_all | solution.py:412
  46.3 0.2 shard_map.133
  46.5 0.5 collective-permute-start.5
  47.0 1.0 collective-permute-done.5.refs_2_
  48.0 10.7 %all-to-all-done.1 = bf16[16,16,1024]{2,1,0:T(8,128)(2,1)S(1)} async-done(((bf16[16,16,1024]{2,1,0:T(8,128)(2,1)}), bf16[16,16,1024]{2,1,0:T(8,128)(2,1)S(1)}, u32[]{:S(2)}, u32[]{:S(2)}) %all-to-all-start.1) | async-done | bytes 524320 | tf_op jit(solution)/shard_map/all_to_all | solution.py:412
  58.7 0.3 shard_map.134
  58.9 0.4 collective-permute-start.7
  59.3 1.5 %collective-permute-start.8 = (bf16[128,1024]{1,0:T(8,128)(2,1)S(1)}, bf16[128,1024]{1,0:T(8,128)(2,1)S(1)}, u32[]{:S(2)}, u32[]{:S(2)}) collective-permute-start(bf16[128,1024]{1,0:T(8,128)(2,1)S(1)} %get-tuple-element.51.refs_0_), channel_id=1, source_target_pairs={{0,32},{16,48},{32,0},{48,16},{64,96},{80,112},{96,64},{112,80},{1... | collective-permute-start | bytes 786440 | tf_op jit(solution)/shard_map/ppermute | solution.py:416
  60.8 0.6 collective-permute-start.9
  61.4 0.0 copy-start.15
  61.5 0.9 copy-done.15
  62.4 2.7 %shard_map.135 = (bf16[64,1024]{1,0:T(8,128)(2,1)S(1)}, bf16[64,1024]{1,0:T(8,128)(2,1)S(1)}) custom-call(bf16[256,1024]{1,0:T(8,128)(2,1)S(1)} %bitcast.7, bf16[1040,256]{1,0:T(8,128)(2,1)S(1)} %copy-done.17, bf16[1040,512]{1,0:T(8,128)(2,1)S(1)} %copy-done.4, bf16[512,256]{1,0:T(8,128)(2,1)S(1)} %copy-done.11, f32[130,256]{1,0:T(8,128)S(1)} %copy-done.15), custom_call_target="tpu_custom_call" | custom-call | tf_op jit(solution)/shard_map/pallas_call | solution.py:395
  65.1 2.9 %collective-permute-start.10 = (bf16[128,1024]{1,0:T(8,128)(2,1)S(1)}, bf16[128,1024]{1,0:T(8,128)(2,1)S(1)}, u32[]{:S(2)}, u32[]{:S(2)}) collective-permute-start(bf16[128,1024]{1,0:T(8,128)(2,1)S(1)} %get-tuple-element.51.refs_0_), channel_id=1, source_target_pairs={{0,48},{16,0},{32,16},{48,32},{64,112},{80,64},{96,80},{112,96},{1... | collective-permute-start | bytes 786440 | tf_op jit(solution)/shard_map/ppermute | solution.py:416
  68.0 2.2 %collective-permute-done.8.refs_2_.refs_6_ = bf16[128,1024]{1,0:T(8,128)(2,1)S(1)} collective-permute-done((bf16[128,1024]{1,0:T(8,128)(2,1)S(1)}, bf16[128,1024]{1,0:T(8,128)(2,1)S(1)}, u32[]{:S(2)}, u32[]{:S(2)}) %collective-permute-start.8) | collective-permute-done | bytes 262176 | tf_op jit(solution)/shard_map/ppermute | solution.py:416
  70.1 3.2 %collective-permute-start.12 = (bf16[128,1024]{1,0:T(8,128)(2,1)S(1)}, bf16[128,1024]{1,0:T(8,128)(2,1)S(1)}, u32[]{:S(2)}, u32[]{:S(2)}) collective-permute-start(bf16[128,1024]{1,0:T(8,128)(2,1)S(1)} %collective-permute-done.7.refs_1_), channel_id=1, source_target_pairs={{0,48},{16,0},{32,16},{48,32},{64,112},{80,64},{96,80},{112,96},{1... | collective-permute-start | bytes 786440 | tf_op jit(solution)/shard_map/ppermute | solution.py:416
  73.4 0.0 collective-permute-done.14.refs_6_.refs_4_
  73.4 1.7 %collective-permute-start.13 = (bf16[128,1024]{1,0:T(8,128)(2,1)S(1)}, bf16[128,1024]{1,0:T(8,128)(2,1)S(1)}, u32[]{:S(2)}, u32[]{:S(2)}) collective-permute-start(bf16[128,1024]{1,0:T(8,128)(2,1)S(1)} %collective-permute-done.8.refs_2_.refs_6_), channel_id=1, source_target_pairs={{0,64},{16,80},{32,96},{48,112},{64,0},{80,16},{96,32},{112,48},{1... | collective-permute-start | bytes 786440 | tf_op jit(solution)/shard_map/ppermute | solution.py:416
  75.1 2.9 %shard_map.136 = (bf16[640,1024]{1,0:T(8,128)(2,1)S(1)}, bf16[256,1024]{1,0:T(8,128)(2,1)S(1)}) custom-call(bf16[128,1024]{1,0:T(8,128)(2,1)S(1)} %get-tuple-element.51.refs_0_, bf16[128,1024]{1,0:T(8,128)(2,1)S(1)} %collective-permute-done.7.refs_1_, bf16[128,1024]{1,0:T(8,128)(2,1)S(1)} %collective-permute-done.9.refs_2_, ...), custom_call_target="tpu_custom_call" | custom-call | tf_op jit(solution)/shard_map/pallas_call | solution.py:395
  77.9 0.6 collective-permute-start.15
  78.5 0.8 collective-permute-done.11.refs_0_.refs_4_
  79.4 0.4 collective-permute-done.12.refs_1_.refs_5_
  79.8 3.5 %shard_map.137 = (bf16[160,1024]{1,0:T(8,128)(2,1)S(1)}, bf16[160,1024]{1,0:T(8,128)(2,1)S(1)}, bf16[160,1024]{1,0:T(8,128)(2,1)S(1)}, bf16[160,1024]{1,0:T(8,128)(2,1)S(1)}, bf16[256,1024]{1,0:T(8,128)(2,1)S(1)}) custom-call(bf16[128,1024]{1,0:T(8,128)(2,1)S(1)} %collective-permute-done.11.refs_0_.refs_4_, ...), custom_call_target="tpu_custom_call" | custom-call | tf_op jit(solution)/shard_map/pallas_call | solution.py:395
  83.4 0.1 collective-permute-start.17
  83.4 1.8 %collective-permute-start.18 = (bf16[160,1024]{1,0:T(8,128)(2,1)S(1)}, bf16[160,1024]{1,0:T(8,128)(2,1)S(1)}, u32[]{:S(2)}, u32[]{:S(2)}) collective-permute-start(bf16[160,1024]{1,0:T(8,128)(2,1)S(1)} %get-tuple-element.63), channel_id=1, source_target_pairs={{0,2},{1,3},{2,0},{3,1},{4,6},{5,7},{6,4},{7,5},{8,10},{9,11},{10,... | collective-permute-start | bytes 983048 | tf_op jit(solution)/shard_map/ppermute | solution.py:553
  85.3 3.2 %collective-permute-start.20 = (bf16[160,1024]{1,0:T(8,128)(2,1)S(1)}, bf16[160,1024]{1,0:T(8,128)(2,1)S(1)}, u32[]{:S(2)}, u32[]{:S(2)}) collective-permute-start(bf16[160,1024]{1,0:T(8,128)(2,1)S(1)} %get-tuple-element.65), channel_id=1, source_target_pairs={{0,12},{1,13},{2,14},{3,15},{4,0},{5,1},{6,2},{7,3},{8,4},{9,5},{1... | collective-permute-start | bytes 983048 | tf_op jit(solution)/shard_map/ppermute | solution.py:554
  88.5 3.2 %shard_map.138 = bf16[1024,1024]{1,0:T(8,128)(2,1)S(1)} custom-call(bf16[128,1024]{1,0:T(8,128)(2,1)S(1)} %get-tuple-element.51.refs_0_, bf16[128,1024]{1,0:T(8,128)(2,1)S(1)} %collective-permute-done.7.refs_1_, bf16[128,1024]{1,0:T(8,128)(2,1)S(1)} %collective-permute-done.9.refs_2_, bf16[128,1024]{1,0:T(8,128)(2,1)S(1)} %collective-permute-done.10.refs_3_, ...), custom_call_target="tpu_custom_call" | custom-call | tf_op jit(solution)/shard_map/pallas_call | solution.py:395
  91.7 2.4 %convolution_convert_fusion.refs_4_ = bf16[1024,1024]{1,0:T(8,128)(2,1)S(1)} fusion(bf16[1024,1024]{1,0:T(8,128)(2,1)S(1)} %shard_map.138, bf16[1024,1024]{1,0:T(8,128)(2,1)S(1)} %copy-done.2), kind=kOutput, calls=%fused_computation | convolution fusion | flops 2148532224 | bytes 6291456 | tf_op jit(solution)/shard_map/dot_general | solution.py:549
  94.2 0.0 copy-start.5
  94.2 0.9 collective-permute-done.18.refs_1_
  95.1 1.1 %collective-permute-done.19.refs_2_ = bf16[160,1024]{1,0:T(8,128)(2,1)S(1)} collective-permute-done((bf16[160,1024]{1,0:T(8,128)(2,1)S(1)}, bf16[160,1024]{1,0:T(8,128)(2,1)S(1)}, u32[]{:S(2)}, u32[]{:S(2)}) %collective-permute-start.19) | collective-permute-done | bytes 327712 | tf_op jit(solution)/shard_map/ppermute | solution.py:554
  96.2 0.1 shard_map.139
  96.4 1.5 %collective-permute-start.21 = (bf16[96,1024]{1,0:T(8,128)(2,1)S(1)}, bf16[96,1024]{1,0:T(8,128)(2,1)S(1)}, u32[]{:S(2)}, u32[]{:S(2)}) collective-permute-start(bf16[96,1024]{1,0:T(8,128)(2,1)S(1)} %get-tuple-element.66.refs_5_), channel_id=1, source_target_pairs={{0,8},{1,9},{2,10},{3,11},{4,12},{5,13},{6,14},{7,15},{8,0},{9,1},... | collective-permute-start | bytes 589832 | tf_op jit(solution)/shard_map/ppermute | solution.py:554
  97.9 1.8 %collective-permute-start.22 = (bf16[96,1024]{1,0:T(8,128)(2,1)S(1)}, bf16[96,1024]{1,0:T(8,128)(2,1)S(1)}, u32[]{:S(2)}, u32[]{:S(2)}) collective-permute-start(bf16[96,1024]{1,0:T(8,128)(2,1)S(1)} %get-tuple-element.68), channel_id=1, source_target_pairs={{0,2},{1,3},{2,0},{3,1},{4,6},{5,7},{6,4},{7,5},{8,10},{9,11},{10,... | collective-permute-start | bytes 589832 | tf_op jit(solution)/shard_map/ppermute | solution.py:553
  99.7 2.1 %shard_map.140 = bf16[1024,128]{1,0:T(8,128)(2,1)} custom-call(f32[128,1024]{1,0:T(8,128)S(1)} %copy-done.8, bf16[128,1024]{1,0:T(8,128)(2,1)} %collective-permute-done.3.refs_1_, bf16[128,1024]{1,0:T(8,128)(2,1)} %collective-permute-done.4.refs_2_, bf16[256,1024]{1,0:T(8,128)(2,1)S(1)} %bitcast.8, ...), custom_call_target="tpu_custom_call" | custom-call | tf_op jit(solution)/shard_map/pallas_call | solution.py:395
  101.9 2.2 %collective-permute-done.21.refs_1_ = bf16[96,1024]{1,0:T(8,128)(2,1)S(1)} collective-permute-done((bf16[96,1024]{1,0:T(8,128)(2,1)S(1)}, bf16[96,1024]{1,0:T(8,128)(2,1)S(1)}, u32[]{:S(2)}, u32[]{:S(2)}) %collective-permute-start.21) | collective-permute-done | bytes 196640 | tf_op jit(solution)/shard_map/ppermute | solution.py:554
  104.1 1.2 %collective-permute-done.22.refs_2_ = bf16[96,1024]{1,0:T(8,128)(2,1)S(1)} collective-permute-done((bf16[96,1024]{1,0:T(8,128)(2,1)S(1)}, bf16[96,1024]{1,0:T(8,128)(2,1)S(1)}, u32[]{:S(2)}, u32[]{:S(2)}) %collective-permute-start.22) | collective-permute-done | bytes 196640 | tf_op jit(solution)/shard_map/ppermute | solution.py:553
  105.3 1.3 %shard_map.141 = (f32[64,1024]{1,0:T(8,128)}, bf16[1024,128]{1,0:T(8,128)(2,1)}, bf16[1024,128]{1,0:T(8,128)(2,1)}) custom-call(f32[64,1024]{1,0:T(8,128)S(1)} %get-tuple-element.67.refs_0_, bf16[96,1024]{1,0:T(8,128)(2,1)S(1)} %collective-permute-done.21.refs_1_, bf16[96,1024]{1,0:T(8,128)(2,1)S(1)} %collective-permute-done.22.refs_2_, ...), custom_call_target="tpu_custom_call" | custom-call | tf_op jit(solution)/shard_map/pallas_call | solution.py:395
  (39 shorter events, 0.1 us)
Async XLA Ops:
  0.6 18.0 %copy-start = (bf16[1024,1024]{1,0:T(8,128)(2,1)S(1)}, bf16[1024,1024]{1,0:T(8,128)(2,1)}, u32[]{:S(2)}) copy-start(bf16[1024,1024]{1,0:T(8,128)(2,1)} %refs_4_.4) | copy-start | bytes 6291460
  6.1 16.5 %collective-permute-start = (bf16[256,1024]{1,0:T(8,128)(2,1)}, bf16[256,1024]{1,0:T(8,128)(2,1)}, u32[]{:S(2)}, u32[]{:S(2)}) collective-permute-start(bf16[256,1024]{1,0:T(8,128)(2,1)} %get-tuple-element.40), channel_id=1, source_target_pairs={{0,16},{16,32},{32,48},{48,0},{64,80},{80,96},{96,112},{112,64},{1... | collective-permute-start | bytes 1572872 | tf_op jit(solution)/shard_map/ppermute | solution.py:416
  8.2 15.1 %collective-permute-start.1 = (bf16[256,1024]{1,0:T(8,128)(2,1)}, bf16[256,1024]{1,0:T(8,128)(2,1)}, u32[]{:S(2)}, u32[]{:S(2)}) collective-permute-start(bf16[256,1024]{1,0:T(8,128)(2,1)} %get-tuple-element.39.refs_2_), channel_id=1, source_target_pairs={{0,64},{16,80},{32,96},{48,112},{64,0},{80,16},{96,32},{112,48},{1... | collective-permute-start | bytes 1572872 | tf_op jit(solution)/shard_map/ppermute | solution.py:416
  9.6 13.6 %collective-permute-start.2 = (bf16[256,1024]{1,0:T(8,128)(2,1)}, bf16[256,1024]{1,0:T(8,128)(2,1)}, u32[]{:S(2)}, u32[]{:S(2)}) collective-permute-start(bf16[256,1024]{1,0:T(8,128)(2,1)} %get-tuple-element.41), channel_id=1, source_target_pairs={{0,48},{16,0},{32,16},{48,32},{64,112},{80,64},{96,80},{112,96},{1... | collective-permute-start | bytes 1572872 | tf_op jit(solution)/shard_map/ppermute | solution.py:416
  11.9 20.3 %all-to-all-start = ((bf16[16,16,1024]{2,1,0:T(8,128)(2,1)}), bf16[16,16,1024]{2,1,0:T(8,128)(2,1)}, u32[]{:S(2)}, u32[]{:S(2)}) async-start(bf16[16,16,1024]{2,1,0:T(8,128)(2,1)} %bitcast.9), calls=%async_computation | async-start | bytes 1048576 | tf_op jit(solution)/shard_map/all_to_all | solution.py:412
  18.7 1.6 %copy-start.1 = (bf16[1024,1024]{1,0:T(8,128)(2,1)S(1)}, bf16[1024,1024]{1,0:T(8,128)(2,1)}, u32[]{:S(2)}) copy-start(bf16[1024,1024]{1,0:T(8,128)(2,1)} %refs_0_.2) | copy-start | bytes 6291460
  20.3 1.0 copy-start.18
  22.5 9.6 %copy-start.3 = (bf16[1040,512]{1,0:T(8,128)(2,1)S(1)}, bf16[1040,512]{1,0:T(8,128)(2,1)}, u32[]{:S(2)}) copy-start(bf16[1040,512]{1,0:T(8,128)(2,1)} %constant.6.clone.refs_1_.first_ref) | copy-start | bytes 3194884
  22.6 9.6 %copy-start.11 = (bf16[512,256]{1,0:T(8,128)(2,1)S(1)}, bf16[512,256]{1,0:T(8,128)(2,1)}, u32[]{:S(2)}) copy-start(bf16[512,256]{1,0:T(8,128)(2,1)} %constant.7.clone.refs_2_.square_ref) | copy-start | bytes 786436
  25.4 0.8 copy-start.6
  26.2 11.4 %collective-permute-start.3 = (bf16[128,1024]{1,0:T(8,128)(2,1)}, bf16[128,1024]{1,0:T(8,128)(2,1)}, u32[]{:S(2)}, u32[]{:S(2)}) collective-permute-start(bf16[128,1024]{1,0:T(8,128)(2,1)} %get-tuple-element.43.refs_4_), channel_id=1, source_target_pairs={{0,32},{16,48},{32,0},{48,16},{64,96},{80,112},{96,64},{112,80},{1... | collective-permute-start | bytes 786440 | tf_op jit(solution)/shard_map/ppermute | solution.py:416
  29.9 7.7 %collective-permute-start.4 = (bf16[128,1024]{1,0:T(8,128)(2,1)}, bf16[128,1024]{1,0:T(8,128)(2,1)}, u32[]{:S(2)}, u32[]{:S(2)}) collective-permute-start(bf16[128,1024]{1,0:T(8,128)(2,1)} %get-tuple-element.44), channel_id=1, source_target_pairs={{0,64},{16,80},{32,96},{48,112},{64,0},{80,16},{96,32},{112,48},{1... | collective-permute-start | bytes 786440 | tf_op jit(solution)/shard_map/ppermute | solution.py:416
  32.1 5.5 %copy-start.7 = (f32[128,1024]{1,0:T(8,128)S(1)}, f32[128,1024]{1,0:T(8,128)}, u32[]{:S(2)}) copy-start(f32[128,1024]{1,0:T(8,128)} %copy-done.6) | copy-start | bytes 1572868
  32.1 5.5 %copy-start.12 = (bf16[1024,128]{1,0:T(8,128)(2,1)S(1)}, bf16[1024,128]{1,0:T(8,128)(2,1)}, u32[]{:S(2)}) copy-start(bf16[1024,128]{1,0:T(8,128)(2,1)} %refs_0_.3) | copy-start | bytes 786436
  32.1 1.0 copy-start.14
  37.6 2.5 %copy-start.16 = (bf16[1040,256]{1,0:T(8,128)(2,1)}, bf16[1040,256]{1,0:T(8,128)(2,1)S(1)}, u32[]{:S(2)}) copy-start(bf16[1040,256]{1,0:T(8,128)(2,1)S(1)} %get-tuple-element.52.h_ref) | copy-start | bytes 1597444
  37.6 8.7 %copy-start.13 = (bf16[1024,128]{1,0:T(8,128)(2,1)S(1)}, bf16[1024,128]{1,0:T(8,128)(2,1)}, u32[]{:S(2)}) copy-start(bf16[1024,128]{1,0:T(8,128)(2,1)} %refs_0_.3) | copy-start | bytes 786436
  40.0 18.6 %collective-permute-start.6 = (bf16[1024,1024]{1,0:T(8,128)(2,1)S(1)}, bf16[1024,1024]{1,0:T(8,128)(2,1)}, u32[]{:S(2)}, u32[]{:S(2)}) collective-permute-start(bf16[1024,1024]{1,0:T(8,128)(2,1)S(1)} %copy-done), channel_id=1, source_target_pairs={{0,1},{1,0},{2,3},{3,2},{4,5},{5,4},{6,7},{7,6},{8,9},{9,8},{10,11... | collective-permute-start | bytes 6291464 | tf_op jit(solution)/shard_map/ppermute | solution.py:481
  40.1 18.5 %all-to-all-start.1 = ((bf16[16,16,1024]{2,1,0:T(8,128)(2,1)}), bf16[16,16,1024]{2,1,0:T(8,128)(2,1)S(1)}, u32[]{:S(2)}, u32[]{:S(2)}) async-start(bf16[16,16,1024]{2,1,0:T(8,128)(2,1)} %bitcast.2), calls=%async_computation.1 | async-start | bytes 1048576 | tf_op jit(solution)/shard_map/all_to_all | solution.py:412
  46.5 1.5 %collective-permute-start.5 = (bf16[64,1024]{1,0:T(8,128)(2,1)S(1)}, bf16[64,1024]{1,0:T(8,128)(2,1)S(1)}, u32[]{:S(2)}, u32[]{:S(2)}) collective-permute-start(bf16[64,1024]{1,0:T(8,128)(2,1)S(1)} %get-tuple-element.49), channel_id=1, source_target_pairs={{0,1},{1,0},{2,3},{3,2},{4,5},{5,4},{6,7},{7,6},{8,9},{9,8},{10,11... | collective-permute-start | bytes 393224 | tf_op jit(solution)/shard_map/ppermute | solution.py:481
  58.6 2.8 %copy-start.4 = (bf16[1040,512]{1,0:T(8,128)(2,1)S(1)}, bf16[1040,512]{1,0:T(8,128)(2,1)}, u32[]{:S(2)}) copy-start(bf16[1040,512]{1,0:T(8,128)(2,1)} %constant.6.clone.refs_1_.first_ref) | copy-start | bytes 3194884
  58.6 2.8 %copy-start.17 = (bf16[1040,256]{1,0:T(8,128)(2,1)S(1)}, bf16[1040,256]{1,0:T(8,128)(2,1)}, u32[]{:S(2)}) copy-start(bf16[1040,256]{1,0:T(8,128)(2,1)} %copy-done.16) | copy-start | bytes 1597444
  58.9 9.0 %collective-permute-start.7 = (bf16[128,1024]{1,0:T(8,128)(2,1)S(1)}, bf16[128,1024]{1,0:T(8,128)(2,1)S(1)}, u32[]{:S(2)}, u32[]{:S(2)}) collective-permute-start(bf16[128,1024]{1,0:T(8,128)(2,1)S(1)} %get-tuple-element.51.refs_0_), channel_id=1, source_target_pairs={{0,64},{16,80},{32,96},{48,112},{64,0},{80,16},{96,32},{112,48},{1... | collective-permute-start | bytes 786440 | tf_op jit(solution)/shard_map/ppermute | solution.py:416
  59.3 10.8 %collective-permute-start.8 = (bf16[128,1024]{1,0:T(8,128)(2,1)S(1)}, bf16[128,1024]{1,0:T(8,128)(2,1)S(1)}, u32[]{:S(2)}, u32[]{:S(2)}) collective-permute-start(bf16[128,1024]{1,0:T(8,128)(2,1)S(1)} %get-tuple-element.51.refs_0_), channel_id=1, source_target_pairs={{0,32},{16,48},{32,0},{48,16},{64,96},{80,112},{96,64},{112,80},{1... | collective-permute-start | bytes 786440 | tf_op jit(solution)/shard_map/ppermute | solution.py:416
  60.8 14.2 %collective-permute-start.9 = (bf16[128,1024]{1,0:T(8,128)(2,1)S(1)}, bf16[128,1024]{1,0:T(8,128)(2,1)S(1)}, u32[]{:S(2)}, u32[]{:S(2)}) collective-permute-start(bf16[128,1024]{1,0:T(8,128)(2,1)S(1)} %get-tuple-element.51.refs_0_), channel_id=1, source_target_pairs={{0,16},{16,32},{32,48},{48,0},{64,80},{80,96},{96,112},{112,64},{1... | collective-permute-start | bytes 786440 | tf_op jit(solution)/shard_map/ppermute | solution.py:416
  61.4 11.9 %collective-permute-start.14 = (bf16[64,1024]{1,0:T(8,128)(2,1)S(1)}, bf16[64,1024]{1,0:T(8,128)(2,1)S(1)}, u32[]{:S(2)}, u32[]{:S(2)}) collective-permute-start(bf16[64,1024]{1,0:T(8,128)(2,1)S(1)} %get-tuple-element.56), channel_id=1, source_target_pairs={{0,1},{1,0},{2,3},{3,2},{4,5},{5,4},{6,7},{7,6},{8,9},{9,8},{10,11... | collective-permute-start | bytes 393224 | tf_op jit(solution)/shard_map/ppermute | solution.py:481
  61.4 0.9 copy-start.15
  65.1 10.0 %collective-permute-start.10 = (bf16[128,1024]{1,0:T(8,128)(2,1)S(1)}, bf16[128,1024]{1,0:T(8,128)(2,1)S(1)}, u32[]{:S(2)}, u32[]{:S(2)}) collective-permute-start(bf16[128,1024]{1,0:T(8,128)(2,1)S(1)} %get-tuple-element.51.refs_0_), channel_id=1, source_target_pairs={{0,48},{16,0},{32,16},{48,32},{64,112},{80,64},{96,80},{112,96},{1... | collective-permute-start | bytes 786440 | tf_op jit(solution)/shard_map/ppermute | solution.py:416
  70.1 9.3 %collective-permute-start.11 = (bf16[128,1024]{1,0:T(8,128)(2,1)S(1)}, bf16[128,1024]{1,0:T(8,128)(2,1)S(1)}, u32[]{:S(2)}, u32[]{:S(2)}) collective-permute-start(bf16[128,1024]{1,0:T(8,128)(2,1)S(1)} %collective-permute-done.7.refs_1_), channel_id=1, source_target_pairs={{0,16},{16,32},{32,48},{48,0},{64,80},{80,96},{96,112},{112,64},{1... | collective-permute-start | bytes 786440 | tf_op jit(solution)/shard_map/ppermute | solution.py:416
  70.1 9.7 %collective-permute-start.12 = (bf16[128,1024]{1,0:T(8,128)(2,1)S(1)}, bf16[128,1024]{1,0:T(8,128)(2,1)S(1)}, u32[]{:S(2)}, u32[]{:S(2)}) collective-permute-start(bf16[128,1024]{1,0:T(8,128)(2,1)S(1)} %collective-permute-done.7.refs_1_), channel_id=1, source_target_pairs={{0,48},{16,0},{32,16},{48,32},{64,112},{80,64},{96,80},{112,96},{1... | collective-permute-start | bytes 786440 | tf_op jit(solution)/shard_map/ppermute | solution.py:416
  73.4 6.4 %collective-permute-start.13 = (bf16[128,1024]{1,0:T(8,128)(2,1)S(1)}, bf16[128,1024]{1,0:T(8,128)(2,1)S(1)}, u32[]{:S(2)}, u32[]{:S(2)}) collective-permute-start(bf16[128,1024]{1,0:T(8,128)(2,1)S(1)} %collective-permute-done.8.refs_2_.refs_6_), channel_id=1, source_target_pairs={{0,64},{16,80},{32,96},{48,112},{64,0},{80,16},{96,32},{112,48},{1... | collective-permute-start | bytes 786440 | tf_op jit(solution)/shard_map/ppermute | solution.py:416
  75.1 3.5 %collective-permute-start.16 = (bf16[64,1024]{1,0:T(8,128)(2,1)S(1)}, bf16[64,1024]{1,0:T(8,128)(2,1)S(1)}, u32[]{:S(2)}, u32[]{:S(2)}) collective-permute-start(bf16[64,1024]{1,0:T(8,128)(2,1)S(1)} %get-tuple-element.59), channel_id=1, source_target_pairs={{0,1},{1,0},{2,3},{3,2},{4,5},{5,4},{6,7},{7,6},{8,9},{9,8},{10,11... | collective-permute-start | bytes 393224 | tf_op jit(solution)/shard_map/ppermute | solution.py:481
  77.9 10.5 %collective-permute-start.15 = (bf16[256,1024]{1,0:T(8,128)(2,1)S(1)}, bf16[256,1024]{1,0:T(8,128)(2,1)S(1)}, u32[]{:S(2)}, u32[]{:S(2)}) collective-permute-start(bf16[256,1024]{1,0:T(8,128)(2,1)S(1)} %get-tuple-element.57), channel_id=1, source_target_pairs={{0,1},{1,0},{2,3},{3,2},{4,5},{5,4},{6,7},{7,6},{8,9},{9,8},{10,11... | collective-permute-start | bytes 1572872 | tf_op jit(solution)/shard_map/ppermute | solution.py:481
  83.4 5.1 %collective-permute-start.17 = (bf16[256,1024]{1,0:T(8,128)(2,1)S(1)}, bf16[256,1024]{1,0:T(8,128)(2,1)S(1)}, u32[]{:S(2)}, u32[]{:S(2)}) collective-permute-start(bf16[256,1024]{1,0:T(8,128)(2,1)S(1)} %get-tuple-element.61), channel_id=1, source_target_pairs={{0,1},{1,0},{2,3},{3,2},{4,5},{5,4},{6,7},{7,6},{8,9},{9,8},{10,11... | collective-permute-start | bytes 1572872 | tf_op jit(solution)/shard_map/ppermute | solution.py:481
  83.4 11.6 %collective-permute-start.18 = (bf16[160,1024]{1,0:T(8,128)(2,1)S(1)}, bf16[160,1024]{1,0:T(8,128)(2,1)S(1)}, u32[]{:S(2)}, u32[]{:S(2)}) collective-permute-start(bf16[160,1024]{1,0:T(8,128)(2,1)S(1)} %get-tuple-element.63), channel_id=1, source_target_pairs={{0,2},{1,3},{2,0},{3,1},{4,6},{5,7},{6,4},{7,5},{8,10},{9,11},{10,... | collective-permute-start | bytes 983048 | tf_op jit(solution)/shard_map/ppermute | solution.py:553
  85.2 11.0 %collective-permute-start.19 = (bf16[160,1024]{1,0:T(8,128)(2,1)S(1)}, bf16[160,1024]{1,0:T(8,128)(2,1)S(1)}, u32[]{:S(2)}, u32[]{:S(2)}) collective-permute-start(bf16[160,1024]{1,0:T(8,128)(2,1)S(1)} %get-tuple-element.64), channel_id=1, source_target_pairs={{0,4},{1,5},{2,6},{3,7},{4,8},{5,9},{6,10},{7,11},{8,12},{9,13},{1... | collective-permute-start | bytes 983048 | tf_op jit(solution)/shard_map/ppermute | solution.py:554
  85.2 6.5 %copy-start.2 = (bf16[1024,1024]{1,0:T(8,128)(2,1)S(1)}, bf16[1024,1024]{1,0:T(8,128)(2,1)}, u32[]{:S(2)}) copy-start(bf16[1024,1024]{1,0:T(8,128)(2,1)} %refs_0_.2) | copy-start | bytes 6291460
  85.3 11.0 %collective-permute-start.20 = (bf16[160,1024]{1,0:T(8,128)(2,1)S(1)}, bf16[160,1024]{1,0:T(8,128)(2,1)S(1)}, u32[]{:S(2)}, u32[]{:S(2)}) collective-permute-start(bf16[160,1024]{1,0:T(8,128)(2,1)S(1)} %get-tuple-element.65), channel_id=1, source_target_pairs={{0,12},{1,13},{2,14},{3,15},{4,0},{5,1},{6,2},{7,3},{8,4},{9,5},{1... | collective-permute-start | bytes 983048 | tf_op jit(solution)/shard_map/ppermute | solution.py:554
  94.2 7.7 %copy-start.5 = (bf16[1024,1024]{1,0:T(8,128)(2,1)}, bf16[1024,1024]{1,0:T(8,128)(2,1)S(1)}, u32[]{:S(2)}) copy-start(bf16[1024,1024]{1,0:T(8,128)(2,1)S(1)} %convolution_convert_fusion.refs_4_) | copy-start | bytes 6291460
  94.2 5.6 %copy-start.8 = (f32[128,1024]{1,0:T(8,128)S(1)}, f32[128,1024]{1,0:T(8,128)}, u32[]{:S(2)}) copy-start(f32[128,1024]{1,0:T(8,128)} %copy-done.6) | copy-start | bytes 1572868
  96.2 9.1 %copy-start.9 = (bf16[1024,128]{1,0:T(8,128)(2,1)S(1)}, bf16[1024,128]{1,0:T(8,128)(2,1)}, u32[]{:S(2)}) copy-start(bf16[1024,128]{1,0:T(8,128)(2,1)} %refs_4_.5) | copy-start | bytes 786436
  96.2 9.1 %copy-start.10 = (bf16[1024,128]{1,0:T(8,128)(2,1)S(1)}, bf16[1024,128]{1,0:T(8,128)(2,1)}, u32[]{:S(2)}) copy-start(bf16[1024,128]{1,0:T(8,128)(2,1)} %refs_5_.1) | copy-start | bytes 786436
  96.4 7.7 %collective-permute-start.21 = (bf16[96,1024]{1,0:T(8,128)(2,1)S(1)}, bf16[96,1024]{1,0:T(8,128)(2,1)S(1)}, u32[]{:S(2)}, u32[]{:S(2)}) collective-permute-start(bf16[96,1024]{1,0:T(8,128)(2,1)S(1)} %get-tuple-element.66.refs_5_), channel_id=1, source_target_pairs={{0,8},{1,9},{2,10},{3,11},{4,12},{5,13},{6,14},{7,15},{8,0},{9,1},... | collective-permute-start | bytes 589832 | tf_op jit(solution)/shard_map/ppermute | solution.py:554
  97.9 7.4 %collective-permute-start.22 = (bf16[96,1024]{1,0:T(8,128)(2,1)S(1)}, bf16[96,1024]{1,0:T(8,128)(2,1)S(1)}, u32[]{:S(2)}, u32[]{:S(2)}) collective-permute-start(bf16[96,1024]{1,0:T(8,128)(2,1)S(1)} %get-tuple-element.68), channel_id=1, source_target_pairs={{0,2},{1,3},{2,0},{3,1},{4,6},{5,7},{6,4},{7,5},{8,10},{9,11},{10,... | collective-permute-start | bytes 589832 | tf_op jit(solution)/shard_map/ppermute | solution.py:553

commit v10 on v9

--- a/solution.py
+++ b/solution.py
@@ -201,7 +201,8 @@
 
 class Tables:
     def __init__(self, first, square, twiddle):
-        self.first, self.square = first, square
+        half = first.shape[1] // 2
+        self.first, self.square = [first.at[:, pl.ds(i * half, half)] for i in range(2)], square
         self.group = first.shape[0] // twiddle.shape[0]
         rows = [jnp.broadcast_to(twiddle[i : i + 1, :], (self.group, FAC)) for i in range(twiddle.shape[0])]
         self.twiddle = jnp.concatenate(rows, axis=0)
@@ -214,7 +215,8 @@
 
 def transform(x, tables):
     x = jnp.concatenate([x[:, u * FAC : (u + 1) * FAC] for u in range(LANE_TILES)], axis=0)
-    section = dot(tables.first[...], x)
+    width = tables.first[0].shape[1]
+    section = sum(dot(part[...], x[i * width : (i + 1) * width]) for i, part in enumerate(tables.first))
     n = section.shape[0] // 2
     twiddle = tables.twiddle
     re, im, tc, ts = section[:n], section[n:], twiddle[:n], twiddle[n:]
@@ -234,7 +236,8 @@
     row = lax.broadcasted_iota(jnp.int32, re.shape, 0)
     weight = jnp.where((row < group) | (row >= n - group), 1.0 / (QF * FAC), 2.0 / (QF * FAC))
     e = jnp.concatenate([(re * tc - im * ts) * weight, (im * tc + re * ts) * weight], axis=0).astype(BF)
-    x = lax.dot_general(tables.first[...], e, (((0,), (0,)), ((), ())), preferred_element_type=F32)
+    turned = lambda part: lax.dot_general(part[...], e, (((0,), (0,)), ((), ())), preferred_element_type=F32)
+    x = jnp.concatenate([turned(part) for part in tables.first], axis=0)
     rows = x.shape[0] // LANE_TILES
     return jnp.concatenate([x[u * rows : (u + 1) * rows] for u in range(LANE_TILES)], axis=1)
 
@@ -527,7 +530,7 @@
     du_away, du_keep = call(
         adjoint_kernel, [half_like, half_like], [arrived, spectrum, *tables], mib=20, flops=2 * flops
     )
-    other, own_far, du_away = lax.optimization_barrier((other, own_far, du_away))
+    own_far, other, du_away = lax.optimization_barrier((own_far, other, du_away))
     du_got = swap(du_away)
     other_far = move_over(own_far, (1, 0))
     other_up, other_down = move_over(other, (0, 1)), move_over(other, (0, -1))

time: 108 us -> 108 us (level)
  starting transfers between devices: 43.8 us -> 42 us
  waiting for transfers between devices: 21.9 us -> 23.4 us
    ppermute x12, waiting for transfers between devices: 4.11 us -> 5.96 us  [move_over(): return lax.ppermute(values, 'fsdp', [(i, place(i, move)) for i in range(8)])]
    ppermute x12, starting transfers between devices: 21.3 us -> 19.9 us  [move_over(): return lax.ppermute(values, 'fsdp', [(i, place(i, move)) for i in range(8)])]
  transfers between devices with their start and end apart: 25 -> 25, of which waited for: 11 -> 13; matrix products, arithmetic and copies ran while one was open for 2% -> 2% of each run, Pallas kernels for 21% -> 21%
where the time goes in v10:
time: 108 us; the launch traced here: 106 us
  starting transfers between devices  42 us (39%)
  Pallas kernels  32.1 us (30%)
  waiting for transfers between devices  23.4 us (22%)
  local copies, waits for them, and re-layouts  5.36 us (5%)
  matrix products  2.43 us (2%)
  between operations  1.13 us (1%)
    pallas_call x14, Pallas kernels, call(): pl.pallas_call(kernel, out_shape=outs, in_specs=[*in_specs, *[ANY] * len(...  32.1 us
    ppermute x12, starting transfers between devices, move_over(): return lax.ppermute(values, 'fsdp', [(i, place(i, move)) for i in range(8)])  19.9 us
    all_to_all x2, starting transfers between devices, spread(): return lax.all_to_all(values, 'ctx', 0, 0, tiled=True)  12.9 us
    all_to_all x2, waiting for transfers between devices, spread(): return lax.all_to_all(values, 'ctx', 0, 0, tiled=True)  11.4 us
    ppermute x12, waiting for transfers between devices, move_over(): return lax.ppermute(values, 'fsdp', [(i, place(i, move)) for i in range(8)])  5.96 us
    unnamed x38, local copies, waits for them, and re-layouts  5.36 us
    ppermute x3, starting transfers between devices, on_device(): lax.ppermute(v, 'ctx', [(i, (i + 4 * step) % ways) for i in range(ways)])  4.78 us
    ppermute x2, starting transfers between devices, on_device(): over_x = lambda v: lax.ppermute(v, 'ctx', [(i, i ^ 2) for i in range(ways)])  3.61 us
  transfers between devices with their start and end apart: 25, of which 13 were waited for; matrix products, arithmetic and copies ran while one was open for 2% of the time, Pallas kernels for 21%

profile of v10, /device:TPU:0, one launch (start us, length us, event | category | flops | bytes accessed | tf_op | source)
XLA Modules:
  0.0 106.4 jit_solution(10777864515335389484)
XLA Ops:
  0.6 5.4 %shard_map.128 = (bf16[256,1024]{1,0:T(8,128)(2,1)}, bf16[256,1024]{1,0:T(8,128)(2,1)}, bf16[256,1024]{1,0:T(8,128)(2,1)}, bf16[256,1024]{1,0:T(8,128)(2,1)}) custom-call(bf16[1024,1024]{1,0:T(8,128)(2,1)} %refs_0_.2, bf16[1024,1024]{1,0:T(8,128)(2,1)} %refs_4_.4, bf16[1024,128]{1,0:T(8,128)(2,1)} %refs_4_.5, bf16[1024,128]{1,0:T(8,128)(2,1)} %refs_5_.1, ...), custom_call_target="tpu_custom_call" | custom-call | tf_op jit(solution)/shard_map/pallas_call | solution.py:398
  6.1 2.1 %collective-permute-start = (bf16[256,1024]{1,0:T(8,128)(2,1)}, bf16[256,1024]{1,0:T(8,128)(2,1)}, u32[]{:S(2)}, u32[]{:S(2)}) collective-permute-start(bf16[256,1024]{1,0:T(8,128)(2,1)} %get-tuple-element.40), channel_id=1, source_target_pairs={{0,16},{16,32},{32,48},{48,0},{64,80},{80,96},{96,112},{112,64},{1... | collective-permute-start | bytes 1572872 | tf_op jit(solution)/shard_map/ppermute | solution.py:419
  8.2 1.5 %collective-permute-start.1 = (bf16[256,1024]{1,0:T(8,128)(2,1)}, bf16[256,1024]{1,0:T(8,128)(2,1)}, u32[]{:S(2)}, u32[]{:S(2)}) collective-permute-start(bf16[256,1024]{1,0:T(8,128)(2,1)} %get-tuple-element.39.refs_2_), channel_id=1, source_target_pairs={{0,64},{16,80},{32,96},{48,112},{64,0},{80,16},{96,32},{112,48},{1... | collective-permute-start | bytes 1572872 | tf_op jit(solution)/shard_map/ppermute | solution.py:419
  9.6 2.2 %collective-permute-start.2 = (bf16[256,1024]{1,0:T(8,128)(2,1)}, bf16[256,1024]{1,0:T(8,128)(2,1)}, u32[]{:S(2)}, u32[]{:S(2)}) collective-permute-start(bf16[256,1024]{1,0:T(8,128)(2,1)} %get-tuple-element.41), channel_id=1, source_target_pairs={{0,48},{16,0},{32,16},{48,32},{64,112},{80,64},{96,80},{112,96},{1... | collective-permute-start | bytes 1572872 | tf_op jit(solution)/shard_map/ppermute | solution.py:419
  11.9 6.8 %all-to-all-start = ((bf16[16,16,1024]{2,1,0:T(8,128)(2,1)}), bf16[16,16,1024]{2,1,0:T(8,128)(2,1)}, u32[]{:S(2)}, u32[]{:S(2)}) async-start(bf16[16,16,1024]{2,1,0:T(8,128)(2,1)} %bitcast.9), calls=%async_computation | async-start | bytes 1048576 | tf_op jit(solution)/shard_map/all_to_all | solution.py:415
  18.7 0.0 copy-start.1
  18.7 1.6 %copy-done.1 = bf16[1024,1024]{1,0:T(8,128)(2,1)S(1)} copy-done((bf16[1024,1024]{1,0:T(8,128)(2,1)S(1)}, bf16[1024,1024]{1,0:T(8,128)(2,1)}, u32[]{:S(2)}) %copy-start.1) | copy-done | bytes 2097176
  20.3 1.0 copy-done.18
  21.3 1.2 %shard_map.129.own_ref = bf16[256,1024]{1,0:T(8,128)(2,1)S(1)} custom-call(bf16[1024,1024]{1,0:T(8,128)(2,1)S(1)} %copy-done.1, bf16[1024,1024]{1,0:T(8,128)(2,1)S(1)} %copy-done, bf16[256,1024]{1,0:T(8,128)(2,1)S(1)} %copy-done.18), custom_call_target="tpu_custom_call" | custom-call | tf_op jit(solution)/shard_map/pallas_call | solution.py:398
  22.5 0.0 copy-start.3
  22.6 0.0 copy-start.11
  22.6 0.0 collective-permute-done.up_ref
  22.6 0.6 collective-permute-done.1.x_ref
  23.2 0.0 collective-permute-done.2.down_ref
  23.2 2.2 %shard_map.130 = (f32[128,1024]{1,0:T(8,128)S(1)}, bf16[128,1024]{1,0:T(8,128)(2,1)}, bf16[128,1024]{1,0:T(8,128)(2,1)}) custom-call(bf16[256,1024]{1,0:T(8,128)(2,1)S(1)} %shard_map.129.own_ref, bf16[256,1024]{1,0:T(8,128)(2,1)} %collective-permute-done.up_ref, bf16[256,1024]{1,0:T(8,128)(2,1)} %collective-permute-done.1.x_ref, ...), custom_call_target="tpu_custom_call" | custom-call | tf_op jit(solution)/shard_map/pallas_call | solution.py:398
  25.4 0.8 copy-done.6
  26.2 3.7 %collective-permute-start.3 = (bf16[128,1024]{1,0:T(8,128)(2,1)}, bf16[128,1024]{1,0:T(8,128)(2,1)}, u32[]{:S(2)}, u32[]{:S(2)}) collective-permute-start(bf16[128,1024]{1,0:T(8,128)(2,1)} %get-tuple-element.43.refs_4_), channel_id=1, source_target_pairs={{0,32},{16,48},{32,0},{48,16},{64,96},{80,112},{96,64},{112,80},{1... | collective-permute-start | bytes 786440 | tf_op jit(solution)/shard_map/ppermute | solution.py:419
  29.9 1.5 %collective-permute-start.4 = (bf16[128,1024]{1,0:T(8,128)(2,1)}, bf16[128,1024]{1,0:T(8,128)(2,1)}, u32[]{:S(2)}, u32[]{:S(2)}) collective-permute-start(bf16[128,1024]{1,0:T(8,128)(2,1)} %get-tuple-element.44), channel_id=1, source_target_pairs={{0,64},{16,80},{32,96},{48,112},{64,0},{80,16},{96,32},{112,48},{1... | collective-permute-start | bytes 786440 | tf_op jit(solution)/shard_map/ppermute | solution.py:419
  31.4 0.7 all-to-all-done
  32.1 0.0 copy-start.14
  32.1 1.0 copy-done.14
  33.1 4.5 %shard_map.131 = (bf16[128,1024]{1,0:T(8,128)(2,1)S(1)}, bf16[1040,256]{1,0:T(8,128)(2,1)S(1)}) custom-call(bf16[256,1024]{1,0:T(8,128)(2,1)} %bitcast.1.refs_0_, bf16[1040,512]{1,0:T(8,128)(2,1)S(1)} %copy-done.3, bf16[512,256]{1,0:T(8,128)(2,1)S(1)} %copy-done.11, f32[130,256]{1,0:T(8,128)S(1)} %copy-done.14, bf16[128,1024]{1,0:T(8,128)(2,1)} %get-tuple-element.43.refs_4_), custom_call_target="tpu_custom_call" | custom-call | tf_op jit(solution)/shard_map/pallas_call | solution.py:398
  37.6 0.0 copy-start.16
  37.6 0.0 copy-start.13
  37.6 2.4 %shard_map.132.refs_1_ = bf16[256,1024]{1,0:T(8,128)(2,1)} custom-call(f32[128,1024]{1,0:T(8,128)S(1)} %copy-done.7, bf16[128,1024]{1,0:T(8,128)(2,1)} %collective-permute-done.3.refs_1_, bf16[128,1024]{1,0:T(8,128)(2,1)} %collective-permute-done.4.refs_2_, bf16[1024,128]{1,0:T(8,128)(2,1)S(1)} %copy-done.12, bf16[128,1024]{1,0:T(8,128)(2,1)S(1)} %get-tuple-element.46.refs_4_), custom_call_target="tpu_custom_call" | custom-call | tf_op jit(solution)/shard_map/pallas_call | solution.py:398
  40.1 0.1 collective-permute-start.6
  40.1 6.1 %all-to-all-start.1 = ((bf16[16,16,1024]{2,1,0:T(8,128)(2,1)}), bf16[16,16,1024]{2,1,0:T(8,128)(2,1)S(1)}, u32[]{:S(2)}, u32[]{:S(2)}) async-start(bf16[16,16,1024]{2,1,0:T(8,128)(2,1)} %bitcast.2), calls=%async_computation.1 | async-start | bytes 1048576 | tf_op jit(solution)/shard_map/all_to_all | solution.py:415
  46.3 0.2 shard_map.133
  46.5 0.5 collective-permute-start.5
  47.0 1.0 collective-permute-done.5.refs_2_
  48.0 10.7 %all-to-all-done.1 = bf16[16,16,1024]{2,1,0:T(8,128)(2,1)S(1)} async-done(((bf16[16,16,1024]{2,1,0:T(8,128)(2,1)}), bf16[16,16,1024]{2,1,0:T(8,128)(2,1)S(1)}, u32[]{:S(2)}, u32[]{:S(2)}) %all-to-all-start.1) | async-done | bytes 524320 | tf_op jit(solution)/shard_map/all_to_all | solution.py:415
  58.7 0.3 shard_map.134
  58.9 1.3 %collective-permute-start.7 = (bf16[128,1024]{1,0:T(8,128)(2,1)S(1)}, bf16[128,1024]{1,0:T(8,128)(2,1)S(1)}, u32[]{:S(2)}, u32[]{:S(2)}) collective-permute-start(bf16[128,1024]{1,0:T(8,128)(2,1)S(1)} %get-tuple-element.51.refs_0_), channel_id=1, source_target_pairs={{0,32},{16,48},{32,0},{48,16},{64,96},{80,112},{96,64},{112,80},{1... | collective-permute-start | bytes 786440 | tf_op jit(solution)/shard_map/ppermute | solution.py:419
  60.2 0.6 collective-permute-start.8
  60.8 0.6 collective-permute-start.9
  61.4 0.0 copy-start.15
  61.5 0.9 copy-done.15
  62.4 2.7 %shard_map.135 = (bf16[64,1024]{1,0:T(8,128)(2,1)S(1)}, bf16[64,1024]{1,0:T(8,128)(2,1)S(1)}) custom-call(bf16[256,1024]{1,0:T(8,128)(2,1)S(1)} %bitcast.7, bf16[1040,256]{1,0:T(8,128)(2,1)S(1)} %copy-done.17, bf16[1040,512]{1,0:T(8,128)(2,1)S(1)} %copy-done.4, bf16[512,256]{1,0:T(8,128)(2,1)S(1)} %copy-done.11, f32[130,256]{1,0:T(8,128)S(1)} %copy-done.15), custom_call_target="tpu_custom_call" | custom-call | tf_op jit(solution)/shard_map/pallas_call | solution.py:398
  65.0 2.9 %collective-permute-start.10 = (bf16[128,1024]{1,0:T(8,128)(2,1)S(1)}, bf16[128,1024]{1,0:T(8,128)(2,1)S(1)}, u32[]{:S(2)}, u32[]{:S(2)}) collective-permute-start(bf16[128,1024]{1,0:T(8,128)(2,1)S(1)} %get-tuple-element.51.refs_0_), channel_id=1, source_target_pairs={{0,48},{16,0},{32,16},{48,32},{64,112},{80,64},{96,80},{112,96},{1... | collective-permute-start | bytes 786440 | tf_op jit(solution)/shard_map/ppermute | solution.py:419
  68.0 1.8 %collective-permute-done.7.refs_2_.refs_6_ = bf16[128,1024]{1,0:T(8,128)(2,1)S(1)} collective-permute-done((bf16[128,1024]{1,0:T(8,128)(2,1)S(1)}, bf16[128,1024]{1,0:T(8,128)(2,1)S(1)}, u32[]{:S(2)}, u32[]{:S(2)}) %collective-permute-start.7) | collective-permute-done | bytes 262176 | tf_op jit(solution)/shard_map/ppermute | solution.py:419
  69.8 3.2 %collective-permute-start.12 = (bf16[128,1024]{1,0:T(8,128)(2,1)S(1)}, bf16[128,1024]{1,0:T(8,128)(2,1)S(1)}, u32[]{:S(2)}, u32[]{:S(2)}) collective-permute-start(bf16[128,1024]{1,0:T(8,128)(2,1)S(1)} %collective-permute-done.8.refs_1_), channel_id=1, source_target_pairs={{0,48},{16,0},{32,16},{48,32},{64,112},{80,64},{96,80},{112,96},{1... | collective-permute-start | bytes 786440 | tf_op jit(solution)/shard_map/ppermute | solution.py:419
  73.0 0.3 collective-permute-start.13
  73.4 0.4 collective-permute-done.9.refs_2_
  73.8 0.8 collective-permute-done.10.refs_3_
  74.6 2.9 %shard_map.136 = (bf16[640,1024]{1,0:T(8,128)(2,1)S(1)}, bf16[256,1024]{1,0:T(8,128)(2,1)S(1)}) custom-call(bf16[128,1024]{1,0:T(8,128)(2,1)S(1)} %get-tuple-element.51.refs_0_, bf16[128,1024]{1,0:T(8,128)(2,1)S(1)} %collective-permute-done.8.refs_1_, bf16[128,1024]{1,0:T(8,128)(2,1)S(1)} %collective-permute-done.9.refs_2_, ...), custom_call_target="tpu_custom_call" | custom-call | tf_op jit(solution)/shard_map/pallas_call | solution.py:398
  77.4 0.1 collective-permute-start.15
  77.5 1.7 %collective-permute-done.11.refs_0_.refs_4_ = bf16[128,1024]{1,0:T(8,128)(2,1)S(1)} collective-permute-done((bf16[128,1024]{1,0:T(8,128)(2,1)S(1)}, bf16[128,1024]{1,0:T(8,128)(2,1)S(1)}, u32[]{:S(2)}, u32[]{:S(2)}) %collective-permute-start.11) | collective-permute-done | bytes 262176 | tf_op jit(solution)/shard_map/ppermute | solution.py:419
  79.3 0.5 collective-permute-done.12.refs_1_.refs_5_
  79.8 3.5 %shard_map.137 = (bf16[160,1024]{1,0:T(8,128)(2,1)S(1)}, bf16[160,1024]{1,0:T(8,128)(2,1)S(1)}, bf16[160,1024]{1,0:T(8,128)(2,1)S(1)}, bf16[160,1024]{1,0:T(8,128)(2,1)S(1)}, bf16[256,1024]{1,0:T(8,128)(2,1)S(1)}) custom-call(bf16[128,1024]{1,0:T(8,128)(2,1)S(1)} %collective-permute-done.11.refs_0_.refs_4_, ...), custom_call_target="tpu_custom_call" | custom-call | tf_op jit(solution)/shard_map/pallas_call | solution.py:398
  83.3 0.1 collective-permute-start.17
  83.4 1.5 %collective-permute-start.18 = (bf16[160,1024]{1,0:T(8,128)(2,1)S(1)}, bf16[160,1024]{1,0:T(8,128)(2,1)S(1)}, u32[]{:S(2)}, u32[]{:S(2)}) collective-permute-start(bf16[160,1024]{1,0:T(8,128)(2,1)S(1)} %get-tuple-element.63), channel_id=1, source_target_pairs={{0,2},{1,3},{2,0},{3,1},{4,6},{5,7},{6,4},{7,5},{8,10},{9,11},{10,... | collective-permute-start | bytes 983048 | tf_op jit(solution)/shard_map/ppermute | solution.py:556
  84.9 3.2 %collective-permute-start.20 = (bf16[160,1024]{1,0:T(8,128)(2,1)S(1)}, bf16[160,1024]{1,0:T(8,128)(2,1)S(1)}, u32[]{:S(2)}, u32[]{:S(2)}) collective-permute-start(bf16[160,1024]{1,0:T(8,128)(2,1)S(1)} %get-tuple-element.65), channel_id=1, source_target_pairs={{0,12},{1,13},{2,14},{3,15},{4,0},{5,1},{6,2},{7,3},{8,4},{9,5},{1... | collective-permute-start | bytes 983048 | tf_op jit(solution)/shard_map/ppermute | solution.py:557
  88.2 3.2 %shard_map.138 = bf16[1024,1024]{1,0:T(8,128)(2,1)S(1)} custom-call(bf16[128,1024]{1,0:T(8,128)(2,1)S(1)} %get-tuple-element.51.refs_0_, bf16[128,1024]{1,0:T(8,128)(2,1)S(1)} %collective-permute-done.8.refs_1_, bf16[128,1024]{1,0:T(8,128)(2,1)S(1)} %collective-permute-done.9.refs_2_, bf16[128,1024]{1,0:T(8,128)(2,1)S(1)} %collective-permute-done.10.refs_3_, ...), custom_call_target="tpu_custom_call" | custom-call | tf_op jit(solution)/shard_map/pallas_call | solution.py:398
  91.4 2.4 %convolution_convert_fusion.refs_4_ = bf16[1024,1024]{1,0:T(8,128)(2,1)S(1)} fusion(bf16[1024,1024]{1,0:T(8,128)(2,1)S(1)} %shard_map.138, bf16[1024,1024]{1,0:T(8,128)(2,1)S(1)} %copy-done.2), kind=kOutput, calls=%fused_computation | convolution fusion | flops 2148532224 | bytes 6291456 | tf_op jit(solution)/shard_map/dot_general | solution.py:552
  93.8 0.0 copy-start.5
  93.9 1.2 %collective-permute-done.18.refs_1_ = bf16[160,1024]{1,0:T(8,128)(2,1)S(1)} collective-permute-done((bf16[160,1024]{1,0:T(8,128)(2,1)S(1)}, bf16[160,1024]{1,0:T(8,128)(2,1)S(1)}, u32[]{:S(2)}, u32[]{:S(2)}) %collective-permute-start.18) | collective-permute-done | bytes 327712 | tf_op jit(solution)/shard_map/ppermute | solution.py:556
  95.1 0.8 collective-permute-done.19.refs_2_
  95.9 0.1 shard_map.139
  96.1 1.5 %collective-permute-start.21 = (bf16[96,1024]{1,0:T(8,128)(2,1)S(1)}, bf16[96,1024]{1,0:T(8,128)(2,1)S(1)}, u32[]{:S(2)}, u32[]{:S(2)}) collective-permute-start(bf16[96,1024]{1,0:T(8,128)(2,1)S(1)} %get-tuple-element.66.refs_5_), channel_id=1, source_target_pairs={{0,8},{1,9},{2,10},{3,11},{4,12},{5,13},{6,14},{7,15},{8,0},{9,1},... | collective-permute-start | bytes 589832 | tf_op jit(solution)/shard_map/ppermute | solution.py:557
  97.6 2.1 %collective-permute-start.22 = (bf16[96,1024]{1,0:T(8,128)(2,1)S(1)}, bf16[96,1024]{1,0:T(8,128)(2,1)S(1)}, u32[]{:S(2)}, u32[]{:S(2)}) collective-permute-start(bf16[96,1024]{1,0:T(8,128)(2,1)S(1)} %get-tuple-element.68), channel_id=1, source_target_pairs={{0,2},{1,3},{2,0},{3,1},{4,6},{5,7},{6,4},{7,5},{8,10},{9,11},{10,... | collective-permute-start | bytes 589832 | tf_op jit(solution)/shard_map/ppermute | solution.py:556
  99.7 2.1 %shard_map.140 = bf16[1024,128]{1,0:T(8,128)(2,1)} custom-call(f32[128,1024]{1,0:T(8,128)S(1)} %copy-done.8, bf16[128,1024]{1,0:T(8,128)(2,1)} %collective-permute-done.3.refs_1_, bf16[128,1024]{1,0:T(8,128)(2,1)} %collective-permute-done.4.refs_2_, bf16[256,1024]{1,0:T(8,128)(2,1)S(1)} %bitcast.8, ...), custom_call_target="tpu_custom_call" | custom-call | tf_op jit(solution)/shard_map/pallas_call | solution.py:398
  101.9 1.9 %collective-permute-done.21.refs_1_ = bf16[96,1024]{1,0:T(8,128)(2,1)S(1)} collective-permute-done((bf16[96,1024]{1,0:T(8,128)(2,1)S(1)}, bf16[96,1024]{1,0:T(8,128)(2,1)S(1)}, u32[]{:S(2)}, u32[]{:S(2)}) %collective-permute-start.21) | collective-permute-done | bytes 196640 | tf_op jit(solution)/shard_map/ppermute | solution.py:557
  103.8 1.2 %collective-permute-done.22.refs_2_ = bf16[96,1024]{1,0:T(8,128)(2,1)S(1)} collective-permute-done((bf16[96,1024]{1,0:T(8,128)(2,1)S(1)}, bf16[96,1024]{1,0:T(8,128)(2,1)S(1)}, u32[]{:S(2)}, u32[]{:S(2)}) %collective-permute-start.22) | collective-permute-done | bytes 196640 | tf_op jit(solution)/shard_map/ppermute | solution.py:556
  105.0 1.3 %shard_map.141 = (f32[64,1024]{1,0:T(8,128)}, bf16[1024,128]{1,0:T(8,128)(2,1)}, bf16[1024,128]{1,0:T(8,128)(2,1)}) custom-call(f32[64,1024]{1,0:T(8,128)S(1)} %get-tuple-element.67.refs_0_, bf16[96,1024]{1,0:T(8,128)(2,1)S(1)} %collective-permute-done.21.refs_1_, bf16[96,1024]{1,0:T(8,128)(2,1)S(1)} %collective-permute-done.22.refs_2_, ...), custom_call_target="tpu_custom_call" | custom-call | tf_op jit(solution)/shard_map/pallas_call | solution.py:398
  (39 shorter events, 0.1 us)
Async XLA Ops:
  0.6 18.0 %copy-start = (bf16[1024,1024]{1,0:T(8,128)(2,1)S(1)}, bf16[1024,1024]{1,0:T(8,128)(2,1)}, u32[]{:S(2)}) copy-start(bf16[1024,1024]{1,0:T(8,128)(2,1)} %refs_4_.4) | copy-start | bytes 6291460
  6.1 16.5 %collective-permute-start = (bf16[256,1024]{1,0:T(8,128)(2,1)}, bf16[256,1024]{1,0:T(8,128)(2,1)}, u32[]{:S(2)}, u32[]{:S(2)}) collective-permute-start(bf16[256,1024]{1,0:T(8,128)(2,1)} %get-tuple-element.40), channel_id=1, source_target_pairs={{0,16},{16,32},{32,48},{48,0},{64,80},{80,96},{96,112},{112,64},{1... | collective-permute-start | bytes 1572872 | tf_op jit(solution)/shard_map/ppermute | solution.py:419
  8.2 15.1 %collective-permute-start.1 = (bf16[256,1024]{1,0:T(8,128)(2,1)}, bf16[256,1024]{1,0:T(8,128)(2,1)}, u32[]{:S(2)}, u32[]{:S(2)}) collective-permute-start(bf16[256,1024]{1,0:T(8,128)(2,1)} %get-tuple-element.39.refs_2_), channel_id=1, source_target_pairs={{0,64},{16,80},{32,96},{48,112},{64,0},{80,16},{96,32},{112,48},{1... | collective-permute-start | bytes 1572872 | tf_op jit(solution)/shard_map/ppermute | solution.py:419
  9.6 13.6 %collective-permute-start.2 = (bf16[256,1024]{1,0:T(8,128)(2,1)}, bf16[256,1024]{1,0:T(8,128)(2,1)}, u32[]{:S(2)}, u32[]{:S(2)}) collective-permute-start(bf16[256,1024]{1,0:T(8,128)(2,1)} %get-tuple-element.41), channel_id=1, source_target_pairs={{0,48},{16,0},{32,16},{48,32},{64,112},{80,64},{96,80},{112,96},{1... | collective-permute-start | bytes 1572872 | tf_op jit(solution)/shard_map/ppermute | solution.py:419
  11.9 20.3 %all-to-all-start = ((bf16[16,16,1024]{2,1,0:T(8,128)(2,1)}), bf16[16,16,1024]{2,1,0:T(8,128)(2,1)}, u32[]{:S(2)}, u32[]{:S(2)}) async-start(bf16[16,16,1024]{2,1,0:T(8,128)(2,1)} %bitcast.9), calls=%async_computation | async-start | bytes 1048576 | tf_op jit(solution)/shard_map/all_to_all | solution.py:415
  18.7 1.6 %copy-start.1 = (bf16[1024,1024]{1,0:T(8,128)(2,1)S(1)}, bf16[1024,1024]{1,0:T(8,128)(2,1)}, u32[]{:S(2)}) copy-start(bf16[1024,1024]{1,0:T(8,128)(2,1)} %refs_0_.2) | copy-start | bytes 6291460
  20.3 1.0 copy-start.18
  22.5 9.6 %copy-start.3 = (bf16[1040,512]{1,0:T(8,128)(2,1)S(1)}, bf16[1040,512]{1,0:T(8,128)(2,1)}, u32[]{:S(2)}) copy-start(bf16[1040,512]{1,0:T(8,128)(2,1)} %constant.6.clone.refs_1_.first_ref) | copy-start | bytes 3194884
  22.6 9.6 %copy-start.11 = (bf16[512,256]{1,0:T(8,128)(2,1)S(1)}, bf16[512,256]{1,0:T(8,128)(2,1)}, u32[]{:S(2)}) copy-start(bf16[512,256]{1,0:T(8,128)(2,1)} %constant.7.clone.refs_2_.square_ref) | copy-start | bytes 786436
  25.4 0.8 copy-start.6
  26.2 11.4 %collective-permute-start.3 = (bf16[128,1024]{1,0:T(8,128)(2,1)}, bf16[128,1024]{1,0:T(8,128)(2,1)}, u32[]{:S(2)}, u32[]{:S(2)}) collective-permute-start(bf16[128,1024]{1,0:T(8,128)(2,1)} %get-tuple-element.43.refs_4_), channel_id=1, source_target_pairs={{0,32},{16,48},{32,0},{48,16},{64,96},{80,112},{96,64},{112,80},{1... | collective-permute-start | bytes 786440 | tf_op jit(solution)/shard_map/ppermute | solution.py:419
  29.9 7.7 %collective-permute-start.4 = (bf16[128,1024]{1,0:T(8,128)(2,1)}, bf16[128,1024]{1,0:T(8,128)(2,1)}, u32[]{:S(2)}, u32[]{:S(2)}) collective-permute-start(bf16[128,1024]{1,0:T(8,128)(2,1)} %get-tuple-element.44), channel_id=1, source_target_pairs={{0,64},{16,80},{32,96},{48,112},{64,0},{80,16},{96,32},{112,48},{1... | collective-permute-start | bytes 786440 | tf_op jit(solution)/shard_map/ppermute | solution.py:419
  32.1 5.5 %copy-start.7 = (f32[128,1024]{1,0:T(8,128)S(1)}, f32[128,1024]{1,0:T(8,128)}, u32[]{:S(2)}) copy-start(f32[128,1024]{1,0:T(8,128)} %copy-done.6) | copy-start | bytes 1572868
  32.1 5.5 %copy-start.12 = (bf16[1024,128]{1,0:T(8,128)(2,1)S(1)}, bf16[1024,128]{1,0:T(8,128)(2,1)}, u32[]{:S(2)}) copy-start(bf16[1024,128]{1,0:T(8,128)(2,1)} %refs_0_.3) | copy-start | bytes 786436
  32.1 1.0 copy-start.14
  37.6 2.5 %copy-start.16 = (bf16[1040,256]{1,0:T(8,128)(2,1)}, bf16[1040,256]{1,0:T(8,128)(2,1)S(1)}, u32[]{:S(2)}) copy-start(bf16[1040,256]{1,0:T(8,128)(2,1)S(1)} %get-tuple-element.52.h_ref) | copy-start | bytes 1597444
  37.6 8.7 %copy-start.13 = (bf16[1024,128]{1,0:T(8,128)(2,1)S(1)}, bf16[1024,128]{1,0:T(8,128)(2,1)}, u32[]{:S(2)}) copy-start(bf16[1024,128]{1,0:T(8,128)(2,1)} %refs_0_.3) | copy-start | bytes 786436
  40.1 18.6 %collective-permute-start.6 = (bf16[1024,1024]{1,0:T(8,128)(2,1)S(1)}, bf16[1024,1024]{1,0:T(8,128)(2,1)}, u32[]{:S(2)}, u32[]{:S(2)}) collective-permute-start(bf16[1024,1024]{1,0:T(8,128)(2,1)S(1)} %copy-done), channel_id=1, source_target_pairs={{0,1},{1,0},{2,3},{3,2},{4,5},{5,4},{6,7},{7,6},{8,9},{9,8},{10,11... | collective-permute-start | bytes 6291464 | tf_op jit(solution)/shard_map/ppermute | solution.py:484
  40.1 18.5 %all-to-all-start.1 = ((bf16[16,16,1024]{2,1,0:T(8,128)(2,1)}), bf16[16,16,1024]{2,1,0:T(8,128)(2,1)S(1)}, u32[]{:S(2)}, u32[]{:S(2)}) async-start(bf16[16,16,1024]{2,1,0:T(8,128)(2,1)} %bitcast.2), calls=%async_computation.1 | async-start | bytes 1048576 | tf_op jit(solution)/shard_map/all_to_all | solution.py:415
  46.5 1.5 %collective-permute-start.5 = (bf16[64,1024]{1,0:T(8,128)(2,1)S(1)}, bf16[64,1024]{1,0:T(8,128)(2,1)S(1)}, u32[]{:S(2)}, u32[]{:S(2)}) collective-permute-start(bf16[64,1024]{1,0:T(8,128)(2,1)S(1)} %get-tuple-element.49), channel_id=1, source_target_pairs={{0,1},{1,0},{2,3},{3,2},{4,5},{5,4},{6,7},{7,6},{8,9},{9,8},{10,11... | collective-permute-start | bytes 393224 | tf_op jit(solution)/shard_map/ppermute | solution.py:484
  58.7 2.8 %copy-start.4 = (bf16[1040,512]{1,0:T(8,128)(2,1)S(1)}, bf16[1040,512]{1,0:T(8,128)(2,1)}, u32[]{:S(2)}) copy-start(bf16[1040,512]{1,0:T(8,128)(2,1)} %constant.6.clone.refs_1_.first_ref) | copy-start | bytes 3194884
  58.7 2.8 %copy-start.17 = (bf16[1040,256]{1,0:T(8,128)(2,1)S(1)}, bf16[1040,256]{1,0:T(8,128)(2,1)}, u32[]{:S(2)}) copy-start(bf16[1040,256]{1,0:T(8,128)(2,1)} %copy-done.16) | copy-start | bytes 1597444
  58.9 10.9 %collective-permute-start.7 = (bf16[128,1024]{1,0:T(8,128)(2,1)S(1)}, bf16[128,1024]{1,0:T(8,128)(2,1)S(1)}, u32[]{:S(2)}, u32[]{:S(2)}) collective-permute-start(bf16[128,1024]{1,0:T(8,128)(2,1)S(1)} %get-tuple-element.51.refs_0_), channel_id=1, source_target_pairs={{0,32},{16,48},{32,0},{48,16},{64,96},{80,112},{96,64},{112,80},{1... | collective-permute-start | bytes 786440 | tf_op jit(solution)/shard_map/ppermute | solution.py:419
  60.2 9.6 %collective-permute-start.8 = (bf16[128,1024]{1,0:T(8,128)(2,1)S(1)}, bf16[128,1024]{1,0:T(8,128)(2,1)S(1)}, u32[]{:S(2)}, u32[]{:S(2)}) collective-permute-start(bf16[128,1024]{1,0:T(8,128)(2,1)S(1)} %get-tuple-element.51.refs_0_), channel_id=1, source_target_pairs={{0,64},{16,80},{32,96},{48,112},{64,0},{80,16},{96,32},{112,48},{1... | collective-permute-start | bytes 786440 | tf_op jit(solution)/shard_map/ppermute | solution.py:419
  60.8 12.9 %collective-permute-start.9 = (bf16[128,1024]{1,0:T(8,128)(2,1)S(1)}, bf16[128,1024]{1,0:T(8,128)(2,1)S(1)}, u32[]{:S(2)}, u32[]{:S(2)}) collective-permute-start(bf16[128,1024]{1,0:T(8,128)(2,1)S(1)} %get-tuple-element.51.refs_0_), channel_id=1, source_target_pairs={{0,16},{16,32},{32,48},{48,0},{64,80},{80,96},{96,112},{112,64},{1... | collective-permute-start | bytes 786440 | tf_op jit(solution)/shard_map/ppermute | solution.py:419
  61.4 11.6 %collective-permute-start.14 = (bf16[64,1024]{1,0:T(8,128)(2,1)S(1)}, bf16[64,1024]{1,0:T(8,128)(2,1)S(1)}, u32[]{:S(2)}, u32[]{:S(2)}) collective-permute-start(bf16[64,1024]{1,0:T(8,128)(2,1)S(1)} %get-tuple-element.56), channel_id=1, source_target_pairs={{0,1},{1,0},{2,3},{3,2},{4,5},{5,4},{6,7},{7,6},{8,9},{9,8},{10,11... | collective-permute-start | bytes 393224 | tf_op jit(solution)/shard_map/ppermute | solution.py:484
  61.4 0.9 copy-start.15
  65.0 9.5 %collective-permute-start.10 = (bf16[128,1024]{1,0:T(8,128)(2,1)S(1)}, bf16[128,1024]{1,0:T(8,128)(2,1)S(1)}, u32[]{:S(2)}, u32[]{:S(2)}) collective-permute-start(bf16[128,1024]{1,0:T(8,128)(2,1)S(1)} %get-tuple-element.51.refs_0_), channel_id=1, source_target_pairs={{0,48},{16,0},{32,16},{48,32},{64,112},{80,64},{96,80},{112,96},{1... | collective-permute-start | bytes 786440 | tf_op jit(solution)/shard_map/ppermute | solution.py:419
  69.8 9.5 %collective-permute-start.11 = (bf16[128,1024]{1,0:T(8,128)(2,1)S(1)}, bf16[128,1024]{1,0:T(8,128)(2,1)S(1)}, u32[]{:S(2)}, u32[]{:S(2)}) collective-permute-start(bf16[128,1024]{1,0:T(8,128)(2,1)S(1)} %collective-permute-done.8.refs_1_), channel_id=1, source_target_pairs={{0,16},{16,32},{32,48},{48,0},{64,80},{80,96},{96,112},{112,64},{1... | collective-permute-start | bytes 786440 | tf_op jit(solution)/shard_map/ppermute | solution.py:419
  69.8 10.0 %collective-permute-start.12 = (bf16[128,1024]{1,0:T(8,128)(2,1)S(1)}, bf16[128,1024]{1,0:T(8,128)(2,1)S(1)}, u32[]{:S(2)}, u32[]{:S(2)}) collective-permute-start(bf16[128,1024]{1,0:T(8,128)(2,1)S(1)} %collective-permute-done.8.refs_1_), channel_id=1, source_target_pairs={{0,48},{16,0},{32,16},{48,32},{64,112},{80,64},{96,80},{112,96},{1... | collective-permute-start | bytes 786440 | tf_op jit(solution)/shard_map/ppermute | solution.py:419
  73.0 6.8 %collective-permute-start.13 = (bf16[128,1024]{1,0:T(8,128)(2,1)S(1)}, bf16[128,1024]{1,0:T(8,128)(2,1)S(1)}, u32[]{:S(2)}, u32[]{:S(2)}) collective-permute-start(bf16[128,1024]{1,0:T(8,128)(2,1)S(1)} %collective-permute-done.7.refs_2_.refs_6_), channel_id=1, source_target_pairs={{0,64},{16,80},{32,96},{48,112},{64,0},{80,16},{96,32},{112,48},{1... | collective-permute-start | bytes 786440 | tf_op jit(solution)/shard_map/ppermute | solution.py:419
  73.8 3.8 %collective-permute-start.16 = (bf16[64,1024]{1,0:T(8,128)(2,1)S(1)}, bf16[64,1024]{1,0:T(8,128)(2,1)S(1)}, u32[]{:S(2)}, u32[]{:S(2)}) collective-permute-start(bf16[64,1024]{1,0:T(8,128)(2,1)S(1)} %get-tuple-element.59), channel_id=1, source_target_pairs={{0,1},{1,0},{2,3},{3,2},{4,5},{5,4},{6,7},{7,6},{8,9},{9,8},{10,11... | collective-permute-start | bytes 393224 | tf_op jit(solution)/shard_map/ppermute | solution.py:484
  77.4 10.7 %collective-permute-start.15 = (bf16[256,1024]{1,0:T(8,128)(2,1)S(1)}, bf16[256,1024]{1,0:T(8,128)(2,1)S(1)}, u32[]{:S(2)}, u32[]{:S(2)}) collective-permute-start(bf16[256,1024]{1,0:T(8,128)(2,1)S(1)} %get-tuple-element.57), channel_id=1, source_target_pairs={{0,1},{1,0},{2,3},{3,2},{4,5},{5,4},{6,7},{7,6},{8,9},{9,8},{10,11... | collective-permute-start | bytes 1572872 | tf_op jit(solution)/shard_map/ppermute | solution.py:484
  83.3 4.8 %collective-permute-start.17 = (bf16[256,1024]{1,0:T(8,128)(2,1)S(1)}, bf16[256,1024]{1,0:T(8,128)(2,1)S(1)}, u32[]{:S(2)}, u32[]{:S(2)}) collective-permute-start(bf16[256,1024]{1,0:T(8,128)(2,1)S(1)} %get-tuple-element.61), channel_id=1, source_target_pairs={{0,1},{1,0},{2,3},{3,2},{4,5},{5,4},{6,7},{7,6},{8,9},{9,8},{10,11... | collective-permute-start | bytes 1572872 | tf_op jit(solution)/shard_map/ppermute | solution.py:484
  83.4 11.6 %collective-permute-start.18 = (bf16[160,1024]{1,0:T(8,128)(2,1)S(1)}, bf16[160,1024]{1,0:T(8,128)(2,1)S(1)}, u32[]{:S(2)}, u32[]{:S(2)}) collective-permute-start(bf16[160,1024]{1,0:T(8,128)(2,1)S(1)} %get-tuple-element.63), channel_id=1, source_target_pairs={{0,2},{1,3},{2,0},{3,1},{4,6},{5,7},{6,4},{7,5},{8,10},{9,11},{10,... | collective-permute-start | bytes 983048 | tf_op jit(solution)/shard_map/ppermute | solution.py:556
  84.9 11.0 %collective-permute-start.19 = (bf16[160,1024]{1,0:T(8,128)(2,1)S(1)}, bf16[160,1024]{1,0:T(8,128)(2,1)S(1)}, u32[]{:S(2)}, u32[]{:S(2)}) collective-permute-start(bf16[160,1024]{1,0:T(8,128)(2,1)S(1)} %get-tuple-element.64), channel_id=1, source_target_pairs={{0,4},{1,5},{2,6},{3,7},{4,8},{5,9},{6,10},{7,11},{8,12},{9,13},{1... | collective-permute-start | bytes 983048 | tf_op jit(solution)/shard_map/ppermute | solution.py:557
  84.9 6.5 %copy-start.2 = (bf16[1024,1024]{1,0:T(8,128)(2,1)S(1)}, bf16[1024,1024]{1,0:T(8,128)(2,1)}, u32[]{:S(2)}) copy-start(bf16[1024,1024]{1,0:T(8,128)(2,1)} %refs_0_.2) | copy-start | bytes 6291460
  84.9 11.0 %collective-permute-start.20 = (bf16[160,1024]{1,0:T(8,128)(2,1)S(1)}, bf16[160,1024]{1,0:T(8,128)(2,1)S(1)}, u32[]{:S(2)}, u32[]{:S(2)}) collective-permute-start(bf16[160,1024]{1,0:T(8,128)(2,1)S(1)} %get-tuple-element.65), channel_id=1, source_target_pairs={{0,12},{1,13},{2,14},{3,15},{4,0},{5,1},{6,2},{7,3},{8,4},{9,5},{1... | collective-permute-start | bytes 983048 | tf_op jit(solution)/shard_map/ppermute | solution.py:557
  93.8 8.0 %copy-start.5 = (bf16[1024,1024]{1,0:T(8,128)(2,1)}, bf16[1024,1024]{1,0:T(8,128)(2,1)S(1)}, u32[]{:S(2)}) copy-start(bf16[1024,1024]{1,0:T(8,128)(2,1)S(1)} %convolution_convert_fusion.refs_4_) | copy-start | bytes 6291460
  93.9 5.9 %copy-start.8 = (f32[128,1024]{1,0:T(8,128)S(1)}, f32[128,1024]{1,0:T(8,128)}, u32[]{:S(2)}) copy-start(f32[128,1024]{1,0:T(8,128)} %copy-done.6) | copy-start | bytes 1572868
  95.9 9.1 %copy-start.9 = (bf16[1024,128]{1,0:T(8,128)(2,1)S(1)}, bf16[1024,128]{1,0:T(8,128)(2,1)}, u32[]{:S(2)}) copy-start(bf16[1024,128]{1,0:T(8,128)(2,1)} %refs_4_.5) | copy-start | bytes 786436
  95.9 9.1 %copy-start.10 = (bf16[1024,128]{1,0:T(8,128)(2,1)S(1)}, bf16[1024,128]{1,0:T(8,128)(2,1)}, u32[]{:S(2)}) copy-start(bf16[1024,128]{1,0:T(8,128)(2,1)} %refs_5_.1) | copy-start | bytes 786436
  96.1 7.7 %collective-permute-start.21 = (bf16[96,1024]{1,0:T(8,128)(2,1)S(1)}, bf16[96,1024]{1,0:T(8,128)(2,1)S(1)}, u32[]{:S(2)}, u32[]{:S(2)}) collective-permute-start(bf16[96,1024]{1,0:T(8,128)(2,1)S(1)} %get-tuple-element.66.refs_5_), channel_id=1, source_target_pairs={{0,8},{1,9},{2,10},{3,11},{4,12},{5,13},{6,14},{7,15},{8,0},{9,1},... | collective-permute-start | bytes 589832 | tf_op jit(solution)/shard_map/ppermute | solution.py:557
  97.6 7.4 %collective-permute-start.22 = (bf16[96,1024]{1,0:T(8,128)(2,1)S(1)}, bf16[96,1024]{1,0:T(8,128)(2,1)S(1)}, u32[]{:S(2)}, u32[]{:S(2)}) collective-permute-start(bf16[96,1024]{1,0:T(8,128)(2,1)S(1)} %get-tuple-element.68), channel_id=1, source_target_pairs={{0,2},{1,3},{2,0},{3,1},{4,6},{5,7},{6,4},{7,5},{8,10},{9,11},{10,... | collective-permute-start | bytes 589832 | tf_op jit(solution)/shard_map/ppermute | solution.py:556

commit v11 on v10

--- a/solution.py
+++ b/solution.py
@@ -242,18 +242,21 @@
     return jnp.concatenate([x[u * rows : (u + 1) * rows] for u in range(LANE_TILES)], axis=1)
 
 
-def conv_kernel(r_ref, first_ref, square_ref, twiddle_ref, z_ref, h_ref):
+def conv_kernel(r_ref, first_ref, square_ref, twiddle_ref, _, z_ref, h_hbm, h_ref, sem):
     tables = Tables(first_ref, square_ref, twiddle_ref)
     rows = z_ref.shape[0]
     group = h_ref.shape[0] // (2 * HALF)
     r = r_ref[...].astype(F32).reshape(-1, 2, group, ROW)
     u, h = (transform(r[:, s].reshape(rows, ROW).astype(BF), tables) for s in range(2))
     h_ref[...] = jnp.concatenate(h, axis=0).astype(BF)
+    store = pltpu.make_async_copy(h_ref, h_hbm, sem.at[0])
+    store.start()
     p_re, p_im = u[0] * h[0] - u[1] * h[1], u[0] * h[1] + u[1] * h[0]
     z = signal(p_re, p_im, tables).astype(BF)
     row, r = iota(0, rows), group // 2
     source = row // (4 * r) * 4 * r + row // r % 2 * 2 * r + row // (2 * r) % 2 * r + row % r
     z_ref[...] = dot((source == iota(1, rows)).astype(F32).astype(BF), z).astype(BF)
+    store.wait()
 
 
 def adjoint_kernel(r_ref, h_ref, first_ref, square_ref, twiddle_ref, away_ref, keep_ref):
@@ -497,10 +500,11 @@
     conv, spectrum = call(
         conv_kernel,
         [rows_like, shape(2 * n, FAC)],
-        [arrived, *tables],
+        [arrived, *tables, far_y],
+        [pltpu.VMEM((2 * n, FAC), BF), pltpu.SemaphoreType.DMA((1,))],
         mib=20,
         flops=3 * flops,
-        after=[far_y],
+        specs=([VMEM] * 4 + [ANY], [VMEM, ANY]),
     )
     dy = (keep_y, move_over(far_y, (0, 2)), move_over(side_y, (1, 0)))
     (send,) = call(

time: 108 us -> 107 us (level)
  no operation moved by 1% of the time
where the time goes in v11:
time: 107 us; the launch traced here: 106 us
  starting transfers between devices  41.6 us (39%)
  Pallas kernels  32.3 us (30%)
  waiting for transfers between devices  23.5 us (22%)
  local copies, waits for them, and re-layouts  5.36 us (5%)
  matrix products  2.43 us (2%)
  between operations  1.12 us (1%)
    pallas_call x14, Pallas kernels, call(): pl.pallas_call(kernel, out_shape=outs, in_specs=[*in_specs, *[ANY] * len(...  32.3 us
    ppermute x12, starting transfers between devices, move_over(): return lax.ppermute(values, 'fsdp', [(i, place(i, move)) for i in range(8)])  19.4 us
    all_to_all x2, starting transfers between devices, spread(): return lax.all_to_all(values, 'ctx', 0, 0, tiled=True)  12.9 us
    all_to_all x2, waiting for transfers between devices, spread(): return lax.all_to_all(values, 'ctx', 0, 0, tiled=True)  11.4 us
    ppermute x12, waiting for transfers between devices, move_over(): return lax.ppermute(values, 'fsdp', [(i, place(i, move)) for i in range(8)])  5.97 us
    unnamed x38, local copies, waits for them, and re-layouts  5.36 us
    ppermute x3, starting transfers between devices, on_device(): lax.ppermute(v, 'ctx', [(i, (i + 4 * step) % ways) for i in range(ways)])  4.78 us
    ppermute x2, starting transfers between devices, on_device(): over_x = lambda v: lax.ppermute(v, 'ctx', [(i, i ^ 2) for i in range(ways)])  3.61 us
  transfers between devices with their start and end apart: 25, of which 13 were waited for; matrix products, arithmetic and copies ran while one was open for 2% of the time, Pallas kernels for 21%

profile of v11, /device:TPU:0, one launch (start us, length us, event | category | flops | bytes accessed | tf_op | source)
XLA Modules:
  0.0 106.3 jit_solution(17576301548102410964)
XLA Ops:
  0.6 5.4 %shard_map.128 = (bf16[256,1024]{1,0:T(8,128)(2,1)}, bf16[256,1024]{1,0:T(8,128)(2,1)}, bf16[256,1024]{1,0:T(8,128)(2,1)}, bf16[256,1024]{1,0:T(8,128)(2,1)}) custom-call(bf16[1024,1024]{1,0:T(8,128)(2,1)} %refs_0_.2, bf16[1024,1024]{1,0:T(8,128)(2,1)} %refs_4_.4, bf16[1024,128]{1,0:T(8,128)(2,1)} %refs_4_.5, bf16[1024,128]{1,0:T(8,128)(2,1)} %refs_5_.1, ...), custom_call_target="tpu_custom_call" | custom-call | tf_op jit(solution)/shard_map/pallas_call | solution.py:401
  6.1 2.1 %collective-permute-start = (bf16[256,1024]{1,0:T(8,128)(2,1)}, bf16[256,1024]{1,0:T(8,128)(2,1)}, u32[]{:S(2)}, u32[]{:S(2)}) collective-permute-start(bf16[256,1024]{1,0:T(8,128)(2,1)} %get-tuple-element.40), channel_id=1, source_target_pairs={{0,16},{16,32},{32,48},{48,0},{64,80},{80,96},{96,112},{112,64},{1... | collective-permute-start | bytes 1572872 | tf_op jit(solution)/shard_map/ppermute | solution.py:422
  8.2 1.5 %collective-permute-start.1 = (bf16[256,1024]{1,0:T(8,128)(2,1)}, bf16[256,1024]{1,0:T(8,128)(2,1)}, u32[]{:S(2)}, u32[]{:S(2)}) collective-permute-start(bf16[256,1024]{1,0:T(8,128)(2,1)} %get-tuple-element.39.refs_2_), channel_id=1, source_target_pairs={{0,64},{16,80},{32,96},{48,112},{64,0},{80,16},{96,32},{112,48},{1... | collective-permute-start | bytes 1572872 | tf_op jit(solution)/shard_map/ppermute | solution.py:422
  9.6 2.2 %collective-permute-start.2 = (bf16[256,1024]{1,0:T(8,128)(2,1)}, bf16[256,1024]{1,0:T(8,128)(2,1)}, u32[]{:S(2)}, u32[]{:S(2)}) collective-permute-start(bf16[256,1024]{1,0:T(8,128)(2,1)} %get-tuple-element.41), channel_id=1, source_target_pairs={{0,48},{16,0},{32,16},{48,32},{64,112},{80,64},{96,80},{112,96},{1... | collective-permute-start | bytes 1572872 | tf_op jit(solution)/shard_map/ppermute | solution.py:422
  11.9 6.8 %all-to-all-start = ((bf16[16,16,1024]{2,1,0:T(8,128)(2,1)}), bf16[16,16,1024]{2,1,0:T(8,128)(2,1)}, u32[]{:S(2)}, u32[]{:S(2)}) async-start(bf16[16,16,1024]{2,1,0:T(8,128)(2,1)} %bitcast.9), calls=%async_computation | async-start | bytes 1048576 | tf_op jit(solution)/shard_map/all_to_all | solution.py:418
  18.7 0.0 copy-start.1
  18.7 1.6 %copy-done.1 = bf16[1024,1024]{1,0:T(8,128)(2,1)S(1)} copy-done((bf16[1024,1024]{1,0:T(8,128)(2,1)S(1)}, bf16[1024,1024]{1,0:T(8,128)(2,1)}, u32[]{:S(2)}) %copy-start.1) | copy-done | bytes 2097176
  20.3 1.0 copy-done.18
  21.3 1.2 %shard_map.129.own_ref = bf16[256,1024]{1,0:T(8,128)(2,1)S(1)} custom-call(bf16[1024,1024]{1,0:T(8,128)(2,1)S(1)} %copy-done.1, bf16[1024,1024]{1,0:T(8,128)(2,1)S(1)} %copy-done, bf16[256,1024]{1,0:T(8,128)(2,1)S(1)} %copy-done.18), custom_call_target="tpu_custom_call" | custom-call | tf_op jit(solution)/shard_map/pallas_call | solution.py:401
  22.5 0.0 copy-start.3
  22.6 0.0 copy-start.11
  22.6 0.6 collective-permute-done.1.x_ref
  23.2 0.0 collective-permute-done.2.down_ref
  23.2 2.2 %shard_map.130 = (f32[128,1024]{1,0:T(8,128)S(1)}, bf16[128,1024]{1,0:T(8,128)(2,1)}, bf16[128,1024]{1,0:T(8,128)(2,1)}) custom-call(bf16[256,1024]{1,0:T(8,128)(2,1)S(1)} %shard_map.129.own_ref, bf16[256,1024]{1,0:T(8,128)(2,1)} %collective-permute-done.up_ref, bf16[256,1024]{1,0:T(8,128)(2,1)} %collective-permute-done.1.x_ref, ...), custom_call_target="tpu_custom_call" | custom-call | tf_op jit(solution)/shard_map/pallas_call | solution.py:401
  25.4 0.8 copy-done.6
  26.2 3.7 %collective-permute-start.3 = (bf16[128,1024]{1,0:T(8,128)(2,1)}, bf16[128,1024]{1,0:T(8,128)(2,1)}, u32[]{:S(2)}, u32[]{:S(2)}) collective-permute-start(bf16[128,1024]{1,0:T(8,128)(2,1)} %get-tuple-element.43._), channel_id=1, source_target_pairs={{0,32},{16,48},{32,0},{48,16},{64,96},{80,112},{96,64},{112,80},{1... | collective-permute-start | bytes 786440 | tf_op jit(solution)/shard_map/ppermute | solution.py:422
  29.9 1.5 %collective-permute-start.4 = (bf16[128,1024]{1,0:T(8,128)(2,1)}, bf16[128,1024]{1,0:T(8,128)(2,1)}, u32[]{:S(2)}, u32[]{:S(2)}) collective-permute-start(bf16[128,1024]{1,0:T(8,128)(2,1)} %get-tuple-element.44), channel_id=1, source_target_pairs={{0,64},{16,80},{32,96},{48,112},{64,0},{80,16},{96,32},{112,48},{1... | collective-permute-start | bytes 786440 | tf_op jit(solution)/shard_map/ppermute | solution.py:422
  31.4 0.7 all-to-all-done
  32.1 0.0 copy-start.14
  32.1 1.0 copy-done.14
  33.1 4.7 %shard_map.131 = (bf16[128,1024]{1,0:T(8,128)(2,1)S(1)}, bf16[1040,256]{1,0:T(8,128)(2,1)S(1)}) custom-call(bf16[256,1024]{1,0:T(8,128)(2,1)} %bitcast.1.r_ref, bf16[1040,512]{1,0:T(8,128)(2,1)S(1)} %copy-done.3, bf16[512,256]{1,0:T(8,128)(2,1)S(1)} %copy-done.11, f32[130,256]{1,0:T(8,128)S(1)} %copy-done.14, bf16[128,1024]{1,0:T(8,128)(2,1)} %get-tuple-element.43._), custom_call_target="tpu_custom_call" | custom-call | tf_op jit(solution)/shard_map/pallas_call | solution.py:401
  37.8 0.0 copy-start.16
  37.8 0.0 copy-start.13
  37.9 2.4 %shard_map.132.refs_1_ = bf16[256,1024]{1,0:T(8,128)(2,1)} custom-call(f32[128,1024]{1,0:T(8,128)S(1)} %copy-done.7, bf16[128,1024]{1,0:T(8,128)(2,1)} %collective-permute-done.3.refs_1_, bf16[128,1024]{1,0:T(8,128)(2,1)} %collective-permute-done.4.refs_2_, bf16[1024,128]{1,0:T(8,128)(2,1)S(1)} %copy-done.12, bf16[128,1024]{1,0:T(8,128)(2,1)S(1)} %get-tuple-element.46.refs_4_), custom_call_target="tpu_custom_call" | custom-call | tf_op jit(solution)/shard_map/pallas_call | solution.py:401
  40.3 0.1 collective-permute-start.6
  40.4 6.1 %all-to-all-start.1 = ((bf16[16,16,1024]{2,1,0:T(8,128)(2,1)}), bf16[16,16,1024]{2,1,0:T(8,128)(2,1)S(1)}, u32[]{:S(2)}, u32[]{:S(2)}) async-start(bf16[16,16,1024]{2,1,0:T(8,128)(2,1)} %bitcast.2), calls=%async_computation.1 | async-start | bytes 1048576 | tf_op jit(solution)/shard_map/all_to_all | solution.py:418
  46.5 0.2 shard_map.133
  46.7 0.5 collective-permute-start.5
  47.2 1.0 collective-permute-done.5.refs_2_
  48.2 10.7 %all-to-all-done.1 = bf16[16,16,1024]{2,1,0:T(8,128)(2,1)S(1)} async-done(((bf16[16,16,1024]{2,1,0:T(8,128)(2,1)}), bf16[16,16,1024]{2,1,0:T(8,128)(2,1)S(1)}, u32[]{:S(2)}, u32[]{:S(2)}) %all-to-all-start.1) | async-done | bytes 524320 | tf_op jit(solution)/shard_map/all_to_all | solution.py:418
  58.9 0.3 shard_map.134
  59.1 1.1 %collective-permute-start.7 = (bf16[128,1024]{1,0:T(8,128)(2,1)S(1)}, bf16[128,1024]{1,0:T(8,128)(2,1)S(1)}, u32[]{:S(2)}, u32[]{:S(2)}) collective-permute-start(bf16[128,1024]{1,0:T(8,128)(2,1)S(1)} %get-tuple-element.51.refs_0_), channel_id=1, source_target_pairs={{0,32},{16,48},{32,0},{48,16},{64,96},{80,112},{96,64},{112,80},{1... | collective-permute-start | bytes 786440 | tf_op jit(solution)/shard_map/ppermute | solution.py:422
  60.2 0.6 collective-permute-start.8
  60.8 0.6 collective-permute-start.9
  61.4 0.0 copy-start.15
  61.5 0.9 copy-done.15
  62.4 2.7 %shard_map.135 = (bf16[64,1024]{1,0:T(8,128)(2,1)S(1)}, bf16[64,1024]{1,0:T(8,128)(2,1)S(1)}) custom-call(bf16[256,1024]{1,0:T(8,128)(2,1)S(1)} %bitcast.7, bf16[1040,256]{1,0:T(8,128)(2,1)S(1)} %copy-done.17, bf16[1040,512]{1,0:T(8,128)(2,1)S(1)} %copy-done.4, bf16[512,256]{1,0:T(8,128)(2,1)S(1)} %copy-done.11, f32[130,256]{1,0:T(8,128)S(1)} %copy-done.15), custom_call_target="tpu_custom_call" | custom-call | tf_op jit(solution)/shard_map/pallas_call | solution.py:401
  65.0 2.7 %collective-permute-start.10 = (bf16[128,1024]{1,0:T(8,128)(2,1)S(1)}, bf16[128,1024]{1,0:T(8,128)(2,1)S(1)}, u32[]{:S(2)}, u32[]{:S(2)}) collective-permute-start(bf16[128,1024]{1,0:T(8,128)(2,1)S(1)} %get-tuple-element.51.refs_0_), channel_id=1, source_target_pairs={{0,48},{16,0},{32,16},{48,32},{64,112},{80,64},{96,80},{112,96},{1... | collective-permute-start | bytes 786440 | tf_op jit(solution)/shard_map/ppermute | solution.py:422
  67.8 2.2 %collective-permute-done.7.refs_2_.refs_6_ = bf16[128,1024]{1,0:T(8,128)(2,1)S(1)} collective-permute-done((bf16[128,1024]{1,0:T(8,128)(2,1)S(1)}, bf16[128,1024]{1,0:T(8,128)(2,1)S(1)}, u32[]{:S(2)}, u32[]{:S(2)}) %collective-permute-start.7) | collective-permute-done | bytes 262176 | tf_op jit(solution)/shard_map/ppermute | solution.py:422
  70.0 3.2 %collective-permute-start.12 = (bf16[128,1024]{1,0:T(8,128)(2,1)S(1)}, bf16[128,1024]{1,0:T(8,128)(2,1)S(1)}, u32[]{:S(2)}, u32[]{:S(2)}) collective-permute-start(bf16[128,1024]{1,0:T(8,128)(2,1)S(1)} %collective-permute-done.8.refs_1_), channel_id=1, source_target_pairs={{0,48},{16,0},{32,16},{48,32},{64,112},{80,64},{96,80},{112,96},{1... | collective-permute-start | bytes 786440 | tf_op jit(solution)/shard_map/ppermute | solution.py:422
  73.3 0.2 collective-permute-start.13
  73.5 0.5 collective-permute-done.9.refs_2_
  74.0 0.4 collective-permute-done.10.refs_3_
  74.4 2.9 %shard_map.136 = (bf16[640,1024]{1,0:T(8,128)(2,1)S(1)}, bf16[256,1024]{1,0:T(8,128)(2,1)S(1)}) custom-call(bf16[128,1024]{1,0:T(8,128)(2,1)S(1)} %get-tuple-element.51.refs_0_, bf16[128,1024]{1,0:T(8,128)(2,1)S(1)} %collective-permute-done.8.refs_1_, bf16[128,1024]{1,0:T(8,128)(2,1)S(1)} %collective-permute-done.9.refs_2_, ...), custom_call_target="tpu_custom_call" | custom-call | tf_op jit(solution)/shard_map/pallas_call | solution.py:401
  77.3 0.2 collective-permute-start.15
  77.5 2.0 %collective-permute-done.11.refs_0_.refs_4_ = bf16[128,1024]{1,0:T(8,128)(2,1)S(1)} collective-permute-done((bf16[128,1024]{1,0:T(8,128)(2,1)S(1)}, bf16[128,1024]{1,0:T(8,128)(2,1)S(1)}, u32[]{:S(2)}, u32[]{:S(2)}) %collective-permute-start.11) | collective-permute-done | bytes 262176 | tf_op jit(solution)/shard_map/ppermute | solution.py:422
  79.5 0.1 collective-permute-done.12.refs_1_.refs_5_
  79.6 0.0 collective-permute-done.13.refs_3_.refs_7_
  79.6 3.5 %shard_map.137 = (bf16[160,1024]{1,0:T(8,128)(2,1)S(1)}, bf16[160,1024]{1,0:T(8,128)(2,1)S(1)}, bf16[160,1024]{1,0:T(8,128)(2,1)S(1)}, bf16[160,1024]{1,0:T(8,128)(2,1)S(1)}, bf16[256,1024]{1,0:T(8,128)(2,1)S(1)}) custom-call(bf16[128,1024]{1,0:T(8,128)(2,1)S(1)} %collective-permute-done.11.refs_0_.refs_4_, ...), custom_call_target="tpu_custom_call" | custom-call | tf_op jit(solution)/shard_map/pallas_call | solution.py:401
  83.2 0.1 collective-permute-start.17
  83.3 1.6 %collective-permute-start.18 = (bf16[160,1024]{1,0:T(8,128)(2,1)S(1)}, bf16[160,1024]{1,0:T(8,128)(2,1)S(1)}, u32[]{:S(2)}, u32[]{:S(2)}) collective-permute-start(bf16[160,1024]{1,0:T(8,128)(2,1)S(1)} %get-tuple-element.63), channel_id=1, source_target_pairs={{0,2},{1,3},{2,0},{3,1},{4,6},{5,7},{6,4},{7,5},{8,10},{9,11},{10,... | collective-permute-start | bytes 983048 | tf_op jit(solution)/shard_map/ppermute | solution.py:560
  84.8 3.2 %collective-permute-start.20 = (bf16[160,1024]{1,0:T(8,128)(2,1)S(1)}, bf16[160,1024]{1,0:T(8,128)(2,1)S(1)}, u32[]{:S(2)}, u32[]{:S(2)}) collective-permute-start(bf16[160,1024]{1,0:T(8,128)(2,1)S(1)} %get-tuple-element.65), channel_id=1, source_target_pairs={{0,12},{1,13},{2,14},{3,15},{4,0},{5,1},{6,2},{7,3},{8,4},{9,5},{1... | collective-permute-start | bytes 983048 | tf_op jit(solution)/shard_map/ppermute | solution.py:561
  88.1 3.2 %shard_map.138 = bf16[1024,1024]{1,0:T(8,128)(2,1)S(1)} custom-call(bf16[128,1024]{1,0:T(8,128)(2,1)S(1)} %get-tuple-element.51.refs_0_, bf16[128,1024]{1,0:T(8,128)(2,1)S(1)} %collective-permute-done.8.refs_1_, bf16[128,1024]{1,0:T(8,128)(2,1)S(1)} %collective-permute-done.9.refs_2_, bf16[128,1024]{1,0:T(8,128)(2,1)S(1)} %collective-permute-done.10.refs_3_, ...), custom_call_target="tpu_custom_call" | custom-call | tf_op jit(solution)/shard_map/pallas_call | solution.py:401
  91.3 2.4 %convolution_convert_fusion.refs_4_ = bf16[1024,1024]{1,0:T(8,128)(2,1)S(1)} fusion(bf16[1024,1024]{1,0:T(8,128)(2,1)S(1)} %shard_map.138, bf16[1024,1024]{1,0:T(8,128)(2,1)S(1)} %copy-done.2), kind=kOutput, calls=%fused_computation | convolution fusion | flops 2148532224 | bytes 6291456 | tf_op jit(solution)/shard_map/dot_general | solution.py:556
  93.7 0.0 copy-start.5
  93.8 1.1 %collective-permute-done.18.refs_1_ = bf16[160,1024]{1,0:T(8,128)(2,1)S(1)} collective-permute-done((bf16[160,1024]{1,0:T(8,128)(2,1)S(1)}, bf16[160,1024]{1,0:T(8,128)(2,1)S(1)}, u32[]{:S(2)}, u32[]{:S(2)}) %collective-permute-start.18) | collective-permute-done | bytes 327712 | tf_op jit(solution)/shard_map/ppermute | solution.py:560
  94.9 0.9 collective-permute-done.19.refs_2_
  95.8 0.1 shard_map.139
  96.0 1.5 %collective-permute-start.21 = (bf16[96,1024]{1,0:T(8,128)(2,1)S(1)}, bf16[96,1024]{1,0:T(8,128)(2,1)S(1)}, u32[]{:S(2)}, u32[]{:S(2)}) collective-permute-start(bf16[96,1024]{1,0:T(8,128)(2,1)S(1)} %get-tuple-element.66.refs_5_), channel_id=1, source_target_pairs={{0,8},{1,9},{2,10},{3,11},{4,12},{5,13},{6,14},{7,15},{8,0},{9,1},... | collective-permute-start | bytes 589832 | tf_op jit(solution)/shard_map/ppermute | solution.py:561
  97.5 2.1 %collective-permute-start.22 = (bf16[96,1024]{1,0:T(8,128)(2,1)S(1)}, bf16[96,1024]{1,0:T(8,128)(2,1)S(1)}, u32[]{:S(2)}, u32[]{:S(2)}) collective-permute-start(bf16[96,1024]{1,0:T(8,128)(2,1)S(1)} %get-tuple-element.68), channel_id=1, source_target_pairs={{0,2},{1,3},{2,0},{3,1},{4,6},{5,7},{6,4},{7,5},{8,10},{9,11},{10,... | collective-permute-start | bytes 589832 | tf_op jit(solution)/shard_map/ppermute | solution.py:560
  99.6 2.1 %shard_map.140 = bf16[1024,128]{1,0:T(8,128)(2,1)} custom-call(f32[128,1024]{1,0:T(8,128)S(1)} %copy-done.8, bf16[128,1024]{1,0:T(8,128)(2,1)} %collective-permute-done.3.refs_1_, bf16[128,1024]{1,0:T(8,128)(2,1)} %collective-permute-done.4.refs_2_, bf16[256,1024]{1,0:T(8,128)(2,1)S(1)} %bitcast.8, ...), custom_call_target="tpu_custom_call" | custom-call | tf_op jit(solution)/shard_map/pallas_call | solution.py:401
  101.7 2.0 %collective-permute-done.21.refs_1_ = bf16[96,1024]{1,0:T(8,128)(2,1)S(1)} collective-permute-done((bf16[96,1024]{1,0:T(8,128)(2,1)S(1)}, bf16[96,1024]{1,0:T(8,128)(2,1)S(1)}, u32[]{:S(2)}, u32[]{:S(2)}) %collective-permute-start.21) | collective-permute-done | bytes 196640 | tf_op jit(solution)/shard_map/ppermute | solution.py:561
  103.7 1.2 %collective-permute-done.22.refs_2_ = bf16[96,1024]{1,0:T(8,128)(2,1)S(1)} collective-permute-done((bf16[96,1024]{1,0:T(8,128)(2,1)S(1)}, bf16[96,1024]{1,0:T(8,128)(2,1)S(1)}, u32[]{:S(2)}, u32[]{:S(2)}) %collective-permute-start.22) | collective-permute-done | bytes 196640 | tf_op jit(solution)/shard_map/ppermute | solution.py:560
  104.9 1.3 %shard_map.141 = (f32[64,1024]{1,0:T(8,128)}, bf16[1024,128]{1,0:T(8,128)(2,1)}, bf16[1024,128]{1,0:T(8,128)(2,1)}) custom-call(f32[64,1024]{1,0:T(8,128)S(1)} %get-tuple-element.67.refs_0_, bf16[96,1024]{1,0:T(8,128)(2,1)S(1)} %collective-permute-done.21.refs_1_, bf16[96,1024]{1,0:T(8,128)(2,1)S(1)} %collective-permute-done.22.refs_2_, ...), custom_call_target="tpu_custom_call" | custom-call | tf_op jit(solution)/shard_map/pallas_call | solution.py:401
  (39 shorter events, 0.1 us)
Async XLA Ops:
  0.6 18.0 %copy-start = (bf16[1024,1024]{1,0:T(8,128)(2,1)S(1)}, bf16[1024,1024]{1,0:T(8,128)(2,1)}, u32[]{:S(2)}) copy-start(bf16[1024,1024]{1,0:T(8,128)(2,1)} %refs_4_.4) | copy-start | bytes 6291460
  6.1 16.5 %collective-permute-start = (bf16[256,1024]{1,0:T(8,128)(2,1)}, bf16[256,1024]{1,0:T(8,128)(2,1)}, u32[]{:S(2)}, u32[]{:S(2)}) collective-permute-start(bf16[256,1024]{1,0:T(8,128)(2,1)} %get-tuple-element.40), channel_id=1, source_target_pairs={{0,16},{16,32},{32,48},{48,0},{64,80},{80,96},{96,112},{112,64},{1... | collective-permute-start | bytes 1572872 | tf_op jit(solution)/shard_map/ppermute | solution.py:422
  8.2 15.1 %collective-permute-start.1 = (bf16[256,1024]{1,0:T(8,128)(2,1)}, bf16[256,1024]{1,0:T(8,128)(2,1)}, u32[]{:S(2)}, u32[]{:S(2)}) collective-permute-start(bf16[256,1024]{1,0:T(8,128)(2,1)} %get-tuple-element.39.refs_2_), channel_id=1, source_target_pairs={{0,64},{16,80},{32,96},{48,112},{64,0},{80,16},{96,32},{112,48},{1... | collective-permute-start | bytes 1572872 | tf_op jit(solution)/shard_map/ppermute | solution.py:422
  9.6 13.6 %collective-permute-start.2 = (bf16[256,1024]{1,0:T(8,128)(2,1)}, bf16[256,1024]{1,0:T(8,128)(2,1)}, u32[]{:S(2)}, u32[]{:S(2)}) collective-permute-start(bf16[256,1024]{1,0:T(8,128)(2,1)} %get-tuple-element.41), channel_id=1, source_target_pairs={{0,48},{16,0},{32,16},{48,32},{64,112},{80,64},{96,80},{112,96},{1... | collective-permute-start | bytes 1572872 | tf_op jit(solution)/shard_map/ppermute | solution.py:422
  11.9 20.3 %all-to-all-start = ((bf16[16,16,1024]{2,1,0:T(8,128)(2,1)}), bf16[16,16,1024]{2,1,0:T(8,128)(2,1)}, u32[]{:S(2)}, u32[]{:S(2)}) async-start(bf16[16,16,1024]{2,1,0:T(8,128)(2,1)} %bitcast.9), calls=%async_computation | async-start | bytes 1048576 | tf_op jit(solution)/shard_map/all_to_all | solution.py:418
  18.7 1.6 %copy-start.1 = (bf16[1024,1024]{1,0:T(8,128)(2,1)S(1)}, bf16[1024,1024]{1,0:T(8,128)(2,1)}, u32[]{:S(2)}) copy-start(bf16[1024,1024]{1,0:T(8,128)(2,1)} %refs_0_.2) | copy-start | bytes 6291460
  20.3 1.0 copy-start.18
  22.5 9.6 %copy-start.3 = (bf16[1040,512]{1,0:T(8,128)(2,1)S(1)}, bf16[1040,512]{1,0:T(8,128)(2,1)}, u32[]{:S(2)}) copy-start(bf16[1040,512]{1,0:T(8,128)(2,1)} %constant.6.clone.first_ref) | copy-start | bytes 3194884
  22.6 9.6 %copy-start.11 = (bf16[512,256]{1,0:T(8,128)(2,1)S(1)}, bf16[512,256]{1,0:T(8,128)(2,1)}, u32[]{:S(2)}) copy-start(bf16[512,256]{1,0:T(8,128)(2,1)} %constant.7.clone.square_ref) | copy-start | bytes 786436
  25.4 0.8 copy-start.6
  26.2 11.6 %collective-permute-start.3 = (bf16[128,1024]{1,0:T(8,128)(2,1)}, bf16[128,1024]{1,0:T(8,128)(2,1)}, u32[]{:S(2)}, u32[]{:S(2)}) collective-permute-start(bf16[128,1024]{1,0:T(8,128)(2,1)} %get-tuple-element.43._), channel_id=1, source_target_pairs={{0,32},{16,48},{32,0},{48,16},{64,96},{80,112},{96,64},{112,80},{1... | collective-permute-start | bytes 786440 | tf_op jit(solution)/shard_map/ppermute | solution.py:422
  29.9 7.9 %collective-permute-start.4 = (bf16[128,1024]{1,0:T(8,128)(2,1)}, bf16[128,1024]{1,0:T(8,128)(2,1)}, u32[]{:S(2)}, u32[]{:S(2)}) collective-permute-start(bf16[128,1024]{1,0:T(8,128)(2,1)} %get-tuple-element.44), channel_id=1, source_target_pairs={{0,64},{16,80},{32,96},{48,112},{64,0},{80,16},{96,32},{112,48},{1... | collective-permute-start | bytes 786440 | tf_op jit(solution)/shard_map/ppermute | solution.py:422
  32.1 5.7 %copy-start.7 = (f32[128,1024]{1,0:T(8,128)S(1)}, f32[128,1024]{1,0:T(8,128)}, u32[]{:S(2)}) copy-start(f32[128,1024]{1,0:T(8,128)} %copy-done.6) | copy-start | bytes 1572868
  32.1 5.7 %copy-start.12 = (bf16[1024,128]{1,0:T(8,128)(2,1)S(1)}, bf16[1024,128]{1,0:T(8,128)(2,1)}, u32[]{:S(2)}) copy-start(bf16[1024,128]{1,0:T(8,128)(2,1)} %refs_0_.3) | copy-start | bytes 786436
  32.1 1.0 copy-start.14
  37.8 2.5 %copy-start.16 = (bf16[1040,256]{1,0:T(8,128)(2,1)}, bf16[1040,256]{1,0:T(8,128)(2,1)S(1)}, u32[]{:S(2)}) copy-start(bf16[1040,256]{1,0:T(8,128)(2,1)S(1)} %get-tuple-element.52.h_ref) | copy-start | bytes 1597444
  37.8 8.7 %copy-start.13 = (bf16[1024,128]{1,0:T(8,128)(2,1)S(1)}, bf16[1024,128]{1,0:T(8,128)(2,1)}, u32[]{:S(2)}) copy-start(bf16[1024,128]{1,0:T(8,128)(2,1)} %refs_0_.3) | copy-start | bytes 786436
  40.3 18.6 %collective-permute-start.6 = (bf16[1024,1024]{1,0:T(8,128)(2,1)S(1)}, bf16[1024,1024]{1,0:T(8,128)(2,1)}, u32[]{:S(2)}, u32[]{:S(2)}) collective-permute-start(bf16[1024,1024]{1,0:T(8,128)(2,1)S(1)} %copy-done), channel_id=1, source_target_pairs={{0,1},{1,0},{2,3},{3,2},{4,5},{5,4},{6,7},{7,6},{8,9},{9,8},{10,11... | collective-permute-start | bytes 6291464 | tf_op jit(solution)/shard_map/ppermute | solution.py:487
  40.4 18.5 %all-to-all-start.1 = ((bf16[16,16,1024]{2,1,0:T(8,128)(2,1)}), bf16[16,16,1024]{2,1,0:T(8,128)(2,1)S(1)}, u32[]{:S(2)}, u32[]{:S(2)}) async-start(bf16[16,16,1024]{2,1,0:T(8,128)(2,1)} %bitcast.2), calls=%async_computation.1 | async-start | bytes 1048576 | tf_op jit(solution)/shard_map/all_to_all | solution.py:418
  46.7 1.5 %collective-permute-start.5 = (bf16[64,1024]{1,0:T(8,128)(2,1)S(1)}, bf16[64,1024]{1,0:T(8,128)(2,1)S(1)}, u32[]{:S(2)}, u32[]{:S(2)}) collective-permute-start(bf16[64,1024]{1,0:T(8,128)(2,1)S(1)} %get-tuple-element.49), channel_id=1, source_target_pairs={{0,1},{1,0},{2,3},{3,2},{4,5},{5,4},{6,7},{7,6},{8,9},{9,8},{10,11... | collective-permute-start | bytes 393224 | tf_op jit(solution)/shard_map/ppermute | solution.py:487
  58.9 2.6 %copy-start.4 = (bf16[1040,512]{1,0:T(8,128)(2,1)S(1)}, bf16[1040,512]{1,0:T(8,128)(2,1)}, u32[]{:S(2)}) copy-start(bf16[1040,512]{1,0:T(8,128)(2,1)} %constant.6.clone.first_ref) | copy-start | bytes 3194884
  58.9 2.6 %copy-start.17 = (bf16[1040,256]{1,0:T(8,128)(2,1)S(1)}, bf16[1040,256]{1,0:T(8,128)(2,1)}, u32[]{:S(2)}) copy-start(bf16[1040,256]{1,0:T(8,128)(2,1)} %copy-done.16) | copy-start | bytes 1597444
  59.1 10.9 %collective-permute-start.7 = (bf16[128,1024]{1,0:T(8,128)(2,1)S(1)}, bf16[128,1024]{1,0:T(8,128)(2,1)S(1)}, u32[]{:S(2)}, u32[]{:S(2)}) collective-permute-start(bf16[128,1024]{1,0:T(8,128)(2,1)S(1)} %get-tuple-element.51.refs_0_), channel_id=1, source_target_pairs={{0,32},{16,48},{32,0},{48,16},{64,96},{80,112},{96,64},{112,80},{1... | collective-permute-start | bytes 786440 | tf_op jit(solution)/shard_map/ppermute | solution.py:422
  60.2 9.8 %collective-permute-start.8 = (bf16[128,1024]{1,0:T(8,128)(2,1)S(1)}, bf16[128,1024]{1,0:T(8,128)(2,1)S(1)}, u32[]{:S(2)}, u32[]{:S(2)}) collective-permute-start(bf16[128,1024]{1,0:T(8,128)(2,1)S(1)} %get-tuple-element.51.refs_0_), channel_id=1, source_target_pairs={{0,64},{16,80},{32,96},{48,112},{64,0},{80,16},{96,32},{112,48},{1... | collective-permute-start | bytes 786440 | tf_op jit(solution)/shard_map/ppermute | solution.py:422
  60.8 13.1 %collective-permute-start.9 = (bf16[128,1024]{1,0:T(8,128)(2,1)S(1)}, bf16[128,1024]{1,0:T(8,128)(2,1)S(1)}, u32[]{:S(2)}, u32[]{:S(2)}) collective-permute-start(bf16[128,1024]{1,0:T(8,128)(2,1)S(1)} %get-tuple-element.51.refs_0_), channel_id=1, source_target_pairs={{0,16},{16,32},{32,48},{48,0},{64,80},{80,96},{96,112},{112,64},{1... | collective-permute-start | bytes 786440 | tf_op jit(solution)/shard_map/ppermute | solution.py:422
  61.4 11.8 %collective-permute-start.14 = (bf16[64,1024]{1,0:T(8,128)(2,1)S(1)}, bf16[64,1024]{1,0:T(8,128)(2,1)S(1)}, u32[]{:S(2)}, u32[]{:S(2)}) collective-permute-start(bf16[64,1024]{1,0:T(8,128)(2,1)S(1)} %get-tuple-element.56), channel_id=1, source_target_pairs={{0,1},{1,0},{2,3},{3,2},{4,5},{5,4},{6,7},{7,6},{8,9},{9,8},{10,11... | collective-permute-start | bytes 393224 | tf_op jit(solution)/shard_map/ppermute | solution.py:487
  61.4 0.9 copy-start.15
  65.0 9.3 %collective-permute-start.10 = (bf16[128,1024]{1,0:T(8,128)(2,1)S(1)}, bf16[128,1024]{1,0:T(8,128)(2,1)S(1)}, u32[]{:S(2)}, u32[]{:S(2)}) collective-permute-start(bf16[128,1024]{1,0:T(8,128)(2,1)S(1)} %get-tuple-element.51.refs_0_), channel_id=1, source_target_pairs={{0,48},{16,0},{32,16},{48,32},{64,112},{80,64},{96,80},{112,96},{1... | collective-permute-start | bytes 786440 | tf_op jit(solution)/shard_map/ppermute | solution.py:422
  70.0 9.5 %collective-permute-start.11 = (bf16[128,1024]{1,0:T(8,128)(2,1)S(1)}, bf16[128,1024]{1,0:T(8,128)(2,1)S(1)}, u32[]{:S(2)}, u32[]{:S(2)}) collective-permute-start(bf16[128,1024]{1,0:T(8,128)(2,1)S(1)} %collective-permute-done.8.refs_1_), channel_id=1, source_target_pairs={{0,16},{16,32},{32,48},{48,0},{64,80},{80,96},{96,112},{112,64},{1... | collective-permute-start | bytes 786440 | tf_op jit(solution)/shard_map/ppermute | solution.py:422
  70.0 9.6 %collective-permute-start.12 = (bf16[128,1024]{1,0:T(8,128)(2,1)S(1)}, bf16[128,1024]{1,0:T(8,128)(2,1)S(1)}, u32[]{:S(2)}, u32[]{:S(2)}) collective-permute-start(bf16[128,1024]{1,0:T(8,128)(2,1)S(1)} %collective-permute-done.8.refs_1_), channel_id=1, source_target_pairs={{0,48},{16,0},{32,16},{48,32},{64,112},{80,64},{96,80},{112,96},{1... | collective-permute-start | bytes 786440 | tf_op jit(solution)/shard_map/ppermute | solution.py:422
  73.3 6.4 %collective-permute-start.13 = (bf16[128,1024]{1,0:T(8,128)(2,1)S(1)}, bf16[128,1024]{1,0:T(8,128)(2,1)S(1)}, u32[]{:S(2)}, u32[]{:S(2)}) collective-permute-start(bf16[128,1024]{1,0:T(8,128)(2,1)S(1)} %collective-permute-done.7.refs_2_.refs_6_), channel_id=1, source_target_pairs={{0,64},{16,80},{32,96},{48,112},{64,0},{80,16},{96,32},{112,48},{1... | collective-permute-start | bytes 786440 | tf_op jit(solution)/shard_map/ppermute | solution.py:422
  74.0 3.5 %collective-permute-start.16 = (bf16[64,1024]{1,0:T(8,128)(2,1)S(1)}, bf16[64,1024]{1,0:T(8,128)(2,1)S(1)}, u32[]{:S(2)}, u32[]{:S(2)}) collective-permute-start(bf16[64,1024]{1,0:T(8,128)(2,1)S(1)} %get-tuple-element.59), channel_id=1, source_target_pairs={{0,1},{1,0},{2,3},{3,2},{4,5},{5,4},{6,7},{7,6},{8,9},{9,8},{10,11... | collective-permute-start | bytes 393224 | tf_op jit(solution)/shard_map/ppermute | solution.py:487
  77.3 10.8 %collective-permute-start.15 = (bf16[256,1024]{1,0:T(8,128)(2,1)S(1)}, bf16[256,1024]{1,0:T(8,128)(2,1)S(1)}, u32[]{:S(2)}, u32[]{:S(2)}) collective-permute-start(bf16[256,1024]{1,0:T(8,128)(2,1)S(1)} %get-tuple-element.57), channel_id=1, source_target_pairs={{0,1},{1,0},{2,3},{3,2},{4,5},{5,4},{6,7},{7,6},{8,9},{9,8},{10,11... | collective-permute-start | bytes 1572872 | tf_op jit(solution)/shard_map/ppermute | solution.py:487
  83.2 4.9 %collective-permute-start.17 = (bf16[256,1024]{1,0:T(8,128)(2,1)S(1)}, bf16[256,1024]{1,0:T(8,128)(2,1)S(1)}, u32[]{:S(2)}, u32[]{:S(2)}) collective-permute-start(bf16[256,1024]{1,0:T(8,128)(2,1)S(1)} %get-tuple-element.61), channel_id=1, source_target_pairs={{0,1},{1,0},{2,3},{3,2},{4,5},{5,4},{6,7},{7,6},{8,9},{9,8},{10,11... | collective-permute-start | bytes 1572872 | tf_op jit(solution)/shard_map/ppermute | solution.py:487
  83.3 11.6 %collective-permute-start.18 = (bf16[160,1024]{1,0:T(8,128)(2,1)S(1)}, bf16[160,1024]{1,0:T(8,128)(2,1)S(1)}, u32[]{:S(2)}, u32[]{:S(2)}) collective-permute-start(bf16[160,1024]{1,0:T(8,128)(2,1)S(1)} %get-tuple-element.63), channel_id=1, source_target_pairs={{0,2},{1,3},{2,0},{3,1},{4,6},{5,7},{6,4},{7,5},{8,10},{9,11},{10,... | collective-permute-start | bytes 983048 | tf_op jit(solution)/shard_map/ppermute | solution.py:560
  84.8 11.0 %collective-permute-start.19 = (bf16[160,1024]{1,0:T(8,128)(2,1)S(1)}, bf16[160,1024]{1,0:T(8,128)(2,1)S(1)}, u32[]{:S(2)}, u32[]{:S(2)}) collective-permute-start(bf16[160,1024]{1,0:T(8,128)(2,1)S(1)} %get-tuple-element.64), channel_id=1, source_target_pairs={{0,4},{1,5},{2,6},{3,7},{4,8},{5,9},{6,10},{7,11},{8,12},{9,13},{1... | collective-permute-start | bytes 983048 | tf_op jit(solution)/shard_map/ppermute | solution.py:561
  84.8 6.5 %copy-start.2 = (bf16[1024,1024]{1,0:T(8,128)(2,1)S(1)}, bf16[1024,1024]{1,0:T(8,128)(2,1)}, u32[]{:S(2)}) copy-start(bf16[1024,1024]{1,0:T(8,128)(2,1)} %refs_0_.2) | copy-start | bytes 6291460
  84.8 11.0 %collective-permute-start.20 = (bf16[160,1024]{1,0:T(8,128)(2,1)S(1)}, bf16[160,1024]{1,0:T(8,128)(2,1)S(1)}, u32[]{:S(2)}, u32[]{:S(2)}) collective-permute-start(bf16[160,1024]{1,0:T(8,128)(2,1)S(1)} %get-tuple-element.65), channel_id=1, source_target_pairs={{0,12},{1,13},{2,14},{3,15},{4,0},{5,1},{6,2},{7,3},{8,4},{9,5},{1... | collective-permute-start | bytes 983048 | tf_op jit(solution)/shard_map/ppermute | solution.py:561
  93.7 7.9 %copy-start.5 = (bf16[1024,1024]{1,0:T(8,128)(2,1)}, bf16[1024,1024]{1,0:T(8,128)(2,1)S(1)}, u32[]{:S(2)}) copy-start(bf16[1024,1024]{1,0:T(8,128)(2,1)S(1)} %convolution_convert_fusion.refs_4_) | copy-start | bytes 6291460
  93.8 5.8 %copy-start.8 = (f32[128,1024]{1,0:T(8,128)S(1)}, f32[128,1024]{1,0:T(8,128)}, u32[]{:S(2)}) copy-start(f32[128,1024]{1,0:T(8,128)} %copy-done.6) | copy-start | bytes 1572868
  95.8 9.1 %copy-start.9 = (bf16[1024,128]{1,0:T(8,128)(2,1)S(1)}, bf16[1024,128]{1,0:T(8,128)(2,1)}, u32[]{:S(2)}) copy-start(bf16[1024,128]{1,0:T(8,128)(2,1)} %refs_4_.5) | copy-start | bytes 786436
  95.8 9.1 %copy-start.10 = (bf16[1024,128]{1,0:T(8,128)(2,1)S(1)}, bf16[1024,128]{1,0:T(8,128)(2,1)}, u32[]{:S(2)}) copy-start(bf16[1024,128]{1,0:T(8,128)(2,1)} %refs_5_.1) | copy-start | bytes 786436
  96.0 7.7 %collective-permute-start.21 = (bf16[96,1024]{1,0:T(8,128)(2,1)S(1)}, bf16[96,1024]{1,0:T(8,128)(2,1)S(1)}, u32[]{:S(2)}, u32[]{:S(2)}) collective-permute-start(bf16[96,1024]{1,0:T(8,128)(2,1)S(1)} %get-tuple-element.66.refs_5_), channel_id=1, source_target_pairs={{0,8},{1,9},{2,10},{3,11},{4,12},{5,13},{6,14},{7,15},{8,0},{9,1},... | collective-permute-start | bytes 589832 | tf_op jit(solution)/shard_map/ppermute | solution.py:561
  97.5 7.4 %collective-permute-start.22 = (bf16[96,1024]{1,0:T(8,128)(2,1)S(1)}, bf16[96,1024]{1,0:T(8,128)(2,1)S(1)}, u32[]{:S(2)}, u32[]{:S(2)}) collective-permute-start(bf16[96,1024]{1,0:T(8,128)(2,1)S(1)} %get-tuple-element.68), channel_id=1, source_target_pairs={{0,2},{1,3},{2,0},{3,1},{4,6},{5,7},{6,4},{7,5},{8,10},{9,11},{10,... | collective-permute-start | bytes 589832 | tf_op jit(solution)/shard_map/ppermute | solution.py:560
